TPU v7x, 32 devices: a whole 2x2x4 slice. The times are simulated.
32 devices in a mesh: dp: 16 (over z, x, core), tensor: 2 (over y).
Axes of the slice: x: 2, y: 2, z: 4, core: 2. Of those that a mesh axis runs over, the one named last changes fastest.
Arguments:
- block_in: bfloat16 [4096, 768], P(('dp', 'tensor')), may hold values from -6 to 6
- attn_gain: float32 [768], replicated, may hold values from 0.5 to 1.5
- w_qkv: bfloat16 [768, 3, 768], P('dp', None, 'tensor'), may hold values from -0.21875 to 0.21875
- w_out: bfloat16 [768, 768], P('dp', 'tensor'), may hold values from -0.875 to 0.875
- rel_bias: float32 [32, 12], replicated, may hold values from -4 to 4
- moe_gain: float32 [768], replicated, may hold values from 0.5 to 1.5
- w_router: float32 [768, 2], replicated, may hold values from -0.15625 to 0.15625
- w_in: bfloat16 [768, 2, 3072], P('dp', None, 'tensor'), may hold values from -0.21875 to 0.21875
- w_down: bfloat16 [768, 2, 3072], P('dp', None, 'tensor'), may hold values from -0.3125 to 0.3125
- seq_lengths: int32 [16, 4], P('dp'), may hold values from 0 to 256, as said below
- expert_ids: int32 [4096, 1], P('dp'), may hold values from 0 to 1; in each aligned block of 256 rows (0 to 255, 256 to 511, ...) at most 168 rows name the same one
- rel_table: int32 [511], replicated, may hold values from 0 to 31
- out_grad: bfloat16 [4096, 768], P(('dp', 'tensor')), may hold values from -6 to 6
Outputs:
- block_out: bfloat16 [4096, 768], P(('dp', 'tensor'))
- grad_in: float32 [4096, 768], P(('dp', 'tensor'))
- grad_attn_gain: float32 [768], replicated
- grad_w_qkv: float32 [768, 3, 768], P('dp', None, 'tensor')
- grad_w_out: float32 [768, 768], P('dp', 'tensor')
- grad_rel_bias: float32 [32, 12], replicated
- grad_moe_gain: float32 [768], replicated
- grad_w_router: float32 [768, 2], replicated
- grad_w_in: float32 [768, 2, 3072], P('dp', None, 'tensor')
- grad_w_down: float32 [768, 2, 3072], P('dp', None, 'tensor')
Inputs may be any that keep to these rules, and one draw needn't show every extreme that they name: `seq_lengths`: in each group the 4 lengths sum to 256, and the first is more than 128. In every draw some group holds one sequence of 256 tokens. `expert_ids`: among the 256 rows of one group no expert is named by more than 168 rows.
All inputs are finite; a program needn't handle non-finite values.
Results may differ from a plain program's by a relative error of at most 0.018.
Values may be sent and summed in bfloat16 or wider, within the bound.
No kernel may reach another device: no remote copies, remote signals or barrier semaphores. Data moves between devices by JAX's collectives and lax.ppermute only.
A program may use at most 192 MiB of HBM per device.

v0:
```python
from functools import partial

import jax
import jax.numpy as jnp
from jax import lax
from jax.sharding import PartitionSpec as P

HEAD_DIM = 64
EXPERTS = 2
CAP = 168


EPS = 1e-06
NEG = -1e30
HIGH = lax.Precision.HIGHEST


def rms_scale(rows):
    return lax.rsqrt(jnp.mean(rows * rows, axis=-1, keepdims=True) + EPS)


def norm_back(grad, normed, scale, gain):
    weighted = grad * gain
    return scale * (weighted - normed * jnp.mean(weighted * normed, axis=-1, keepdims=True))


def slot_flat(expert_col, capacity):
    hits = (expert_col[:, None] == jnp.arange(EXPERTS, dtype=jnp.int32)[None, :]).astype(jnp.int32)
    running = jnp.cumsum(hits, axis=0)
    slot = jnp.sum(running * hits, axis=1) - 1
    return expert_col * capacity + slot


def toeplitz_rows(by_offset_heads, count):
    heads_here = by_offset_heads.shape[0]
    padded = jnp.concatenate(
        [by_offset_heads, jnp.zeros((heads_here, 1), by_offset_heads.dtype)], axis=1
    )
    tiled = jnp.tile(padded, (1, count))
    window = tiled[:, count - 1 : count - 1 + count * (2 * count - 1)]
    return window.reshape(heads_here, count, 2 * count - 1)[:, :, :count]


def diagonal_sums(matrix):
    heads_here, count, _ = matrix.shape
    widened = jnp.concatenate(
        [matrix, jnp.zeros((heads_here, count, count - 1), matrix.dtype)], axis=2
    )
    line = widened.reshape(heads_here, count * (2 * count - 1))
    line = jnp.concatenate(
        [
            jnp.zeros((heads_here, count - 1), matrix.dtype),
            line,
            jnp.zeros((heads_here, 1), matrix.dtype),
        ],
        axis=1,
    )
    return jnp.sum(line.reshape(heads_here, count, 2 * count), axis=1)[:, : 2 * count - 1]


def as_rows(first, second, groups):
    return jnp.concatenate([first.reshape(groups, -1), second.reshape(groups, -1)], axis=1)


def from_rows(summed, first_shape, second_shape):
    line = summed.reshape(-1)
    first_size = 1
    for extent in first_shape:
        first_size = first_size * extent
    return (line[:first_size].reshape(first_shape), line[first_size:].reshape(second_shape))


def body(
    block_in,
    attn_gain,
    w_qkv,
    w_out,
    rel_bias,
    moe_gain,
    w_router,
    w_in,
    w_down,
    seq_lengths,
    expert_ids,
    rel_table,
    out_grad,
):
    rows_local = block_in.shape[0]
    tensor_rank = lax.axis_index("tensor")
    groups = lax.axis_size("dp")
    residual = block_in.astype(jnp.float32)
    scale_one = rms_scale(residual)
    normed_one = residual * scale_one
    gathered_one = lax.all_gather(
        (normed_one * attn_gain).astype(jnp.bfloat16), "tensor", axis=0, tiled=True
    )
    rows_all = gathered_one.shape[0]
    w_qkv_all, w_out_all = (
        lax.all_gather(w_qkv, "dp", axis=0, tiled=True),
        lax.all_gather(w_out, "dp", axis=0, tiled=True),
    )
    heads_local = w_out_all.shape[1] // HEAD_DIM
    projected = jnp.einsum(
        "td,dsk->stk", gathered_one, w_qkv_all, preferred_element_type=jnp.float32
    ).astype(jnp.bfloat16)
    queries = projected[0].reshape(rows_all, heads_local, HEAD_DIM)
    keys_all = projected[1].reshape(rows_all, heads_local, HEAD_DIM)
    values_all = projected[2].reshape(rows_all, heads_local, HEAD_DIM)
    places = jnp.arange(rows_all, dtype=jnp.int32)
    ends = jnp.cumsum(seq_lengths[0])
    seq_ids = jnp.sum((places[:, None] >= ends[None, :]).astype(jnp.int32), axis=1)
    same_seq = seq_ids[:, None] == seq_ids[None, :]
    bucket_count = rel_bias.shape[0]
    bias_local = lax.dynamic_slice_in_dim(rel_bias, tensor_rank * heads_local, heads_local, 1)
    bucket_hits = (rel_table[:, None] == jnp.arange(bucket_count, dtype=jnp.int32)[None, :]).astype(
        jnp.float32
    )
    by_offset = jnp.dot(bucket_hits, bias_local, precision=HIGH)
    bias = toeplitz_rows(by_offset.T, rows_all)
    scale = HEAD_DIM ** (-0.5)

    def scores_of(query_part):
        raw = (
            jnp.einsum("qhd,khd->hqk", query_part, keys_all, preferred_element_type=jnp.float32)
            * scale
            + bias
        )
        return jnp.where(same_seq[None], raw, NEG)

    scores = scores_of(queries)
    row_max = jnp.max(scores, axis=-1, keepdims=True)
    expo = jnp.exp(scores - row_max)
    total = jnp.sum(expo, axis=-1, keepdims=True)
    probs = (expo / total).astype(jnp.bfloat16)
    log_total = row_max + jnp.log(total)
    context = jnp.einsum("hqk,khd->qhd", probs, values_all, preferred_element_type=jnp.float32)
    context = context.reshape(rows_all, heads_local * HEAD_DIM).astype(jnp.bfloat16)
    attn_part = jnp.einsum("tk,dk->td", context, w_out_all, preferred_element_type=jnp.float32)
    attended = lax.psum_scatter(
        attn_part.astype(jnp.bfloat16), "tensor", scatter_dimension=0, tiled=True
    ).astype(jnp.float32)
    hidden = residual + attended
    scale_two = rms_scale(hidden)
    normed_two = hidden * scale_two
    mixed = normed_two * moe_gain
    router_probs = jax.nn.softmax(jnp.dot(mixed, w_router, precision=HIGH), axis=-1)
    expert_col = expert_ids[:, 0]
    own_experts = lax.dynamic_slice_in_dim(expert_col, tensor_rank * rows_local, rows_local)
    own_hits = (own_experts[:, None] == jnp.arange(EXPERTS, dtype=jnp.int32)[None, :]).astype(
        jnp.float32
    )
    gate = jnp.sum(router_probs * own_hits, axis=1)
    gathered_two = lax.all_gather(mixed.astype(jnp.bfloat16), "tensor", axis=0, tiled=True)
    flat = slot_flat(expert_col, CAP)
    dispatch_low = (flat[:, None] == jnp.arange(EXPERTS * CAP, dtype=jnp.int32)[None, :]).astype(
        jnp.bfloat16
    )
    dispatch_full = dispatch_low.astype(jnp.float32)
    blocks = (
        jnp.dot(dispatch_low.T, gathered_two, preferred_element_type=jnp.float32)
        .astype(jnp.bfloat16)
        .reshape(EXPERTS, CAP, -1)
    )
    w_in_all, w_down_all = (
        lax.all_gather(w_in, "dp", axis=0, tiled=True),
        lax.all_gather(w_down, "dp", axis=0, tiled=True),
    )
    pre = jnp.einsum("ecd,def->ecf", blocks, w_in_all, preferred_element_type=jnp.float32)
    active = jax.nn.gelu(pre, approximate=True).astype(jnp.bfloat16)
    returned = jnp.einsum("ecf,def->ecd", active, w_down_all, preferred_element_type=jnp.float32)
    routed_part = jnp.dot(dispatch_full, returned.reshape(EXPERTS * CAP, -1), precision=HIGH)
    routed = lax.psum_scatter(
        routed_part.astype(jnp.bfloat16), "tensor", scatter_dimension=0, tiled=True
    ).astype(jnp.float32)
    result = hidden + gate[:, None] * routed
    grad_out = out_grad.astype(jnp.float32)
    grad_routed = (gate[:, None] * grad_out).astype(jnp.bfloat16)
    grad_gate = jnp.sum(grad_out * routed, axis=1)
    grad_gathered = lax.all_gather(grad_routed, "tensor", axis=0, tiled=True)
    grad_blocks = (
        jnp.dot(dispatch_low.T, grad_gathered, preferred_element_type=jnp.float32)
        .astype(jnp.bfloat16)
        .reshape(EXPERTS, CAP, -1)
    )
    w_qkv_back, w_out_back, w_in_back, w_down_back = (
        lax.all_gather(w_qkv, "dp", axis=0, tiled=True),
        lax.all_gather(w_out, "dp", axis=0, tiled=True),
        lax.all_gather(w_in, "dp", axis=0, tiled=True),
        lax.all_gather(w_down, "dp", axis=0, tiled=True),
    )
    grad_active = jnp.einsum(
        "ecd,def->ecf", grad_blocks, w_down_back, preferred_element_type=jnp.float32
    )
    grad_w_down = jnp.einsum(
        "ecd,ecf->def", grad_blocks, active, preferred_element_type=jnp.float32
    )
    _, gelu_pull = jax.vjp(partial(jax.nn.gelu, approximate=True), pre)
    grad_pre = gelu_pull(grad_active)[0].astype(jnp.bfloat16)
    grad_w_in = jnp.einsum("ecd,ecf->def", blocks, grad_pre, preferred_element_type=jnp.float32)
    expert_summed = lax.psum_scatter(
        as_rows(grad_w_in, grad_w_down, groups), "dp", scatter_dimension=0, tiled=True
    )
    grad_w_in_mine, grad_w_down_mine = from_rows(expert_summed, w_in.shape, w_down.shape)
    grad_sent = jnp.einsum("ecf,def->ecd", grad_pre, w_in_back, preferred_element_type=jnp.float32)
    grad_sent_rows = jnp.dot(dispatch_full, grad_sent.reshape(EXPERTS * CAP, -1), precision=HIGH)
    grad_mixed_share = lax.psum_scatter(
        grad_sent_rows.astype(jnp.bfloat16), "tensor", scatter_dimension=0, tiled=True
    ).astype(jnp.float32)
    grad_logits = (grad_gate * gate)[:, None] * (own_hits - router_probs)
    grad_router = jnp.dot(mixed.T, grad_logits, precision=HIGH)
    grad_mixed = grad_mixed_share + jnp.dot(grad_logits, w_router.T, precision=HIGH)
    grad_moe_gain = jnp.sum(grad_mixed * normed_two, axis=0)
    grad_hidden = grad_out + norm_back(grad_mixed, normed_two, scale_two, moe_gain)
    grad_attended = lax.all_gather(grad_hidden.astype(jnp.bfloat16), "tensor", axis=0, tiled=True)
    grad_context = jnp.einsum(
        "td,dk->tk", grad_attended, w_out_back, preferred_element_type=jnp.float32
    ).astype(jnp.bfloat16)
    grad_w_out = jnp.einsum("td,tk->dk", grad_attended, context, preferred_element_type=jnp.float32)
    grad_context_heads = grad_context.reshape(rows_all, heads_local, HEAD_DIM)
    probs_back = jnp.exp(scores_of(queries) - log_total)
    grad_probs = jnp.einsum(
        "qhd,khd->hqk", grad_context_heads, values_all, preferred_element_type=jnp.float32
    )
    inner = jnp.sum(probs_back * grad_probs, axis=-1, keepdims=True)
    grad_scores = (probs_back * (grad_probs - inner)).astype(jnp.bfloat16)
    grad_queries = (
        jnp.einsum("hqk,khd->qhd", grad_scores, keys_all, preferred_element_type=jnp.float32)
        * scale
    )
    grad_keys = (
        jnp.einsum("hqk,qhd->khd", grad_scores, queries, preferred_element_type=jnp.float32) * scale
    )
    grad_values = jnp.einsum(
        "hqk,qhd->khd",
        probs_back.astype(jnp.bfloat16),
        grad_context_heads,
        preferred_element_type=jnp.float32,
    )
    grad_projected = (
        jnp.stack([grad_queries, grad_keys, grad_values])
        .reshape(3, rows_all, -1)
        .astype(jnp.bfloat16)
    )
    grad_w_qkv = jnp.einsum(
        "td,stk->dsk", gathered_one, grad_projected, preferred_element_type=jnp.float32
    )
    grad_normed_part = jnp.einsum(
        "stk,dsk->td", grad_projected, w_qkv_back, preferred_element_type=jnp.float32
    )
    attn_summed = lax.psum_scatter(
        as_rows(grad_w_qkv, grad_w_out, groups), "dp", scatter_dimension=0, tiled=True
    )
    grad_w_qkv_mine, grad_w_out_mine = from_rows(attn_summed, w_qkv.shape, w_out.shape)
    grad_normed = lax.psum_scatter(
        grad_normed_part.astype(jnp.bfloat16), "tensor", scatter_dimension=0, tiled=True
    ).astype(jnp.float32)
    grad_attn_gain = jnp.sum(grad_normed * normed_one, axis=0)
    grad_block = grad_hidden + norm_back(grad_normed, normed_one, scale_one, attn_gain)
    offset_sums = diagonal_sums(grad_scores.astype(jnp.float32))
    grad_bias_heads = jnp.dot(offset_sums, bucket_hits, precision=HIGH)
    grad_rel_full = lax.dynamic_update_slice_in_dim(
        jnp.zeros(rel_bias.shape, jnp.float32), grad_bias_heads.T, tensor_rank * heads_local, 1
    )
    summed = lax.psum((grad_attn_gain, grad_rel_full, grad_moe_gain, grad_router), ("dp", "tensor"))
    return (
        result.astype(jnp.bfloat16),
        grad_block,
        summed[0],
        grad_w_qkv_mine,
        grad_w_out_mine,
        summed[1],
        summed[2],
        summed[3],
        grad_w_in_mine,
        grad_w_down_mine,
    )


def solution(mesh):
    placed = (
        P(("dp", "tensor"), None),
        P(),
        P("dp", None, "tensor"),
        P("dp", "tensor"),
        P(),
        P(),
        P(),
        P("dp", None, "tensor"),
        P("dp", None, "tensor"),
        P("dp", None),
        P("dp", None),
        P(),
        P(("dp", "tensor"), None),
    )
    return jax.shard_map(
        body,
        mesh=mesh,
        in_specs=placed,
        out_specs=(
            P(("dp", "tensor"), None),
            P(("dp", "tensor"), None),
            P(),
            P("dp", None, "tensor"),
            P("dp", "tensor"),
            P(),
            P(),
            P(),
            P("dp", None, "tensor"),
            P("dp", None, "tensor"),
        ),
        check_vma=False,
    )
```

profile of v0, /device:TPU:0, one launch (start us, length us, event | category | flops | bytes accessed | tf_op | source)
XLA Modules:
  0.0 778.0 jit_solution(4715739377143249571)
XLA Ops:
  8.0 1.0 fusion.39
  9.4 1.9 copy.108
  11.3 3.1 slice.55
  14.4 4.8 reshape.223
  19.2 1.3 slice.56
  20.5 3.1 copy.107
  24.0 8.5 %all_gather.28 = bf16[256,768]{1,0:T(8,128)(2,1)S(1)} all-gather(bf16[128,768]{1,0:T(8,128)(2,1)S(1)} %fusion.24), channel_id=1, replica_groups=mesh['dp'=16,'tensor'=2] {'tensor'}, dimensions={0}, use_global_device_ids=true | all-gather | bytes 589824 | tf_op jit(solution)/shard_map/all_gather | solution.py:94
  32.8 25.0 %all_gather.30 = bf16[768,384]{1,0:T(8,128)(2,1)S(1)} all-gather(bf16[48,384]{1,0:T(8,128)(2,1)S(1)} %copy-done.25), channel_id=1, replica_groups=mesh['dp'=16,'tensor'=2] {'dp'}, dimensions={0}, use_global_device_ids=true | all-gather | bytes 626688 | tf_op jit(solution)/shard_map/all_gather | solution.py:100
  57.7 2.2 fusion.9
  60.5 1.9 fusion.62
  63.1 1.1 convolution_convert_fusion.5
  65.1 1.7 copy.87
  68.0 6.5 reduce-scatter.5.cloned.1.call-done
  74.6 1.1 multiply_reduce_fusion.3
  75.7 1.0 multiply_convert_fusion.2
  76.7 7.8 all_gather.31
  84.9 45.5 %all-gather.6.cloned.1.call-done = bf16[768,2,1536]{2,0,1:T(8,128)(2,1)} async-done(((bf16[48,2,1536]{2,0,1:T(8,128)(2,1)}), bf16[768,2,1536]{2,0,1:T(8,128)(2,1)}) %all-gather.6.cloned.1.call-update) | async-done | bytes 4718608 | tf_op jit(solution)/shard_map/all_gather | solution.py:165
  130.4 4.7 fusion.64
  135.1 50.1 %all-gather.8.cloned.1.call-done = bf16[768,2,1536]{2,0,1:T(8,128)(2,1)} async-done(((bf16[48,2,1536]{2,0,1:T(8,128)(2,1)}), bf16[768,2,1536]{2,0,1:T(8,128)(2,1)}) %all-gather.8.cloned.1.call-update) | async-done | bytes 4718608 | tf_op jit(solution)/shard_map/all_gather | solution.py:166
  185.2 4.7 fusion.59
  189.9 1.7 convolution_convert_fusion.4
  192.3 11.1 %reduce-scatter.7.cloned.1.call-done = bf16[128,768]{1,0:T(8,128)(2,1)} async-done(((bf16[256,768]{1,0:T(8,128)(2,1)}), bf16[128,768]{1,0:T(8,128)(2,1)}) %reduce-scatter.7.cloned.1.call-update) | async-done | bytes 196624 | tf_op jit(solution)/shard_map/reduce_scatter | solution.py:172
  203.4 1.3 fusion.29
  204.7 7.3 all_gather.34
  212.5 5.2 convolution_bitcast_fusion
  217.6 4.2 fusion.6
  221.8 5.1 convolution_bitcast_fusion.1
  227.0 1.7 fusion.65
  228.7 1.7 convolution_convert_fusion.3
  230.6 14.9 %copy.99 = f32[768,2,1536]{2,1,0:T(2,128)} copy(f32[768,2,1536]{0,2,1:T(8,128)} %convolution_bitcast_fusion) | data formatting | bytes 18874368 | tf_op jit(solution)/shard_map/ecd,ecf->def/transpose | solution.py:194
  245.5 17.2 %reshape.238 = f32[16,147456]{1,0:T(8,128)} reshape(f32[768,2,1536]{2,1,0:T(2,128)} %copy.99) | data formatting | bytes 18874368 | tf_op jit(solution)/shard_map/reshape | solution.py:62
  262.6 14.9 %copy.98 = f32[768,2,1536]{2,1,0:T(2,128)} copy(f32[768,2,1536]{0,2,1:T(8,128)} %convolution_bitcast_fusion.1) | data formatting | bytes 18874368 | tf_op jit(solution)/shard_map/ecd,ecf->def/transpose | solution.py:199
  277.6 17.1 %reshape.237 = f32[16,147456]{1,0:T(8,128)} reshape(f32[768,2,1536]{2,1,0:T(2,128)} %copy.98) | data formatting | bytes 18874368 | tf_op jit(solution)/shard_map/reshape | solution.py:62
  294.7 15.7 %pad_maximum_fusion = f32[16,294912]{1,0:T(8,128)} fusion(f32[16,147456]{1,0:T(8,128)} %reshape.238, f32[16,147456]{1,0:T(8,128)} %reshape.237), kind=kLoop, calls=%fused_computation | loop fusion | flops 4718592 | bytes 37748736 | tf_op jit(solution)/shard_map/concatenate | solution.py:62
  310.5 2.2 multiply_reduce_fusion.1
  312.9 6.8 all_gather.35
  319.8 1.1 convolution_convert_fusion.7
  320.8 1.1 copy.88
  324.4 1.4 fusion.66
  325.8 0.8 copy.94
  326.6 0.8 copy.93
  328.3 2.1 fusion.30
  330.4 1.5 fusion.8
  331.9 2.5 reshape.231
  334.4 4.6 copy.96
  339.0 3.6 reshape.230
  342.6 3.7 pad_maximum_fusion.1
  347.6 1.3 dynamic-update-slice
  348.9 1.0 fusion.34
  349.9 2.0 pad_convert_fusion
  351.9 2.4 copy.97
  354.3 4.7 reshape.242
  359.1 12.3 %dynamic-update-slice.1 = f32[6,131072]{1,0:T(8,128)} dynamic-update-slice(f32[6,131072]{1,0:T(8,128)} %dynamic-update-slice, f32[6,130816]{1,0:T(8,128)} %reshape.242, s32[]{} %constant.87, s32[]{} %constant.88) | dynamic-update-slice | bytes 6279172
  371.4 1.6 dynamic-update-slice.2
  373.0 4.0 bitcast_reduce_fusion
  377.5 1.2 fusion.26
  378.7 41.9 %all-reduce.4 = (f32[768]{0:T(1024)}, f32[32,12]{0,1:T(8,128)}, f32[768]{0:T(1024)}, f32[768,2]{0,1:T(2,128)}) all-reduce(f32[768]{0:T(1024)S(1)} %get-tuple-element.44, f32[32,12]{0,1:T(8,128)S(1)} %dynamic_update_slice.3, f32[768]{0:T(1024)S(1)} %copy-done.35, ...), channel_id=1, replica_groups=mesh['dp'=16,'tensor'=2] {'dp','tensor'}, use_global_device_ids=true, to_apply=%region_21.22 | all-reduce | flops 3456 | bytes 27648 | tf_op jit(solution)/shard_map/psum | solution.py:264
  420.6 2.0 fusion.21
  422.7 330.3 %all-reduce.8.cloned.1.call-done = (f32[16,73728]{1,0:T(8,128)}, f32[16,294912]{1,0:T(8,128)}) async-done(((f32[16,73728]{1,0:T(8,128)}, f32[16,294912]{1,0:T(8,128)}), (f32[16,73728]{1,0:T(8,128)}, f32[16,294912]{1,0:T(8,128)})) %all-reduce.8.cloned.1.call-update) | async-done | bytes 23592976
  753.0 2.7 dynamic-slice_reduce_fusion.2
  756.5 2.0 dynamic-slice_reduce_fusion.3
  759.1 9.3 %dynamic-slice_reduce_fusion = (f32[147456]{0:T(1024)S(1)}, f32[147456]{0:T(1024)S(1)}) fusion(f32[16,294912]{1,0:T(8,128)} %get-tuple-element.51, u32[]{:T(128)} %bitcast.34, u32[]{:T(128)S(6)} %convert.22), kind=kLoop, calls=%fused_computation.53 | loop fusion | bytes 2359304 | tf_op jit(solution)/shard_map/slice | solution.py:70
  768.5 1.1 reshape.239
  769.6 1.1 reshape.240
  (173 shorter events, 13.5 us)
Async XLA Ops:
  7.2 0.8 copy-start
  7.2 50.5 %all-gather.4.cloned.1.call-start = ((), (), s32[]{:S(2)}) async-start(), calls=%async_computation.4 | async-start | bytes 1880064 | tf_op jit(solution)/shard_map/all_gather | solution.py:99
  7.9 66.7 %reduce-scatter.5.cloned.1.call-start = ((), (), s32[]{:S(2)}) async-start(), calls=%async_computation.5 | async-start | bytes 589824 | tf_op jit(solution)/shard_map/reduce_scatter | solution.py:139
  20.5 3.1 copy-start.45
  20.5 3.3 copy-start.5
  20.5 3.4 copy-start.23
  20.5 12.3 %copy-start.25 = (bf16[48,384]{1,0:T(8,128)(2,1)S(1)}, bf16[48,384]{1,0:T(8,128)(2,1)}, u32[]{:S(2)}) copy-start(bf16[48,384]{1,0:T(8,128)(2,1)} %param.16) | copy-start | bytes 110596
  23.9 36.0 %copy-start.28 = (f32[128]{0:T(128)}, f32[128]{0:T(128)S(1)}, u32[]{:S(2)}) copy-start(f32[128]{0:T(128)S(1)} %add_rsqrt_fusion.1) | copy-start | bytes 1540
  32.5 27.5 %copy-start.11 = (bf16[256,768]{1,0:T(8,128)(2,1)}, bf16[256,768]{1,0:T(8,128)(2,1)S(1)}, u32[]{:S(2)}) copy-start(bf16[256,768]{1,0:T(8,128)(2,1)S(1)} %all_gather.28) | copy-start | bytes 1179652
  60.2 2.4 copy-start.19
  62.6 1.7 copy-start.22
  63.0 13.7 %copy-start.17 = (bf16[6,64,256]{2,1,0:T(8,128)(2,1)}, bf16[6,64,256]{2,1,0:T(8,128)(2,1)S(1)}, u32[]{:S(2)}) copy-start(bf16[6,64,256]{2,1,0:T(8,128)(2,1)S(1)} %convolution_convert_fusion.8) | copy-start | bytes 589828
  63.0 3.9 copy-start.26
  63.0 12.6 %copy-start.24 = (f32[768]{0:T(1024)S(1)}, f32[768]{0:T(1024)}, u32[]{:S(2)}) copy-start(f32[768]{0:T(1024)} %param.18) | copy-start | bytes 9220
  64.2 66.2 %all-gather.6.cloned.1.call-start = ((), (), s32[]{:S(2)}) async-start(), calls=%async_computation.6 | async-start | bytes 5013504 | tf_op jit(solution)/shard_map/all_gather | solution.py:165
  65.0 120.2 %all-gather.8.cloned.1.call-start = ((), (), s32[]{:S(2)}) async-start(), calls=%async_computation.7 | async-start | bytes 5013504 | tf_op jit(solution)/shard_map/all_gather | solution.py:166
  66.8 136.6 %reduce-scatter.7.cloned.1.call-start = ((), (), s32[]{:S(2)}) async-start(), calls=%async_computation.8 | async-start | bytes 589824 | tf_op jit(solution)/shard_map/reduce_scatter | solution.py:172
  67.9 242.5 %copy-start.40 = (s32[128]{0:T(128)}, s32[128]{0:T(128)S(1)}, u32[]{:S(2)}) copy-start(s32[128]{0:T(128)S(1)} %dynamic-slice_bitcast_fusion) | copy-start | bytes 1540
  75.7 237.0 %copy-start.32 = (f32[128]{0:T(128)}, f32[128]{0:T(128)S(1)}, u32[]{:S(2)}) copy-start(f32[128]{0:T(128)S(1)} %add_rsqrt_fusion) | copy-start | bytes 1540
  135.1 56.6 %copy-start.7 = (bf16[128,768]{1,0:T(8,128)(2,1)S(1)}, bf16[128,768]{1,0:T(8,128)(2,1)}, u32[]{:S(2)}) copy-start(bf16[128,768]{1,0:T(8,128)(2,1)} %reduce-scatter.5.cloned.1.call-done) | copy-start | bytes 589828
  135.1 56.6 %copy-start.43 = (f32[768,2]{0,1:T(2,128)S(1)}, f32[768,2]{0,1:T(2,128)}, u32[]{:S(2)}) copy-start(f32[768,2]{0,1:T(2,128)} %param.19) | copy-start | bytes 18436
  191.6 118.9 %reduce-scatter.9.cloned.1.call-start = ((), (), s32[]{:S(2)}) async-start(), calls=%async_computation.9 | async-start | bytes 589824 | tf_op jit(solution)/shard_map/reduce_scatter | solution.py:206
  192.2 118.2 %copy-start.30 = (f32[128]{0:T(128)}, f32[128]{0:T(128)S(1)}, u32[]{:S(2)}) copy-start(f32[128]{0:T(128)S(1)} %get-tuple-element.52) | copy-start | bytes 1540
  192.2 118.2 %copy-start.38 = (f32[128,2]{0,1:T(2,128)}, f32[128,2]{0,1:T(2,128)S(1)}, u32[]{:S(2)}) copy-start(f32[128,2]{0,1:T(2,128)S(1)} %get-tuple-element.53) | copy-start | bytes 3076
  203.4 9.1 %copy-start.2 = (f32[2,168,1536]{2,1,0:T(8,128)S(1)}, f32[2,168,1536]{2,1,0:T(8,128)}, u32[]{:S(2)}) copy-start(f32[2,168,1536]{2,1,0:T(8,128)} %fusion.64) | copy-start | bytes 6193156
  212.4 14.5 %slice-start = ((s8[4718592]{0:T(1024)(128)(4,1)}), s8[4194304]{0:T(1024)(128)(4,1)S(1)}, s32[]{:S(2)}) async-start(s8[4718592]{0:T(1024)(128)(4,1)} %bitcast.96), calls=%async_computation.12 | async-start | bytes 8388608
  217.6 9.3 %slice-start.1 = ((s8[4718592]{0:T(1024)(128)(4,1)}), s8[524288]{0:T(1024)(128)(4,1)S(1)}, s32[]{:S(2)}) async-start(s8[4718592]{0:T(1024)(128)(4,1)} %bitcast.96), calls=%async_computation.13 | async-start | bytes 1048576
  230.3 147.2 %reduce-scatter.11.cloned.1.call-start = ((), (), s32[]{:S(2)}) async-start(), calls=%async_computation.10 | async-start | bytes 589824 | tf_op jit(solution)/shard_map/reduce_scatter | solution.py:254
  294.7 18.0 %copy-start.9 = (bf16[128,768]{1,0:T(8,128)(2,1)S(1)}, bf16[128,768]{1,0:T(8,128)(2,1)}, u32[]{:S(2)}) copy-start(bf16[128,768]{1,0:T(8,128)(2,1)} %param.25) | copy-start | bytes 589828
  310.4 11.5 %copy-start.47 = (f32[128]{0:T(128)}, f32[128]{0:T(128)S(1)}, u32[]{:S(2)}) copy-start(f32[128]{0:T(128)S(1)} %mul.247) | copy-start | bytes 1540
  312.7 7.1 copy-start.12
  312.7 9.2 %copy-start.36 = (f32[128]{0:T(128)}, f32[128]{0:T(128)S(1)}, u32[]{:S(2)}) copy-start(f32[128]{0:T(128)S(1)} %broadcast_multiply_fusion.1) | copy-start | bytes 1540
  312.9 9.3 %copy-start.20 = (bf16[1,256,384]{1,2,0:T(8,128)(2,1)S(1)}, bf16[1,256,384]{1,2,0:T(8,128)(2,1)}, u32[]{:S(2)}) copy-start(bf16[1,256,384]{1,2,0:T(8,128)(2,1)} %copy-done.19) | copy-start | bytes 589828
  323.2 0.9 copy-start.3
  323.2 1.1 copy-start.18
  328.3 2.1 copy-start.14
  328.3 2.1 copy-start.15
  328.3 2.1 copy-start.16
  328.3 2.1 copy-start.42
  331.9 421.1 %all-reduce.8.cloned.1.call-start = ((), (), s32[]{:S(2)}) async-start(), calls=%async_computation.11 | async-start | bytes 47185920
  346.3 0.7 copy-start.46
  346.3 2.6 copy-start.6
  346.3 2.6 copy-start.8
  346.3 2.6 copy-start.33
  346.3 2.6 copy-start.39
  346.4 2.6 copy-start.41
  346.4 2.6 copy-start.48
  346.4 3.6 copy-start.4
  372.9 4.1 copy-start.44
  372.9 4.6 copy-start.29
  372.9 5.8 copy-start.27
  372.9 5.8 copy-start.35
  372.9 47.7 %copy-start.10 = (bf16[128,768]{1,0:T(8,128)(2,1)S(1)}, bf16[128,768]{1,0:T(8,128)(2,1)}, u32[]{:S(2)}) copy-start(bf16[128,768]{1,0:T(8,128)(2,1)} %param.25) | copy-start | bytes 589828
  373.0 47.7 %copy-start.13 = (f32[128,768]{1,0:T(8,128)S(1)}, f32[128,768]{1,0:T(8,128)}, u32[]{:S(2)}) copy-start(f32[128,768]{1,0:T(8,128)} %copy-done.12) | copy-start | bytes 1179652
  373.0 47.6 %copy-start.21 = (bf16[128,768]{1,0:T(8,128)(2,1)S(1)}, bf16[128,768]{1,0:T(8,128)(2,1)}, u32[]{:S(2)}) copy-start(bf16[128,768]{1,0:T(8,128)(2,1)} %reduce-scatter.7.cloned.1.call-done) | copy-start | bytes 589828
  373.0 47.6 %copy-start.31 = (f32[128]{0:T(128)S(1)}, f32[128]{0:T(128)}, u32[]{:S(2)}) copy-start(f32[128]{0:T(128)} %copy-done.30) | copy-start | bytes 1540
  373.0 47.6 %copy-start.34 = (f32[128]{0:T(128)S(1)}, f32[128]{0:T(128)}, u32[]{:S(2)}) copy-start(f32[128]{0:T(128)} %copy-done.32) | copy-start | bytes 1540
  373.0 47.6 %copy-start.37 = (f32[128]{0:T(128)S(1)}, f32[128]{0:T(128)}, u32[]{:S(2)}) copy-start(f32[128]{0:T(128)} %copy-done.36) | copy-start | bytes 1540
  759.1 11.5 %copy-start.1 = (f32[32,12]{0,1:T(8,128)S(1)}, f32[32,12]{0,1:T(8,128)}, u32[]{:S(2)}) copy-start(f32[32,12]{0,1:T(8,128)} %param.17) | copy-start | bytes 4612
Sparse Core Ops, SparseCore 0:
  10.3 44.2 all-gather.3
  64.3 10.1 reduce-scatter.4
  77.1 53.2 all-gather.5
  133.4 51.7 all-gather.7
  191.7 11.6 reduce-scatter.6
  230.5 13.1 reduce-scatter.8
  332.0 13.1 reduce-scatter.10
  349.4 403.5 all-reduce.7
where the time goes:
time: 787 us; the launch traced here: 778 us
  waiting for transfers between devices  444 us (56%)
  local copies, waits for them, and re-layouts  138 us (18%)
  blocking collectives  97.2 us (12%)
  matrix products  47.8 us (6%)
  other arithmetic  34.6 us (4%)
  between operations  15.4 us (2%)
    unnamed x9, waiting for transfers between devices  331 us
    all_gather x1, waiting for transfers between devices, body(): lax.all_gather(w_down, 'dp', axis=0, tiled=True)  50.1 us
    all_gather x1, waiting for transfers between devices, body(): lax.all_gather(w_in, 'dp', axis=0, tiled=True)  45.5 us
    psum x1, blocking collectives, body(): lax.psum((grad_attn_gain, grad_rel_full, grad_moe_gain, grad_router), ('d...  41.9 us
    all_gather x1, blocking collectives, body(): lax.all_gather(w_out, 'dp', axis=0, tiled=True)  25 us
    unnamed x111, local copies, waits for them, and re-layouts  24 us
    reshape x2, local copies, waits for them, and re-layouts, as_rows(): first.reshape(groups, -1)  20.7 us
    reshape x2, local copies, waits for them, and re-layouts, as_rows(): second.reshape(groups, -1)  19.6 us
  transfers between devices with their start and end apart: 8, of which 5 were waited for; matrix products, arithmetic and copies ran while one was open for 20% of the time, Pallas kernels for 0%

commit v1 on v0

v1 whole, which is shorter than its diff:
```python
import jax
import jax.numpy as jnp
from jax import lax
from jax.experimental import pallas as pl
from jax.experimental.pallas import tpu as pltpu
from jax.sharding import PartitionSpec as P

HEAD_DIM = 64
EXPERTS = 2
CAP = 176

LONGEST = 16

EPS = 1e-06
NEG = -1e30
HIGH = lax.Precision.HIGHEST
BF = jnp.bfloat16
F32 = jnp.float32


def ring_chip(place, chips):
    place = place % chips
    return jnp.where(place < chips // 2, 2 * place, 2 * (chips - 1 - place) + 1)


def ring_place(chip, chips):
    return jnp.where(chip % 2 == 0, chip // 2, chips - 1 - chip // 2)


class Ring:
    def __init__(self):
        self.n = lax.axis_size("dp")
        self.chips = self.n // 2
        order = [2 * i for i in range(self.chips // 2)]
        order = order + [c + 1 for c in reversed(order)]
        pairs = [
            (order[i] * 2 + k, order[(i + 1) % self.chips] * 2 + k)
            for i in range(self.chips)
            for k in (0, 1)
        ]
        self.right = pairs
        self.left = [(b, a) for a, b in pairs]
        self.swap = [(i, i ^ 1) for i in range(self.n)]
        index = lax.axis_index("dp")
        self.core = index % 2
        self.place = ring_place(index // 2, self.chips)
        reach = self.chips // 2
        self.distances = [0] + [d for s in range(1, reach) for d in (-s, s)] + [reach]

    def chip_at(self, distance):
        return ring_chip(self.place + distance + self.chips, self.chips)

    def gather(self, x):
        rows, width = x.shape
        if self.chips > LONGEST:
            return lax.all_gather(x, "dp", axis=0, tiled=True)
        reach = self.chips // 2
        r = l = x
        pieces = [x]
        for _ in range(reach - 1):
            r = lax.ppermute(r, "dp", self.right)
            l = lax.ppermute(l, "dp", self.left)
            pieces += [r, l]
        half = width // 2
        main = jnp.concatenate(pieces, axis=0)
        main_sib = lax.ppermute(main, "dp", self.swap)
        r = lax.ppermute(r[:, :half], "dp", self.right)
        l = lax.ppermute(l[:, half:], "dp", self.left)
        tail = jnp.concatenate([r, l], axis=1)
        tail_sib = lax.ppermute(tail, "dp", self.swap)
        chips = jnp.stack([self.chip_at(d) for d in self.distances])
        own = chips * 2 + self.core
        sib = chips * 2 + 1 - self.core
        return assemble(main, tail, main_sib, tail_sib, jnp.concatenate([own, sib]))

    def scatter(self, grads, rows):
        width = grads.shape[1]
        if self.chips > LONGEST:
            return lax.psum_scatter(grads, "dp", scatter_dimension=0, tiled=True).astype(F32)
        reach = self.chips // 2
        half = width // 2
        split = grads.reshape(self.chips, 2, rows, width)
        other = lax.dynamic_index_in_dim(split, 1 - self.core, 1, keepdims=False)
        mine = lax.dynamic_index_in_dim(split, self.core, 1, keepdims=False)
        got = lax.ppermute(other, "dp", self.swap)
        both = (mine.astype(F32) + got.astype(F32)).astype(BF)

        def local(distance):
            return lax.dynamic_index_in_dim(both, self.chip_at(distance), 0, keepdims=False)

        far = local(reach)
        r = lax.ppermute(far[:, :half], "dp", self.right)
        l = lax.ppermute(far[:, half:], "dp", self.left)
        for s in range(reach - 1, 0, -1):
            near_r, near_l = local(s), local(-s)
            if s == reach - 1:
                r = jnp.concatenate([add_low(r, near_r[:, :half]), near_r[:, half:]], axis=1)
                l = jnp.concatenate([near_l[:, :half], add_low(l, near_l[:, half:])], axis=1)
            else:
                r, l = add_low(r, near_r), add_low(l, near_l)
            r = lax.ppermute(r, "dp", self.right)
            l = lax.ppermute(l, "dp", self.left)
        return local(0).astype(F32) + r.astype(F32) + l.astype(F32)


def add_low(a, b):
    return (a.astype(F32) + b.astype(F32)).astype(BF)


def assemble(main, tail, main_sib, tail_sib, owners):
    rows, width = tail.shape
    chips = main.shape[0] // rows + 1
    if rows % 16:
        own = jnp.concatenate([main, tail]).reshape(chips, rows, width)
        sib = jnp.concatenate([main_sib, tail_sib]).reshape(chips, rows, width)
        out = jnp.zeros((2 * chips, rows, width), main.dtype).at[owners].set(
            jnp.concatenate([own, sib])
        )
        return out.reshape(2 * chips * rows, width)

    def kernel(owners_ref, main_ref, tail_ref, main_sib_ref, tail_sib_ref, out_ref, sems):
        copies = []
        for at, (big, small) in enumerate(((main_ref, tail_ref), (main_sib_ref, tail_sib_ref))):
            for i in range(chips):
                source = small if i == chips - 1 else big.at[pl.ds(i * rows, rows)]
                owner = owners_ref[at * chips + i]
                target = out_ref.at[pl.ds(pl.multiple_of(owner * rows, 16), rows)]
                copies.append(pltpu.make_async_copy(source, target, sems.at[at * chips + i]))
        for copy in copies:
            copy.start()
        for copy in copies:
            copy.wait()

    anywhere = pl.BlockSpec(memory_space=pl.ANY)
    return pl.pallas_call(
        kernel,
        out_shape=jax.ShapeDtypeStruct((2 * chips * rows, width), main.dtype),
        in_specs=[pl.BlockSpec(memory_space=pltpu.SMEM)] + [anywhere] * 4,
        out_specs=anywhere,
        scratch_shapes=[pltpu.SemaphoreType.DMA((2 * chips,))],
        cost_estimate=pl.CostEstimate(
            flops=0, bytes_accessed=8 * chips * rows * width, transcendentals=0
        ),
        name="assemble",
    )(owners, main, tail, main_sib, tail_sib)


def swap_tensor(x):
    return lax.ppermute(x, "tensor", [(0, 1), (1, 0)])


def whole_rows(own, other, rank):
    return jnp.where(
        rank == 0, jnp.concatenate([own, other], axis=0), jnp.concatenate([other, own], axis=0)
    )


def sum_everywhere(x):
    x = x + swap_tensor(x)
    step = 1
    while step < lax.axis_size("dp"):
        x = x + lax.ppermute(x, "dp", [(i, i ^ step) for i in range(lax.axis_size("dp"))])
        step *= 2
    return x


def rms_scale(rows):
    return lax.rsqrt(jnp.mean(rows * rows, axis=-1, keepdims=True) + EPS)


def norm_back(grad, normed, scale, gain):
    weighted = grad * gain
    return scale * (weighted - normed * jnp.mean(weighted * normed, axis=-1, keepdims=True))


def toeplitz_rows(by_offset_heads, count):
    heads_here = by_offset_heads.shape[0]
    padded = jnp.concatenate(
        [by_offset_heads, jnp.zeros((heads_here, 1), by_offset_heads.dtype)], axis=1
    )
    tiled = jnp.tile(padded, (1, count))
    window = tiled[:, count - 1 : count - 1 + count * (2 * count - 1)]
    return window.reshape(heads_here, count, 2 * count - 1)[:, :, :count]


def diagonal_sums(matrix):
    heads_here, count, _ = matrix.shape
    widened = jnp.concatenate(
        [matrix, jnp.zeros((heads_here, count, count - 1), matrix.dtype)], axis=2
    )
    line = widened.reshape(heads_here, count * (2 * count - 1))
    line = jnp.concatenate(
        [
            jnp.zeros((heads_here, count - 1), matrix.dtype),
            line,
            jnp.zeros((heads_here, 1), matrix.dtype),
        ],
        axis=1,
    )
    return jnp.sum(line.reshape(heads_here, count, 2 * count), axis=1)[:, : 2 * count - 1]


def dot32(a, b, dims):
    return lax.dot_general(a, b, (dims, ((), ())), preferred_element_type=F32)


NN = ((1,), (0,))
NT = ((1,), (1,))
TN = ((0,), (0,))


def body(
    block_in,
    attn_gain,
    w_qkv,
    w_out,
    rel_bias,
    moe_gain,
    w_router,
    w_in,
    w_down,
    seq_lengths,
    expert_ids,
    rel_table,
    out_grad,
):
    rows_local, width = block_in.shape
    rank = lax.axis_index("tensor")
    ring = Ring()
    shard = w_out.shape[0]
    head_cols = w_out.shape[1]
    units = w_in.shape[2]
    heads_local = head_cols // HEAD_DIM
    count = 2 * rows_local

    attn_shard = jnp.concatenate([w_qkv.reshape(shard, 3 * head_cols), w_out], axis=1)
    x_all = whole_rows(block_in, swap_tensor(block_in), rank).astype(F32)
    attn_all = ring.gather(attn_shard)
    in_all = ring.gather(w_in.reshape(shard, EXPERTS * units))
    down_all = ring.gather(w_down.reshape(shard, EXPERTS * units))
    qkv_all, out_all = attn_all[:, : 3 * head_cols], attn_all[:, 3 * head_cols :]
    grad_out = whole_rows(out_grad, swap_tensor(out_grad), rank).astype(F32)

    scale_one = rms_scale(x_all)
    n_one = x_all * scale_one
    normed_one = (n_one * attn_gain).astype(BF)
    projected = dot32(normed_one, qkv_all, NN).astype(BF).reshape(count, 3, heads_local, HEAD_DIM)
    queries, keys_all, values_all = projected[:, 0], projected[:, 1], projected[:, 2]

    places = jnp.arange(count, dtype=jnp.int32)
    ends = jnp.cumsum(seq_lengths[0])
    seq_ids = jnp.sum((places[:, None] >= ends[None, :]).astype(jnp.int32), axis=1)
    same_seq = seq_ids[:, None] == seq_ids[None, :]
    bias_local = lax.dynamic_slice_in_dim(rel_bias, rank * heads_local, heads_local, 1)
    bucket_hits = (
        rel_table[:, None] == jnp.arange(rel_bias.shape[0], dtype=jnp.int32)[None, :]
    ).astype(F32)
    by_offset = jnp.dot(bucket_hits, bias_local, precision=HIGH)
    bias = jnp.where(same_seq[None], toeplitz_rows(by_offset.T, count), NEG)
    scale = HEAD_DIM ** (-0.5)
    scores = (
        jnp.einsum("qhd,khd->hqk", queries, keys_all, preferred_element_type=F32) * scale + bias
    )
    row_max = jnp.max(scores, axis=-1, keepdims=True)
    expo = jnp.exp(scores - row_max)
    p_full = expo / jnp.sum(expo, axis=-1, keepdims=True)
    probs = p_full.astype(BF)
    context = jnp.einsum("hqk,khd->qhd", probs, values_all, preferred_element_type=F32)
    context = context.reshape(count, head_cols).astype(BF)
    attn_part = dot32(context, out_all, NT).astype(BF)
    hidden = x_all + (attn_part.astype(F32) + swap_tensor(attn_part).astype(F32))

    scale_two = rms_scale(hidden)
    n_two = hidden * scale_two
    mixed = n_two * moe_gain
    logits = jnp.stack([jnp.sum(mixed * w_router[:, e], axis=1) for e in range(EXPERTS)], axis=1)
    router_probs = jax.nn.softmax(logits, axis=-1)
    expert_col = expert_ids[:, 0]
    hits = expert_col[:, None] == jnp.arange(EXPERTS, dtype=jnp.int32)[None, :]
    hits_f = hits.astype(F32)
    gate = jnp.sum(router_probs * hits_f, axis=1, keepdims=True)
    hits_i = hits.astype(jnp.int32)
    slot = jnp.sum(jnp.cumsum(hits_i, axis=0) * hits_i, axis=1) - 1
    flat = expert_col * CAP + slot
    dispatch = (flat[:, None] == jnp.arange(EXPERTS * CAP, dtype=jnp.int32)[None, :]).astype(BF)
    grad_routed = (gate * grad_out).astype(BF)
    blocks = dot32(dispatch, mixed.astype(BF), TN).astype(BF)
    grad_blocks = dot32(dispatch, grad_routed, TN).astype(BF)

    def part(x, e):
        return x[e * CAP : (e + 1) * CAP]

    def cols(x, e):
        return x[:, e * units : (e + 1) * units]

    pre = [dot32(part(blocks, e), cols(in_all, e), NN) for e in range(EXPERTS)]
    active = [jax.nn.gelu(v, approximate=True).astype(BF) for v in pre]
    grad_w_down = jnp.concatenate(
        [dot32(part(grad_blocks, e), active[e], TN).astype(BF) for e in range(EXPERTS)], axis=1
    )
    returned = jnp.concatenate(
        [dot32(active[e], cols(down_all, e), NT).astype(BF) for e in range(EXPERTS)], axis=0
    )
    grad_pre = []
    for e in range(EXPERTS):
        grad_active = dot32(part(grad_blocks, e), cols(down_all, e), NN)
        _, pull = jax.vjp(lambda v: jax.nn.gelu(v, approximate=True), pre[e])
        grad_pre.append(pull(grad_active)[0].astype(BF))
    grad_sent = jnp.concatenate(
        [dot32(grad_pre[e], cols(in_all, e), NT).astype(BF) for e in range(EXPERTS)], axis=0
    )
    grad_w_in = jnp.concatenate(
        [dot32(part(blocks, e), grad_pre[e], TN).astype(BF) for e in range(EXPERTS)], axis=1
    )
    routed_part = dot32(dispatch, returned, NN)
    sent_part = dot32(dispatch, grad_sent, NN)
    gate_part = jnp.sum(grad_out * routed_part, axis=1, keepdims=True)
    logits_part = gate_part * gate * (hits_f - router_probs)
    mixed_part = sent_part + sum(
        logits_part[:, e : e + 1] * w_router[:, e] for e in range(EXPERTS)
    )
    mixed_low = mixed_part.astype(BF)
    grad_mixed = mixed_low.astype(F32) + swap_tensor(mixed_low).astype(F32)
    moe_gain_part = jnp.sum(mixed_part * n_two, axis=0)
    router_part = [jnp.sum(mixed * logits_part[:, e : e + 1], axis=0) for e in range(EXPERTS)]

    def own_rows(x):
        return lax.dynamic_slice_in_dim(x, rank * rows_local, rows_local, 0)

    def other_rows(x):
        return lax.dynamic_slice_in_dim(x, (1 - rank) * rows_local, rows_local, 0)

    routed_low = routed_part.astype(BF)
    routed = own_rows(routed_low).astype(F32) + swap_tensor(other_rows(routed_low)).astype(F32)
    result = own_rows(hidden) + own_rows(gate) * routed

    grad_w_down_mine = ring.scatter(grad_w_down, shard)
    grad_w_in_mine = ring.scatter(grad_w_in, shard)

    grad_hidden = grad_out + norm_back(grad_mixed, n_two, scale_two, moe_gain)
    grad_attended = grad_hidden.astype(BF)
    grad_context = dot32(grad_attended, out_all, NN).astype(BF)
    grad_w_out = dot32(grad_attended, context, TN).astype(BF)
    grad_context_heads = grad_context.reshape(count, heads_local, HEAD_DIM)
    grad_probs = jnp.einsum(
        "qhd,khd->hqk", grad_context_heads, values_all, preferred_element_type=F32
    )
    inner = jnp.sum(p_full * grad_probs, axis=-1, keepdims=True)
    grad_scores = (p_full * (grad_probs - inner)).astype(BF)
    grad_queries = (
        jnp.einsum("hqk,khd->qhd", grad_scores, keys_all, preferred_element_type=F32) * scale
    )
    grad_keys = (
        jnp.einsum("hqk,qhd->khd", grad_scores, queries, preferred_element_type=F32) * scale
    )
    grad_values = jnp.einsum(
        "hqk,qhd->khd", probs, grad_context_heads, preferred_element_type=F32
    )
    grad_projected = jnp.concatenate(
        [g.reshape(count, head_cols) for g in (grad_queries, grad_keys, grad_values)], axis=1
    ).astype(BF)
    grad_w_qkv = dot32(normed_one, grad_projected, TN).astype(BF)
    attn_mine = ring.scatter(jnp.concatenate([grad_w_qkv, grad_w_out], axis=1), shard)
    normed_part = dot32(grad_projected, qkv_all, NT)
    attn_gain_part = jnp.sum(normed_part * n_one, axis=0)
    normed_low = normed_part.astype(BF)
    grad_normed = own_rows(normed_low).astype(F32) + swap_tensor(other_rows(normed_low)).astype(F32)
    grad_block = own_rows(grad_hidden) + norm_back(
        grad_normed, own_rows(n_one), own_rows(scale_one), attn_gain
    )
    offset_sums = diagonal_sums(grad_scores.astype(F32))
    grad_bias_heads = jnp.dot(offset_sums, bucket_hits, precision=HIGH)
    grad_rel = lax.dynamic_update_slice_in_dim(
        jnp.zeros(rel_bias.shape, F32), grad_bias_heads.T, rank * heads_local, 1
    )
    small = [attn_gain_part, moe_gain_part] + router_part + [grad_rel.reshape(-1)]
    line = jnp.concatenate(small)
    summed = sum_everywhere(line.reshape(-1, 128)).reshape(-1)
    return (
        result.astype(BF),
        grad_block,
        summed[:width],
        attn_mine[:, : 3 * head_cols].reshape(w_qkv.shape),
        attn_mine[:, 3 * head_cols :],
        summed[4 * width :].reshape(rel_bias.shape),
        summed[width : 2 * width],
        jnp.stack([summed[2 * width : 3 * width], summed[3 * width : 4 * width]], axis=1),
        grad_w_in_mine.reshape(w_in.shape),
        grad_w_down_mine.reshape(w_down.shape),
    )


def solution(mesh):
    placed = (
        P(("dp", "tensor"), None),
        P(),
        P("dp", None, "tensor"),
        P("dp", "tensor"),
        P(),
        P(),
        P(),
        P("dp", None, "tensor"),
        P("dp", None, "tensor"),
        P("dp", None),
        P("dp", None),
        P(),
        P(("dp", "tensor"), None),
    )
    return jax.shard_map(
        body,
        mesh=mesh,
        in_specs=placed,
        out_specs=(
            P(("dp", "tensor"), None),
            P(("dp", "tensor"), None),
            P(),
            P("dp", None, "tensor"),
            P("dp", "tensor"),
            P(),
            P(),
            P(),
            P("dp", None, "tensor"),
            P("dp", None, "tensor"),
        ),
        check_vma=False,
    )
```

time: 787 us -> 693 us (0.88)
  Pallas kernels: 0 us -> 363 us
  waiting for transfers between devices: 444 us -> 91.6 us
  blocking collectives: 97.2 us -> 0 us
  starting transfers between devices: 0.5 us -> 65.9 us
  local copies, waits for them, and re-layouts: 138 us -> 87.3 us
  between operations: 15.4 us -> 2.26 us
    pallas_call x0 -> x3, Pallas kernels: none -> 363 us  [assemble(): pl.pallas_call(kernel, out_shape=jax.ShapeDtypeStruct((2 * chips * rows,...]
    unnamed x9 -> x0, waiting for transfers between devices: 331 us -> none
    all_gather x3 -> x0, waiting for transfers between devices: 95.6 us -> none  [the longest x1 50.1 us: body(): lax.all_gather(w_down, 'dp', axis=0, tiled=True)]
    ppermute x0 -> x68, waiting for transfers between devices: none -> 91.6 us  [the longest x7 21.2 us: swap_tensor(): return lax.ppermute(x, 'tensor', [(0, 1), (1, 0)])]
    ppermute x0 -> x68, starting transfers between devices: none -> 65.9 us  [the longest x9 16.6 us: gather(): r = lax.ppermute(r, 'dp', self.right)]
    all_gather x5 -> x0, blocking collectives: 55.4 us -> none  [the longest x1 25 us: body(): lax.all_gather(w_out, 'dp', axis=0, tiled=True)]
    psum x1 -> x0, blocking collectives: 41.9 us -> none  [body(): lax.psum((grad_attn_gain, grad_rel_full, grad_moe_gain, grad_router), ('d...]
    reshape x8 -> x6, local copies, waits for them, and re-layouts: 43.3 us -> 4.43 us  [the longest x1 1.31 us: body(): grad_w_in_mine.reshape(w_in.shape)]
  transfers between devices with their start and end apart: 8 -> 68, of which waited for: 5 -> 38; matrix products, arithmetic and copies ran while one was open for 20% -> 20% of each run, Pallas kernels for 0% -> 32%
where the time goes in v1:
time: 693 us; the launch traced here: 684 us
  Pallas kernels  363 us (52%)
  waiting for transfers between devices  91.6 us (13%)
  local copies, waits for them, and re-layouts  87.3 us (13%)
  starting transfers between devices  65.9 us (10%)
  matrix products  41.8 us (6%)
  other arithmetic  32.3 us (5%)
    pallas_call x3, Pallas kernels, assemble(): pl.pallas_call(kernel, out_shape=jax.ShapeDtypeStruct((2 * chips * rows,...  363 us
    unnamed x126, local copies, waits for them, and re-layouts  45.8 us
    dot_general x22, matrix products, dot32(): return lax.dot_general(a, b, (dims, ((), ())), preferred_element_type=F32)  33.4 us
    ppermute x7, waiting for transfers between devices, swap_tensor(): return lax.ppermute(x, 'tensor', [(0, 1), (1, 0)])  21.2 us
    ppermute x9, waiting for transfers between devices, scatter(): r = lax.ppermute(r, 'dp', self.right)  17.6 us
    ppermute x9, starting transfers between devices, gather(): r = lax.ppermute(r, 'dp', self.right)  16.6 us
  transfers between devices with their start and end apart: 68, of which 38 were waited for; matrix products, arithmetic and copies ran while one was open for 20% of the time, Pallas kernels for 32%

profile of v1, /device:TPU:0, one launch (start us, length us, event | category | flops | bytes accessed | tf_op | source)
XLA Modules:
  0.0 684.2 jit_solution(10581055913069831474)
XLA Ops:
  0.7 1.7 copy.76
  2.4 3.0 collective-permute-start.22
  6.4 2.1 collective-permute-start.12
  10.8 2.0 collective-permute-start.1
  12.8 1.7 constant_dynamic-update-slice_fusion.27
  19.0 1.9 copy.73
  20.9 3.1 slice.241
  24.1 4.8 reshape.283
  30.2 1.9 copy.69
  35.2 3.8 collective-permute-done.2
  41.2 4.5 collective-permute-done
  49.6 1.7 constant_dynamic-update-slice_fusion.26
  51.8 1.7 constant_dynamic-update-slice_fusion.25
  55.0 1.7 constant_dynamic-update-slice_fusion.17
  57.2 1.7 constant_dynamic-update-slice_fusion.16
  63.4 4.6 collective-permute-done.5
  69.1 4.0 collective-permute-done.6
  75.4 2.1 collective-permute-done.7
  77.9 3.9 collective-permute-done.8
  86.7 2.1 collective-permute-done.15
  89.9 3.3 collective-permute-done.26
  97.5 3.9 collective-permute-done.16
  109.0 2.9 collective-permute-done.18
  112.6 1.6 collective-permute-start.19
  115.2 73.4 %assemble.3 = bf16[768,1536]{1,0:T(8,128)(2,1)} custom-call(s32[16]{0:T(128)} %pad_add_fusion.owners_ref, bf16[336,1536]{1,0:T(8,128)(2,1)} %constant_dynamic-update-slice_fusion.2.main_ref, bf16[48,1536]{1,0:T(8,128)(2,1)} %copy-done.15, bf16[336,1536]{1,0:T(8,128)(2,1)} %copy-done.6, bf16[48,1536]{1,0:T(8,128)(2,1)} %copy-done.17), custom_call_target="tpu_custom_call" | custom-call | bytes 4718592 | tf_op jit(solution)/shard_map/assemble/pallas_call | solution.py:135
  188.7 2.2 convolution_convert_fusion.5
  200.0 1.6 constant_dynamic-update-slice_fusion.19.tail_ref
  201.6 7.6 %collective-permute-done.11 = bf16[256,768]{1,0:T(8,128)(2,1)S(1)} collective-permute-done((bf16[256,768]{1,0:T(8,128)(2,1)S(1)}, bf16[256,768]{1,0:T(8,128)(2,1)S(1)}, u32[]{:S(2)}, u32[]{:S(2)}) %collective-permute-start.11) | collective-permute-done | bytes 393248 | tf_op jit(solution)/shard_map/ppermute | solution.py:149
  209.9 2.5 convolution_convert_fusion.7
  213.6 144.9 %assemble.4 = bf16[768,3072]{1,0:T(8,128)(2,1)} custom-call(s32[16]{0:T(128)} %pad_add_fusion.owners_ref, bf16[336,3072]{1,0:T(8,128)(2,1)} %constant_dynamic-update-slice_fusion.12.main_ref, bf16[48,3072]{1,0:T(8,128)(2,1)} %constant_dynamic-update-slice_fusion.19.tail_ref, bf16[336,3072]{1,0:T(8,128)(2,1)} %collective-permute-done.20.main_sib_ref, ...), custom_call_target="tpu_custom_call" | custom-call | bytes 9437184 | tf_op jit(solution)/shard_map/assemble/pallas_call | solution.py:135
  358.4 3.2 fusion.10
  361.7 3.3 fusion.18
  365.0 144.9 %assemble.5 = bf16[768,3072]{1,0:T(8,128)(2,1)} custom-call(s32[16]{0:T(128)} %pad_add_fusion.owners_ref, bf16[336,3072]{1,0:T(8,128)(2,1)} %constant_dynamic-update-slice_fusion.21.main_ref, bf16[48,3072]{1,0:T(8,128)(2,1)} %constant_dynamic-update-slice_fusion.28.tail_ref, bf16[336,3072]{1,0:T(8,128)(2,1)} %collective-permute-done.30.main_sib_ref, ...), custom_call_target="tpu_custom_call" | custom-call | bytes 9437184 | tf_op jit(solution)/shard_map/assemble/pallas_call | solution.py:135
  509.9 3.1 fusion.34
  522.9 1.7 fusion.59
  526.4 1.6 collective-permute-start.34
  528.7 1.7 dynamic-slice_bitcast_fusion.1
  531.6 2.8 pad_maximum_fusion.1
  534.3 7.0 %collective-permute-done.34 = bf16[256,768]{1,0:T(8,128)(2,1)S(1)} collective-permute-done((bf16[256,768]{1,0:T(8,128)(2,1)S(1)}, bf16[256,768]{1,0:T(8,128)(2,1)S(1)}, u32[]{:S(2)}, u32[]{:S(2)}) %collective-permute-start.34) | collective-permute-done | bytes 393248 | tf_op jit(solution)/shard_map/ppermute | solution.py:149
  546.3 2.2 convolution_convert_fusion.10
  548.5 2.0 multiply_reduce_fusion
  552.2 1.9 pad_convert_fusion
  554.6 3.6 copy.57
  558.1 6.5 reshape.304
  564.6 12.2 %dynamic-update-slice.6 = f32[6,131072]{1,0:T(8,128)} dynamic-update-slice(f32[6,131072]{1,0:T(8,128)} %dynamic-update-slice.5, f32[6,130816]{1,0:T(8,128)} %reshape.304, s32[]{} %constant.331, s32[]{} %constant.336) | dynamic-update-slice | bytes 6279172
  578.4 3.9 bitcast_reduce_fusion
  583.1 3.4 multiply_reduce_fusion.4
  588.3 2.1 collective-permute-done.36
  591.6 1.6 collective-permute-start.38
  596.5 1.7 add_convert_fusion
  599.1 2.1 collective-permute-start.40
  601.9 1.8 collective-permute-done.40
  606.9 2.3 collective-permute-done.42
  616.0 2.8 collective-permute-start.44
  618.9 3.7 collective-permute-done.44
  626.1 1.9 multiply_add_fusion
  631.4 3.7 fusion.2
  637.5 2.5 fusion.1
  644.5 2.5 collective-permute-done.60
  649.3 4.0 collective-permute-done.52
  656.8 2.9 collective-permute-done.61
  663.1 2.9 collective-permute-done.53
  669.4 2.4 collective-permute-done.62
  677.8 3.2 collective-permute-done.67
  (362 shorter events, 135.2 us)
Async XLA Ops:
  2.4 45.6 %collective-permute-start.22 = (bf16[48,3072]{1,0:T(8,128)(2,1)}, bf16[48,3072]{1,0:T(8,128)(2,1)}, u32[]{:S(2)}, u32[]{:S(2)}) collective-permute-start(bf16[48,3072]{1,0:T(8,128)(2,1)} %bitcast.103), channel_id=1, source_target_pairs={{0,8},{2,10},{8,16},{10,18},{16,24},{18,26},{24,28},{26,30},{28,20... | collective-permute-start | bytes 884744 | tf_op jit(solution)/shard_map/ppermute | solution.py:61
  5.4 45.9 %collective-permute-start.23 = (bf16[48,3072]{1,0:T(8,128)(2,1)}, bf16[48,3072]{1,0:T(8,128)(2,1)}, u32[]{:S(2)}, u32[]{:S(2)}) collective-permute-start(bf16[48,3072]{1,0:T(8,128)(2,1)} %bitcast.103), channel_id=1, source_target_pairs={{8,0},{10,2},{16,8},{18,10},{24,16},{26,18},{28,24},{30,26},{20,28... | collective-permute-start | bytes 884744 | tf_op jit(solution)/shard_map/ppermute | solution.py:62
  6.4 47.0 %collective-permute-start.12 = (bf16[48,3072]{1,0:T(8,128)(2,1)S(1)}, bf16[48,3072]{1,0:T(8,128)(2,1)}, u32[]{:S(2)}, u32[]{:S(2)}) collective-permute-start(bf16[48,3072]{1,0:T(8,128)(2,1)S(1)} %bitcast.212), channel_id=1, source_target_pairs={{0,8},{2,10},{8,16},{10,18},{16,24},{18,26},{24,28},{26,30},{28,20... | collective-permute-start | bytes 884744 | tf_op jit(solution)/shard_map/ppermute | solution.py:61
  8.5 48.2 %collective-permute-start.13 = (bf16[48,3072]{1,0:T(8,128)(2,1)S(1)}, bf16[48,3072]{1,0:T(8,128)(2,1)}, u32[]{:S(2)}, u32[]{:S(2)}) collective-permute-start(bf16[48,3072]{1,0:T(8,128)(2,1)S(1)} %bitcast.213), channel_id=1, source_target_pairs={{8,0},{10,2},{16,8},{18,10},{24,16},{26,18},{28,24},{30,26},{20,28... | collective-permute-start | bytes 884744 | tf_op jit(solution)/shard_map/ppermute | solution.py:62
  10.8 22.8 %collective-permute-start.1 = (bf16[48,1536]{1,0:T(8,128)(2,1)}, bf16[48,1536]{1,0:T(8,128)(2,1)}, u32[]{:S(2)}, u32[]{:S(2)}) collective-permute-start(bf16[48,1536]{1,0:T(8,128)(2,1)} %get-tuple-element.76), channel_id=1, source_target_pairs={{0,8},{2,10},{8,16},{10,18},{16,24},{18,26},{24,28},{26,30},{28,20... | collective-permute-start | bytes 442376 | tf_op jit(solution)/shard_map/ppermute | solution.py:61
  33.6 5.4 collective-permute-start.2
  39.0 6.7 collective-permute-start
  45.7 164.2 %collective-permute-start.33 = (bf16[128,768]{1,0:T(8,128)(2,1)}, bf16[128,768]{1,0:T(8,128)(2,1)}, u32[]{:S(2)}, u32[]{:S(2)}) collective-permute-start(bf16[128,768]{1,0:T(8,128)(2,1)} %param.25), channel_id=1, source_target_pairs={{0,1},{1,0},{2,3},{3,2},{4,5},{5,4},{6,7},{7,6},{8,9},{9,8},{10,11... | collective-permute-start | bytes 589832 | tf_op jit(solution)/shard_map/ppermute | solution.py:149
  48.0 10.8 %collective-permute-start.3 = (bf16[48,1536]{1,0:T(8,128)(2,1)}, bf16[48,1536]{1,0:T(8,128)(2,1)S(1)}, u32[]{:S(2)}, u32[]{:S(2)}) collective-permute-start(bf16[48,1536]{1,0:T(8,128)(2,1)} %collective-permute-done.1), channel_id=1, source_target_pairs={{0,8},{2,10},{8,16},{10,18},{16,24},{18,26},{24,28},{26,30},{28,20... | collective-permute-start | bytes 442376 | tf_op jit(solution)/shard_map/ppermute | solution.py:61
  51.3 9.8 %collective-permute-start.4 = (bf16[48,1536]{1,0:T(8,128)(2,1)S(1)}, bf16[48,1536]{1,0:T(8,128)(2,1)S(1)}, u32[]{:S(2)}, u32[]{:S(2)}) collective-permute-start(bf16[48,1536]{1,0:T(8,128)(2,1)S(1)} %collective-permute-done.2), channel_id=1, source_target_pairs={{8,0},{10,2},{16,8},{18,10},{24,16},{26,18},{28,24},{30,26},{20,28... | collective-permute-start | bytes 442376 | tf_op jit(solution)/shard_map/ppermute | solution.py:62
  53.4 28.9 %collective-permute-start.24 = (bf16[48,3072]{1,0:T(8,128)(2,1)}, bf16[48,3072]{1,0:T(8,128)(2,1)S(1)}, u32[]{:S(2)}, u32[]{:S(2)}) collective-permute-start(bf16[48,3072]{1,0:T(8,128)(2,1)} %collective-permute-done.22), channel_id=1, source_target_pairs={{0,8},{2,10},{8,16},{10,18},{16,24},{18,26},{24,28},{26,30},{28,20... | collective-permute-start | bytes 884744 | tf_op jit(solution)/shard_map/ppermute | solution.py:61
  56.7 26.4 %collective-permute-start.25 = (bf16[48,3072]{1,0:T(8,128)(2,1)}, bf16[48,3072]{1,0:T(8,128)(2,1)S(1)}, u32[]{:S(2)}, u32[]{:S(2)}) collective-permute-start(bf16[48,3072]{1,0:T(8,128)(2,1)} %collective-permute-done.23), channel_id=1, source_target_pairs={{8,0},{10,2},{16,8},{18,10},{24,16},{26,18},{28,24},{30,26},{20,28... | collective-permute-start | bytes 884744 | tf_op jit(solution)/shard_map/ppermute | solution.py:62
  58.8 25.5 %collective-permute-start.14 = (bf16[48,3072]{1,0:T(8,128)(2,1)}, bf16[48,3072]{1,0:T(8,128)(2,1)S(1)}, u32[]{:S(2)}, u32[]{:S(2)}) collective-permute-start(bf16[48,3072]{1,0:T(8,128)(2,1)} %collective-permute-done.12), channel_id=1, source_target_pairs={{0,8},{2,10},{8,16},{10,18},{16,24},{18,26},{24,28},{26,30},{28,20... | collective-permute-start | bytes 884744 | tf_op jit(solution)/shard_map/ppermute | solution.py:61
  61.1 6.9 %collective-permute-start.5 = (bf16[48,1536]{1,0:T(8,128)(2,1)S(1)}, bf16[48,1536]{1,0:T(8,128)(2,1)S(1)}, u32[]{:S(2)}, u32[]{:S(2)}) collective-permute-start(bf16[48,1536]{1,0:T(8,128)(2,1)S(1)} %collective-permute-done.3), channel_id=1, source_target_pairs={{0,8},{2,10},{8,16},{10,18},{16,24},{18,26},{24,28},{26,30},{28,20... | collective-permute-start | bytes 442376 | tf_op jit(solution)/shard_map/ppermute | solution.py:61
  68.0 5.1 collective-permute-start.6
  73.1 4.4 collective-permute-start.7
  77.5 4.4 collective-permute-start.8
  81.8 6.9 %collective-permute-start.15 = (bf16[48,3072]{1,0:T(8,128)(2,1)}, bf16[48,3072]{1,0:T(8,128)(2,1)S(1)}, u32[]{:S(2)}, u32[]{:S(2)}) collective-permute-start(bf16[48,3072]{1,0:T(8,128)(2,1)} %collective-permute-done.13), channel_id=1, source_target_pairs={{8,0},{10,2},{16,8},{18,10},{24,16},{26,18},{28,24},{30,26},{20,28... | collective-permute-start | bytes 884744 | tf_op jit(solution)/shard_map/ppermute | solution.py:62
  82.3 31.9 %collective-permute-start.9 = (bf16[336,1536]{1,0:T(8,128)(2,1)}, bf16[336,1536]{1,0:T(8,128)(2,1)S(1)}, u32[]{:S(2)}, u32[]{:S(2)}) collective-permute-start(bf16[336,1536]{1,0:T(8,128)(2,1)} %constant_dynamic-update-slice_fusion.2.main_ref), channel_id=1, source_target_pairs={{0,2},{2,0},{4,6},{6,4},{8,10},{10,8},{12,14},{14,12},{16,18},{18,... | collective-permute-start | bytes 3096584 | tf_op jit(solution)/shard_map/ppermute | solution.py:66
  83.1 29.5 %collective-permute-start.10 = (bf16[48,1536]{1,0:T(8,128)(2,1)S(1)}, bf16[48,1536]{1,0:T(8,128)(2,1)S(1)}, u32[]{:S(2)}, u32[]{:S(2)}) collective-permute-start(bf16[48,1536]{1,0:T(8,128)(2,1)S(1)} %constant_dynamic-update-slice_fusion.10.tail_ref), channel_id=1, source_target_pairs={{0,2},{2,0},{4,6},{6,4},{8,10},{10,8},{12,14},{14,12},{16,18},{18,... | collective-permute-start | bytes 442376 | tf_op jit(solution)/shard_map/ppermute | solution.py:70
  84.4 8.9 %collective-permute-start.26 = (bf16[48,3072]{1,0:T(8,128)(2,1)S(1)}, bf16[48,3072]{1,0:T(8,128)(2,1)S(1)}, u32[]{:S(2)}, u32[]{:S(2)}) collective-permute-start(bf16[48,3072]{1,0:T(8,128)(2,1)S(1)} %collective-permute-done.24), channel_id=1, source_target_pairs={{0,8},{2,10},{8,16},{10,18},{16,24},{18,26},{24,28},{26,30},{28,20... | collective-permute-start | bytes 884744 | tf_op jit(solution)/shard_map/ppermute | solution.py:61
  88.8 6.8 %collective-permute-start.27 = (bf16[48,3072]{1,0:T(8,128)(2,1)S(1)}, bf16[48,3072]{1,0:T(8,128)(2,1)S(1)}, u32[]{:S(2)}, u32[]{:S(2)}) collective-permute-start(bf16[48,3072]{1,0:T(8,128)(2,1)S(1)} %collective-permute-done.25), channel_id=1, source_target_pairs={{8,0},{10,2},{16,8},{18,10},{24,16},{26,18},{28,24},{30,26},{20,28... | collective-permute-start | bytes 884744 | tf_op jit(solution)/shard_map/ppermute | solution.py:62
  93.3 8.1 %collective-permute-start.16 = (bf16[48,3072]{1,0:T(8,128)(2,1)S(1)}, bf16[48,3072]{1,0:T(8,128)(2,1)S(1)}, u32[]{:S(2)}, u32[]{:S(2)}) collective-permute-start(bf16[48,3072]{1,0:T(8,128)(2,1)S(1)} %collective-permute-done.14), channel_id=1, source_target_pairs={{0,8},{2,10},{8,16},{10,18},{16,24},{18,26},{24,28},{26,30},{28,20... | collective-permute-start | bytes 884744 | tf_op jit(solution)/shard_map/ppermute | solution.py:61
  95.6 8.1 %collective-permute-start.17 = (bf16[48,3072]{1,0:T(8,128)(2,1)S(1)}, bf16[48,3072]{1,0:T(8,128)(2,1)S(1)}, u32[]{:S(2)}, u32[]{:S(2)}) collective-permute-start(bf16[48,3072]{1,0:T(8,128)(2,1)S(1)} %collective-permute-done.15), channel_id=1, source_target_pairs={{8,0},{10,2},{16,8},{18,10},{24,16},{26,18},{28,24},{30,26},{20,28... | collective-permute-start | bytes 884744 | tf_op jit(solution)/shard_map/ppermute | solution.py:62
  101.4 5.4 collective-permute-start.28
  103.7 94.2 %collective-permute-start.29 = (bf16[48,1536]{1,0:T(8,128)(2,1)}, bf16[48,1536]{1,0:T(8,128)(2,1)}, u32[]{:S(2)}, u32[]{:S(2)}) collective-permute-start(bf16[48,1536]{1,0:T(8,128)(2,1)} %slice.250), channel_id=1, source_target_pairs={{8,0},{10,2},{16,8},{18,10},{24,16},{26,18},{28,24},{30,26},{20,28... | collective-permute-start | bytes 442376 | tf_op jit(solution)/shard_map/ppermute | solution.py:68
  106.8 5.1 collective-permute-start.18
  111.9 253.1 %collective-permute-start.30 = (bf16[336,3072]{1,0:T(8,128)(2,1)}, bf16[336,3072]{1,0:T(8,128)(2,1)}, u32[]{:S(2)}, u32[]{:S(2)}) collective-permute-start(bf16[336,3072]{1,0:T(8,128)(2,1)} %constant_dynamic-update-slice_fusion.21.main_ref), channel_id=1, source_target_pairs={{0,2},{2,0},{4,6},{6,4},{8,10},{10,8},{12,14},{14,12},{16,18},{18,... | collective-permute-start | bytes 6193160 | tf_op jit(solution)/shard_map/ppermute | solution.py:66
  112.6 87.4 %collective-permute-start.19 = (bf16[48,1536]{1,0:T(8,128)(2,1)}, bf16[48,1536]{1,0:T(8,128)(2,1)}, u32[]{:S(2)}, u32[]{:S(2)}) collective-permute-start(bf16[48,1536]{1,0:T(8,128)(2,1)} %slice.247), channel_id=1, source_target_pairs={{8,0},{10,2},{16,8},{18,10},{24,16},{26,18},{28,24},{30,26},{20,28... | collective-permute-start | bytes 442376 | tf_op jit(solution)/shard_map/ppermute | solution.py:68
  114.3 99.3 %collective-permute-start.20 = (bf16[336,3072]{1,0:T(8,128)(2,1)}, bf16[336,3072]{1,0:T(8,128)(2,1)}, u32[]{:S(2)}, u32[]{:S(2)}) collective-permute-start(bf16[336,3072]{1,0:T(8,128)(2,1)} %constant_dynamic-update-slice_fusion.12.main_ref), channel_id=1, source_target_pairs={{0,2},{2,0},{4,6},{6,4},{8,10},{10,8},{12,14},{14,12},{16,18},{18,... | collective-permute-start | bytes 6193160 | tf_op jit(solution)/shard_map/ppermute | solution.py:66
  197.9 11.3 %collective-permute-start.11 = (bf16[256,768]{1,0:T(8,128)(2,1)S(1)}, bf16[256,768]{1,0:T(8,128)(2,1)S(1)}, u32[]{:S(2)}, u32[]{:S(2)}) collective-permute-start(bf16[256,768]{1,0:T(8,128)(2,1)S(1)} %convolution_convert_fusion.9), channel_id=1, source_target_pairs={{0,1},{1,0},{2,3},{3,2},{4,5},{5,4},{6,7},{7,6},{8,9},{9,8},{10,11... | collective-permute-start | bytes 1179656 | tf_op jit(solution)/shard_map/ppermute | solution.py:149
  200.0 164.9 %collective-permute-start.31 = (bf16[48,3072]{1,0:T(8,128)(2,1)}, bf16[48,3072]{1,0:T(8,128)(2,1)}, u32[]{:S(2)}, u32[]{:S(2)}) collective-permute-start(bf16[48,3072]{1,0:T(8,128)(2,1)} %constant_dynamic-update-slice_fusion.28.tail_ref), channel_id=1, source_target_pairs={{0,2},{2,0},{4,6},{6,4},{8,10},{10,8},{12,14},{14,12},{16,18},{18,... | collective-permute-start | bytes 884744 | tf_op jit(solution)/shard_map/ppermute | solution.py:70
  209.2 4.3 collective-permute-start.21
  525.4 71.0 %collective-permute-start.32 = (bf16[128,768]{1,0:T(8,128)(2,1)}, bf16[128,768]{1,0:T(8,128)(2,1)}, u32[]{:S(2)}, u32[]{:S(2)}) collective-permute-start(bf16[128,768]{1,0:T(8,128)(2,1)} %constant_dynamic-slice_fusion.1), channel_id=1, source_target_pairs={{0,1},{1,0},{2,3},{3,2},{4,5},{5,4},{6,7},{7,6},{8,9},{9,8},{10,11... | collective-permute-start | bytes 589832 | tf_op jit(solution)/shard_map/ppermute | solution.py:149
  526.4 15.0 %collective-permute-start.34 = (bf16[256,768]{1,0:T(8,128)(2,1)S(1)}, bf16[256,768]{1,0:T(8,128)(2,1)S(1)}, u32[]{:S(2)}, u32[]{:S(2)}) collective-permute-start(bf16[256,768]{1,0:T(8,128)(2,1)S(1)} %get-tuple-element.89), channel_id=1, source_target_pairs={{0,1},{1,0},{2,3},{3,2},{4,5},{5,4},{6,7},{7,6},{8,9},{9,8},{10,11... | collective-permute-start | bytes 1179656 | tf_op jit(solution)/shard_map/ppermute | solution.py:149
  531.6 99.9 %collective-permute-start.50 = (bf16[8,48,3072]{2,1,0:T(8,128)(2,1)}, bf16[8,48,3072]{2,1,0:T(8,128)(2,1)}, u32[]{:S(2)}, u32[]{:S(2)}) collective-permute-start(bf16[8,48,3072]{2,1,0:T(8,128)(2,1)} %dynamic-slice_bitcast_fusion.1), channel_id=1, source_target_pairs={{0,2},{2,0},{4,6},{6,4},{8,10},{10,8},{12,14},{14,12},{16,18},{18,... | collective-permute-start | bytes 7077896 | tf_op jit(solution)/shard_map/ppermute | solution.py:85
  590.5 13.8 %collective-permute-start.41 = (bf16[8,48,1536]{2,1,0:T(8,128)(2,1)S(1)}, bf16[8,48,1536]{2,1,0:T(8,128)(2,1)S(1)}, u32[]{:S(2)}, u32[]{:S(2)}) collective-permute-start(bf16[8,48,1536]{2,1,0:T(8,128)(2,1)S(1)} %dynamic-slice_bitcast_fusion.2), channel_id=1, source_target_pairs={{0,2},{2,0},{4,6},{6,4},{8,10},{10,8},{12,14},{14,12},{16,18},{18,... | collective-permute-start | bytes 3538952 | tf_op jit(solution)/shard_map/ppermute | solution.py:85
  594.7 42.7 %collective-permute-start.59 = (bf16[8,48,3072]{2,1,0:T(8,128)(2,1)}, bf16[8,48,3072]{2,1,0:T(8,128)(2,1)}, u32[]{:S(2)}, u32[]{:S(2)}) collective-permute-start(bf16[8,48,3072]{2,1,0:T(8,128)(2,1)} %dynamic-slice_bitcast_fusion), channel_id=1, source_target_pairs={{0,2},{2,0},{4,6},{6,4},{8,10},{10,8},{12,14},{14,12},{16,18},{18,... | collective-permute-start | bytes 7077896 | tf_op jit(solution)/shard_map/ppermute | solution.py:85
  599.1 4.6 collective-permute-start.40
  601.2 11.9 %collective-permute-start.35 = (bf16[128,768]{1,0:T(8,128)(2,1)S(1)}, bf16[128,768]{1,0:T(8,128)(2,1)S(1)}, u32[]{:S(2)}, u32[]{:S(2)}) collective-permute-start(bf16[128,768]{1,0:T(8,128)(2,1)S(1)} %constant_dynamic-slice_fusion), channel_id=1, source_target_pairs={{0,1},{1,0},{2,3},{3,2},{4,5},{5,4},{6,7},{7,6},{8,9},{9,8},{10,11... | collective-permute-start | bytes 589832 | tf_op jit(solution)/shard_map/ppermute | solution.py:149
  604.7 4.4 collective-permute-start.42
  605.9 4.7 collective-permute-start.46
  609.2 5.8 collective-permute-start.43
  610.7 5.3 collective-permute-start.47
  616.0 6.5 collective-permute-start.44
  618.8 5.1 collective-permute-start.48
  624.1 5.2 collective-permute-start.49
  624.6 5.4 collective-permute-start.45
  635.3 7.0 %collective-permute-start.51 = (bf16[48,1536]{1,0:T(8,128)(2,1)S(1)}, bf16[48,1536]{1,0:T(8,128)(2,1)S(1)}, u32[]{:S(2)}, u32[]{:S(2)}) collective-permute-start(bf16[48,1536]{1,0:T(8,128)(2,1)S(1)} %get-tuple-element.70), channel_id=1, source_target_pairs={{0,8},{2,10},{8,16},{10,18},{16,24},{18,26},{24,28},{26,30},{28,20... | collective-permute-start | bytes 442376 | tf_op jit(solution)/shard_map/ppermute | solution.py:92
  636.6 7.0 %collective-permute-start.55 = (bf16[48,1536]{1,0:T(8,128)(2,1)S(1)}, bf16[48,1536]{1,0:T(8,128)(2,1)S(1)}, u32[]{:S(2)}, u32[]{:S(2)}) collective-permute-start(bf16[48,1536]{1,0:T(8,128)(2,1)S(1)} %get-tuple-element.71), channel_id=1, source_target_pairs={{8,0},{10,2},{16,8},{18,10},{24,16},{26,18},{28,24},{30,26},{20,28... | collective-permute-start | bytes 442376 | tf_op jit(solution)/shard_map/ppermute | solution.py:93
  640.2 6.8 collective-permute-start.60
  641.4 6.9 %collective-permute-start.64 = (bf16[48,1536]{1,0:T(8,128)(2,1)S(1)}, bf16[48,1536]{1,0:T(8,128)(2,1)S(1)}, u32[]{:S(2)}, u32[]{:S(2)}) collective-permute-start(bf16[48,1536]{1,0:T(8,128)(2,1)S(1)} %get-tuple-element.69), channel_id=1, source_target_pairs={{8,0},{10,2},{16,8},{18,10},{24,16},{26,18},{28,24},{30,26},{20,28... | collective-permute-start | bytes 442376 | tf_op jit(solution)/shard_map/ppermute | solution.py:93
  642.3 11.0 %collective-permute-start.52 = (bf16[48,3072]{1,0:T(8,128)(2,1)S(1)}, bf16[48,3072]{1,0:T(8,128)(2,1)S(1)}, u32[]{:S(2)}, u32[]{:S(2)}) collective-permute-start(bf16[48,3072]{1,0:T(8,128)(2,1)S(1)} %pad_maximum_fusion.4), channel_id=1, source_target_pairs={{0,8},{2,10},{8,16},{10,18},{16,24},{18,26},{24,28},{26,30},{28,20... | collective-permute-start | bytes 884744 | tf_op jit(solution)/shard_map/ppermute | solution.py:101
  643.7 10.9 %collective-permute-start.56 = (bf16[48,3072]{1,0:T(8,128)(2,1)S(1)}, bf16[48,3072]{1,0:T(8,128)(2,1)S(1)}, u32[]{:S(2)}, u32[]{:S(2)}) collective-permute-start(bf16[48,3072]{1,0:T(8,128)(2,1)S(1)} %pad_maximum_fusion.5), channel_id=1, source_target_pairs={{8,0},{10,2},{16,8},{18,10},{24,16},{26,18},{28,24},{30,26},{20,28... | collective-permute-start | bytes 884744 | tf_op jit(solution)/shard_map/ppermute | solution.py:102
  647.1 12.6 %collective-permute-start.61 = (bf16[48,3072]{1,0:T(8,128)(2,1)S(1)}, bf16[48,3072]{1,0:T(8,128)(2,1)S(1)}, u32[]{:S(2)}, u32[]{:S(2)}) collective-permute-start(bf16[48,3072]{1,0:T(8,128)(2,1)S(1)} %pad_maximum_fusion.6), channel_id=1, source_target_pairs={{0,8},{2,10},{8,16},{10,18},{16,24},{18,26},{24,28},{26,30},{28,20... | collective-permute-start | bytes 884744 | tf_op jit(solution)/shard_map/ppermute | solution.py:101
  648.4 12.4 %collective-permute-start.65 = (bf16[48,3072]{1,0:T(8,128)(2,1)S(1)}, bf16[48,3072]{1,0:T(8,128)(2,1)S(1)}, u32[]{:S(2)}, u32[]{:S(2)}) collective-permute-start(bf16[48,3072]{1,0:T(8,128)(2,1)S(1)} %pad_maximum_fusion.7), channel_id=1, source_target_pairs={{8,0},{10,2},{16,8},{18,10},{24,16},{26,18},{28,24},{30,26},{20,28... | collective-permute-start | bytes 884744 | tf_op jit(solution)/shard_map/ppermute | solution.py:102
  654.7 11.3 %collective-permute-start.53 = (bf16[48,3072]{1,0:T(8,128)(2,1)S(1)}, bf16[48,3072]{1,0:T(8,128)(2,1)S(1)}, u32[]{:S(2)}, u32[]{:S(2)}) collective-permute-start(bf16[48,3072]{1,0:T(8,128)(2,1)S(1)} %get-tuple-element.51), channel_id=1, source_target_pairs={{0,8},{2,10},{8,16},{10,18},{16,24},{18,26},{24,28},{26,30},{28,20... | collective-permute-start | bytes 884744 | tf_op jit(solution)/shard_map/ppermute | solution.py:101
  656.0 11.1 %collective-permute-start.57 = (bf16[48,3072]{1,0:T(8,128)(2,1)S(1)}, bf16[48,3072]{1,0:T(8,128)(2,1)S(1)}, u32[]{:S(2)}, u32[]{:S(2)}) collective-permute-start(bf16[48,3072]{1,0:T(8,128)(2,1)S(1)} %get-tuple-element.52), channel_id=1, source_target_pairs={{8,0},{10,2},{16,8},{18,10},{24,16},{26,18},{28,24},{30,26},{20,28... | collective-permute-start | bytes 884744 | tf_op jit(solution)/shard_map/ppermute | solution.py:102
  661.0 10.8 %collective-permute-start.62 = (bf16[48,3072]{1,0:T(8,128)(2,1)S(1)}, bf16[48,3072]{1,0:T(8,128)(2,1)S(1)}, u32[]{:S(2)}, u32[]{:S(2)}) collective-permute-start(bf16[48,3072]{1,0:T(8,128)(2,1)S(1)} %get-tuple-element.44), channel_id=1, source_target_pairs={{0,8},{2,10},{8,16},{10,18},{16,24},{18,26},{24,28},{26,30},{28,20... | collective-permute-start | bytes 884744 | tf_op jit(solution)/shard_map/ppermute | solution.py:101
  662.4 10.8 %collective-permute-start.66 = (bf16[48,3072]{1,0:T(8,128)(2,1)S(1)}, bf16[48,3072]{1,0:T(8,128)(2,1)S(1)}, u32[]{:S(2)}, u32[]{:S(2)}) collective-permute-start(bf16[48,3072]{1,0:T(8,128)(2,1)S(1)} %get-tuple-element.45), channel_id=1, source_target_pairs={{8,0},{10,2},{16,8},{18,10},{24,16},{26,18},{28,24},{30,26},{20,28... | collective-permute-start | bytes 884744 | tf_op jit(solution)/shard_map/ppermute | solution.py:102
  667.3 9.0 %collective-permute-start.58 = (bf16[48,3072]{1,0:T(8,128)(2,1)S(1)}, bf16[48,3072]{1,0:T(8,128)(2,1)S(1)}, u32[]{:S(2)}, u32[]{:S(2)}) collective-permute-start(bf16[48,3072]{1,0:T(8,128)(2,1)S(1)} %get-tuple-element.50), channel_id=1, source_target_pairs={{8,0},{10,2},{16,8},{18,10},{24,16},{26,18},{28,24},{30,26},{20,28... | collective-permute-start | bytes 884744 | tf_op jit(solution)/shard_map/ppermute | solution.py:102
  668.2 8.2 %collective-permute-start.54 = (bf16[48,3072]{1,0:T(8,128)(2,1)S(1)}, bf16[48,3072]{1,0:T(8,128)(2,1)S(1)}, u32[]{:S(2)}, u32[]{:S(2)}) collective-permute-start(bf16[48,3072]{1,0:T(8,128)(2,1)S(1)} %get-tuple-element.49), channel_id=1, source_target_pairs={{0,8},{2,10},{8,16},{10,18},{16,24},{18,26},{24,28},{26,30},{28,20... | collective-permute-start | bytes 884744 | tf_op jit(solution)/shard_map/ppermute | solution.py:101
  674.1 6.9 %collective-permute-start.67 = (bf16[48,3072]{1,0:T(8,128)(2,1)}, bf16[48,3072]{1,0:T(8,128)(2,1)S(1)}, u32[]{:S(2)}, u32[]{:S(2)}) collective-permute-start(bf16[48,3072]{1,0:T(8,128)(2,1)} %get-tuple-element.43), channel_id=1, source_target_pairs={{8,0},{10,2},{16,8},{18,10},{24,16},{26,18},{28,24},{30,26},{20,28... | collective-permute-start | bytes 884744 | tf_op jit(solution)/shard_map/ppermute | solution.py:102
  674.6 6.8 collective-permute-start.63
  (50 other events, 611.8 us)

commit v2 on v1

--- a/solution.py
+++ b/solution.py
@@ -118,26 +118,23 @@
         )
         return out.reshape(2 * chips * rows, width)
 
-    def kernel(owners_ref, main_ref, tail_ref, main_sib_ref, tail_sib_ref, out_ref, sems):
-        copies = []
+    def kernel(owners_ref, main_ref, tail_ref, main_sib_ref, tail_sib_ref, out_ref):
         for at, (big, small) in enumerate(((main_ref, tail_ref), (main_sib_ref, tail_sib_ref))):
             for i in range(chips):
-                source = small if i == chips - 1 else big.at[pl.ds(i * rows, rows)]
                 owner = owners_ref[at * chips + i]
-                target = out_ref.at[pl.ds(pl.multiple_of(owner * rows, 16), rows)]
-                copies.append(pltpu.make_async_copy(source, target, sems.at[at * chips + i]))
-        for copy in copies:
-            copy.start()
-        for copy in copies:
-            copy.wait()
-
-    anywhere = pl.BlockSpec(memory_space=pl.ANY)
+                target = pl.ds(pl.multiple_of(owner * rows, 16), rows)
+                if i == chips - 1:
+                    out_ref[target, :] = small[...]
+                else:
+                    out_ref[target, :] = big[pl.ds(i * rows, rows), :]
+
+    inside = pl.BlockSpec(memory_space=pltpu.VMEM)
     return pl.pallas_call(
         kernel,
         out_shape=jax.ShapeDtypeStruct((2 * chips * rows, width), main.dtype),
-        in_specs=[pl.BlockSpec(memory_space=pltpu.SMEM)] + [anywhere] * 4,
-        out_specs=anywhere,
-        scratch_shapes=[pltpu.SemaphoreType.DMA((2 * chips,))],
+        in_specs=[pl.BlockSpec(memory_space=pltpu.SMEM)] + [inside] * 4,
+        out_specs=inside,
+        compiler_params=pltpu.CompilerParams(vmem_limit_bytes=32 << 20),
         cost_estimate=pl.CostEstimate(
             flops=0, bytes_accessed=8 * chips * rows * width, transcendentals=0
         ),
@@ -173,33 +170,6 @@
     return scale * (weighted - normed * jnp.mean(weighted * normed, axis=-1, keepdims=True))
 
 
-def toeplitz_rows(by_offset_heads, count):
-    heads_here = by_offset_heads.shape[0]
-    padded = jnp.concatenate(
-        [by_offset_heads, jnp.zeros((heads_here, 1), by_offset_heads.dtype)], axis=1
-    )
-    tiled = jnp.tile(padded, (1, count))
-    window = tiled[:, count - 1 : count - 1 + count * (2 * count - 1)]
-    return window.reshape(heads_here, count, 2 * count - 1)[:, :, :count]
-
-
-def diagonal_sums(matrix):
-    heads_here, count, _ = matrix.shape
-    widened = jnp.concatenate(
-        [matrix, jnp.zeros((heads_here, count, count - 1), matrix.dtype)], axis=2
-    )
-    line = widened.reshape(heads_here, count * (2 * count - 1))
-    line = jnp.concatenate(
-        [
-            jnp.zeros((heads_here, count - 1), matrix.dtype),
-            line,
-            jnp.zeros((heads_here, 1), matrix.dtype),
-        ],
-        axis=1,
-    )
-    return jnp.sum(line.reshape(heads_here, count, 2 * count), axis=1)[:, : 2 * count - 1]
-
-
 def dot32(a, b, dims):
     return lax.dot_general(a, b, (dims, ((), ())), preferred_element_type=F32)
 
@@ -207,6 +177,111 @@
 NN = ((1,), (0,))
 NT = ((1,), (1,))
 TN = ((0,), (0,))
+
+
+VMEM_BYTES = 48 << 20
+
+
+def attention_forward(x, gain, weights, by_offset, seq_col, seq_row):
+    count, d = x.shape
+    head_cols = weights.shape[1] // 4
+    heads = head_cols // HEAD_DIM
+    scale = HEAD_DIM ** (-0.5)
+    lanes = by_offset.shape[1]
+
+    def kernel(x_ref, gain_ref, w_ref, off_ref, col_ref, row_ref, *outs):
+        normed_ref, scale_ref, proj_ref, p_ref, context_ref, part_ref = outs
+        rows = x_ref[...].astype(F32)
+        r = lax.rsqrt(jnp.mean(rows * rows, axis=-1, keepdims=True) + EPS)
+        scale_ref[...] = r
+        normed = (rows * r * gain_ref[...]).astype(BF)
+        normed_ref[...] = normed
+        for s in range(3):
+            at = pl.ds(s * head_cols, head_cols)
+            proj_ref[:, at] = dot32(normed, w_ref[:, at], NN).astype(BF)
+        same = col_ref[...] == row_ref[...]
+        for h in range(heads):
+            q = proj_ref[:, pl.ds(h * HEAD_DIM, HEAD_DIM)]
+            k = proj_ref[:, pl.ds(head_cols + h * HEAD_DIM, HEAD_DIM)]
+            v = proj_ref[:, pl.ds(2 * head_cols + h * HEAD_DIM, HEAD_DIM)]
+            line = jnp.broadcast_to(off_ref[pl.ds(h, 1), :], (count, lanes))
+            bias = pltpu.roll(line, lanes - (count - 1), 1, stride=1, stride_axis=0)[:, :count]
+            scores = jnp.where(same, dot32(q, k, NT) * scale + bias, NEG)
+            expo = jnp.exp(scores - jnp.max(scores, axis=-1, keepdims=True))
+            p = expo / jnp.sum(expo, axis=-1, keepdims=True)
+            p_ref[h] = p
+            context_ref[:, pl.ds(h * HEAD_DIM, HEAD_DIM)] = dot32(p.astype(BF), v, NN).astype(BF)
+        out_w = w_ref[:, pl.ds(3 * head_cols, head_cols)]
+        part_ref[...] = dot32(context_ref[...], out_w, NT).astype(BF)
+
+    inside = pl.BlockSpec(memory_space=pltpu.VMEM)
+    return pl.pallas_call(
+        kernel,
+        out_shape=(
+            jax.ShapeDtypeStruct((count, d), BF),
+            jax.ShapeDtypeStruct((count, 1), F32),
+            jax.ShapeDtypeStruct((count, 3 * head_cols), BF),
+            jax.ShapeDtypeStruct((heads, count, count), F32),
+            jax.ShapeDtypeStruct((count, head_cols), BF),
+            jax.ShapeDtypeStruct((count, d), BF),
+        ),
+        in_specs=[inside] * 6,
+        out_specs=(inside,) * 6,
+        compiler_params=pltpu.CompilerParams(vmem_limit_bytes=VMEM_BYTES),
+        cost_estimate=pl.CostEstimate(
+            flops=8 * count * d * head_cols + 4 * heads * count * count * HEAD_DIM,
+            bytes_accessed=2 * d * 4 * head_cols + 4 * heads * count * count + 8 * count * d,
+            transcendentals=heads * count * count,
+        ),
+        name="attention_forward",
+    )(x, gain, weights, by_offset, seq_col, seq_row)
+
+
+def attention_backward(grad, weights, proj, p_full, context, lanes):
+    count, d = grad.shape
+    head_cols = weights.shape[1] // 4
+    heads = head_cols // HEAD_DIM
+    scale = HEAD_DIM ** (-0.5)
+
+    def kernel(grad_ref, w_ref, proj_ref, p_ref, out_ref, sums_ref, gc_ref):
+        out_w = w_ref[:, pl.ds(3 * head_cols, head_cols)]
+        gc_ref[...] = dot32(grad_ref[...], out_w, NN).astype(BF)
+        down = lax.broadcasted_iota(jnp.int32, (count, count), 0)
+        across = lax.broadcasted_iota(jnp.int32, (count, count), 1)
+        flip = (down + across == count - 1).astype(F32).astype(BF)
+        for h in range(heads):
+            at = [pl.ds(s * head_cols + h * HEAD_DIM, HEAD_DIM) for s in range(3)]
+            q, k, v = proj_ref[:, at[0]], proj_ref[:, at[1]], proj_ref[:, at[2]]
+            p = p_ref[h]
+            gc = gc_ref[:, at[0]]
+            dp = dot32(gc, v, NT)
+            ds = (p * (dp - jnp.sum(p * dp, axis=-1, keepdims=True))).astype(BF)
+            out_ref[:, at[0]] = (dot32(ds, k, NN) * scale).astype(BF)
+            out_ref[:, at[1]] = (dot32(ds, q, TN) * scale).astype(BF)
+            out_ref[:, at[2]] = dot32(p.astype(BF), gc, TN).astype(BF)
+            turned = dot32(ds, flip, TN)
+            wide = jnp.concatenate([turned, jnp.zeros((count, lanes - count), F32)], axis=1)
+            rolled = pltpu.roll(wide, 0, 1, stride=1, stride_axis=0)
+            sums_ref[pl.ds(h, 1), :] = jnp.sum(rolled, axis=0, keepdims=True)
+
+    inside = pl.BlockSpec(memory_space=pltpu.VMEM)
+    return pl.pallas_call(
+        kernel,
+        out_shape=(
+            jax.ShapeDtypeStruct((count, 3 * head_cols), BF),
+            jax.ShapeDtypeStruct((heads, lanes), F32),
+        ),
+        in_specs=[inside] * 4,
+        out_specs=(inside,) * 2,
+        scratch_shapes=[pltpu.VMEM((count, head_cols), BF)],
+        compiler_params=pltpu.CompilerParams(vmem_limit_bytes=VMEM_BYTES),
+        cost_estimate=pl.CostEstimate(
+            flops=2 * count * d * head_cols + 12 * heads * count * count * HEAD_DIM,
+            bytes_accessed=4 * heads * count * count + 8 * count * d,
+            transcendentals=0,
+        ),
+        name="attention_backward",
+    )(grad, weights, proj, p_full)
 
 
 def body(
@@ -234,40 +309,27 @@
     count = 2 * rows_local
 
     attn_shard = jnp.concatenate([w_qkv.reshape(shard, 3 * head_cols), w_out], axis=1)
-    x_all = whole_rows(block_in, swap_tensor(block_in), rank).astype(F32)
+    x_low = whole_rows(block_in, swap_tensor(block_in), rank)
+    x_all = x_low.astype(F32)
     attn_all = ring.gather(attn_shard)
     in_all = ring.gather(w_in.reshape(shard, EXPERTS * units))
     down_all = ring.gather(w_down.reshape(shard, EXPERTS * units))
-    qkv_all, out_all = attn_all[:, : 3 * head_cols], attn_all[:, 3 * head_cols :]
     grad_out = whole_rows(out_grad, swap_tensor(out_grad), rank).astype(F32)
-
-    scale_one = rms_scale(x_all)
-    n_one = x_all * scale_one
-    normed_one = (n_one * attn_gain).astype(BF)
-    projected = dot32(normed_one, qkv_all, NN).astype(BF).reshape(count, 3, heads_local, HEAD_DIM)
-    queries, keys_all, values_all = projected[:, 0], projected[:, 1], projected[:, 2]
 
     places = jnp.arange(count, dtype=jnp.int32)
     ends = jnp.cumsum(seq_lengths[0])
     seq_ids = jnp.sum((places[:, None] >= ends[None, :]).astype(jnp.int32), axis=1)
-    same_seq = seq_ids[:, None] == seq_ids[None, :]
     bias_local = lax.dynamic_slice_in_dim(rel_bias, rank * heads_local, heads_local, 1)
     bucket_hits = (
         rel_table[:, None] == jnp.arange(rel_bias.shape[0], dtype=jnp.int32)[None, :]
     ).astype(F32)
     by_offset = jnp.dot(bucket_hits, bias_local, precision=HIGH)
-    bias = jnp.where(same_seq[None], toeplitz_rows(by_offset.T, count), NEG)
-    scale = HEAD_DIM ** (-0.5)
-    scores = (
-        jnp.einsum("qhd,khd->hqk", queries, keys_all, preferred_element_type=F32) * scale + bias
-    )
-    row_max = jnp.max(scores, axis=-1, keepdims=True)
-    expo = jnp.exp(scores - row_max)
-    p_full = expo / jnp.sum(expo, axis=-1, keepdims=True)
-    probs = p_full.astype(BF)
-    context = jnp.einsum("hqk,khd->qhd", probs, values_all, preferred_element_type=F32)
-    context = context.reshape(count, head_cols).astype(BF)
-    attn_part = dot32(context, out_all, NT).astype(BF)
+    lanes = 2 * count
+    by_offset = jnp.pad(by_offset.T, ((0, 0), (0, lanes - by_offset.shape[0])))
+    normed_one, scale_one, projected, p_full, context, attn_part = attention_forward(
+        x_low, attn_gain[None, :], attn_all, by_offset, seq_ids[:, None], seq_ids[None, :]
+    )
+    n_one = x_all * scale_one
     hidden = x_all + (attn_part.astype(F32) + swap_tensor(attn_part).astype(F32))
 
     scale_two = rms_scale(hidden)
@@ -339,37 +401,20 @@
 
     grad_hidden = grad_out + norm_back(grad_mixed, n_two, scale_two, moe_gain)
     grad_attended = grad_hidden.astype(BF)
-    grad_context = dot32(grad_attended, out_all, NN).astype(BF)
+    grad_projected, offset_sums = attention_backward(
+        grad_attended, attn_all, projected, p_full, context, lanes
+    )
     grad_w_out = dot32(grad_attended, context, TN).astype(BF)
-    grad_context_heads = grad_context.reshape(count, heads_local, HEAD_DIM)
-    grad_probs = jnp.einsum(
-        "qhd,khd->hqk", grad_context_heads, values_all, preferred_element_type=F32
-    )
-    inner = jnp.sum(p_full * grad_probs, axis=-1, keepdims=True)
-    grad_scores = (p_full * (grad_probs - inner)).astype(BF)
-    grad_queries = (
-        jnp.einsum("hqk,khd->qhd", grad_scores, keys_all, preferred_element_type=F32) * scale
-    )
-    grad_keys = (
-        jnp.einsum("hqk,qhd->khd", grad_scores, queries, preferred_element_type=F32) * scale
-    )
-    grad_values = jnp.einsum(
-        "hqk,qhd->khd", probs, grad_context_heads, preferred_element_type=F32
-    )
-    grad_projected = jnp.concatenate(
-        [g.reshape(count, head_cols) for g in (grad_queries, grad_keys, grad_values)], axis=1
-    ).astype(BF)
     grad_w_qkv = dot32(normed_one, grad_projected, TN).astype(BF)
     attn_mine = ring.scatter(jnp.concatenate([grad_w_qkv, grad_w_out], axis=1), shard)
-    normed_part = dot32(grad_projected, qkv_all, NT)
+    normed_part = dot32(grad_projected, attn_all[:, : 3 * head_cols], NT)
     attn_gain_part = jnp.sum(normed_part * n_one, axis=0)
     normed_low = normed_part.astype(BF)
     grad_normed = own_rows(normed_low).astype(F32) + swap_tensor(other_rows(normed_low)).astype(F32)
     grad_block = own_rows(grad_hidden) + norm_back(
         grad_normed, own_rows(n_one), own_rows(scale_one), attn_gain
     )
-    offset_sums = diagonal_sums(grad_scores.astype(F32))
-    grad_bias_heads = jnp.dot(offset_sums, bucket_hits, precision=HIGH)
+    grad_bias_heads = jnp.dot(offset_sums[:, : rel_table.shape[0]], bucket_hits, precision=HIGH)
     grad_rel = lax.dynamic_update_slice_in_dim(
         jnp.zeros(rel_bias.shape, F32), grad_bias_heads.T, rank * heads_local, 1
     )

time: 693 us -> 275 us (0.40)
  Pallas kernels: 363 us -> 13.8 us
  local copies, waits for them, and re-layouts: 87.3 us -> 32.7 us
  matrix products: 41.8 us -> 19.9 us
  waiting for transfers between devices: 91.6 us -> 103 us
    pallas_call x3, Pallas kernels: 363 us -> 5.74 us  [assemble(): pl.pallas_call(kernel, out_shape=jax.ShapeDtypeStruct((2 * chips * rows,...]
    unnamed x126 -> x107, local copies, waits for them, and re-layouts: 45.8 us -> 16.7 us
    reshape x3 -> x0, local copies, waits for them, and re-layouts: 14.8 us -> none  [the longest x2 10.1 us: diagonal_sums(): line = widened.reshape(heads_here, count * (2 * count - 1))]
    dot_general x22 -> x19, matrix products: 33.4 us -> 19.3 us  [dot32(): return lax.dot_general(a, b, (dims, ((), ())), preferred_element_type=F32)]
    ppermute x9, waiting for transfers between devices: 11.8 us -> 20.7 us  [gather(): r = lax.ppermute(r, 'dp', self.right)]
    pallas_call x0 -> x2, Pallas kernels: none -> 8.08 us  [the longest x1 4.17 us: attention_forward(): pl.pallas_call(kernel, out_shape=(jax.ShapeDtypeStruct((count, d), BF), j...]
    dot_general x7 -> x1, matrix products: 8.08 us -> 0.36 us  [body(): jnp.dot(offset_sums[:, :rel_table.shape[0]], bucket_hits, precision=HIGH)]
  transfers between devices with their start and end apart: 68 -> 68, of which waited for: 38 -> 36; matrix products, arithmetic and copies ran while one was open for 20% -> 23% of each run, Pallas kernels for 32% -> 4%
where the time goes in v2:
time: 275 us; the launch traced here: 270 us
  waiting for transfers between devices  103 us (37%)
  starting transfers between devices  69.4 us (25%)
  local copies, waits for them, and re-layouts  32.7 us (12%)
  other arithmetic  29.5 us (11%)
  matrix products  19.9 us (7%)
  Pallas kernels  13.8 us (5%)
    ppermute x7, waiting for transfers between devices, swap_tensor(): return lax.ppermute(x, 'tensor', [(0, 1), (1, 0)])  21.9 us
    ppermute x9, waiting for transfers between devices, gather(): r = lax.ppermute(r, 'dp', self.right)  20.7 us
    ppermute x9, waiting for transfers between devices, scatter(): r = lax.ppermute(r, 'dp', self.right)  19.3 us
    dot_general x19, matrix products, dot32(): return lax.dot_general(a, b, (dims, ((), ())), preferred_element_type=F32)  19.3 us
    unnamed x107, local copies, waits for them, and re-layouts  16.7 us
    ppermute x9, starting transfers between devices, gather(): r = lax.ppermute(r, 'dp', self.right)  14.7 us
    ppermute x9, starting transfers between devices, scatter(): l = lax.ppermute(l, 'dp', self.left)  9.55 us
    ppermute x9, waiting for transfers between devices, scatter(): l = lax.ppermute(l, 'dp', self.left)  9.44 us
  transfers between devices with their start and end apart: 68, of which 36 were waited for; matrix products, arithmetic and copies ran while one was open for 23% of the time, Pallas kernels for 4%

profile of v2, /device:TPU:0, one launch (start us, length us, event | category | flops | bytes accessed | tf_op | source)
XLA Modules:
  0.0 270.4 jit_solution(15520344381367999715)
XLA Ops:
  1.8 3.1 %collective-permute-start.22 = (bf16[48,3072]{1,0:T(8,128)(2,1)S(1)}, bf16[48,3072]{1,0:T(8,128)(2,1)S(1)}, u32[]{:S(2)}, u32[]{:S(2)}) collective-permute-start(bf16[48,3072]{1,0:T(8,128)(2,1)S(1)} %bitcast.172), channel_id=1, source_target_pairs={{0,8},{2,10},{8,16},{10,18},{16,24},{18,26},{24,28},{26,30},{28,20... | collective-permute-start | bytes 884744 | tf_op jit(solution)/shard_map/ppermute | solution.py:61
  5.8 2.1 collective-permute-start.12
  9.5 1.4 constant_dynamic-update-slice_fusion
  10.9 2.0 collective-permute-start.1
  17.2 4.0 %collective-permute-done.1 = bf16[48,1536]{1,0:T(8,128)(2,1)S(1)} collective-permute-done((bf16[48,1536]{1,0:T(8,128)(2,1)}, bf16[48,1536]{1,0:T(8,128)(2,1)S(1)}, u32[]{:S(2)}, u32[]{:S(2)}) %collective-permute-start.1) | collective-permute-done | bytes 147488 | tf_op jit(solution)/shard_map/ppermute | solution.py:61
  21.2 1.7 collective-permute-start.2
  23.0 3.6 %collective-permute-done.2 = bf16[48,1536]{1,0:T(8,128)(2,1)S(1)} collective-permute-done((bf16[48,1536]{1,0:T(8,128)(2,1)}, bf16[48,1536]{1,0:T(8,128)(2,1)S(1)}, u32[]{:S(2)}, u32[]{:S(2)}) %collective-permute-start.2) | collective-permute-done | bytes 147488 | tf_op jit(solution)/shard_map/ppermute | solution.py:62
  26.6 1.8 collective-permute-start
  28.4 4.0 %collective-permute-done = bf16[128,768]{1,0:T(8,128)(2,1)S(1)} collective-permute-done((bf16[128,768]{1,0:T(8,128)(2,1)S(1)}, bf16[128,768]{1,0:T(8,128)(2,1)S(1)}, u32[]{:S(2)}, u32[]{:S(2)}) %collective-permute-start) | collective-permute-done | bytes 196640 | tf_op jit(solution)/shard_map/ppermute | solution.py:146
  32.4 2.1 collective-permute-start.33
  35.6 1.6 collective-permute-start.3
  39.2 1.6 collective-permute-start.24
  42.7 1.6 collective-permute-start.14
  44.3 1.6 collective-permute-start.5
  45.9 8.6 %collective-permute-done.5 = bf16[48,1536]{1,0:T(8,128)(2,1)S(1)} collective-permute-done((bf16[48,1536]{1,0:T(8,128)(2,1)S(1)}, bf16[48,1536]{1,0:T(8,128)(2,1)S(1)}, u32[]{:S(2)}, u32[]{:S(2)}) %collective-permute-start.5) | collective-permute-done | bytes 147488 | tf_op jit(solution)/shard_map/ppermute | solution.py:61
  54.5 1.5 collective-permute-start.6
  56.0 3.6 %collective-permute-done.6 = bf16[48,1536]{1,0:T(8,128)(2,1)S(1)} collective-permute-done((bf16[48,1536]{1,0:T(8,128)(2,1)S(1)}, bf16[48,1536]{1,0:T(8,128)(2,1)S(1)}, u32[]{:S(2)}, u32[]{:S(2)}) %collective-permute-start.6) | collective-permute-done | bytes 147488 | tf_op jit(solution)/shard_map/ppermute | solution.py:62
  59.7 1.6 collective-permute-start.7
  61.3 2.7 %collective-permute-done.7 = bf16[48,768]{1,0:T(8,128)(2,1)S(1)} collective-permute-done((bf16[48,768]{1,0:T(8,128)(2,1)S(1)}, bf16[48,768]{1,0:T(8,128)(2,1)S(1)}, u32[]{:S(2)}, u32[]{:S(2)}) %collective-permute-start.7) | collective-permute-done | bytes 73760 | tf_op jit(solution)/shard_map/ppermute | solution.py:67
  64.0 1.5 collective-permute-start.8
  65.5 2.9 %collective-permute-done.8 = bf16[48,768]{1,0:T(8,128)(2,1)S(1)} collective-permute-done((bf16[48,768]{1,0:T(8,128)(2,1)S(1)}, bf16[48,768]{1,0:T(8,128)(2,1)S(1)}, u32[]{:S(2)}, u32[]{:S(2)}) %collective-permute-start.8) | collective-permute-done | bytes 73760 | tf_op jit(solution)/shard_map/ppermute | solution.py:68
  68.4 1.5 collective-permute-start.15
  73.2 1.8 collective-permute-done.15
  75.1 1.5 collective-permute-start.27
  77.3 3.6 %collective-permute-done.26 = bf16[48,3072]{1,0:T(8,128)(2,1)S(1)} collective-permute-done((bf16[48,3072]{1,0:T(8,128)(2,1)S(1)}, bf16[48,3072]{1,0:T(8,128)(2,1)S(1)}, u32[]{:S(2)}, u32[]{:S(2)}) %collective-permute-start.26) | collective-permute-done | bytes 294944 | tf_op jit(solution)/shard_map/ppermute | solution.py:61
  82.2 1.5 collective-permute-start.17
  84.5 4.5 %collective-permute-done.16 = bf16[48,3072]{1,0:T(8,128)(2,1)S(1)} collective-permute-done((bf16[48,3072]{1,0:T(8,128)(2,1)S(1)}, bf16[48,3072]{1,0:T(8,128)(2,1)S(1)}, u32[]{:S(2)}, u32[]{:S(2)}) %collective-permute-start.16) | collective-permute-done | bytes 294944 | tf_op jit(solution)/shard_map/ppermute | solution.py:61
  90.3 1.5 collective-permute-start.29
  92.5 1.8 collective-permute-done.28
  94.9 4.6 %collective-permute-done.18 = bf16[48,1536]{1,0:T(8,128)(2,1)S(1)} collective-permute-done((bf16[48,1536]{1,0:T(8,128)(2,1)S(1)}, bf16[48,1536]{1,0:T(8,128)(2,1)S(1)}, u32[]{:S(2)}, u32[]{:S(2)}) %collective-permute-start.18) | collective-permute-done | bytes 147488 | tf_op jit(solution)/shard_map/ppermute | solution.py:67
  100.2 1.7 collective-permute-start.19
  102.6 4.2 %attention_forward.1 = (bf16[256,768]{1,0:T(8,128)(2,1)S(1)}, f32[256,1]{1,0:T(8,128)S(1)}, bf16[256,1152]{1,0:T(8,128)(2,1)S(1)}, f32[6,256,256]{2,1,0:T(8,128)...) custom-call(bf16[256,768]{1,0:T(8,128)(2,1)S(1)} %maximum_select_fusion.x_ref, ...), custom_call_target="tpu_custom_call" | custom-call | flops 704643072 | bytes 5505024 | tf_op jit(solution)/shard_map/attention_forward/pallas_call | solution.py:218
  111.2 1.5 dynamic-slice_reduce_fusion
  112.7 7.9 %collective-permute-done.11 = bf16[256,768]{1,0:T(8,128)(2,1)} collective-permute-done((bf16[256,768]{1,0:T(8,128)(2,1)}, bf16[256,768]{1,0:T(8,128)(2,1)}, u32[]{:S(2)}, u32[]{:S(2)}) %collective-permute-start.11) | collective-permute-done | bytes 393248 | tf_op jit(solution)/shard_map/ppermute | solution.py:146
  122.4 1.7 convolution_convert_fusion.6
  124.6 2.5 assemble.4
  128.4 2.5 assemble.5
  140.9 1.7 fusion.52
  144.3 1.6 collective-permute-start.34
  146.6 1.7 dynamic-slice_bitcast_fusion.1
  148.3 2.9 %pad_maximum_fusion.1 = bf16[768,3072]{1,0:T(8,128)(2,1)} fusion(bf16[768,1536]{1,0:T(8,128)(2,1)S(1)} %convolution_convert_fusion, bf16[768,1536]{1,0:T(8,128)(2,1)S(1)} %convolution_convert_fusion.1), kind=kLoop, calls=%fused_computation.1 | loop fusion | flops 9437184 | bytes 9437184 | tf_op jit(solution)/shard_map/concatenate | solution.py:360
  151.2 8.1 %collective-permute-done.34 = bf16[256,768]{1,0:T(8,128)(2,1)S(1)} collective-permute-done((bf16[256,768]{1,0:T(8,128)(2,1)S(1)}, bf16[256,768]{1,0:T(8,128)(2,1)S(1)}, u32[]{:S(2)}, u32[]{:S(2)}) %collective-permute-start.34) | collective-permute-done | bytes 393248 | tf_op jit(solution)/shard_map/ppermute | solution.py:146
  159.9 2.6 fusion.106
  162.5 3.9 %attention_backward.1 = (bf16[256,1152]{1,0:T(8,128)(2,1)S(1)}, f32[6,512]{1,0:T(8,128)S(1)}) custom-call(bf16[256,768]{1,0:T(8,128)(2,1)S(1)} %get-tuple-element.54.grad_ref, bf16[768,1536]{1,0:T(8,128)(2,1)S(1)} %assemble.3.w_ref, bf16[256,1152]{1,0:T(8,128)(2,1)S(1)} %copy-done.7, f32[6,256,256]{2,1,0:T(8,128)S(1)} %copy-done.3), custom_call_target="tpu_custom_call" | custom-call | flops 452984832 | bytes 3145728 | tf_op jit(solution)/shard_map/attention_backward/pallas_call | solution.py:268
  168.0 2.8 %multiply_reduce_fusion.3 = (f32[768]{0:T(1024)S(1)}, bf16[256,768]{1,0:T(8,128)(2,1)S(1)}, f32[256,768]{1,0:T(8,128)}) fusion(f32[256]{0:T(256)S(1)} %reduce.6, bf16[256,768]{1,0:T(8,128)(2,1)S(1)} %maximum_select_fusion.x_ref, bf16[256,1152]{1,0:T(8,128)(2,1)} %copy-done.8, bf16[768,1536]{1,0:T(8,128)(2,1)S(1)} %assemble.3.w_ref), kind=kOutput, calls=%fused_computation.73 | convolution fusion | flops 453967104 | bytes 3936256 | tf_op jit(solution)/shard_map/dot_general | solution.py:174
  172.8 1.8 collective-permute-done.36
  175.8 1.6 collective-permute-start.38
  177.7 1.8 collective-permute-done.38
  180.7 1.7 add_convert_fusion
  185.7 2.2 collective-permute-done.40
  189.0 1.4 collective-permute-start.42
  191.4 2.5 collective-permute-done.42
  200.0 1.5 multiply_reduce_fusion.8
  203.9 1.5 collective-permute-start.48
  205.4 4.2 %collective-permute-done.44 = bf16[48,1536]{1,0:T(8,128)(2,1)S(1)} collective-permute-done((bf16[48,1536]{1,0:T(8,128)(2,1)S(1)}, bf16[48,1536]{1,0:T(8,128)(2,1)S(1)}, u32[]{:S(2)}, u32[]{:S(2)}) %collective-permute-start.44) | collective-permute-done | bytes 147488 | tf_op jit(solution)/shard_map/ppermute | solution.py:101
  211.8 1.8 multiply_add_fusion
  217.4 3.7 %fusion.1 = bf16[8,48,3072]{2,1,0:T(8,128)(2,1)S(1)} fusion(bf16[8,48,3072]{2,1,0:T(8,128)(2,1)} %collective-permute-done.50, bf16[8,2,48,3072]{3,2,1,0:T(8,128)(2,1)} %bitcast.166, s32[]{:T(128)S(6)} %select_n.308), kind=kLoop, calls=%fused_computation.5 | loop fusion | flops 4718592 | bytes 7077892 | tf_op jit(solution)/shard_map/convert_element_type | solution.py:86
  223.4 2.6 fusion
  230.5 2.5 collective-permute-done.60
  235.3 4.0 %collective-permute-done.52 = bf16[48,3072]{1,0:T(8,128)(2,1)S(1)} collective-permute-done((bf16[48,3072]{1,0:T(8,128)(2,1)S(1)}, bf16[48,3072]{1,0:T(8,128)(2,1)S(1)}, u32[]{:S(2)}, u32[]{:S(2)}) %collective-permute-start.52) | collective-permute-done | bytes 294944 | tf_op jit(solution)/shard_map/ppermute | solution.py:101
  242.4 3.2 %collective-permute-done.61 = bf16[48,3072]{1,0:T(8,128)(2,1)S(1)} collective-permute-done((bf16[48,3072]{1,0:T(8,128)(2,1)S(1)}, bf16[48,3072]{1,0:T(8,128)(2,1)S(1)}, u32[]{:S(2)}, u32[]{:S(2)}) %collective-permute-start.61) | collective-permute-done | bytes 294944 | tf_op jit(solution)/shard_map/ppermute | solution.py:101
  248.8 3.2 %collective-permute-done.53 = bf16[48,3072]{1,0:T(8,128)(2,1)S(1)} collective-permute-done((bf16[48,3072]{1,0:T(8,128)(2,1)S(1)}, bf16[48,3072]{1,0:T(8,128)(2,1)S(1)}, u32[]{:S(2)}, u32[]{:S(2)}) %collective-permute-start.53) | collective-permute-done | bytes 294944 | tf_op jit(solution)/shard_map/ppermute | solution.py:101
  255.1 3.0 %collective-permute-done.62 = bf16[48,3072]{1,0:T(8,128)(2,1)S(1)} collective-permute-done((bf16[48,3072]{1,0:T(8,128)(2,1)S(1)}, bf16[48,3072]{1,0:T(8,128)(2,1)S(1)}, u32[]{:S(2)}, u32[]{:S(2)}) %collective-permute-start.62) | collective-permute-done | bytes 294944 | tf_op jit(solution)/shard_map/ppermute | solution.py:101
  263.8 3.2 %collective-permute-done.67 = bf16[48,3072]{1,0:T(8,128)(2,1)S(1)} collective-permute-done((bf16[48,3072]{1,0:T(8,128)(2,1)}, bf16[48,3072]{1,0:T(8,128)(2,1)S(1)}, u32[]{:S(2)}, u32[]{:S(2)}) %collective-permute-start.67) | collective-permute-done | bytes 294944 | tf_op jit(solution)/shard_map/ppermute | solution.py:102
  (321 shorter events, 96.7 us)
Async XLA Ops:
  1.8 33.9 %collective-permute-start.22 = (bf16[48,3072]{1,0:T(8,128)(2,1)S(1)}, bf16[48,3072]{1,0:T(8,128)(2,1)S(1)}, u32[]{:S(2)}, u32[]{:S(2)}) collective-permute-start(bf16[48,3072]{1,0:T(8,128)(2,1)S(1)} %bitcast.172), channel_id=1, source_target_pairs={{0,8},{2,10},{8,16},{10,18},{16,24},{18,26},{24,28},{26,30},{28,20... | collective-permute-start | bytes 884744 | tf_op jit(solution)/shard_map/ppermute | solution.py:61
  4.8 33.1 %collective-permute-start.23 = (bf16[48,3072]{1,0:T(8,128)(2,1)S(1)}, bf16[48,3072]{1,0:T(8,128)(2,1)S(1)}, u32[]{:S(2)}, u32[]{:S(2)}) collective-permute-start(bf16[48,3072]{1,0:T(8,128)(2,1)S(1)} %bitcast.173), channel_id=1, source_target_pairs={{8,0},{10,2},{16,8},{18,10},{24,16},{26,18},{28,24},{30,26},{20,28... | collective-permute-start | bytes 884744 | tf_op jit(solution)/shard_map/ppermute | solution.py:62
  5.8 33.3 %collective-permute-start.12 = (bf16[48,3072]{1,0:T(8,128)(2,1)S(1)}, bf16[48,3072]{1,0:T(8,128)(2,1)S(1)}, u32[]{:S(2)}, u32[]{:S(2)}) collective-permute-start(bf16[48,3072]{1,0:T(8,128)(2,1)S(1)} %bitcast.169), channel_id=1, source_target_pairs={{0,8},{2,10},{8,16},{10,18},{16,24},{18,26},{24,28},{26,30},{28,20... | collective-permute-start | bytes 884744 | tf_op jit(solution)/shard_map/ppermute | solution.py:61
  7.9 33.6 %collective-permute-start.13 = (bf16[48,3072]{1,0:T(8,128)(2,1)S(1)}, bf16[48,3072]{1,0:T(8,128)(2,1)S(1)}, u32[]{:S(2)}, u32[]{:S(2)}) collective-permute-start(bf16[48,3072]{1,0:T(8,128)(2,1)S(1)} %bitcast.170), channel_id=1, source_target_pairs={{8,0},{10,2},{16,8},{18,10},{24,16},{26,18},{28,24},{30,26},{20,28... | collective-permute-start | bytes 884744 | tf_op jit(solution)/shard_map/ppermute | solution.py:62
  10.9 10.4 %collective-permute-start.1 = (bf16[48,1536]{1,0:T(8,128)(2,1)}, bf16[48,1536]{1,0:T(8,128)(2,1)S(1)}, u32[]{:S(2)}, u32[]{:S(2)}) collective-permute-start(bf16[48,1536]{1,0:T(8,128)(2,1)} %get-tuple-element.94), channel_id=1, source_target_pairs={{0,8},{2,10},{8,16},{10,18},{16,24},{18,26},{24,28},{26,30},{28,20... | collective-permute-start | bytes 442376 | tf_op jit(solution)/shard_map/ppermute | solution.py:61
  21.2 5.4 %collective-permute-start.2 = (bf16[48,1536]{1,0:T(8,128)(2,1)}, bf16[48,1536]{1,0:T(8,128)(2,1)S(1)}, u32[]{:S(2)}, u32[]{:S(2)}) collective-permute-start(bf16[48,1536]{1,0:T(8,128)(2,1)} %get-tuple-element.94), channel_id=1, source_target_pairs={{8,0},{10,2},{16,8},{18,10},{24,16},{26,18},{28,24},{30,26},{20,28... | collective-permute-start | bytes 442376 | tf_op jit(solution)/shard_map/ppermute | solution.py:62
  26.6 5.8 %collective-permute-start = (bf16[128,768]{1,0:T(8,128)(2,1)S(1)}, bf16[128,768]{1,0:T(8,128)(2,1)S(1)}, u32[]{:S(2)}, u32[]{:S(2)}) collective-permute-start(bf16[128,768]{1,0:T(8,128)(2,1)S(1)} %copy-done.25), channel_id=1, source_target_pairs={{0,1},{1,0},{2,3},{3,2},{4,5},{5,4},{6,7},{7,6},{8,9},{9,8},{10,11... | collective-permute-start | bytes 589832 | tf_op jit(solution)/shard_map/ppermute | solution.py:146
  32.4 90.0 %collective-permute-start.33 = (bf16[128,768]{1,0:T(8,128)(2,1)}, bf16[128,768]{1,0:T(8,128)(2,1)}, u32[]{:S(2)}, u32[]{:S(2)}) collective-permute-start(bf16[128,768]{1,0:T(8,128)(2,1)} %param.25), channel_id=1, source_target_pairs={{0,1},{1,0},{2,3},{3,2},{4,5},{5,4},{6,7},{7,6},{8,9},{9,8},{10,11... | collective-permute-start | bytes 589832 | tf_op jit(solution)/shard_map/ppermute | solution.py:146
  35.6 7.1 %collective-permute-start.3 = (bf16[48,1536]{1,0:T(8,128)(2,1)}, bf16[48,1536]{1,0:T(8,128)(2,1)S(1)}, u32[]{:S(2)}, u32[]{:S(2)}) collective-permute-start(bf16[48,1536]{1,0:T(8,128)(2,1)} %copy-done.26), channel_id=1, source_target_pairs={{0,8},{2,10},{8,16},{10,18},{16,24},{18,26},{24,28},{26,30},{28,20... | collective-permute-start | bytes 442376 | tf_op jit(solution)/shard_map/ppermute | solution.py:61
  38.0 6.3 %collective-permute-start.4 = (bf16[48,1536]{1,0:T(8,128)(2,1)S(1)}, bf16[48,1536]{1,0:T(8,128)(2,1)S(1)}, u32[]{:S(2)}, u32[]{:S(2)}) collective-permute-start(bf16[48,1536]{1,0:T(8,128)(2,1)S(1)} %collective-permute-done.2), channel_id=1, source_target_pairs={{8,0},{10,2},{16,8},{18,10},{24,16},{26,18},{28,24},{30,26},{20,28... | collective-permute-start | bytes 442376 | tf_op jit(solution)/shard_map/ppermute | solution.py:62
  39.2 30.7 %collective-permute-start.24 = (bf16[48,3072]{1,0:T(8,128)(2,1)S(1)}, bf16[48,3072]{1,0:T(8,128)(2,1)S(1)}, u32[]{:S(2)}, u32[]{:S(2)}) collective-permute-start(bf16[48,3072]{1,0:T(8,128)(2,1)S(1)} %collective-permute-done.22), channel_id=1, source_target_pairs={{0,8},{2,10},{8,16},{10,18},{16,24},{18,26},{24,28},{26,30},{28,20... | collective-permute-start | bytes 884744 | tf_op jit(solution)/shard_map/ppermute | solution.py:61
  41.5 29.2 %collective-permute-start.25 = (bf16[48,3072]{1,0:T(8,128)(2,1)S(1)}, bf16[48,3072]{1,0:T(8,128)(2,1)S(1)}, u32[]{:S(2)}, u32[]{:S(2)}) collective-permute-start(bf16[48,3072]{1,0:T(8,128)(2,1)S(1)} %collective-permute-done.23), channel_id=1, source_target_pairs={{8,0},{10,2},{16,8},{18,10},{24,16},{26,18},{28,24},{30,26},{20,28... | collective-permute-start | bytes 884744 | tf_op jit(solution)/shard_map/ppermute | solution.py:62
  42.7 29.3 %collective-permute-start.14 = (bf16[48,3072]{1,0:T(8,128)(2,1)S(1)}, bf16[48,3072]{1,0:T(8,128)(2,1)S(1)}, u32[]{:S(2)}, u32[]{:S(2)}) collective-permute-start(bf16[48,3072]{1,0:T(8,128)(2,1)S(1)} %collective-permute-done.12), channel_id=1, source_target_pairs={{0,8},{2,10},{8,16},{10,18},{16,24},{18,26},{24,28},{26,30},{28,20... | collective-permute-start | bytes 884744 | tf_op jit(solution)/shard_map/ppermute | solution.py:61
  44.3 10.2 %collective-permute-start.5 = (bf16[48,1536]{1,0:T(8,128)(2,1)S(1)}, bf16[48,1536]{1,0:T(8,128)(2,1)S(1)}, u32[]{:S(2)}, u32[]{:S(2)}) collective-permute-start(bf16[48,1536]{1,0:T(8,128)(2,1)S(1)} %collective-permute-done.3), channel_id=1, source_target_pairs={{0,8},{2,10},{8,16},{10,18},{16,24},{18,26},{24,28},{26,30},{28,20... | collective-permute-start | bytes 442376 | tf_op jit(solution)/shard_map/ppermute | solution.py:61
  54.5 5.1 %collective-permute-start.6 = (bf16[48,1536]{1,0:T(8,128)(2,1)S(1)}, bf16[48,1536]{1,0:T(8,128)(2,1)S(1)}, u32[]{:S(2)}, u32[]{:S(2)}) collective-permute-start(bf16[48,1536]{1,0:T(8,128)(2,1)S(1)} %collective-permute-done.4), channel_id=1, source_target_pairs={{8,0},{10,2},{16,8},{18,10},{24,16},{26,18},{28,24},{30,26},{20,28... | collective-permute-start | bytes 442376 | tf_op jit(solution)/shard_map/ppermute | solution.py:62
  59.7 4.4 %collective-permute-start.7 = (bf16[48,768]{1,0:T(8,128)(2,1)S(1)}, bf16[48,768]{1,0:T(8,128)(2,1)S(1)}, u32[]{:S(2)}, u32[]{:S(2)}) collective-permute-start(bf16[48,768]{1,0:T(8,128)(2,1)S(1)} %slice.211), channel_id=1, source_target_pairs={{0,8},{2,10},{8,16},{10,18},{16,24},{18,26},{24,28},{26,30},{28,20... | collective-permute-start | bytes 221192 | tf_op jit(solution)/shard_map/ppermute | solution.py:67
  64.0 4.4 %collective-permute-start.8 = (bf16[48,768]{1,0:T(8,128)(2,1)S(1)}, bf16[48,768]{1,0:T(8,128)(2,1)S(1)}, u32[]{:S(2)}, u32[]{:S(2)}) collective-permute-start(bf16[48,768]{1,0:T(8,128)(2,1)S(1)} %slice.212), channel_id=1, source_target_pairs={{8,0},{10,2},{16,8},{18,10},{24,16},{26,18},{28,24},{30,26},{20,28... | collective-permute-start | bytes 221192 | tf_op jit(solution)/shard_map/ppermute | solution.py:68
  68.4 6.7 %collective-permute-start.15 = (bf16[48,3072]{1,0:T(8,128)(2,1)S(1)}, bf16[48,3072]{1,0:T(8,128)(2,1)S(1)}, u32[]{:S(2)}, u32[]{:S(2)}) collective-permute-start(bf16[48,3072]{1,0:T(8,128)(2,1)S(1)} %collective-permute-done.13), channel_id=1, source_target_pairs={{8,0},{10,2},{16,8},{18,10},{24,16},{26,18},{28,24},{30,26},{20,28... | collective-permute-start | bytes 884744 | tf_op jit(solution)/shard_map/ppermute | solution.py:62
  69.9 30.3 %collective-permute-start.9 = (bf16[336,1536]{1,0:T(8,128)(2,1)S(1)}, bf16[336,1536]{1,0:T(8,128)(2,1)S(1)}, u32[]{:S(2)}, u32[]{:S(2)}) collective-permute-start(bf16[336,1536]{1,0:T(8,128)(2,1)S(1)} %constant_dynamic-update-slice_fusion.2.main_ref), channel_id=1, source_target_pairs={{0,2},{2,0},{4,6},{6,4},{8,10},{10,8},{12,14},{14,12},{16,18},{18,... | collective-permute-start | bytes 3096584 | tf_op jit(solution)/shard_map/ppermute | solution.py:66
  70.7 28.9 %collective-permute-start.10 = (bf16[48,1536]{1,0:T(8,128)(2,1)S(1)}, bf16[48,1536]{1,0:T(8,128)(2,1)S(1)}, u32[]{:S(2)}, u32[]{:S(2)}) collective-permute-start(bf16[48,1536]{1,0:T(8,128)(2,1)S(1)} %constant_dynamic-update-slice_fusion.10.tail_ref), channel_id=1, source_target_pairs={{0,2},{2,0},{4,6},{6,4},{8,10},{10,8},{12,14},{14,12},{16,18},{18,... | collective-permute-start | bytes 442376 | tf_op jit(solution)/shard_map/ppermute | solution.py:70
  72.0 8.9 %collective-permute-start.26 = (bf16[48,3072]{1,0:T(8,128)(2,1)S(1)}, bf16[48,3072]{1,0:T(8,128)(2,1)S(1)}, u32[]{:S(2)}, u32[]{:S(2)}) collective-permute-start(bf16[48,3072]{1,0:T(8,128)(2,1)S(1)} %collective-permute-done.24), channel_id=1, source_target_pairs={{0,8},{2,10},{8,16},{10,18},{16,24},{18,26},{24,28},{26,30},{28,20... | collective-permute-start | bytes 884744 | tf_op jit(solution)/shard_map/ppermute | solution.py:61
  75.1 7.1 %collective-permute-start.27 = (bf16[48,3072]{1,0:T(8,128)(2,1)S(1)}, bf16[48,3072]{1,0:T(8,128)(2,1)S(1)}, u32[]{:S(2)}, u32[]{:S(2)}) collective-permute-start(bf16[48,3072]{1,0:T(8,128)(2,1)S(1)} %collective-permute-done.25), channel_id=1, source_target_pairs={{8,0},{10,2},{16,8},{18,10},{24,16},{26,18},{28,24},{30,26},{20,28... | collective-permute-start | bytes 884744 | tf_op jit(solution)/shard_map/ppermute | solution.py:62
  80.9 8.1 %collective-permute-start.16 = (bf16[48,3072]{1,0:T(8,128)(2,1)S(1)}, bf16[48,3072]{1,0:T(8,128)(2,1)S(1)}, u32[]{:S(2)}, u32[]{:S(2)}) collective-permute-start(bf16[48,3072]{1,0:T(8,128)(2,1)S(1)} %collective-permute-done.14), channel_id=1, source_target_pairs={{0,8},{2,10},{8,16},{10,18},{16,24},{18,26},{24,28},{26,30},{28,20... | collective-permute-start | bytes 884744 | tf_op jit(solution)/shard_map/ppermute | solution.py:61
  82.2 8.1 %collective-permute-start.17 = (bf16[48,3072]{1,0:T(8,128)(2,1)S(1)}, bf16[48,3072]{1,0:T(8,128)(2,1)S(1)}, u32[]{:S(2)}, u32[]{:S(2)}) collective-permute-start(bf16[48,3072]{1,0:T(8,128)(2,1)S(1)} %collective-permute-done.15), channel_id=1, source_target_pairs={{8,0},{10,2},{16,8},{18,10},{24,16},{26,18},{28,24},{30,26},{20,28... | collective-permute-start | bytes 884744 | tf_op jit(solution)/shard_map/ppermute | solution.py:62
  89.0 5.4 %collective-permute-start.28 = (bf16[48,1536]{1,0:T(8,128)(2,1)S(1)}, bf16[48,1536]{1,0:T(8,128)(2,1)S(1)}, u32[]{:S(2)}, u32[]{:S(2)}) collective-permute-start(bf16[48,1536]{1,0:T(8,128)(2,1)S(1)} %slice.218), channel_id=1, source_target_pairs={{0,8},{2,10},{8,16},{10,18},{16,24},{18,26},{24,28},{26,30},{28,20... | collective-permute-start | bytes 442376 | tf_op jit(solution)/shard_map/ppermute | solution.py:67
  90.3 19.1 %collective-permute-start.29 = (bf16[48,1536]{1,0:T(8,128)(2,1)S(1)}, bf16[48,1536]{1,0:T(8,128)(2,1)S(1)}, u32[]{:S(2)}, u32[]{:S(2)}) collective-permute-start(bf16[48,1536]{1,0:T(8,128)(2,1)S(1)} %slice.219), channel_id=1, source_target_pairs={{8,0},{10,2},{16,8},{18,10},{24,16},{26,18},{28,24},{30,26},{20,28... | collective-permute-start | bytes 442376 | tf_op jit(solution)/shard_map/ppermute | solution.py:68
  94.4 5.1 %collective-permute-start.18 = (bf16[48,1536]{1,0:T(8,128)(2,1)S(1)}, bf16[48,1536]{1,0:T(8,128)(2,1)S(1)}, u32[]{:S(2)}, u32[]{:S(2)}) collective-permute-start(bf16[48,1536]{1,0:T(8,128)(2,1)S(1)} %slice.215), channel_id=1, source_target_pairs={{0,8},{2,10},{8,16},{10,18},{16,24},{18,26},{24,28},{26,30},{28,20... | collective-permute-start | bytes 442376 | tf_op jit(solution)/shard_map/ppermute | solution.py:67
  99.5 25.1 %collective-permute-start.20 = (bf16[336,3072]{1,0:T(8,128)(2,1)}, bf16[336,3072]{1,0:T(8,128)(2,1)}, u32[]{:S(2)}, u32[]{:S(2)}) collective-permute-start(bf16[336,3072]{1,0:T(8,128)(2,1)} %constant_dynamic-update-slice_fusion.12.main_ref), channel_id=1, source_target_pairs={{0,2},{2,0},{4,6},{6,4},{8,10},{10,8},{12,14},{14,12},{16,18},{18,... | collective-permute-start | bytes 6193160 | tf_op jit(solution)/shard_map/ppermute | solution.py:66
  99.6 28.8 %collective-permute-start.30 = (bf16[336,3072]{1,0:T(8,128)(2,1)}, bf16[336,3072]{1,0:T(8,128)(2,1)}, u32[]{:S(2)}, u32[]{:S(2)}) collective-permute-start(bf16[336,3072]{1,0:T(8,128)(2,1)} %constant_dynamic-update-slice_fusion.21.main_ref), channel_id=1, source_target_pairs={{0,2},{2,0},{4,6},{6,4},{8,10},{10,8},{12,14},{14,12},{16,18},{18,... | collective-permute-start | bytes 6193160 | tf_op jit(solution)/shard_map/ppermute | solution.py:66
  100.2 9.8 %collective-permute-start.19 = (bf16[48,1536]{1,0:T(8,128)(2,1)S(1)}, bf16[48,1536]{1,0:T(8,128)(2,1)S(1)}, u32[]{:S(2)}, u32[]{:S(2)}) collective-permute-start(bf16[48,1536]{1,0:T(8,128)(2,1)S(1)} %slice.216), channel_id=1, source_target_pairs={{8,0},{10,2},{16,8},{18,10},{24,16},{26,18},{28,24},{30,26},{20,28... | collective-permute-start | bytes 442376 | tf_op jit(solution)/shard_map/ppermute | solution.py:68
  109.4 11.2 %collective-permute-start.11 = (bf16[256,768]{1,0:T(8,128)(2,1)}, bf16[256,768]{1,0:T(8,128)(2,1)}, u32[]{:S(2)}, u32[]{:S(2)}) collective-permute-start(bf16[256,768]{1,0:T(8,128)(2,1)} %get-tuple-element.18), channel_id=1, source_target_pairs={{0,1},{1,0},{2,3},{3,2},{4,5},{5,4},{6,7},{7,6},{8,9},{9,8},{10,11... | collective-permute-start | bytes 1179656 | tf_op jit(solution)/shard_map/ppermute | solution.py:146
  110.0 18.4 %collective-permute-start.31 = (bf16[48,3072]{1,0:T(8,128)(2,1)S(1)}, bf16[48,3072]{1,0:T(8,128)(2,1)}, u32[]{:S(2)}, u32[]{:S(2)}) collective-permute-start(bf16[48,3072]{1,0:T(8,128)(2,1)S(1)} %constant_dynamic-update-slice_fusion.28.tail_ref), channel_id=1, source_target_pairs={{0,2},{2,0},{4,6},{6,4},{8,10},{10,8},{12,14},{14,12},{16,18},{18,... | collective-permute-start | bytes 884744 | tf_op jit(solution)/shard_map/ppermute | solution.py:70
  120.6 4.0 %collective-permute-start.21 = (bf16[48,3072]{1,0:T(8,128)(2,1)S(1)}, bf16[48,3072]{1,0:T(8,128)(2,1)S(1)}, u32[]{:S(2)}, u32[]{:S(2)}) collective-permute-start(bf16[48,3072]{1,0:T(8,128)(2,1)S(1)} %constant_dynamic-update-slice_fusion.19.tail_ref), channel_id=1, source_target_pairs={{0,2},{2,0},{4,6},{6,4},{8,10},{10,8},{12,14},{14,12},{16,18},{18,... | collective-permute-start | bytes 884744 | tf_op jit(solution)/shard_map/ppermute | solution.py:70
  143.4 37.3 %collective-permute-start.32 = (bf16[128,768]{1,0:T(8,128)(2,1)}, bf16[128,768]{1,0:T(8,128)(2,1)}, u32[]{:S(2)}, u32[]{:S(2)}) collective-permute-start(bf16[128,768]{1,0:T(8,128)(2,1)} %constant_dynamic-slice_fusion.1), channel_id=1, source_target_pairs={{0,1},{1,0},{2,3},{3,2},{4,5},{5,4},{6,7},{7,6},{8,9},{9,8},{10,11... | collective-permute-start | bytes 589832 | tf_op jit(solution)/shard_map/ppermute | solution.py:146
  144.3 15.0 %collective-permute-start.34 = (bf16[256,768]{1,0:T(8,128)(2,1)S(1)}, bf16[256,768]{1,0:T(8,128)(2,1)S(1)}, u32[]{:S(2)}, u32[]{:S(2)}) collective-permute-start(bf16[256,768]{1,0:T(8,128)(2,1)S(1)} %get-tuple-element.105), channel_id=1, source_target_pairs={{0,1},{1,0},{2,3},{3,2},{4,5},{5,4},{6,7},{7,6},{8,9},{9,8},{10,11... | collective-permute-start | bytes 1179656 | tf_op jit(solution)/shard_map/ppermute | solution.py:146
  148.3 69.1 %collective-permute-start.50 = (bf16[8,48,3072]{2,1,0:T(8,128)(2,1)}, bf16[8,48,3072]{2,1,0:T(8,128)(2,1)}, u32[]{:S(2)}, u32[]{:S(2)}) collective-permute-start(bf16[8,48,3072]{2,1,0:T(8,128)(2,1)} %dynamic-slice_bitcast_fusion.1), channel_id=1, source_target_pairs={{0,2},{2,0},{4,6},{6,4},{8,10},{10,8},{12,14},{14,12},{16,18},{18,... | collective-permute-start | bytes 7077896 | tf_op jit(solution)/shard_map/ppermute | solution.py:85
  174.7 13.8 %collective-permute-start.41 = (bf16[8,48,1536]{2,1,0:T(8,128)(2,1)S(1)}, bf16[8,48,1536]{2,1,0:T(8,128)(2,1)S(1)}, u32[]{:S(2)}, u32[]{:S(2)}) collective-permute-start(bf16[8,48,1536]{2,1,0:T(8,128)(2,1)S(1)} %dynamic-slice_bitcast_fusion.2), channel_id=1, source_target_pairs={{0,2},{2,0},{4,6},{6,4},{8,10},{10,8},{12,14},{14,12},{16,18},{18,... | collective-permute-start | bytes 3538952 | tf_op jit(solution)/shard_map/ppermute | solution.py:85
  177.7 45.8 %collective-permute-start.59 = (bf16[8,48,3072]{2,1,0:T(8,128)(2,1)S(1)}, bf16[8,48,3072]{2,1,0:T(8,128)(2,1)}, u32[]{:S(2)}, u32[]{:S(2)}) collective-permute-start(bf16[8,48,3072]{2,1,0:T(8,128)(2,1)S(1)} %dynamic-slice_bitcast_fusion), channel_id=1, source_target_pairs={{0,2},{2,0},{4,6},{6,4},{8,10},{10,8},{12,14},{14,12},{16,18},{18,... | collective-permute-start | bytes 7077896 | tf_op jit(solution)/shard_map/ppermute | solution.py:85
  183.3 4.6 %collective-permute-start.40 = (f32[27,128]{1,0:T(8,128)S(1)}, f32[27,128]{1,0:T(8,128)S(1)}, u32[]{:S(2)}, u32[]{:S(2)}) collective-permute-start(f32[27,128]{1,0:T(8,128)S(1)} %add.566), channel_id=1, source_target_pairs={{0,16},{2,18},{4,20},{6,22},{8,24},{10,26},{12,28},{14,30},{16,0},... | collective-permute-start | bytes 41480 | tf_op jit(solution)/shard_map/ppermute | solution.py:159
  185.1 14.9 %collective-permute-start.35 = (bf16[128,768]{1,0:T(8,128)(2,1)}, bf16[128,768]{1,0:T(8,128)(2,1)}, u32[]{:S(2)}, u32[]{:S(2)}) collective-permute-start(bf16[128,768]{1,0:T(8,128)(2,1)} %constant_dynamic-slice_fusion), channel_id=1, source_target_pairs={{0,1},{1,0},{2,3},{3,2},{4,5},{5,4},{6,7},{7,6},{8,9},{9,8},{10,11... | collective-permute-start | bytes 589832 | tf_op jit(solution)/shard_map/ppermute | solution.py:146
  189.0 4.9 %collective-permute-start.42 = (bf16[48,768]{1,0:T(8,128)(2,1)S(1)}, bf16[48,768]{1,0:T(8,128)(2,1)S(1)}, u32[]{:S(2)}, u32[]{:S(2)}) collective-permute-start(bf16[48,768]{1,0:T(8,128)(2,1)S(1)} %get-tuple-element.90), channel_id=1, source_target_pairs={{0,8},{2,10},{8,16},{10,18},{16,24},{18,26},{24,28},{26,30},{28,20... | collective-permute-start | bytes 221192 | tf_op jit(solution)/shard_map/ppermute | solution.py:92
  190.4 5.4 %collective-permute-start.46 = (bf16[48,768]{1,0:T(8,128)(2,1)S(1)}, bf16[48,768]{1,0:T(8,128)(2,1)S(1)}, u32[]{:S(2)}, u32[]{:S(2)}) collective-permute-start(bf16[48,768]{1,0:T(8,128)(2,1)S(1)} %get-tuple-element.91), channel_id=1, source_target_pairs={{8,0},{10,2},{16,8},{18,10},{24,16},{26,18},{28,24},{30,26},{20,28... | collective-permute-start | bytes 221192 | tf_op jit(solution)/shard_map/ppermute | solution.py:93
  194.5 6.9 %collective-permute-start.43 = (bf16[48,1536]{1,0:T(8,128)(2,1)}, bf16[48,1536]{1,0:T(8,128)(2,1)}, u32[]{:S(2)}, u32[]{:S(2)}) collective-permute-start(bf16[48,1536]{1,0:T(8,128)(2,1)} %pad_maximum_fusion.7), channel_id=1, source_target_pairs={{0,8},{2,10},{8,16},{10,18},{16,24},{18,26},{24,28},{26,30},{28,20... | collective-permute-start | bytes 442376 | tf_op jit(solution)/shard_map/ppermute | solution.py:101
  196.5 5.8 %collective-permute-start.47 = (bf16[48,1536]{1,0:T(8,128)(2,1)}, bf16[48,1536]{1,0:T(8,128)(2,1)}, u32[]{:S(2)}, u32[]{:S(2)}) collective-permute-start(bf16[48,1536]{1,0:T(8,128)(2,1)} %pad_maximum_fusion.8), channel_id=1, source_target_pairs={{8,0},{10,2},{16,8},{18,10},{24,16},{26,18},{28,24},{30,26},{20,28... | collective-permute-start | bytes 442376 | tf_op jit(solution)/shard_map/ppermute | solution.py:102
  203.3 6.3 %collective-permute-start.44 = (bf16[48,1536]{1,0:T(8,128)(2,1)S(1)}, bf16[48,1536]{1,0:T(8,128)(2,1)S(1)}, u32[]{:S(2)}, u32[]{:S(2)}) collective-permute-start(bf16[48,1536]{1,0:T(8,128)(2,1)S(1)} %get-tuple-element.76), channel_id=1, source_target_pairs={{0,8},{2,10},{8,16},{10,18},{16,24},{18,26},{24,28},{26,30},{28,20... | collective-permute-start | bytes 442376 | tf_op jit(solution)/shard_map/ppermute | solution.py:101
  203.9 5.7 %collective-permute-start.48 = (bf16[48,1536]{1,0:T(8,128)(2,1)S(1)}, bf16[48,1536]{1,0:T(8,128)(2,1)S(1)}, u32[]{:S(2)}, u32[]{:S(2)}) collective-permute-start(bf16[48,1536]{1,0:T(8,128)(2,1)S(1)} %get-tuple-element.77), channel_id=1, source_target_pairs={{8,0},{10,2},{16,8},{18,10},{24,16},{26,18},{28,24},{30,26},{20,28... | collective-permute-start | bytes 442376 | tf_op jit(solution)/shard_map/ppermute | solution.py:102
  209.7 5.2 %collective-permute-start.49 = (bf16[48,1536]{1,0:T(8,128)(2,1)S(1)}, bf16[48,1536]{1,0:T(8,128)(2,1)S(1)}, u32[]{:S(2)}, u32[]{:S(2)}) collective-permute-start(bf16[48,1536]{1,0:T(8,128)(2,1)S(1)} %get-tuple-element.75), channel_id=1, source_target_pairs={{8,0},{10,2},{16,8},{18,10},{24,16},{26,18},{28,24},{30,26},{20,28... | collective-permute-start | bytes 442376 | tf_op jit(solution)/shard_map/ppermute | solution.py:102
  210.7 5.3 %collective-permute-start.45 = (bf16[48,1536]{1,0:T(8,128)(2,1)S(1)}, bf16[48,1536]{1,0:T(8,128)(2,1)S(1)}, u32[]{:S(2)}, u32[]{:S(2)}) collective-permute-start(bf16[48,1536]{1,0:T(8,128)(2,1)S(1)} %get-tuple-element.74), channel_id=1, source_target_pairs={{0,8},{2,10},{8,16},{10,18},{16,24},{18,26},{24,28},{26,30},{28,20... | collective-permute-start | bytes 442376 | tf_op jit(solution)/shard_map/ppermute | solution.py:101
  221.3 7.0 %collective-permute-start.51 = (bf16[48,1536]{1,0:T(8,128)(2,1)S(1)}, bf16[48,1536]{1,0:T(8,128)(2,1)S(1)}, u32[]{:S(2)}, u32[]{:S(2)}) collective-permute-start(bf16[48,1536]{1,0:T(8,128)(2,1)S(1)} %get-tuple-element.88), channel_id=1, source_target_pairs={{0,8},{2,10},{8,16},{10,18},{16,24},{18,26},{24,28},{26,30},{28,20... | collective-permute-start | bytes 442376 | tf_op jit(solution)/shard_map/ppermute | solution.py:92
  222.3 7.0 %collective-permute-start.55 = (bf16[48,1536]{1,0:T(8,128)(2,1)S(1)}, bf16[48,1536]{1,0:T(8,128)(2,1)S(1)}, u32[]{:S(2)}, u32[]{:S(2)}) collective-permute-start(bf16[48,1536]{1,0:T(8,128)(2,1)S(1)} %get-tuple-element.89), channel_id=1, source_target_pairs={{8,0},{10,2},{16,8},{18,10},{24,16},{26,18},{28,24},{30,26},{20,28... | collective-permute-start | bytes 442376 | tf_op jit(solution)/shard_map/ppermute | solution.py:93
  226.2 6.8 %collective-permute-start.60 = (bf16[48,1536]{1,0:T(8,128)(2,1)S(1)}, bf16[48,1536]{1,0:T(8,128)(2,1)S(1)}, u32[]{:S(2)}, u32[]{:S(2)}) collective-permute-start(bf16[48,1536]{1,0:T(8,128)(2,1)S(1)} %get-tuple-element.86), channel_id=1, source_target_pairs={{0,8},{2,10},{8,16},{10,18},{16,24},{18,26},{24,28},{26,30},{28,20... | collective-permute-start | bytes 442376 | tf_op jit(solution)/shard_map/ppermute | solution.py:92
  227.1 6.9 %collective-permute-start.64 = (bf16[48,1536]{1,0:T(8,128)(2,1)S(1)}, bf16[48,1536]{1,0:T(8,128)(2,1)S(1)}, u32[]{:S(2)}, u32[]{:S(2)}) collective-permute-start(bf16[48,1536]{1,0:T(8,128)(2,1)S(1)} %get-tuple-element.87), channel_id=1, source_target_pairs={{8,0},{10,2},{16,8},{18,10},{24,16},{26,18},{28,24},{30,26},{20,28... | collective-permute-start | bytes 442376 | tf_op jit(solution)/shard_map/ppermute | solution.py:93
  228.3 11.0 %collective-permute-start.52 = (bf16[48,3072]{1,0:T(8,128)(2,1)S(1)}, bf16[48,3072]{1,0:T(8,128)(2,1)S(1)}, u32[]{:S(2)}, u32[]{:S(2)}) collective-permute-start(bf16[48,3072]{1,0:T(8,128)(2,1)S(1)} %pad_maximum_fusion.3), channel_id=1, source_target_pairs={{0,8},{2,10},{8,16},{10,18},{16,24},{18,26},{24,28},{26,30},{28,20... | collective-permute-start | bytes 884744 | tf_op jit(solution)/shard_map/ppermute | solution.py:101
  229.4 10.9 %collective-permute-start.56 = (bf16[48,3072]{1,0:T(8,128)(2,1)S(1)}, bf16[48,3072]{1,0:T(8,128)(2,1)S(1)}, u32[]{:S(2)}, u32[]{:S(2)}) collective-permute-start(bf16[48,3072]{1,0:T(8,128)(2,1)S(1)} %pad_maximum_fusion.4), channel_id=1, source_target_pairs={{8,0},{10,2},{16,8},{18,10},{24,16},{26,18},{28,24},{30,26},{20,28... | collective-permute-start | bytes 884744 | tf_op jit(solution)/shard_map/ppermute | solution.py:102
  233.1 12.6 %collective-permute-start.61 = (bf16[48,3072]{1,0:T(8,128)(2,1)S(1)}, bf16[48,3072]{1,0:T(8,128)(2,1)S(1)}, u32[]{:S(2)}, u32[]{:S(2)}) collective-permute-start(bf16[48,3072]{1,0:T(8,128)(2,1)S(1)} %pad_maximum_fusion.5), channel_id=1, source_target_pairs={{0,8},{2,10},{8,16},{10,18},{16,24},{18,26},{24,28},{26,30},{28,20... | collective-permute-start | bytes 884744 | tf_op jit(solution)/shard_map/ppermute | solution.py:101
  234.1 12.4 %collective-permute-start.65 = (bf16[48,3072]{1,0:T(8,128)(2,1)S(1)}, bf16[48,3072]{1,0:T(8,128)(2,1)S(1)}, u32[]{:S(2)}, u32[]{:S(2)}) collective-permute-start(bf16[48,3072]{1,0:T(8,128)(2,1)S(1)} %pad_maximum_fusion.6), channel_id=1, source_target_pairs={{8,0},{10,2},{16,8},{18,10},{24,16},{26,18},{28,24},{30,26},{20,28... | collective-permute-start | bytes 884744 | tf_op jit(solution)/shard_map/ppermute | solution.py:102
  240.4 11.6 %collective-permute-start.53 = (bf16[48,3072]{1,0:T(8,128)(2,1)S(1)}, bf16[48,3072]{1,0:T(8,128)(2,1)S(1)}, u32[]{:S(2)}, u32[]{:S(2)}) collective-permute-start(bf16[48,3072]{1,0:T(8,128)(2,1)S(1)} %get-tuple-element.69), channel_id=1, source_target_pairs={{0,8},{2,10},{8,16},{10,18},{16,24},{18,26},{24,28},{26,30},{28,20... | collective-permute-start | bytes 884744 | tf_op jit(solution)/shard_map/ppermute | solution.py:101
  241.4 11.4 %collective-permute-start.57 = (bf16[48,3072]{1,0:T(8,128)(2,1)S(1)}, bf16[48,3072]{1,0:T(8,128)(2,1)S(1)}, u32[]{:S(2)}, u32[]{:S(2)}) collective-permute-start(bf16[48,3072]{1,0:T(8,128)(2,1)S(1)} %get-tuple-element.70), channel_id=1, source_target_pairs={{8,0},{10,2},{16,8},{18,10},{24,16},{26,18},{28,24},{30,26},{20,28... | collective-permute-start | bytes 884744 | tf_op jit(solution)/shard_map/ppermute | solution.py:102
  246.7 11.4 %collective-permute-start.62 = (bf16[48,3072]{1,0:T(8,128)(2,1)S(1)}, bf16[48,3072]{1,0:T(8,128)(2,1)S(1)}, u32[]{:S(2)}, u32[]{:S(2)}) collective-permute-start(bf16[48,3072]{1,0:T(8,128)(2,1)S(1)} %get-tuple-element.62), channel_id=1, source_target_pairs={{0,8},{2,10},{8,16},{10,18},{16,24},{18,26},{24,28},{26,30},{28,20... | collective-permute-start | bytes 884744 | tf_op jit(solution)/shard_map/ppermute | solution.py:101
  247.8 11.4 %collective-permute-start.66 = (bf16[48,3072]{1,0:T(8,128)(2,1)S(1)}, bf16[48,3072]{1,0:T(8,128)(2,1)S(1)}, u32[]{:S(2)}, u32[]{:S(2)}) collective-permute-start(bf16[48,3072]{1,0:T(8,128)(2,1)S(1)} %get-tuple-element.63), channel_id=1, source_target_pairs={{8,0},{10,2},{16,8},{18,10},{24,16},{26,18},{28,24},{30,26},{20,28... | collective-permute-start | bytes 884744 | tf_op jit(solution)/shard_map/ppermute | solution.py:102
  253.0 9.3 %collective-permute-start.58 = (bf16[48,3072]{1,0:T(8,128)(2,1)S(1)}, bf16[48,3072]{1,0:T(8,128)(2,1)S(1)}, u32[]{:S(2)}, u32[]{:S(2)}) collective-permute-start(bf16[48,3072]{1,0:T(8,128)(2,1)S(1)} %get-tuple-element.68), channel_id=1, source_target_pairs={{8,0},{10,2},{16,8},{18,10},{24,16},{26,18},{28,24},{30,26},{20,28... | collective-permute-start | bytes 884744 | tf_op jit(solution)/shard_map/ppermute | solution.py:102
  254.2 8.1 %collective-permute-start.54 = (bf16[48,3072]{1,0:T(8,128)(2,1)S(1)}, bf16[48,3072]{1,0:T(8,128)(2,1)S(1)}, u32[]{:S(2)}, u32[]{:S(2)}) collective-permute-start(bf16[48,3072]{1,0:T(8,128)(2,1)S(1)} %get-tuple-element.67), channel_id=1, source_target_pairs={{0,8},{2,10},{8,16},{10,18},{16,24},{18,26},{24,28},{26,30},{28,20... | collective-permute-start | bytes 884744 | tf_op jit(solution)/shard_map/ppermute | solution.py:101
  260.0 6.9 %collective-permute-start.67 = (bf16[48,3072]{1,0:T(8,128)(2,1)}, bf16[48,3072]{1,0:T(8,128)(2,1)S(1)}, u32[]{:S(2)}, u32[]{:S(2)}) collective-permute-start(bf16[48,3072]{1,0:T(8,128)(2,1)} %get-tuple-element.61), channel_id=1, source_target_pairs={{8,0},{10,2},{16,8},{18,10},{24,16},{26,18},{28,24},{30,26},{20,28... | collective-permute-start | bytes 884744 | tf_op jit(solution)/shard_map/ppermute | solution.py:102
  260.8 6.8 %collective-permute-start.63 = (bf16[48,3072]{1,0:T(8,128)(2,1)S(1)}, bf16[48,3072]{1,0:T(8,128)(2,1)}, u32[]{:S(2)}, u32[]{:S(2)}) collective-permute-start(bf16[48,3072]{1,0:T(8,128)(2,1)S(1)} %get-tuple-element.60), channel_id=1, source_target_pairs={{0,8},{2,10},{8,16},{10,18},{16,24},{18,26},{24,28},{26,30},{28,20... | collective-permute-start | bytes 884744 | tf_op jit(solution)/shard_map/ppermute | solution.py:101
  (43 other events, 375.0 us)

commit v3 on v2

--- a/solution.py
+++ b/solution.py
@@ -13,6 +13,7 @@
 
 EPS = 1e-06
 NEG = -1e30
+VMEM_BYTES = 48 << 20
 HIGH = lax.Precision.HIGHEST
 BF = jnp.bfloat16
 F32 = jnp.float32
@@ -43,103 +44,210 @@
         self.swap = [(i, i ^ 1) for i in range(self.n)]
         index = lax.axis_index("dp")
         self.core = index % 2
+        self.long = self.chips > LONGEST
         self.place = ring_place(index // 2, self.chips)
         reach = self.chips // 2
         self.distances = [0] + [d for s in range(1, reach) for d in (-s, s)] + [reach]
 
+    def other_core(self, x):
+        return lax.ppermute(x, "dp", self.swap)
+
+    def by_core(self, own, other, axis):
+        return jnp.where(
+            self.core == 0,
+            jnp.concatenate([own, other], axis=axis),
+            jnp.concatenate([other, own], axis=axis),
+        )
+
     def chip_at(self, distance):
         return ring_chip(self.place + distance + self.chips, self.chips)
 
-    def gather(self, x):
-        rows, width = x.shape
-        if self.chips > LONGEST:
-            return lax.all_gather(x, "dp", axis=0, tiled=True)
-        reach = self.chips // 2
-        r = l = x
-        pieces = [x]
-        for _ in range(reach - 1):
-            r = lax.ppermute(r, "dp", self.right)
-            l = lax.ppermute(l, "dp", self.left)
-            pieces += [r, l]
-        half = width // 2
-        main = jnp.concatenate(pieces, axis=0)
-        main_sib = lax.ppermute(main, "dp", self.swap)
-        r = lax.ppermute(r[:, :half], "dp", self.right)
-        l = lax.ppermute(l[:, half:], "dp", self.left)
-        tail = jnp.concatenate([r, l], axis=1)
-        tail_sib = lax.ppermute(tail, "dp", self.swap)
-        chips = jnp.stack([self.chip_at(d) for d in self.distances])
-        own = chips * 2 + self.core
-        sib = chips * 2 + 1 - self.core
-        return assemble(main, tail, main_sib, tail_sib, jnp.concatenate([own, sib]))
-
-    def scatter(self, grads, rows):
-        width = grads.shape[1]
-        if self.chips > LONGEST:
-            return lax.psum_scatter(grads, "dp", scatter_dimension=0, tiled=True).astype(F32)
-        reach = self.chips // 2
-        half = width // 2
-        split = grads.reshape(self.chips, 2, rows, width)
-        other = lax.dynamic_index_in_dim(split, 1 - self.core, 1, keepdims=False)
-        mine = lax.dynamic_index_in_dim(split, self.core, 1, keepdims=False)
-        got = lax.ppermute(other, "dp", self.swap)
-        both = (mine.astype(F32) + got.astype(F32)).astype(BF)
-
-        def local(distance):
-            return lax.dynamic_index_in_dim(both, self.chip_at(distance), 0, keepdims=False)
-
-        far = local(reach)
-        r = lax.ppermute(far[:, :half], "dp", self.right)
-        l = lax.ppermute(far[:, half:], "dp", self.left)
-        for s in range(reach - 1, 0, -1):
-            near_r, near_l = local(s), local(-s)
-            if s == reach - 1:
-                r = jnp.concatenate([add_low(r, near_r[:, :half]), near_r[:, half:]], axis=1)
-                l = jnp.concatenate([near_l[:, :half], add_low(l, near_l[:, half:])], axis=1)
-            else:
-                r, l = add_low(r, near_r), add_low(l, near_l)
-            r = lax.ppermute(r, "dp", self.right)
-            l = lax.ppermute(l, "dp", self.left)
-        return local(0).astype(F32) + r.astype(F32) + l.astype(F32)
-
-
-def add_low(a, b):
-    return (a.astype(F32) + b.astype(F32)).astype(BF)
-
-
-def assemble(main, tail, main_sib, tail_sib, owners):
-    rows, width = tail.shape
-    chips = main.shape[0] // rows + 1
-    if rows % 16:
-        own = jnp.concatenate([main, tail]).reshape(chips, rows, width)
-        sib = jnp.concatenate([main_sib, tail_sib]).reshape(chips, rows, width)
-        out = jnp.zeros((2 * chips, rows, width), main.dtype).at[owners].set(
-            jnp.concatenate([own, sib])
-        )
-        return out.reshape(2 * chips * rows, width)
-
-    def kernel(owners_ref, main_ref, tail_ref, main_sib_ref, tail_sib_ref, out_ref):
-        for at, (big, small) in enumerate(((main_ref, tail_ref), (main_sib_ref, tail_sib_ref))):
-            for i in range(chips):
-                owner = owners_ref[at * chips + i]
-                target = pl.ds(pl.multiple_of(owner * rows, 16), rows)
-                if i == chips - 1:
-                    out_ref[target, :] = small[...]
-                else:
-                    out_ref[target, :] = big[pl.ds(i * rows, rows), :]
+
+class Gather:
+    def __init__(self, ring, shard, far):
+        self.ring, self.shard, self.far = ring, shard, far
+        self.reach = ring.chips // 2
+        self.pieces = [shard]
+        self.sent = (shard, shard)
+        self.steps = 0
+
+    def step(self, *deps):
+        ring = self.ring
+        if ring.long or self.steps == self.reach:
+            return ()
+        self.steps += 1
+        r, l = after(self.sent, deps)
+        if self.steps < self.reach:
+            self.sent = (lax.ppermute(r, "dp", ring.right), lax.ppermute(l, "dp", ring.left))
+        elif self.far == "right":
+            self.sent = (lax.ppermute(r, "dp", ring.right),)
+        else:
+            self.sent = (lax.ppermute(l, "dp", ring.left),)
+        self.pieces += self.sent
+        return self.sent
+
+    def whole(self):
+        return assemble(self.pieces, jnp.stack([self.ring.chip_at(d) for d in self.ring.distances]))
+
+
+class Scatter:
+    def __init__(self, ring, pairs, rows, far, both_cores):
+        self.ring, self.rows, self.far = ring, rows, far
+        self.reach = ring.chips // 2
+        self.steps = 0
+        if ring.long:
+            terms = [dot32(lhs, rhs, TN).astype(BF) for lhs, rhs in pairs]
+            self.grads = jnp.concatenate(terms, axis=1)
+            return
+        near = [d for s in range(self.reach - 1, 0, -1) for d in (s, -s)]
+        self.slots = [self.reach] + near + [0]
+        chips = jnp.stack([ring.chip_at(d) for d in self.slots])
+        if both_cores:
+            self.cuts = []
+            (self.mine,) = outer(pairs, chips, rows, [ring.chips])
+        else:
+            self.cuts = [3, ring.chips] if ring.chips > 4 else [ring.chips]
+            owners = jnp.concatenate([chips * 2 + ring.core, chips * 2 + 1 - ring.core])
+            sizes = [y - x for x, y in zip([0] + self.cuts[:-1], self.cuts)]
+            self.mine, *sib = outer(pairs, owners, rows, [ring.chips] + sizes)
+            self.got = [lax.ppermute(part, "dp", ring.swap) for part in sib]
+
+    def local(self, distance):
+        slot = self.slots.index(distance)
+        term = self.mine[slot * self.rows : (slot + 1) * self.rows].astype(F32)
+        if self.cuts:
+            part = next(i for i, cut in enumerate(self.cuts) if slot < cut)
+            begin = slot - (self.cuts[part - 1] if part else 0)
+            got = self.got[part][begin * self.rows : (begin + 1) * self.rows]
+            term = term + got.astype(F32)
+        return term
+
+    def step(self, *deps):
+        ring = self.ring
+        if ring.long or self.steps == self.reach:
+            return ()
+        distance = self.reach - self.steps
+        self.steps += 1
+        if distance == self.reach:
+            (far,) = after((self.local(distance).astype(BF),), deps)
+            way = ring.right if self.far == "right" else ring.left
+            self.sent = (lax.ppermute(far, "dp", way),)
+            return self.sent
+        r, l = self.local(distance), self.local(-distance)
+        if distance < self.reach - 1:
+            r, l = r + self.sent[0].astype(F32), l + self.sent[1].astype(F32)
+        elif self.far == "right":
+            r = r + self.sent[0].astype(F32)
+        else:
+            l = l + self.sent[0].astype(F32)
+        r, l = after((r.astype(BF), l.astype(BF)), deps)
+        self.sent = (lax.ppermute(r, "dp", ring.right), lax.ppermute(l, "dp", ring.left))
+        return self.sent
+
+    def total(self):
+        r, l = self.sent
+        return self.local(0) + r.astype(F32) + l.astype(F32)
+
+
+def outer(pairs, owners, rows, counts):
+    height = pairs[0][0].shape[1]
+    widths = [rhs.shape[1] for _, rhs in pairs]
+    width = sum(widths)
+    tile = 768
+
+    def kernel(owners_ref, *refs):
+        ins, outs, held_ref = refs[: 2 * len(pairs)], refs[2 * len(pairs) : -1], refs[-1]
+        at = 0
+        for i, wide in enumerate(widths):
+            lhs = ins[2 * i][...]
+            for start in range(0, wide, tile):
+                size = min(tile, wide - start)
+                held_ref[:, pl.ds(at, size)] = dot32(
+                    lhs, ins[2 * i + 1][:, pl.ds(start, size)], TN
+                ).astype(BF)
+                at += size
+        slot = 0
+        for ref, number in zip(outs, counts):
+            for to in range(number):
+                source = pl.multiple_of(owners_ref[slot] * rows, 16)
+                ref[pl.ds(to * rows, rows), :] = held_ref[pl.ds(source, rows), :]
+                slot += 1
 
     inside = pl.BlockSpec(memory_space=pltpu.VMEM)
     return pl.pallas_call(
         kernel,
-        out_shape=jax.ShapeDtypeStruct((2 * chips * rows, width), main.dtype),
-        in_specs=[pl.BlockSpec(memory_space=pltpu.SMEM)] + [inside] * 4,
+        out_shape=[jax.ShapeDtypeStruct((number * rows, width), BF) for number in counts],
+        in_specs=[pl.BlockSpec(memory_space=pltpu.SMEM)] + [inside] * (2 * len(pairs)),
+        out_specs=[inside] * len(counts),
+        scratch_shapes=[pltpu.VMEM((height, width), BF)],
+        compiler_params=pltpu.CompilerParams(vmem_limit_bytes=VMEM_BYTES),
+        cost_estimate=pl.CostEstimate(
+            flops=sum(2 * lhs.shape[0] * height * rhs.shape[1] for lhs, rhs in pairs),
+            bytes_accessed=4 * height * width,
+            transcendentals=0,
+        ),
+        name="outer",
+    )(owners, *[x for pair in pairs for x in pair])
+
+
+def after(values, deps):
+    if not deps:
+        return values
+    return lax.optimization_barrier((tuple(values), deps))[0]
+
+
+def assemble(pieces, owners):
+    rows, width = pieces[0].shape
+    number = len(pieces)
+
+    def kernel(owners_ref, *refs):
+        ins, out_ref, sems = refs[:number], refs[number], refs[number + 1]
+        copies = []
+        for i in range(number):
+            target = out_ref.at[pl.ds(pl.multiple_of(owners_ref[i] * rows, 16), rows)]
+            copies.append(pltpu.make_async_copy(ins[i], target, sems.at[i]))
+        for copy in copies:
+            copy.start()
+        for copy in copies:
+            copy.wait()
+
+    return pl.pallas_call(
+        kernel,
+        out_shape=jax.ShapeDtypeStruct((number * rows, width), BF),
+        in_specs=[pl.BlockSpec(memory_space=pltpu.SMEM)]
+        + [pl.BlockSpec(memory_space=pl.ANY)] * number,
+        out_specs=pl.BlockSpec(memory_space=pltpu.VMEM),
+        scratch_shapes=[pltpu.SemaphoreType.DMA((number,))],
+        compiler_params=pltpu.CompilerParams(vmem_limit_bytes=VMEM_BYTES),
+        cost_estimate=pl.CostEstimate(
+            flops=0, bytes_accessed=4 * number * rows * width, transcendentals=0
+        ),
+        name="assemble",
+    )(owners, *pieces)
+
+
+def interleave(own, other, core, rows):
+    chips, width = own.shape[0] // rows, own.shape[1]
+
+    def kernel(core_ref, own_ref, other_ref, out_ref):
+        for k, ref in enumerate((own_ref, other_ref)):
+            first = (1 - core_ref[0]) if k else core_ref[0]
+            for chip in range(chips):
+                target = pl.multiple_of((2 * chip + first) * rows, 16)
+                out_ref[pl.ds(target, rows), :] = ref[pl.ds(chip * rows, rows), :]
+
+    inside = pl.BlockSpec(memory_space=pltpu.VMEM)
+    return pl.pallas_call(
+        kernel,
+        out_shape=jax.ShapeDtypeStruct((2 * chips * rows, width), BF),
+        in_specs=[pl.BlockSpec(memory_space=pltpu.SMEM), inside, inside],
         out_specs=inside,
-        compiler_params=pltpu.CompilerParams(vmem_limit_bytes=32 << 20),
+        compiler_params=pltpu.CompilerParams(vmem_limit_bytes=VMEM_BYTES),
         cost_estimate=pl.CostEstimate(
             flops=0, bytes_accessed=8 * chips * rows * width, transcendentals=0
         ),
-        name="assemble",
-    )(owners, main, tail, main_sib, tail_sib)
+        name="interleave",
+    )(core[None], own, other)
 
 
 def swap_tensor(x):
@@ -177,9 +285,6 @@
 NN = ((1,), (0,))
 NT = ((1,), (1,))
 TN = ((0,), (0,))
-
-
-VMEM_BYTES = 48 << 20
 
 
 def attention_forward(x, gain, weights, by_offset, seq_col, seq_row):
@@ -309,12 +414,43 @@
     count = 2 * rows_local
 
     attn_shard = jnp.concatenate([w_qkv.reshape(shard, 3 * head_cols), w_out], axis=1)
-    x_low = whole_rows(block_in, swap_tensor(block_in), rank)
+    x_other = swap_tensor(block_in)
+    split = units // 2
+
+    def unit_half(w, core):
+        return lax.dynamic_slice_in_dim(w, core * split, split, axis=2)
+
+    def unit_shard(w, got):
+        own = unit_half(w, ring.core).reshape(shard, EXPERTS * split)
+        return ring.by_core(own, got.reshape(shard, EXPERTS * split), 0)
+
+    ring_a = Gather(ring, attn_shard, "right")
+    ring_a.step()
+    if not ring.long:
+        other_half = 1 - ring.core
+        got_in = ring.other_core(unit_half(w_in, other_half))
+        got_down = ring.other_core(unit_half(w_down, other_half))
+        ring_in = Gather(ring, unit_shard(w_in, got_in), "right")
+        ring_down = Gather(ring, unit_shard(w_down, got_down), "left")
+        ring_a.step()
+        a3 = ring_a.step()
+        ring_a.step()
+        ring_in.step(*a3)
+        ring_down.step(*a3)
+        own_a = ring_a.whole()
+        attn_all = interleave(own_a, ring.other_core(own_a), ring.core, shard)
+    else:
+        attn_all = lax.all_gather(attn_shard, "dp", axis=0, tiled=True)
+        in_all, down_all = (
+            unit_half(lax.all_gather(w, "dp", axis=0, tiled=True), ring.core).reshape(
+                -1, EXPERTS * split
+            )
+            for w in (w_in, w_down)
+        )
+    x_low = whole_rows(block_in, x_other, rank)
     x_all = x_low.astype(F32)
-    attn_all = ring.gather(attn_shard)
-    in_all = ring.gather(w_in.reshape(shard, EXPERTS * units))
-    down_all = ring.gather(w_down.reshape(shard, EXPERTS * units))
-    grad_out = whole_rows(out_grad, swap_tensor(out_grad), rank).astype(F32)
+    grad_other = swap_tensor(out_grad)
+    grad_out = whole_rows(out_grad, grad_other, rank).astype(F32)
 
     places = jnp.arange(count, dtype=jnp.int32)
     ends = jnp.cumsum(seq_lengths[0])
@@ -330,6 +466,9 @@
         x_low, attn_gain[None, :], attn_all, by_offset, seq_ids[:, None], seq_ids[None, :]
     )
     n_one = x_all * scale_one
+    if not ring.long:
+        ring_in.step(attn_part)
+        ring_down.step(attn_part)
     hidden = x_all + (attn_part.astype(F32) + swap_tensor(attn_part).astype(F32))
 
     scale_two = rms_scale(hidden)
@@ -349,31 +488,47 @@
     blocks = dot32(dispatch, mixed.astype(BF), TN).astype(BF)
     grad_blocks = dot32(dispatch, grad_routed, TN).astype(BF)
 
-    def part(x, e):
-        return x[e * CAP : (e + 1) * CAP]
+
+    def shared_slots(x):
+        got = ring.other_core(x)
+        return [
+            jnp.concatenate([y[e * CAP : (e + 1) * CAP] for y in (x, got)], axis=0)
+            for e in range(EXPERTS)
+        ]
+
+    blocks = shared_slots(blocks)
+    grad_blocks = shared_slots(grad_blocks)
+    if not ring.long:
+        ring_in.step(*blocks, *grad_blocks)
+        ring_down.step(*blocks, *grad_blocks)
+        ring_in.step()
+        ring_down.step()
+        in_all = ring_in.whole()
+        down_all = ring_down.whole()
 
     def cols(x, e):
-        return x[:, e * units : (e + 1) * units]
-
-    pre = [dot32(part(blocks, e), cols(in_all, e), NN) for e in range(EXPERTS)]
+        return x[:, e * split : (e + 1) * split]
+
+    def own_sum(parts):
+        away = jnp.concatenate([x[CAP:] for x in parts], axis=0)
+        mine = jnp.concatenate([x[:CAP] for x in parts], axis=0)
+        return (mine.astype(F32) + ring.other_core(away).astype(F32)).astype(BF)
+
+    experts = range(EXPERTS)
+    pre = [dot32(blocks[e], cols(in_all, e), NN) for e in experts]
     active = [jax.nn.gelu(v, approximate=True).astype(BF) for v in pre]
-    grad_w_down = jnp.concatenate(
-        [dot32(part(grad_blocks, e), active[e], TN).astype(BF) for e in range(EXPERTS)], axis=1
-    )
-    returned = jnp.concatenate(
-        [dot32(active[e], cols(down_all, e), NT).astype(BF) for e in range(EXPERTS)], axis=0
-    )
+    send_down = Scatter(
+        ring, [(grad_blocks[e], active[e]) for e in experts], 2 * shard, "right", True
+    )
+    send_down.step()
+    returned = own_sum([dot32(active[e], cols(down_all, e), NT).astype(BF) for e in experts])
     grad_pre = []
-    for e in range(EXPERTS):
-        grad_active = dot32(part(grad_blocks, e), cols(down_all, e), NN)
+    for e in experts:
+        grad_active = dot32(grad_blocks[e], cols(down_all, e), NN)
         _, pull = jax.vjp(lambda v: jax.nn.gelu(v, approximate=True), pre[e])
         grad_pre.append(pull(grad_active)[0].astype(BF))
-    grad_sent = jnp.concatenate(
-        [dot32(grad_pre[e], cols(in_all, e), NT).astype(BF) for e in range(EXPERTS)], axis=0
-    )
-    grad_w_in = jnp.concatenate(
-        [dot32(part(blocks, e), grad_pre[e], TN).astype(BF) for e in range(EXPERTS)], axis=1
-    )
+    grad_sent = own_sum([dot32(grad_pre[e], cols(in_all, e), NT).astype(BF) for e in experts])
+    send_in = Scatter(ring, [(blocks[e], grad_pre[e]) for e in experts], 2 * shard, "left", True)
     routed_part = dot32(dispatch, returned, NN)
     sent_part = dot32(dispatch, grad_sent, NN)
     gate_part = jnp.sum(grad_out * routed_part, axis=1, keepdims=True)
@@ -382,7 +537,11 @@
         logits_part[:, e : e + 1] * w_router[:, e] for e in range(EXPERTS)
     )
     mixed_low = mixed_part.astype(BF)
-    grad_mixed = mixed_low.astype(F32) + swap_tensor(mixed_low).astype(F32)
+    mixed_other = swap_tensor(mixed_low)
+    in1 = send_in.step(mixed_low)
+    send_down.step(mixed_low)
+    (mixed_other,) = after((mixed_other,), in1)
+    grad_mixed = mixed_low.astype(F32) + mixed_other.astype(F32)
     moe_gain_part = jnp.sum(mixed_part * n_two, axis=0)
     router_part = [jnp.sum(mixed * logits_part[:, e : e + 1], axis=0) for e in range(EXPERTS)]
 
@@ -396,17 +555,17 @@
     routed = own_rows(routed_low).astype(F32) + swap_tensor(other_rows(routed_low)).astype(F32)
     result = own_rows(hidden) + own_rows(gate) * routed
 
-    grad_w_down_mine = ring.scatter(grad_w_down, shard)
-    grad_w_in_mine = ring.scatter(grad_w_in, shard)
-
     grad_hidden = grad_out + norm_back(grad_mixed, n_two, scale_two, moe_gain)
     grad_attended = grad_hidden.astype(BF)
+    in2 = send_in.step()
+    send_down.step()
+    (grad_attended,) = after((grad_attended,), in2)
     grad_projected, offset_sums = attention_backward(
         grad_attended, attn_all, projected, p_full, context, lanes
     )
-    grad_w_out = dot32(grad_attended, context, TN).astype(BF)
-    grad_w_qkv = dot32(normed_one, grad_projected, TN).astype(BF)
-    attn_mine = ring.scatter(jnp.concatenate([grad_w_qkv, grad_w_out], axis=1), shard)
+    send_a = Scatter(ring, [(normed_one, grad_projected), (grad_attended, context)], shard, "right", False)
+    send_in.step(grad_projected)
+    send_down.step(grad_projected)
     normed_part = dot32(grad_projected, attn_all[:, : 3 * head_cols], NT)
     attn_gain_part = jnp.sum(normed_part * n_one, axis=0)
     normed_low = normed_part.astype(BF)
@@ -420,6 +579,29 @@
     )
     small = [attn_gain_part, moe_gain_part] + router_part + [grad_rel.reshape(-1)]
     line = jnp.concatenate(small)
+    for _ in range(ring.chips // 2):
+        send_a.step()
+        send_in.step()
+        send_down.step()
+
+    def unit_total(send):
+        if ring.long:
+            zeros = jnp.zeros(send.grads.shape[:1] + (EXPERTS, units), BF)
+            terms = send.grads.reshape(-1, EXPERTS, split)
+            terms = lax.dynamic_update_slice_in_dim(zeros, terms, ring.core * split, 2)
+            return lax.psum_scatter(terms, "dp", scatter_dimension=0, tiled=True).astype(F32)
+        sums = send.total().reshape(2, shard, EXPERTS, split)
+        away = lax.dynamic_index_in_dim(sums, 1 - ring.core, 0, keepdims=False)
+        mine = lax.dynamic_index_in_dim(sums, ring.core, 0, keepdims=False)
+        return ring.by_core(mine, ring.other_core(away), 2)
+
+    grad_w_down_mine = unit_total(send_down)
+    grad_w_in_mine = unit_total(send_in)
+    if ring.long:
+        attn_mine = lax.psum_scatter(send_a.grads, "dp", scatter_dimension=0, tiled=True)
+        attn_mine = attn_mine.astype(F32)
+    else:
+        attn_mine = send_a.total()
     summed = sum_everywhere(line.reshape(-1, 128)).reshape(-1)
     return (
         result.astype(BF),
@@ -430,8 +612,8 @@
         summed[4 * width :].reshape(rel_bias.shape),
         summed[width : 2 * width],
         jnp.stack([summed[2 * width : 3 * width], summed[3 * width : 4 * width]], axis=1),
-        grad_w_in_mine.reshape(w_in.shape),
-        grad_w_down_mine.reshape(w_down.shape),
+        grad_w_in_mine,
+        grad_w_down_mine,
     )
 
 

time: 275 us -> 228 us (0.83); the launches traced: 270 us -> 227 us
  waiting for transfers between devices: 103 us -> 70.8 us
  matrix products: 19.9 us -> 11.2 us
  starting transfers between devices: 69.4 us -> 63.1 us
  Pallas kernels: 13.8 us -> 19.8 us
  local copies, waits for them, and re-layouts: 32.7 us -> 28.2 us
    ppermute x57 -> x53, waiting for transfers between devices: 75.5 us -> 58.9 us  [the longest x18 25.8 us: step(): lax.ppermute(r, 'dp', ring.right)]
    ppermute x7, waiting for transfers between devices: 21.9 us -> 6.57 us  [swap_tensor(): return lax.ppermute(x, 'tensor', [(0, 1), (1, 0)])]
    dot_general x19 -> x13, matrix products: 19.3 us -> 10.6 us  [dot32(): return lax.dot_general(a, b, (dims, ((), ())), preferred_element_type=F32)]
    pallas_call x3 -> x7, Pallas kernels: 5.74 us -> 12.4 us  [the longest x3 6.37 us: assemble(): pl.pallas_call(kernel, out_shape=jax.ShapeDtypeStruct((number * rows, wid...]
    ppermute x57 -> x53, starting transfers between devices: 57.8 us -> 51.4 us  [the longest x18 25.2 us: step(): lax.ppermute(r, 'dp', ring.right)]
    convert_element_type x15 -> x12, other arithmetic: 9.26 us -> 15.3 us  [the longest x11 14.3 us: step(): r, l = after((r.astype(BF), l.astype(BF)), deps)]
    concatenate x10 -> x5, other arithmetic: 5.22 us -> 1.3 us  [the longest x2 1.15 us: shared_slots(): jnp.concatenate([y[e * CAP:(e + 1) * CAP] for y in (x, got)], axis=0)]
    unnamed x107 -> x163, local copies, waits for them, and re-layouts: 16.7 us -> 14.5 us
  transfers between devices with their start and end apart: 68 -> 64, of which waited for: 36 -> 27; matrix products, arithmetic and copies ran while one was open for 23% -> 22% of each run, Pallas kernels for 4% -> 5%
where the time goes in v3:
time: 228 us; the launch traced here: 227 us
  waiting for transfers between devices  70.8 us (31%)
  starting transfers between devices  63.1 us (28%)
  other arithmetic  32 us (14%)
  local copies, waits for them, and re-layouts  28.2 us (12%)
  Pallas kernels  19.8 us (9%)
  matrix products  11.2 us (5%)
    ppermute x18, waiting for transfers between devices, step(): lax.ppermute(r, 'dp', ring.right)  25.8 us
    ppermute x18, starting transfers between devices, step(): lax.ppermute(r, 'dp', ring.right)  25.2 us
    ppermute x18, waiting for transfers between devices, step(): lax.ppermute(l, 'dp', ring.left)  19.3 us
    ppermute x18, starting transfers between devices, step(): lax.ppermute(l, 'dp', ring.left)  16.9 us
    unnamed x163, local copies, waits for them, and re-layouts  14.5 us
    convert_element_type x11, other arithmetic, step(): r, l = after((r.astype(BF), l.astype(BF)), deps)  14.3 us
    ppermute x3, waiting for transfers between devices, step(): self.sent = (lax.ppermute(far, 'dp', way),)  12.5 us
    dot_general x13, matrix products, dot32(): return lax.dot_general(a, b, (dims, ((), ())), preferred_element_type=F32)  10.6 us
  transfers between devices with their start and end apart: 64, of which 27 were waited for; matrix products, arithmetic and copies ran while one was open for 22% of the time, Pallas kernels for 5%

profile of v3, /device:TPU:0, one launch (start us, length us, event | category | flops | bytes accessed | tf_op | source)
XLA Modules:
  0.0 227.0 jit_solution(8904689955306402632)
XLA Ops:
  2.4 3.0 %collective-permute-start.1 = (bf16[48,1536]{1,0:T(8,128)(2,1)S(1)}, bf16[48,1536]{1,0:T(8,128)(2,1)S(1)}, u32[]{:S(2)}, u32[]{:S(2)}) collective-permute-start(bf16[48,1536]{1,0:T(8,128)(2,1)S(1)} %constant_dynamic-update-slice_fusion.refs_0_), channel_id=1, source_target_pairs={{0,8},{2,10},{8,16},{10,18},{16,24},{18,26},{24,28},{26,30},{28,20... | collective-permute-start | bytes 442376 | tf_op jit(solution)/shard_map/ppermute | solution.py:81
  5.5 3.8 %collective-permute-done.1.refs_1_ = bf16[48,1536]{1,0:T(8,128)(2,1)S(1)} collective-permute-done((bf16[48,1536]{1,0:T(8,128)(2,1)S(1)}, bf16[48,1536]{1,0:T(8,128)(2,1)S(1)}, u32[]{:S(2)}, u32[]{:S(2)}) %collective-permute-start.1) | collective-permute-done | bytes 147488 | tf_op jit(solution)/shard_map/ppermute | solution.py:81
  9.2 1.8 collective-permute-start.3
  11.1 1.5 collective-permute-start
  13.0 1.3 collective-permute-done.3.refs_3_
  14.4 1.8 collective-permute-start.5
  16.2 1.8 constant_dynamic-slice_fusion.5
  19.6 1.8 collective-permute-start.7
  22.5 2.7 %collective-permute-done.6.refs_6_ = bf16[48,1536]{1,0:T(8,128)(2,1)S(1)} collective-permute-done((bf16[48,1536]{1,0:T(8,128)(2,1)S(1)}, bf16[48,1536]{1,0:T(8,128)(2,1)S(1)}, u32[]{:S(2)}, u32[]{:S(2)}) %collective-permute-start.6) | collective-permute-done | bytes 147488 | tf_op jit(solution)/shard_map/ppermute | solution.py:81
  25.3 2.3 %assemble.3.own_ref = bf16[384,1536]{1,0:T(8,128)(2,1)S(1)} custom-call(s32[8]{0:T(128)S(1)} %stack.40.owners_ref, bf16[48,1536]{1,0:T(8,128)(2,1)S(1)} %constant_dynamic-update-slice_fusion.refs_0_, bf16[48,1536]{1,0:T(8,128)(2,1)S(1)} %collective-permute-done.1.refs_1_, bf16[48,1536]{1,0:T(8,128)(2,1)S(1)} %collective-permute-done.2.refs_2_, ...), custom_call_target="tpu_custom_call" | custom-call | bytes 2359296 | tf_op jit(solution)/shard_map/assemble/pallas_call | solution.py:214
  33.7 3.5 %attention_forward.1 = (bf16[256,768]{1,0:T(8,128)(2,1)S(1)}, f32[256,1]{1,0:T(8,128)S(1)}, bf16[256,1152]{1,0:T(8,128)(2,1)S(1)}, f32[6,256,256]{2,1,0:T(8,128)...) custom-call(bf16[256,768]{1,0:T(8,128)(2,1)S(1)} %maximum_select_fusion.2.x_ref, ...), custom_call_target="tpu_custom_call" | custom-call | flops 704643072 | bytes 5505024 | tf_op jit(solution)/shard_map/attention_forward/pallas_call | solution.py:323
  38.0 1.7 collective-permute-start.9
  39.8 1.6 collective-permute-start.22
  41.9 1.6 collective-permute-start.12
  43.9 5.9 %collective-permute-done.22.refs_1_ = bf16[96,1536]{1,0:T(8,128)(2,1)} collective-permute-done((bf16[96,1536]{1,0:T(8,128)(2,1)S(1)}, bf16[96,1536]{1,0:T(8,128)(2,1)}, u32[]{:S(2)}, u32[]{:S(2)}) %collective-permute-start.22) | collective-permute-done | bytes 294944 | tf_op jit(solution)/shard_map/ppermute | solution.py:81
  51.4 3.7 %collective-permute-done.12.refs_1_ = bf16[96,1536]{1,0:T(8,128)(2,1)S(1)} collective-permute-done((bf16[96,1536]{1,0:T(8,128)(2,1)S(1)}, bf16[96,1536]{1,0:T(8,128)(2,1)S(1)}, u32[]{:S(2)}, u32[]{:S(2)}) %collective-permute-start.12) | collective-permute-done | bytes 294944 | tf_op jit(solution)/shard_map/ppermute | solution.py:81
  56.4 1.6 collective-permute-start.14
  58.5 1.6 collective-permute-start.24
  67.2 1.6 collective-permute-start.18
  68.9 2.3 %collective-permute-done.24.refs_3_ = bf16[96,1536]{1,0:T(8,128)(2,1)} collective-permute-done((bf16[96,1536]{1,0:T(8,128)(2,1)}, bf16[96,1536]{1,0:T(8,128)(2,1)}, u32[]{:S(2)}, u32[]{:S(2)}) %collective-permute-start.24) | collective-permute-done | bytes 294944 | tf_op jit(solution)/shard_map/ppermute | solution.py:81
  72.7 1.9 collective-permute-start.27
  74.5 2.4 %collective-permute-done.18.refs_5_ = bf16[96,1536]{1,0:T(8,128)(2,1)} collective-permute-done((bf16[96,1536]{1,0:T(8,128)(2,1)}, bf16[96,1536]{1,0:T(8,128)(2,1)}, u32[]{:S(2)}, u32[]{:S(2)}) %collective-permute-start.18) | collective-permute-done | bytes 294944 | tf_op jit(solution)/shard_map/ppermute | solution.py:81
  77.0 1.6 collective-permute-start.20
  79.6 1.6 dynamic-slice_reduce_fusion
  81.3 1.6 collective-permute-start.26
  82.9 4.2 %collective-permute-done.27.refs_6_ = bf16[96,1536]{1,0:T(8,128)(2,1)} collective-permute-done((bf16[96,1536]{1,0:T(8,128)(2,1)}, bf16[96,1536]{1,0:T(8,128)(2,1)}, u32[]{:S(2)}, u32[]{:S(2)}) %collective-permute-start.27) | collective-permute-done | bytes 294944 | tf_op jit(solution)/shard_map/ppermute | solution.py:81
  91.4 2.0 assemble.4
  95.5 2.0 assemble.5
  101.8 2.1 outer.3
  106.2 1.6 collective-permute-start.34
  107.8 2.1 outer.5
  110.7 1.6 collective-permute-start.56
  114.4 7.0 %collective-permute-done.56 = bf16[96,1536]{1,0:T(8,128)(2,1)S(1)} collective-permute-done((bf16[96,1536]{1,0:T(8,128)(2,1)S(1)}, bf16[96,1536]{1,0:T(8,128)(2,1)S(1)}, u32[]{:S(2)}, u32[]{:S(2)}) %collective-permute-start.56) | collective-permute-done | bytes 294944 | tf_op jit(solution)/shard_map/ppermute | solution.py:134
  122.8 1.6 collective-permute-start.57
  126.4 6.0 %collective-permute-done.32 = bf16[256,768]{1,0:T(8,128)(2,1)S(1)} collective-permute-done((bf16[256,768]{1,0:T(8,128)(2,1)S(1)}, bf16[256,768]{1,0:T(8,128)(2,1)S(1)}, u32[]{:S(2)}, u32[]{:S(2)}) %collective-permute-start.32) | collective-permute-done | bytes 393248 | tf_op jit(solution)/shard_map/ppermute | solution.py:254
  133.0 1.3 fusion.64
  134.3 4.1 %collective-permute-done.35 = bf16[96,1536]{1,0:T(8,128)(2,1)S(1)} collective-permute-done((bf16[96,1536]{1,0:T(8,128)(2,1)S(1)}, bf16[96,1536]{1,0:T(8,128)(2,1)S(1)}, u32[]{:S(2)}, u32[]{:S(2)}) %collective-permute-start.35) | collective-permute-done | bytes 294944 | tf_op jit(solution)/shard_map/ppermute | solution.py:144
  138.5 3.9 %attention_backward.1 = (bf16[256,1152]{1,0:T(8,128)(2,1)S(1)}, f32[6,512]{1,0:T(8,128)S(1)}) custom-call(bf16[256,768]{1,0:T(8,128)(2,1)S(1)} %get-tuple-element.58.grad_ref.refs_2_, bf16[768,1536]{1,0:T(8,128)(2,1)S(1)} %interleave.1.w_ref, bf16[256,1152]{1,0:T(8,128)(2,1)S(1)} %copy-done.17, f32[6,256,256]{2,1,0:T(8,128)S(1)} %copy-done.9), custom_call_target="tpu_custom_call" | custom-call | flops 452984832 | bytes 3145728 | tf_op jit(solution)/shard_map/attention_backward/pallas_call | solution.py:373
  144.0 2.6 %multiply_reduce_fusion.3 = (f32[768]{0:T(1024)S(1)}, bf16[256,768]{1,0:T(8,128)(2,1)S(1)}, f32[256,768]{1,0:T(8,128)}) fusion(f32[256]{0:T(256)S(1)} %reduce.6, bf16[256,768]{1,0:T(8,128)(2,1)S(1)} %copy-done.5, bf16[256,1152]{1,0:T(8,128)(2,1)} %copy-done.28, bf16[768,1536]{1,0:T(8,128)(2,1)S(1)} %interleave.1.w_ref), kind=kOutput, calls=%fused_computation.53 | convolution fusion | flops 453967104 | bytes 3936256 | tf_op jit(solution)/shard_map/dot_general | solution.py:282
  146.7 1.7 collective-permute-start.37
  151.2 1.6 collective-permute-start.36
  153.3 2.0 add_convert_fusion.9
  158.7 2.1 add_convert_fusion.2
  161.6 4.4 %collective-permute-done.40 = f32[27,128]{1,0:T(8,128)S(1)} collective-permute-done((f32[27,128]{1,0:T(8,128)S(1)}, f32[27,128]{1,0:T(8,128)S(1)}, u32[]{:S(2)}, u32[]{:S(2)}) %collective-permute-start.40) | collective-permute-done | bytes 13856 | tf_op jit(solution)/shard_map/ppermute | solution.py:267
  166.0 2.0 collective-permute-start.41
  168.1 1.6 outer.4
  171.9 1.4 reshape.162
  173.2 1.4 copy.34
  175.8 1.3 multiply_reduce_fusion.8
  177.1 2.0 multiply_add_fusion
  179.1 1.4 add_convert_fusion.8
  181.7 2.1 collective-permute-start.54
  185.4 1.8 add_convert_fusion.4
  187.2 2.0 collective-permute-start.61
  189.2 5.5 %collective-permute-done.44 = bf16[48,1536]{1,0:T(8,128)(2,1)S(1)} collective-permute-done((bf16[48,1536]{1,0:T(8,128)(2,1)S(1)}, bf16[48,1536]{1,0:T(8,128)(2,1)S(1)}, u32[]{:S(2)}, u32[]{:S(2)}) %collective-permute-start.44) | collective-permute-done | bytes 147488 | tf_op jit(solution)/shard_map/ppermute | solution.py:134
  194.7 2.1 collective-permute-start.62
  196.8 1.8 add_convert_fusion.20
  198.6 2.0 collective-permute-start.48
  202.2 1.9 collective-permute-done.45
  207.5 4.0 %collective-permute-done.46 = bf16[48,1536]{1,0:T(8,128)(2,1)} collective-permute-done((bf16[48,1536]{1,0:T(8,128)(2,1)S(1)}, bf16[48,1536]{1,0:T(8,128)(2,1)}, u32[]{:S(2)}, u32[]{:S(2)}) %collective-permute-start.46) | collective-permute-done | bytes 147488 | tf_op jit(solution)/shard_map/ppermute | solution.py:144
  213.1 1.7 collective-permute-start.49
  216.1 2.4 %collective-permute-done.49 = bf16[48,1536]{1,0:T(8,128)(2,1)S(1)} collective-permute-done((bf16[48,1536]{1,0:T(8,128)(2,1)S(1)}, bf16[48,1536]{1,0:T(8,128)(2,1)S(1)}, u32[]{:S(2)}, u32[]{:S(2)}) %collective-permute-start.49) | collective-permute-done | bytes 147488 | tf_op jit(solution)/shard_map/ppermute | solution.py:144
  219.5 1.6 collective-permute-start.50
  222.4 2.3 %collective-permute-done.50 = bf16[48,1536]{1,0:T(8,128)(2,1)S(1)} collective-permute-done((bf16[48,1536]{1,0:T(8,128)(2,1)S(1)}, bf16[48,1536]{1,0:T(8,128)(2,1)S(1)}, u32[]{:S(2)}, u32[]{:S(2)}) %collective-permute-start.50) | collective-permute-done | bytes 147488 | tf_op jit(solution)/shard_map/ppermute | solution.py:144
  (348 shorter events, 72.5 us)
Async XLA Ops:
  2.4 6.8 %collective-permute-start.1 = (bf16[48,1536]{1,0:T(8,128)(2,1)S(1)}, bf16[48,1536]{1,0:T(8,128)(2,1)S(1)}, u32[]{:S(2)}, u32[]{:S(2)}) collective-permute-start(bf16[48,1536]{1,0:T(8,128)(2,1)S(1)} %constant_dynamic-update-slice_fusion.refs_0_), channel_id=1, source_target_pairs={{0,8},{2,10},{8,16},{10,18},{16,24},{18,26},{24,28},{26,30},{28,20... | collective-permute-start | bytes 442376 | tf_op jit(solution)/shard_map/ppermute | solution.py:81
  5.5 7.1 %collective-permute-start.2 = (bf16[48,1536]{1,0:T(8,128)(2,1)S(1)}, bf16[48,1536]{1,0:T(8,128)(2,1)S(1)}, u32[]{:S(2)}, u32[]{:S(2)}) collective-permute-start(bf16[48,1536]{1,0:T(8,128)(2,1)S(1)} %constant_dynamic-update-slice_fusion.refs_0_), channel_id=1, source_target_pairs={{8,0},{10,2},{16,8},{18,10},{24,16},{26,18},{28,24},{30,26},{20,28... | collective-permute-start | bytes 442376 | tf_op jit(solution)/shard_map/ppermute | solution.py:81
  9.2 5.1 %collective-permute-start.3 = (bf16[48,1536]{1,0:T(8,128)(2,1)S(1)}, bf16[48,1536]{1,0:T(8,128)(2,1)S(1)}, u32[]{:S(2)}, u32[]{:S(2)}) collective-permute-start(bf16[48,1536]{1,0:T(8,128)(2,1)S(1)} %collective-permute-done.1.refs_1_), channel_id=1, source_target_pairs={{0,8},{2,10},{8,16},{10,18},{16,24},{18,26},{24,28},{26,30},{28,20... | collective-permute-start | bytes 442376 | tf_op jit(solution)/shard_map/ppermute | solution.py:81
  11.1 19.1 %collective-permute-start = (bf16[128,768]{1,0:T(8,128)(2,1)}, bf16[128,768]{1,0:T(8,128)(2,1)S(1)}, u32[]{:S(2)}, u32[]{:S(2)}) collective-permute-start(bf16[128,768]{1,0:T(8,128)(2,1)} %param.13), channel_id=1, source_target_pairs={{0,1},{1,0},{2,3},{3,2},{4,5},{5,4},{6,7},{7,6},{8,9},{9,8},{10,11... | collective-permute-start | bytes 589832 | tf_op jit(solution)/shard_map/ppermute | solution.py:254
  12.6 6.8 %collective-permute-start.4 = (bf16[48,1536]{1,0:T(8,128)(2,1)S(1)}, bf16[48,1536]{1,0:T(8,128)(2,1)S(1)}, u32[]{:S(2)}, u32[]{:S(2)}) collective-permute-start(bf16[48,1536]{1,0:T(8,128)(2,1)S(1)} %collective-permute-done.2.refs_2_), channel_id=1, source_target_pairs={{8,0},{10,2},{16,8},{18,10},{24,16},{26,18},{28,24},{30,26},{20,28... | collective-permute-start | bytes 442376 | tf_op jit(solution)/shard_map/ppermute | solution.py:81
  14.4 5.3 %collective-permute-start.5 = (bf16[48,1536]{1,0:T(8,128)(2,1)S(1)}, bf16[48,1536]{1,0:T(8,128)(2,1)S(1)}, u32[]{:S(2)}, u32[]{:S(2)}) collective-permute-start(bf16[48,1536]{1,0:T(8,128)(2,1)S(1)} %collective-permute-done.3.refs_3_), channel_id=1, source_target_pairs={{0,8},{2,10},{8,16},{10,18},{16,24},{18,26},{24,28},{26,30},{28,20... | collective-permute-start | bytes 442376 | tf_op jit(solution)/shard_map/ppermute | solution.py:81
  18.0 12.0 %collective-permute-start.11 = (bf16[48,2,768]{2,1,0:T(2,128)(2,1)}, bf16[48,2,768]{2,1,0:T(2,128)(2,1)S(1)}, u32[]{:S(2)}, u32[]{:S(2)}) collective-permute-start(bf16[48,2,768]{2,1,0:T(2,128)(2,1)} %get-tuple-element.160), channel_id=1, source_target_pairs={{0,2},{2,0},{4,6},{6,4},{8,10},{10,8},{12,14},{14,12},{16,18},{18,... | collective-permute-start | bytes 442376 | tf_op jit(solution)/shard_map/ppermute | solution.py:53
  18.9 11.1 %collective-permute-start.21 = (bf16[48,2,768]{2,1,0:T(2,128)(2,1)}, bf16[48,2,768]{2,1,0:T(2,128)(2,1)S(1)}, u32[]{:S(2)}, u32[]{:S(2)}) collective-permute-start(bf16[48,2,768]{2,1,0:T(2,128)(2,1)} %get-tuple-element.158), channel_id=1, source_target_pairs={{0,2},{2,0},{4,6},{6,4},{8,10},{10,8},{12,14},{14,12},{16,18},{18,... | collective-permute-start | bytes 442376 | tf_op jit(solution)/shard_map/ppermute | solution.py:53
  19.4 5.8 %collective-permute-start.6 = (bf16[48,1536]{1,0:T(8,128)(2,1)S(1)}, bf16[48,1536]{1,0:T(8,128)(2,1)S(1)}, u32[]{:S(2)}, u32[]{:S(2)}) collective-permute-start(bf16[48,1536]{1,0:T(8,128)(2,1)S(1)} %collective-permute-done.4.refs_4_), channel_id=1, source_target_pairs={{8,0},{10,2},{16,8},{18,10},{24,16},{26,18},{28,24},{30,26},{20,28... | collective-permute-start | bytes 442376 | tf_op jit(solution)/shard_map/ppermute | solution.py:81
  19.6 5.6 %collective-permute-start.7 = (bf16[48,1536]{1,0:T(8,128)(2,1)S(1)}, bf16[48,1536]{1,0:T(8,128)(2,1)S(1)}, u32[]{:S(2)}, u32[]{:S(2)}) collective-permute-start(bf16[48,1536]{1,0:T(8,128)(2,1)S(1)} %collective-permute-done.5.refs_5_), channel_id=1, source_target_pairs={{0,8},{2,10},{8,16},{10,18},{16,24},{18,26},{24,28},{26,30},{28,20... | collective-permute-start | bytes 442376 | tf_op jit(solution)/shard_map/ppermute | solution.py:83
  27.6 2.9 %collective-permute-start.8 = (bf16[384,1536]{1,0:T(8,128)(2,1)S(1)}, bf16[384,1536]{1,0:T(8,128)(2,1)S(1)}, u32[]{:S(2)}, u32[]{:S(2)}) collective-permute-start(bf16[384,1536]{1,0:T(8,128)(2,1)S(1)} %assemble.3.own_ref), channel_id=1, source_target_pairs={{0,2},{2,0},{4,6},{6,4},{8,10},{10,8},{12,14},{14,12},{16,18},{18,... | collective-permute-start | bytes 3538952 | tf_op jit(solution)/shard_map/ppermute | solution.py:53
  38.0 22.0 %collective-permute-start.9 = (bf16[256,768]{1,0:T(8,128)(2,1)S(1)}, bf16[256,768]{1,0:T(8,128)(2,1)S(1)}, u32[]{:S(2)}, u32[]{:S(2)}) collective-permute-start(bf16[256,768]{1,0:T(8,128)(2,1)S(1)} %get-tuple-element.42), channel_id=1, source_target_pairs={{0,1},{1,0},{2,3},{3,2},{4,5},{5,4},{6,7},{7,6},{8,9},{9,8},{10,11... | collective-permute-start | bytes 1179656 | tf_op jit(solution)/shard_map/ppermute | solution.py:254
  39.8 10.0 %collective-permute-start.22 = (bf16[96,1536]{1,0:T(8,128)(2,1)S(1)}, bf16[96,1536]{1,0:T(8,128)(2,1)}, u32[]{:S(2)}, u32[]{:S(2)}) collective-permute-start(bf16[96,1536]{1,0:T(8,128)(2,1)S(1)} %maximum_select_fusion.5.refs_0_), channel_id=1, source_target_pairs={{0,8},{2,10},{8,16},{10,18},{16,24},{18,26},{24,28},{26,30},{28,20... | collective-permute-start | bytes 884744 | tf_op jit(solution)/shard_map/ppermute | solution.py:81
  41.4 10.0 %collective-permute-start.23 = (bf16[96,1536]{1,0:T(8,128)(2,1)S(1)}, bf16[96,1536]{1,0:T(8,128)(2,1)}, u32[]{:S(2)}, u32[]{:S(2)}) collective-permute-start(bf16[96,1536]{1,0:T(8,128)(2,1)S(1)} %maximum_select_fusion.5.refs_0_), channel_id=1, source_target_pairs={{8,0},{10,2},{16,8},{18,10},{24,16},{26,18},{28,24},{30,26},{20,28... | collective-permute-start | bytes 884744 | tf_op jit(solution)/shard_map/ppermute | solution.py:81
  41.9 13.3 %collective-permute-start.12 = (bf16[96,1536]{1,0:T(8,128)(2,1)S(1)}, bf16[96,1536]{1,0:T(8,128)(2,1)S(1)}, u32[]{:S(2)}, u32[]{:S(2)}) collective-permute-start(bf16[96,1536]{1,0:T(8,128)(2,1)S(1)} %maximum_select_fusion.4.refs_0_), channel_id=1, source_target_pairs={{0,8},{2,10},{8,16},{10,18},{16,24},{18,26},{24,28},{26,30},{28,20... | collective-permute-start | bytes 884744 | tf_op jit(solution)/shard_map/ppermute | solution.py:81
  43.4 13.0 %collective-permute-start.13 = (bf16[96,1536]{1,0:T(8,128)(2,1)S(1)}, bf16[96,1536]{1,0:T(8,128)(2,1)S(1)}, u32[]{:S(2)}, u32[]{:S(2)}) collective-permute-start(bf16[96,1536]{1,0:T(8,128)(2,1)S(1)} %maximum_select_fusion.4.refs_0_), channel_id=1, source_target_pairs={{8,0},{10,2},{16,8},{18,10},{24,16},{26,18},{28,24},{30,26},{20,28... | collective-permute-start | bytes 884744 | tf_op jit(solution)/shard_map/ppermute | solution.py:81
  49.8 11.5 %collective-permute-start.16 = (bf16[128,768]{1,0:T(8,128)(2,1)S(1)}, bf16[128,768]{1,0:T(8,128)(2,1)S(1)}, u32[]{:S(2)}, u32[]{:S(2)}) collective-permute-start(bf16[128,768]{1,0:T(8,128)(2,1)S(1)} %copy-done.61), channel_id=1, source_target_pairs={{0,1},{1,0},{2,3},{3,2},{4,5},{5,4},{6,7},{7,6},{8,9},{9,8},{10,11... | collective-permute-start | bytes 589832 | tf_op jit(solution)/shard_map/ppermute | solution.py:254
  56.4 10.1 %collective-permute-start.14 = (bf16[96,1536]{1,0:T(8,128)(2,1)S(1)}, bf16[96,1536]{1,0:T(8,128)(2,1)}, u32[]{:S(2)}, u32[]{:S(2)}) collective-permute-start(bf16[96,1536]{1,0:T(8,128)(2,1)S(1)} %collective-permute-done.12.refs_1_), channel_id=1, source_target_pairs={{0,8},{2,10},{8,16},{10,18},{16,24},{18,26},{24,28},{26,30},{28,20... | collective-permute-start | bytes 884744 | tf_op jit(solution)/shard_map/ppermute | solution.py:81
  58.0 8.5 %collective-permute-start.15 = (bf16[96,1536]{1,0:T(8,128)(2,1)S(1)}, bf16[96,1536]{1,0:T(8,128)(2,1)S(1)}, u32[]{:S(2)}, u32[]{:S(2)}) collective-permute-start(bf16[96,1536]{1,0:T(8,128)(2,1)S(1)} %collective-permute-done.13.refs_2_), channel_id=1, source_target_pairs={{8,0},{10,2},{16,8},{18,10},{24,16},{26,18},{28,24},{30,26},{20,28... | collective-permute-start | bytes 884744 | tf_op jit(solution)/shard_map/ppermute | solution.py:81
  58.5 12.7 %collective-permute-start.24 = (bf16[96,1536]{1,0:T(8,128)(2,1)}, bf16[96,1536]{1,0:T(8,128)(2,1)}, u32[]{:S(2)}, u32[]{:S(2)}) collective-permute-start(bf16[96,1536]{1,0:T(8,128)(2,1)} %collective-permute-done.22.refs_1_), channel_id=1, source_target_pairs={{0,8},{2,10},{8,16},{10,18},{16,24},{18,26},{24,28},{26,30},{28,20... | collective-permute-start | bytes 884744 | tf_op jit(solution)/shard_map/ppermute | solution.py:81
  60.9 2.0 collective-permute-start.10
  62.0 2.1 collective-permute-start.17
  62.9 9.4 %collective-permute-start.25 = (bf16[96,1536]{1,0:T(8,128)(2,1)}, bf16[96,1536]{1,0:T(8,128)(2,1)}, u32[]{:S(2)}, u32[]{:S(2)}) collective-permute-start(bf16[96,1536]{1,0:T(8,128)(2,1)} %collective-permute-done.23.refs_2_), channel_id=1, source_target_pairs={{8,0},{10,2},{16,8},{18,10},{24,16},{26,18},{28,24},{30,26},{20,28... | collective-permute-start | bytes 884744 | tf_op jit(solution)/shard_map/ppermute | solution.py:81
  67.2 9.8 %collective-permute-start.18 = (bf16[96,1536]{1,0:T(8,128)(2,1)}, bf16[96,1536]{1,0:T(8,128)(2,1)}, u32[]{:S(2)}, u32[]{:S(2)}) collective-permute-start(bf16[96,1536]{1,0:T(8,128)(2,1)} %collective-permute-done.14.refs_3_), channel_id=1, source_target_pairs={{0,8},{2,10},{8,16},{10,18},{16,24},{18,26},{24,28},{26,30},{28,20... | collective-permute-start | bytes 884744 | tf_op jit(solution)/shard_map/ppermute | solution.py:81
  72.2 15.3 %collective-permute-start.19 = (bf16[96,1536]{1,0:T(8,128)(2,1)}, bf16[96,1536]{1,0:T(8,128)(2,1)}, u32[]{:S(2)}, u32[]{:S(2)}) collective-permute-start(bf16[96,1536]{1,0:T(8,128)(2,1)} %copy-done.23), channel_id=1, source_target_pairs={{8,0},{10,2},{16,8},{18,10},{24,16},{26,18},{28,24},{30,26},{20,28... | collective-permute-start | bytes 884744 | tf_op jit(solution)/shard_map/ppermute | solution.py:81
  72.7 14.4 %collective-permute-start.27 = (bf16[96,1536]{1,0:T(8,128)(2,1)}, bf16[96,1536]{1,0:T(8,128)(2,1)}, u32[]{:S(2)}, u32[]{:S(2)}) collective-permute-start(bf16[96,1536]{1,0:T(8,128)(2,1)} %collective-permute-done.25.refs_4_), channel_id=1, source_target_pairs={{8,0},{10,2},{16,8},{18,10},{24,16},{26,18},{28,24},{30,26},{20,28... | collective-permute-start | bytes 884744 | tf_op jit(solution)/shard_map/ppermute | solution.py:81
  77.0 10.6 %collective-permute-start.20 = (bf16[96,1536]{1,0:T(8,128)(2,1)}, bf16[96,1536]{1,0:T(8,128)(2,1)}, u32[]{:S(2)}, u32[]{:S(2)}) collective-permute-start(bf16[96,1536]{1,0:T(8,128)(2,1)} %collective-permute-done.18.refs_5_), channel_id=1, source_target_pairs={{0,8},{2,10},{8,16},{10,18},{16,24},{18,26},{24,28},{26,30},{28,20... | collective-permute-start | bytes 884744 | tf_op jit(solution)/shard_map/ppermute | solution.py:83
  81.3 14.0 %collective-permute-start.26 = (bf16[96,1536]{1,0:T(8,128)(2,1)}, bf16[96,1536]{1,0:T(8,128)(2,1)S(1)}, u32[]{:S(2)}, u32[]{:S(2)}) collective-permute-start(bf16[96,1536]{1,0:T(8,128)(2,1)} %collective-permute-done.24.refs_3_), channel_id=1, source_target_pairs={{0,8},{2,10},{8,16},{10,18},{16,24},{18,26},{24,28},{26,30},{28,20... | collective-permute-start | bytes 884744 | tf_op jit(solution)/shard_map/ppermute | solution.py:81
  87.1 8.2 %collective-permute-start.28 = (bf16[96,1536]{1,0:T(8,128)(2,1)}, bf16[96,1536]{1,0:T(8,128)(2,1)S(1)}, u32[]{:S(2)}, u32[]{:S(2)}) collective-permute-start(bf16[96,1536]{1,0:T(8,128)(2,1)} %collective-permute-done.27.refs_6_), channel_id=1, source_target_pairs={{8,0},{10,2},{16,8},{18,10},{24,16},{26,18},{28,24},{30,26},{20,28... | collective-permute-start | bytes 884744 | tf_op jit(solution)/shard_map/ppermute | solution.py:85
  105.4 8.0 %collective-permute-start.31 = (bf16[352,768]{1,0:T(8,128)(2,1)S(1)}, bf16[352,768]{1,0:T(8,128)(2,1)S(1)}, u32[]{:S(2)}, u32[]{:S(2)}) collective-permute-start(bf16[352,768]{1,0:T(8,128)(2,1)S(1)} %pad_maximum_fusion.5), channel_id=1, source_target_pairs={{0,2},{2,0},{4,6},{6,4},{8,10},{10,8},{12,14},{14,12},{16,18},{18,... | collective-permute-start | bytes 1622024 | tf_op jit(solution)/shard_map/ppermute | solution.py:53
  105.6 6.7 %collective-permute-start.29 = (bf16[352,768]{1,0:T(8,128)(2,1)S(1)}, bf16[352,768]{1,0:T(8,128)(2,1)S(1)}, u32[]{:S(2)}, u32[]{:S(2)}) collective-permute-start(bf16[352,768]{1,0:T(8,128)(2,1)S(1)} %pad_maximum_fusion.4), channel_id=1, source_target_pairs={{0,2},{2,0},{4,6},{6,4},{8,10},{10,8},{12,14},{14,12},{16,18},{18,... | collective-permute-start | bytes 1622024 | tf_op jit(solution)/shard_map/ppermute | solution.py:53
  106.2 28.1 %collective-permute-start.34 = (bf16[96,1536]{1,0:T(8,128)(2,1)S(1)}, bf16[96,1536]{1,0:T(8,128)(2,1)S(1)}, u32[]{:S(2)}, u32[]{:S(2)}) collective-permute-start(bf16[96,1536]{1,0:T(8,128)(2,1)S(1)} %get-tuple-element.126), channel_id=1, source_target_pairs={{0,8},{2,10},{8,16},{10,18},{16,24},{18,26},{24,28},{26,30},{28,20... | collective-permute-start | bytes 884744 | tf_op jit(solution)/shard_map/ppermute | solution.py:144
  110.7 10.8 %collective-permute-start.56 = (bf16[96,1536]{1,0:T(8,128)(2,1)S(1)}, bf16[96,1536]{1,0:T(8,128)(2,1)S(1)}, u32[]{:S(2)}, u32[]{:S(2)}) collective-permute-start(bf16[96,1536]{1,0:T(8,128)(2,1)S(1)} %get-tuple-element.121), channel_id=1, source_target_pairs={{0,8},{2,10},{8,16},{10,18},{16,24},{18,26},{24,28},{26,30},{28,20... | collective-permute-start | bytes 884744 | tf_op jit(solution)/shard_map/ppermute | solution.py:134
  112.9 11.5 %collective-permute-start.30 = (bf16[128,768]{1,0:T(8,128)(2,1)S(1)}, bf16[128,768]{1,0:T(8,128)(2,1)S(1)}, u32[]{:S(2)}, u32[]{:S(2)}) collective-permute-start(bf16[128,768]{1,0:T(8,128)(2,1)S(1)} %constant_dynamic-slice_fusion.1), channel_id=1, source_target_pairs={{0,1},{1,0},{2,3},{3,2},{4,5},{5,4},{6,7},{7,6},{8,9},{9,8},{10,11... | collective-permute-start | bytes 589832 | tf_op jit(solution)/shard_map/ppermute | solution.py:254
  113.9 11.7 %collective-permute-start.33 = (bf16[96,1536]{1,0:T(8,128)(2,1)S(1)}, bf16[96,1536]{1,0:T(8,128)(2,1)S(1)}, u32[]{:S(2)}, u32[]{:S(2)}) collective-permute-start(bf16[96,1536]{1,0:T(8,128)(2,1)S(1)} %get-tuple-element.55), channel_id=1, source_target_pairs={{8,0},{10,2},{16,8},{18,10},{24,16},{26,18},{28,24},{30,26},{20,28... | collective-permute-start | bytes 884744 | tf_op jit(solution)/shard_map/ppermute | solution.py:134
  122.3 10.2 %collective-permute-start.32 = (bf16[256,768]{1,0:T(8,128)(2,1)S(1)}, bf16[256,768]{1,0:T(8,128)(2,1)S(1)}, u32[]{:S(2)}, u32[]{:S(2)}) collective-permute-start(bf16[256,768]{1,0:T(8,128)(2,1)S(1)} %get-tuple-element.174), channel_id=1, source_target_pairs={{0,1},{1,0},{2,3},{3,2},{4,5},{5,4},{6,7},{7,6},{8,9},{9,8},{10,11... | collective-permute-start | bytes 1179656 | tf_op jit(solution)/shard_map/ppermute | solution.py:254
  122.8 34.7 %collective-permute-start.57 = (bf16[96,1536]{1,0:T(8,128)(2,1)}, bf16[96,1536]{1,0:T(8,128)(2,1)S(1)}, u32[]{:S(2)}, u32[]{:S(2)}) collective-permute-start(bf16[96,1536]{1,0:T(8,128)(2,1)} %add_convert_fusion.6), channel_id=1, source_target_pairs={{0,8},{2,10},{8,16},{10,18},{16,24},{18,26},{24,28},{26,30},{28,20... | collective-permute-start | bytes 884744 | tf_op jit(solution)/shard_map/ppermute | solution.py:144
  124.4 24.0 %collective-permute-start.59 = (bf16[96,1536]{1,0:T(8,128)(2,1)}, bf16[96,1536]{1,0:T(8,128)(2,1)}, u32[]{:S(2)}, u32[]{:S(2)}) collective-permute-start(bf16[96,1536]{1,0:T(8,128)(2,1)} %get-tuple-element.71), channel_id=1, source_target_pairs={{8,0},{10,2},{16,8},{18,10},{24,16},{26,18},{28,24},{30,26},{20,28... | collective-permute-start | bytes 884744 | tf_op jit(solution)/shard_map/ppermute | solution.py:144
  125.7 12.8 %collective-permute-start.35 = (bf16[96,1536]{1,0:T(8,128)(2,1)S(1)}, bf16[96,1536]{1,0:T(8,128)(2,1)S(1)}, u32[]{:S(2)}, u32[]{:S(2)}) collective-permute-start(bf16[96,1536]{1,0:T(8,128)(2,1)S(1)} %add_convert_fusion.11), channel_id=1, source_target_pairs={{8,0},{10,2},{16,8},{18,10},{24,16},{26,18},{28,24},{30,26},{20,28... | collective-permute-start | bytes 884744 | tf_op jit(solution)/shard_map/ppermute | solution.py:144
  146.7 3.8 %collective-permute-start.37 = (f32[27,128]{1,0:T(8,128)S(1)}, f32[27,128]{1,0:T(8,128)S(1)}, u32[]{:S(2)}, u32[]{:S(2)}) collective-permute-start(f32[27,128]{1,0:T(8,128)S(1)} %bitcast.99), channel_id=1, source_target_pairs={{0,1},{1,0},{2,3},{3,2},{4,5},{5,4},{6,7},{7,6},{8,9},{9,8},{10,11... | collective-permute-start | bytes 41480 | tf_op jit(solution)/shard_map/ppermute | solution.py:254
  149.5 9.2 %collective-permute-start.60 = (bf16[96,1536]{1,0:T(8,128)(2,1)S(1)}, bf16[96,1536]{1,0:T(8,128)(2,1)S(1)}, u32[]{:S(2)}, u32[]{:S(2)}) collective-permute-start(bf16[96,1536]{1,0:T(8,128)(2,1)S(1)} %add_convert_fusion.3), channel_id=1, source_target_pairs={{8,0},{10,2},{16,8},{18,10},{24,16},{26,18},{28,24},{30,26},{20,28... | collective-permute-start | bytes 884744 | tf_op jit(solution)/shard_map/ppermute | solution.py:144
  150.5 2.3 %collective-permute-start.38 = (f32[27,128]{1,0:T(8,128)S(1)}, f32[27,128]{1,0:T(8,128)S(1)}, u32[]{:S(2)}, u32[]{:S(2)}) collective-permute-start(f32[27,128]{1,0:T(8,128)S(1)} %bitcast_add_fusion), channel_id=1, source_target_pairs={{0,2},{2,0},{4,6},{6,4},{8,10},{10,8},{12,14},{14,12},{16,18},{18,... | collective-permute-start | bytes 41480 | tf_op jit(solution)/shard_map/ppermute | solution.py:267
  151.2 24.1 %collective-permute-start.36 = (bf16[128,768]{1,0:T(8,128)(2,1)}, bf16[128,768]{1,0:T(8,128)(2,1)}, u32[]{:S(2)}, u32[]{:S(2)}) collective-permute-start(bf16[128,768]{1,0:T(8,128)(2,1)} %constant_dynamic-slice_fusion), channel_id=1, source_target_pairs={{0,1},{1,0},{2,3},{3,2},{4,5},{5,4},{6,7},{7,6},{8,9},{9,8},{10,11... | collective-permute-start | bytes 589832 | tf_op jit(solution)/shard_map/ppermute | solution.py:254
  152.8 3.8 %collective-permute-start.39 = (f32[27,128]{1,0:T(8,128)S(1)}, f32[27,128]{1,0:T(8,128)S(1)}, u32[]{:S(2)}, u32[]{:S(2)}) collective-permute-start(f32[27,128]{1,0:T(8,128)S(1)} %fusion.82), channel_id=1, source_target_pairs={{0,4},{2,6},{4,0},{6,2},{8,12},{10,14},{12,8},{14,10},{16,20},{18,... | collective-permute-start | bytes 41480 | tf_op jit(solution)/shard_map/ppermute | solution.py:267
  155.4 23.7 %collective-permute-start.51 = (bf16[96,1536]{1,0:T(8,128)(2,1)}, bf16[96,1536]{1,0:T(8,128)(2,1)}, u32[]{:S(2)}, u32[]{:S(2)}) collective-permute-start(bf16[96,1536]{1,0:T(8,128)(2,1)} %get-tuple-element.68), channel_id=1, source_target_pairs={{0,8},{2,10},{8,16},{10,18},{16,24},{18,26},{24,28},{26,30},{28,20... | collective-permute-start | bytes 884744 | tf_op jit(solution)/shard_map/ppermute | solution.py:144
  156.6 22.5 %collective-permute-start.53 = (bf16[96,1536]{1,0:T(8,128)(2,1)}, bf16[96,1536]{1,0:T(8,128)(2,1)}, u32[]{:S(2)}, u32[]{:S(2)}) collective-permute-start(bf16[96,1536]{1,0:T(8,128)(2,1)} %get-tuple-element.69), channel_id=1, source_target_pairs={{8,0},{10,2},{16,8},{18,10},{24,16},{26,18},{28,24},{30,26},{20,28... | collective-permute-start | bytes 884744 | tf_op jit(solution)/shard_map/ppermute | solution.py:144
  157.5 8.5 %collective-permute-start.40 = (f32[27,128]{1,0:T(8,128)S(1)}, f32[27,128]{1,0:T(8,128)S(1)}, u32[]{:S(2)}, u32[]{:S(2)}) collective-permute-start(f32[27,128]{1,0:T(8,128)S(1)} %add.536), channel_id=1, source_target_pairs={{0,8},{2,10},{4,12},{6,14},{8,0},{10,2},{12,4},{14,6},{16,24},{18,... | collective-permute-start | bytes 41480 | tf_op jit(solution)/shard_map/ppermute | solution.py:267
  160.8 24.6 %collective-permute-start.58 = (bf16[96,1536]{1,0:T(8,128)(2,1)}, bf16[96,1536]{1,0:T(8,128)(2,1)}, u32[]{:S(2)}, u32[]{:S(2)}) collective-permute-start(bf16[96,1536]{1,0:T(8,128)(2,1)} %get-tuple-element.119), channel_id=1, source_target_pairs={{0,8},{2,10},{8,16},{10,18},{16,24},{18,26},{24,28},{26,30},{28,20... | collective-permute-start | bytes 884744 | tf_op jit(solution)/shard_map/ppermute | solution.py:144
  166.0 4.6 %collective-permute-start.41 = (f32[27,128]{1,0:T(8,128)S(1)}, f32[27,128]{1,0:T(8,128)S(1)}, u32[]{:S(2)}, u32[]{:S(2)}) collective-permute-start(f32[27,128]{1,0:T(8,128)S(1)} %add.537), channel_id=1, source_target_pairs={{0,16},{2,18},{4,20},{6,22},{8,24},{10,26},{12,28},{14,30},{16,0},... | collective-permute-start | bytes 41480 | tf_op jit(solution)/shard_map/ppermute | solution.py:267
  170.7 13.2 %collective-permute-start.43 = (bf16[144,1536]{1,0:T(8,128)(2,1)S(1)}, bf16[144,1536]{1,0:T(8,128)(2,1)}, u32[]{:S(2)}, u32[]{:S(2)}) collective-permute-start(bf16[144,1536]{1,0:T(8,128)(2,1)S(1)} %get-tuple-element.67), channel_id=1, source_target_pairs={{0,2},{2,0},{4,6},{6,4},{8,10},{10,8},{12,14},{14,12},{16,18},{18,... | collective-permute-start | bytes 1327112 | tf_op jit(solution)/shard_map/ppermute | solution.py:113
  175.2 28.8 %collective-permute-start.42 = (bf16[240,1536]{1,0:T(8,128)(2,1)S(1)}, bf16[240,1536]{1,0:T(8,128)(2,1)}, u32[]{:S(2)}, u32[]{:S(2)}) collective-permute-start(bf16[240,1536]{1,0:T(8,128)(2,1)S(1)} %get-tuple-element.66), channel_id=1, source_target_pairs={{0,2},{2,0},{4,6},{6,4},{8,10},{10,8},{12,14},{14,12},{16,18},{18,... | collective-permute-start | bytes 2211848 | tf_op jit(solution)/shard_map/ppermute | solution.py:113
  180.5 18.1 %collective-permute-start.52 = (bf16[96,1536]{1,0:T(8,128)(2,1)S(1)}, bf16[96,1536]{1,0:T(8,128)(2,1)S(1)}, u32[]{:S(2)}, u32[]{:S(2)}) collective-permute-start(bf16[96,1536]{1,0:T(8,128)(2,1)S(1)} %get-tuple-element.122), channel_id=1, source_target_pairs={{0,8},{2,10},{8,16},{10,18},{16,24},{18,26},{24,28},{26,30},{28,20... | collective-permute-start | bytes 884744 | tf_op jit(solution)/shard_map/ppermute | solution.py:144
  181.7 16.9 %collective-permute-start.54 = (bf16[96,1536]{1,0:T(8,128)(2,1)S(1)}, bf16[96,1536]{1,0:T(8,128)(2,1)S(1)}, u32[]{:S(2)}, u32[]{:S(2)}) collective-permute-start(bf16[96,1536]{1,0:T(8,128)(2,1)S(1)} %get-tuple-element.123), channel_id=1, source_target_pairs={{8,0},{10,2},{16,8},{18,10},{24,16},{26,18},{28,24},{30,26},{20,28... | collective-permute-start | bytes 884744 | tf_op jit(solution)/shard_map/ppermute | solution.py:144
  184.8 9.9 %collective-permute-start.44 = (bf16[48,1536]{1,0:T(8,128)(2,1)S(1)}, bf16[48,1536]{1,0:T(8,128)(2,1)S(1)}, u32[]{:S(2)}, u32[]{:S(2)}) collective-permute-start(bf16[48,1536]{1,0:T(8,128)(2,1)S(1)} %add_convert_fusion.21), channel_id=1, source_target_pairs={{0,8},{2,10},{8,16},{10,18},{16,24},{18,26},{24,28},{26,30},{28,20... | collective-permute-start | bytes 442376 | tf_op jit(solution)/shard_map/ppermute | solution.py:134
  187.2 18.0 %collective-permute-start.61 = (bf16[96,1536]{1,0:T(8,128)(2,1)}, bf16[96,1536]{1,0:T(8,128)(2,1)}, u32[]{:S(2)}, u32[]{:S(2)}) collective-permute-start(bf16[96,1536]{1,0:T(8,128)(2,1)} %add_convert_fusion.4), channel_id=1, source_target_pairs={{0,8},{2,10},{8,16},{10,18},{16,24},{18,26},{24,28},{26,30},{28,20... | collective-permute-start | bytes 884744 | tf_op jit(solution)/shard_map/ppermute | solution.py:144
  194.7 10.5 %collective-permute-start.62 = (bf16[96,1536]{1,0:T(8,128)(2,1)}, bf16[96,1536]{1,0:T(8,128)(2,1)}, u32[]{:S(2)}, u32[]{:S(2)}) collective-permute-start(bf16[96,1536]{1,0:T(8,128)(2,1)} %get-tuple-element.73), channel_id=1, source_target_pairs={{8,0},{10,2},{16,8},{18,10},{24,16},{26,18},{28,24},{30,26},{20,28... | collective-permute-start | bytes 884744 | tf_op jit(solution)/shard_map/ppermute | solution.py:144
  198.6 5.5 %collective-permute-start.45 = (bf16[48,1536]{1,0:T(8,128)(2,1)}, bf16[48,1536]{1,0:T(8,128)(2,1)}, u32[]{:S(2)}, u32[]{:S(2)}) collective-permute-start(bf16[48,1536]{1,0:T(8,128)(2,1)} %get-tuple-element.130), channel_id=1, source_target_pairs={{0,8},{2,10},{8,16},{10,18},{16,24},{18,26},{24,28},{26,30},{28,20... | collective-permute-start | bytes 442376 | tf_op jit(solution)/shard_map/ppermute | solution.py:144
  198.6 8.9 %collective-permute-start.48 = (bf16[48,1536]{1,0:T(8,128)(2,1)}, bf16[48,1536]{1,0:T(8,128)(2,1)S(1)}, u32[]{:S(2)}, u32[]{:S(2)}) collective-permute-start(bf16[48,1536]{1,0:T(8,128)(2,1)} %get-tuple-element.131), channel_id=1, source_target_pairs={{8,0},{10,2},{16,8},{18,10},{24,16},{26,18},{28,24},{30,26},{20,28... | collective-permute-start | bytes 442376 | tf_op jit(solution)/shard_map/ppermute | solution.py:144
  204.1 10.8 %collective-permute-start.55 = (f32[48,2,768]{2,1,0:T(2,128)S(1)}, f32[48,2,768]{2,1,0:T(2,128)S(1)}, u32[]{:S(2)}, u32[]{:S(2)}) collective-permute-start(f32[48,2,768]{2,1,0:T(2,128)S(1)} %get-tuple-element.139), channel_id=1, source_target_pairs={{0,2},{2,0},{4,6},{6,4},{8,10},{10,8},{12,14},{14,12},{16,18},{18,... | collective-permute-start | bytes 884744 | tf_op jit(solution)/shard_map/ppermute | solution.py:53
  205.1 6.4 %collective-permute-start.46 = (bf16[48,1536]{1,0:T(8,128)(2,1)S(1)}, bf16[48,1536]{1,0:T(8,128)(2,1)}, u32[]{:S(2)}, u32[]{:S(2)}) collective-permute-start(bf16[48,1536]{1,0:T(8,128)(2,1)S(1)} %add_convert_fusion.19), channel_id=1, source_target_pairs={{0,8},{2,10},{8,16},{10,18},{16,24},{18,26},{24,28},{26,30},{28,20... | collective-permute-start | bytes 442376 | tf_op jit(solution)/shard_map/ppermute | solution.py:144
  206.9 14.2 %collective-permute-start.63 = (f32[48,2,768]{2,1,0:T(2,128)S(1)}, f32[48,2,768]{2,1,0:T(2,128)S(1)}, u32[]{:S(2)}, u32[]{:S(2)}) collective-permute-start(f32[48,2,768]{2,1,0:T(2,128)S(1)} %get-tuple-element.137), channel_id=1, source_target_pairs={{0,2},{2,0},{4,6},{6,4},{8,10},{10,8},{12,14},{14,12},{16,18},{18,... | collective-permute-start | bytes 884744 | tf_op jit(solution)/shard_map/ppermute | solution.py:53
  212.7 9.6 %collective-permute-start.47 = (bf16[48,1536]{1,0:T(8,128)(2,1)S(1)}, bf16[48,1536]{1,0:T(8,128)(2,1)S(1)}, u32[]{:S(2)}, u32[]{:S(2)}) collective-permute-start(bf16[48,1536]{1,0:T(8,128)(2,1)S(1)} %get-tuple-element.128), channel_id=1, source_target_pairs={{0,8},{2,10},{8,16},{10,18},{16,24},{18,26},{24,28},{26,30},{28,20... | collective-permute-start | bytes 442376 | tf_op jit(solution)/shard_map/ppermute | solution.py:144
  213.1 5.4 %collective-permute-start.49 = (bf16[48,1536]{1,0:T(8,128)(2,1)S(1)}, bf16[48,1536]{1,0:T(8,128)(2,1)S(1)}, u32[]{:S(2)}, u32[]{:S(2)}) collective-permute-start(bf16[48,1536]{1,0:T(8,128)(2,1)S(1)} %get-tuple-element.129), channel_id=1, source_target_pairs={{8,0},{10,2},{16,8},{18,10},{24,16},{26,18},{28,24},{30,26},{20,28... | collective-permute-start | bytes 442376 | tf_op jit(solution)/shard_map/ppermute | solution.py:144
  219.5 5.2 %collective-permute-start.50 = (bf16[48,1536]{1,0:T(8,128)(2,1)S(1)}, bf16[48,1536]{1,0:T(8,128)(2,1)S(1)}, u32[]{:S(2)}, u32[]{:S(2)}) collective-permute-start(bf16[48,1536]{1,0:T(8,128)(2,1)S(1)} %add_convert_fusion.15), channel_id=1, source_target_pairs={{8,0},{10,2},{16,8},{18,10},{24,16},{26,18},{28,24},{30,26},{20,28... | collective-permute-start | bytes 442376 | tf_op jit(solution)/shard_map/ppermute | solution.py:144
  (75 other events, 548.1 us)

commit v4 on v3

v4 whole, which is shorter than its diff:
```python
import jax
import jax.numpy as jnp
from jax import lax
from jax.experimental import pallas as pl
from jax.experimental.pallas import tpu as pltpu
from jax.sharding import PartitionSpec as P

HEAD_DIM = 64
EXPERTS = 2
CAP = 176

LONGEST = 16

EPS = 1e-06
NEG = -1e30
VMEM_BYTES = 12 << 20
EXPERT_VMEM_BYTES = 24 << 20
SMALL = pl.CostEstimate(flops=1, bytes_accessed=1, transcendentals=0)
HIGH = lax.Precision.HIGHEST
BF = jnp.bfloat16
F32 = jnp.float32


def ring_chip(place, chips):
    place = place % chips
    return jnp.where(place < chips // 2, 2 * place, 2 * (chips - 1 - place) + 1)


def ring_place(chip, chips):
    return jnp.where(chip % 2 == 0, chip // 2, chips - 1 - chip // 2)


class Ring:
    def __init__(self):
        self.n = lax.axis_size("dp")
        self.chips = self.n // 2
        order = [2 * i for i in range(self.chips // 2)]
        order = order + [c + 1 for c in reversed(order)]
        pairs = [
            (order[i] * 2 + k, order[(i + 1) % self.chips] * 2 + k)
            for i in range(self.chips)
            for k in (0, 1)
        ]
        self.right = pairs
        self.left = [(b, a) for a, b in pairs]
        self.swap = [(i, i ^ 1) for i in range(self.n)]
        index = lax.axis_index("dp")
        self.core = index % 2
        self.long = self.chips > LONGEST
        self.place = ring_place(index // 2, self.chips)
        reach = self.chips // 2
        self.distances = [0] + [d for s in range(1, reach) for d in (-s, s)] + [reach]
        self.slots = [reach] + [d for s in range(reach - 1, 0, -1) for d in (s, -s)] + [0]

    def other_core(self, x):
        return lax.ppermute(x, "dp", self.swap)

    def by_core(self, own, other, axis):
        return jnp.where(
            self.core == 0,
            jnp.concatenate([own, other], axis=axis),
            jnp.concatenate([other, own], axis=axis),
        )

    def slot_chips(self):
        return jnp.stack([self.chip_at(d) for d in self.slots])

    def chip_at(self, distance):
        return ring_chip(self.place + distance + self.chips, self.chips)


class Gather:
    def __init__(self, ring, shard, halves):
        self.ring, self.shard, self.halves = ring, shard, halves
        self.reach = ring.chips // 2
        self.pieces = [shard]
        self.sent = (shard, shard)
        self.steps = 0

    def step(self, *deps):
        ring, half = self.ring, self.shard.shape[1] // 2
        self.steps += 1
        r, l = after(self.sent, deps)
        if self.steps < self.reach:
            self.sent = (lax.ppermute(r, "dp", ring.right), lax.ppermute(l, "dp", ring.left))
        elif self.halves:
            self.sent = (
                lax.ppermute(r[:, :half], "dp", ring.right),
                lax.ppermute(l[:, half:], "dp", ring.left),
            )
        else:
            self.sent = (lax.ppermute(r, "dp", ring.right),)
        self.pieces += self.sent
        return self.sent

    def owners(self):
        chips = [self.ring.chip_at(d) for d in self.ring.distances]
        return jnp.stack(chips + chips[-1:] if self.halves else chips)


class Scatter:
    def __init__(self, ring, terms, rows):
        self.ring, self.rows = ring, rows
        self.reach = ring.chips // 2
        self.steps = 0
        self.slots = ring.slots
        self.terms = terms
        self.each = len(self.terms) > 2
        self.got = None if self.each else ring.other_core(self.terms[1])

    def blocks(self, distance):
        at = self.slots.index(distance)
        return [(self.terms[at], 0)] if self.each else [(self.terms[0], at), (self.got, at)]

    def step(self, *deps):
        ring = self.ring
        distance = self.reach - self.steps
        self.steps += 1
        if distance == self.reach:
            r, l = ring_far(self.blocks(distance), self.rows)
        else:
            sent = after(self.sent, deps)
            r, l = ring_add(self.blocks(distance), self.blocks(-distance), sent, self.rows)
        self.sent = (lax.ppermute(r, "dp", ring.right), lax.ppermute(l, "dp", ring.left))
        return self.sent

    def total(self):
        r, l = self.sent
        terms = [
            x[at * self.rows : (at + 1) * self.rows].astype(F32) for x, at in self.blocks(0)
        ]
        return sum(terms) + r.astype(F32) + l.astype(F32)


def row_block(rows, width, at):
    return pl.BlockSpec((rows, width), lambda i: (at, 0))


def ring_far(blocks, rows):
    width = blocks[0][0].shape[1]
    half = width // 2

    def kernel(*refs):
        ins, (r_ref, l_ref) = refs[:-2], refs[-2:]
        total = sum(ref[...].astype(F32) for ref in ins).astype(BF)
        r_ref[...] = total[:, :half]
        l_ref[...] = total[:, half:]

    return pl.pallas_call(
        kernel,
        out_shape=[jax.ShapeDtypeStruct((rows, half), BF)] * 2,
        in_specs=[row_block(rows, width, at) for _, at in blocks],
        out_specs=[row_block(rows, half, 0)] * 2,
        compiler_params=pltpu.CompilerParams(vmem_limit_bytes=VMEM_BYTES),
        cost_estimate=SMALL,
        grid=(1,),
        name="ring_far",
    )(*[x for x, _ in blocks])


def ring_add(right, left, sent, rows):
    width = right[0][0].shape[1]
    arrived = sent[0].shape[1]
    number = len(right)
    tiles = 2 if arrived < width else max(1, width // 768)
    tile = width // tiles

    def kernel(*refs):
        ins, outs = refs[:-2], refs[-2:]
        for k, out_ref in enumerate(outs):
            own = ins[k * (number + 1) : (k + 1) * (number + 1) - 1]
            got = ins[(k + 1) * (number + 1) - 1]
            total = sum(ref[...].astype(F32) for ref in own)
            more = got[...].astype(F32)
            if arrived < width:
                more = jnp.where(pl.program_id(0) == k, more, 0.0)
            out_ref[...] = (total + more).astype(BF)

    def block(at):
        return pl.BlockSpec((rows, tile), lambda i: (at, i))

    got_block = block(0) if arrived == width else row_block(rows, tile, 0)
    specs, args = [], []
    for blocks, got in ((right, sent[0]), (left, sent[1])):
        specs += [block(at) for _, at in blocks] + [got_block]
        args += [x for x, _ in blocks] + [got]
    return pl.pallas_call(
        kernel,
        out_shape=[jax.ShapeDtypeStruct((rows, width), BF)] * 2,
        in_specs=specs,
        out_specs=[block(0)] * 2,
        compiler_params=pltpu.CompilerParams(vmem_limit_bytes=VMEM_BYTES),
        cost_estimate=SMALL,
        grid=(tiles,),
        name="ring_add",
    )(*args)


def outer(pairs, owners, rows, counts):
    height = pairs[0][0].shape[1]
    widths = [rhs.shape[1] for _, rhs in pairs]
    width = sum(widths)
    tile = 768

    def kernel(owners_ref, *refs):
        ins, outs, held_ref = refs[: 2 * len(pairs)], refs[2 * len(pairs) : -1], refs[-1]
        at = 0
        for i, wide in enumerate(widths):
            lhs = ins[2 * i][...]
            for start in range(0, wide, tile):
                size = min(tile, wide - start)
                held_ref[:, pl.ds(at, size)] = dot32(
                    lhs, ins[2 * i + 1][:, pl.ds(start, size)], TN
                ).astype(BF)
                at += size
        slot = 0
        for ref, number in zip(outs, counts):
            for to in range(number):
                source = pl.multiple_of(owners_ref[slot] * rows, 16)
                ref[pl.ds(to * rows, rows), :] = held_ref[pl.ds(source, rows), :]
                slot += 1

    inside = pl.BlockSpec(memory_space=pltpu.VMEM)
    return pl.pallas_call(
        kernel,
        out_shape=[jax.ShapeDtypeStruct((number * rows, width), BF) for number in counts],
        in_specs=[pl.BlockSpec(memory_space=pltpu.SMEM)] + [inside] * (2 * len(pairs)),
        out_specs=[inside] * len(counts),
        scratch_shapes=[pltpu.VMEM((height, width), BF)],
        compiler_params=pltpu.CompilerParams(vmem_limit_bytes=VMEM_BYTES),
        cost_estimate=SMALL,
        name="outer",
    )(owners, *[x for pair in pairs for x in pair])


def after(values, deps):
    if not deps:
        return values
    return lax.optimization_barrier((tuple(values), deps))[0]


def ring_total(block, sent, core):
    x, at = block
    rows, width = sent[0].shape
    tile, half = 768, rows // 2

    def kernel(core_ref, own_ref, r_ref, l_ref, mine_ref, away_ref, total_ref):
        total_ref[...] = (
            own_ref[...].astype(F32) + r_ref[...].astype(F32) + l_ref[...].astype(F32)
        )
        begin = pl.multiple_of(core_ref[0] * half, 8)
        mine_ref[...] = total_ref[pl.ds(begin, half), :]
        away_ref[...] = total_ref[pl.ds(half - begin, half), :]

    def block_of(number, at):
        return pl.BlockSpec((number, tile), lambda i: (at, i))

    return pl.pallas_call(
        kernel,
        out_shape=[jax.ShapeDtypeStruct((half, width), F32)] * 2,
        in_specs=[pl.BlockSpec(memory_space=pltpu.SMEM), block_of(rows, at)]
        + [block_of(rows, 0)] * 2,
        out_specs=[block_of(half, 0)] * 2,
        scratch_shapes=[pltpu.VMEM((rows, tile), F32)],
        compiler_params=pltpu.CompilerParams(vmem_limit_bytes=VMEM_BYTES),
        cost_estimate=SMALL,
        grid=(width // tile,),
        name="ring_total",
    )(core[None], x, *sent)


def combine(mine, got, core):
    rows, width = mine.shape
    split = width // 2 // EXPERTS

    def kernel(core_ref, mine_ref, got_ref, *outs):
        for k, ref in enumerate((mine_ref, got_ref)):
            first = (1 - core_ref[0]) if k else core_ref[0]
            at = pl.ds(pl.multiple_of(first * split, 128), split)
            for i, out_ref in enumerate(outs):
                for e in range(EXPERTS):
                    out_ref[:, e, at] = ref[:, pl.ds((i * EXPERTS + e) * split, split)]

    inside = pl.BlockSpec(memory_space=pltpu.VMEM)
    return pl.pallas_call(
        kernel,
        out_shape=[jax.ShapeDtypeStruct((rows, EXPERTS, 2 * split), F32)] * 2,
        in_specs=[pl.BlockSpec(memory_space=pltpu.SMEM)] + [inside] * 2,
        out_specs=[inside] * 2,
        compiler_params=pltpu.CompilerParams(vmem_limit_bytes=VMEM_BYTES),
        cost_estimate=SMALL,
        name="combine",
    )(core[None], mine, got)


def place_pieces(ins, owners_ref, outs, sems, rows):
    copies = []
    wide = outs[0].shape[1]
    for i, ref in enumerate(ins):
        target = pl.ds(pl.multiple_of(owners_ref[i] * rows, 16), rows)
        shift = wide if i > 0 and ref.shape[1] < ins[0].shape[1] and i == len(ins) - 1 else 0
        for begin in range(0, ref.shape[1], wide):
            to = outs[(begin + shift) // wide].at[target]
            source = ref if ref.shape[1] == wide else ref.at[:, pl.ds(begin, wide)]
            copies.append(pltpu.make_async_copy(source, to, sems.at[len(copies)]))
    return copies


def assemble(pieces, owners):
    rows, width = pieces[0].shape
    number = len(pieces)

    def kernel(owners_ref, *refs):
        copies = place_pieces(
            refs[:number], owners_ref, refs[number : number + 1], refs[number + 1], rows
        )
        for copy in copies:
            copy.start()
        for copy in copies:
            copy.wait()

    return pl.pallas_call(
        kernel,
        out_shape=jax.ShapeDtypeStruct((number * rows, width), BF),
        in_specs=[pl.BlockSpec(memory_space=pltpu.SMEM)]
        + [pl.BlockSpec(memory_space=pl.ANY)] * number,
        out_specs=pl.BlockSpec(memory_space=pltpu.VMEM),
        scratch_shapes=[pltpu.SemaphoreType.DMA((number,))],
        compiler_params=pltpu.CompilerParams(vmem_limit_bytes=VMEM_BYTES),
        cost_estimate=SMALL,
        name="assemble",
    )(owners, *pieces)


def gelu_and_slope(v):
    c = 0.7978845608028654
    t = jnp.tanh(c * (v + 0.044715 * (v * v * v)))
    slope = 0.5 * (1.0 + t) + 0.5 * v * (1.0 - t * t) * c * (1.0 + 3 * 0.044715 * (v * v))
    return 0.5 * v * (1.0 + t), slope


def expert_rows(own_ref, got_ref, e, begin, width):
    at = (pl.ds(e * CAP, CAP), pl.ds(begin, width))
    return jnp.concatenate([own_ref[at], got_ref[at]], axis=0)


def expert_layers(own, got, pieces, owners, slots, rows_out):
    filled, d = own.shape[0], own.shape[1] // 2
    rows, width = pieces[0].shape
    count = len(pieces)
    number = count - (pieces[-1].shape[1] < width)
    units = width // 2 // EXPERTS
    chips = slots.shape[0]

    def kernel(owners_ref, slots_ref, own_ref, got_ref, *refs):
        ins, mine_ref, away_ref = refs[:count], refs[count], refs[count + 1]
        outs = refs[count + 2 : count + 2 + chips]
        in_ref, down_ref, held_ref, sems, out_sems = refs[count + 2 + chips :]
        copies = place_pieces(ins, owners_ref, (in_ref, down_ref), sems, rows)
        for copy in copies:
            copy.start()
        for copy in copies:
            copy.wait()
        for e in range(EXPERTS):
            cols = pl.ds(e * units, units)
            w_i, w_d = in_ref[:, cols], down_ref[:, cols]
            x, g = (expert_rows(own_ref, got_ref, e, k * d, d) for k in range(2))
            active, slope = gelu_and_slope(dot32(x, w_i, NN))
            active = active.astype(BF)
            grad_pre = (dot32(g, w_d, NN) * slope).astype(BF)
            back = dot32(active, w_d, NT).astype(BF)
            sent = dot32(grad_pre, w_i, NT).astype(BF)
            for k, ref in enumerate((mine_ref, away_ref)):
                ref[pl.ds(e * CAP, CAP), pl.ds(0, d)] = back[k * CAP : (k + 1) * CAP]
                ref[pl.ds(e * CAP, CAP), pl.ds(d, d)] = sent[k * CAP : (k + 1) * CAP]
            held_ref[:, pl.ds(e * units, units)] = dot32(x, grad_pre, TN).astype(BF)
            held_ref[:, pl.ds((EXPERTS + e) * units, units)] = dot32(g, active, TN).astype(BF)
        copies = []
        for slot in range(chips):
            begin = pl.multiple_of(slots_ref[slot] * rows_out, 16)
            source = held_ref.at[pl.ds(begin, rows_out)]
            copies.append(pltpu.make_async_copy(source, outs[slot], out_sems.at[slot]))
        for copy in copies:
            copy.start()
        for copy in copies:
            copy.wait()

    inside = pl.BlockSpec(memory_space=pltpu.VMEM)
    anywhere = pl.BlockSpec(memory_space=pl.ANY)
    scalars = pl.BlockSpec(memory_space=pltpu.SMEM)
    mine, away, *terms = pl.pallas_call(
        kernel,
        out_shape=[jax.ShapeDtypeStruct((filled, 2 * d), BF)] * 2
        + [jax.ShapeDtypeStruct((rows_out, width), BF)] * chips,
        in_specs=[scalars, scalars, inside, inside] + [anywhere] * count,
        out_specs=[inside, inside] + [anywhere] * chips,
        scratch_shapes=[pltpu.VMEM((number * rows, width // 2), BF)] * 2
        + [
            pltpu.VMEM((d, width), BF),
            pltpu.SemaphoreType.DMA((2 * number,)),
            pltpu.SemaphoreType.DMA((chips,)),
        ],
        compiler_params=pltpu.CompilerParams(vmem_limit_bytes=EXPERT_VMEM_BYTES),
        cost_estimate=SMALL,
        name="expert_layers",
    )(owners, slots, own, got, *pieces)
    return mine, away, terms


def interleave(own, other, core, rows):
    chips, width = own.shape[0] // rows, own.shape[1]

    def kernel(core_ref, own_ref, other_ref, out_ref):
        for k, ref in enumerate((own_ref, other_ref)):
            first = (1 - core_ref[0]) if k else core_ref[0]
            for chip in range(chips):
                target = pl.multiple_of((2 * chip + first) * rows, 16)
                out_ref[pl.ds(target, rows), :] = ref[pl.ds(chip * rows, rows), :]

    inside = pl.BlockSpec(memory_space=pltpu.VMEM)
    return pl.pallas_call(
        kernel,
        out_shape=jax.ShapeDtypeStruct((2 * chips * rows, width), BF),
        in_specs=[pl.BlockSpec(memory_space=pltpu.SMEM), inside, inside],
        out_specs=inside,
        compiler_params=pltpu.CompilerParams(vmem_limit_bytes=VMEM_BYTES),
        cost_estimate=SMALL,
        name="interleave",
    )(core[None], own, other)


def swap_tensor(x):
    return lax.ppermute(x, "tensor", [(0, 1), (1, 0)])


def whole_rows(own, other, rank):
    return jnp.where(
        rank == 0, jnp.concatenate([own, other], axis=0), jnp.concatenate([other, own], axis=0)
    )


def sum_chips(x):
    step = 2
    while step < lax.axis_size("dp"):
        x = x + lax.ppermute(x, "dp", [(i, i ^ step) for i in range(lax.axis_size("dp"))])
        step *= 2
    return x


def rms_scale(rows):
    return lax.rsqrt(jnp.mean(rows * rows, axis=-1, keepdims=True) + EPS)


def norm_back(grad, normed, scale, gain):
    weighted = grad * gain
    return scale * (weighted - normed * jnp.mean(weighted * normed, axis=-1, keepdims=True))


def dot32(a, b, dims):
    return lax.dot_general(a, b, (dims, ((), ())), preferred_element_type=F32)


NN = ((1,), (0,))
NT = ((1,), (1,))
TN = ((0,), (0,))


def attention_forward(x, gain, weights, by_offset, seq_col, seq_row):
    count, d = x.shape
    head_cols = weights.shape[1] // 4
    heads = head_cols // HEAD_DIM
    scale = HEAD_DIM ** (-0.5)
    lanes = by_offset.shape[1]

    def kernel(x_ref, gain_ref, w_ref, off_ref, col_ref, row_ref, *outs):
        normed_ref, scale_ref, proj_ref, p_ref, context_ref, part_ref = outs
        rows = x_ref[...].astype(F32)
        r = lax.rsqrt(jnp.mean(rows * rows, axis=-1, keepdims=True) + EPS)
        scale_ref[...] = r
        normed = (rows * r * gain_ref[...]).astype(BF)
        normed_ref[...] = normed
        for s in range(3):
            at = pl.ds(s * head_cols, head_cols)
            proj_ref[:, at] = dot32(normed, w_ref[:, at], NN).astype(BF)
        same = col_ref[...] == row_ref[...]
        for h in range(heads):
            q = proj_ref[:, pl.ds(h * HEAD_DIM, HEAD_DIM)]
            k = proj_ref[:, pl.ds(head_cols + h * HEAD_DIM, HEAD_DIM)]
            v = proj_ref[:, pl.ds(2 * head_cols + h * HEAD_DIM, HEAD_DIM)]
            line = jnp.broadcast_to(off_ref[pl.ds(h, 1), :], (count, lanes))
            bias = pltpu.roll(line, lanes - (count - 1), 1, stride=1, stride_axis=0)[:, :count]
            scores = jnp.where(same, dot32(q, k, NT) * scale + bias, NEG)
            expo = jnp.exp(scores - jnp.max(scores, axis=-1, keepdims=True))
            p = expo / jnp.sum(expo, axis=-1, keepdims=True)
            p_ref[h] = p
            context_ref[:, pl.ds(h * HEAD_DIM, HEAD_DIM)] = dot32(p.astype(BF), v, NN).astype(BF)
        out_w = w_ref[:, pl.ds(3 * head_cols, head_cols)]
        part_ref[...] = dot32(context_ref[...], out_w, NT).astype(BF)

    inside = pl.BlockSpec(memory_space=pltpu.VMEM)
    return pl.pallas_call(
        kernel,
        out_shape=(
            jax.ShapeDtypeStruct((count, d), BF),
            jax.ShapeDtypeStruct((count, 1), F32),
            jax.ShapeDtypeStruct((count, 3 * head_cols), BF),
            jax.ShapeDtypeStruct((heads, count, count), F32),
            jax.ShapeDtypeStruct((count, head_cols), BF),
            jax.ShapeDtypeStruct((count, d), BF),
        ),
        in_specs=[inside] * 6,
        out_specs=(inside,) * 6,
        compiler_params=pltpu.CompilerParams(vmem_limit_bytes=VMEM_BYTES),
        cost_estimate=SMALL,
        name="attention_forward",
    )(x, gain, weights, by_offset, seq_col, seq_row)


def attention_backward(low, other, hidden, scales, gain, out_grad, weights, proj, p_full, lanes):
    count, d = low.shape
    head_cols = weights.shape[1] // 4
    heads = head_cols // HEAD_DIM
    scale = HEAD_DIM ** (-0.5)

    def kernel(low_ref, other_ref, hidden_ref, scales_ref, gain_ref, g_ref, w_ref, proj_ref, p_ref,
               hidden_grad_ref, grad_ref, out_ref, sums_ref, gc_ref):
        r2 = scales_ref[:, 3:4]
        n = hidden_ref[...] * r2
        u = (low_ref[...].astype(F32) + other_ref[...].astype(F32)) * gain_ref[...]
        total = g_ref[...].astype(F32) + r2 * (u - n * jnp.mean(u * n, axis=-1, keepdims=True))
        hidden_grad_ref[...] = total
        grad_ref[...] = total.astype(BF)
        out_w = w_ref[:, pl.ds(3 * head_cols, head_cols)]
        gc_ref[...] = dot32(grad_ref[...], out_w, NN).astype(BF)
        down = lax.broadcasted_iota(jnp.int32, (count, count), 0)
        across = lax.broadcasted_iota(jnp.int32, (count, count), 1)
        flip = (down + across == count - 1).astype(F32).astype(BF)
        for h in range(heads):
            at = [pl.ds(s * head_cols + h * HEAD_DIM, HEAD_DIM) for s in range(3)]
            q, k, v = proj_ref[:, at[0]], proj_ref[:, at[1]], proj_ref[:, at[2]]
            p = p_ref[h]
            gc = gc_ref[:, at[0]]
            dp = dot32(gc, v, NT)
            ds = (p * (dp - jnp.sum(p * dp, axis=-1, keepdims=True))).astype(BF)
            out_ref[:, at[0]] = (dot32(ds, k, NN) * scale).astype(BF)
            out_ref[:, at[1]] = (dot32(ds, q, TN) * scale).astype(BF)
            out_ref[:, at[2]] = dot32(p.astype(BF), gc, TN).astype(BF)
            turned = dot32(ds, flip, TN)
            wide = jnp.concatenate([turned, jnp.zeros((count, lanes - count), F32)], axis=1)
            rolled = pltpu.roll(wide, 0, 1, stride=1, stride_axis=0)
            sums_ref[pl.ds(h, 1), :] = jnp.sum(rolled, axis=0, keepdims=True)

    inside = pl.BlockSpec(memory_space=pltpu.VMEM)
    return pl.pallas_call(
        kernel,
        out_shape=(
            jax.ShapeDtypeStruct((count, d), F32),
            jax.ShapeDtypeStruct((count, d), BF),
            jax.ShapeDtypeStruct((count, 3 * head_cols), BF),
            jax.ShapeDtypeStruct((heads, lanes), F32),
        ),
        in_specs=[inside] * 9,
        out_specs=(inside,) * 4,
        scratch_shapes=[pltpu.VMEM((count, head_cols), BF)],
        compiler_params=pltpu.CompilerParams(vmem_limit_bytes=VMEM_BYTES),
        cost_estimate=SMALL,
        name="attention_backward",
    )(low, other, hidden, scales, gain, out_grad, weights, proj, p_full)


def route(x, part, other, gain, w_router, expert_col, flat, out_grad):
    count, d = x.shape

    def kernel(x_ref, part_ref, other_ref, gain_ref, w_ref, expert_ref, flat_ref, g_ref,
               hidden_ref, blocks_ref, scales_ref):
        hidden = x_ref[...].astype(F32) + (part_ref[...].astype(F32) + other_ref[...].astype(F32))
        hidden_ref[...] = hidden
        r2 = lax.rsqrt(jnp.mean(hidden * hidden, axis=-1, keepdims=True) + EPS)
        mixed = hidden * r2 * gain_ref[...]
        logits = [
            jnp.sum(mixed * w_ref[e : e + 1, :], axis=-1, keepdims=True) for e in range(EXPERTS)
        ]
        top = jnp.maximum(logits[0], logits[1])
        expo = [jnp.exp(v - top) for v in logits]
        probs = [v / (expo[0] + expo[1]) for v in expo]
        hits = [(expert_ref[...] == e).astype(F32) for e in range(EXPERTS)]
        gate = probs[0] * hits[0] + probs[1] * hits[1]
        lane = lax.broadcasted_iota(jnp.int32, (count, 128), 1)
        columns = [gate] + [gate * (h - p) for h, p in zip(hits, probs)] + [r2]
        scales_ref[...] = sum(jnp.where(lane == i, v, 0.0) for i, v in enumerate(columns))
        slots = lax.broadcasted_iota(jnp.int32, (EXPERTS * CAP, count), 0)
        chosen = (slots == flat_ref[...]).astype(F32).astype(BF)
        blocks_ref[:, pl.ds(0, d)] = dot32(chosen, mixed.astype(BF), NN).astype(BF)
        grad_routed = (gate * g_ref[...].astype(F32)).astype(BF)
        blocks_ref[:, pl.ds(d, d)] = dot32(chosen, grad_routed, NN).astype(BF)

    inside = pl.BlockSpec(memory_space=pltpu.VMEM)
    return pl.pallas_call(
        kernel,
        out_shape=(
            jax.ShapeDtypeStruct((count, d), F32),
            jax.ShapeDtypeStruct((EXPERTS * CAP, 2 * d), BF),
            jax.ShapeDtypeStruct((count, 128), F32),
        ),
        in_specs=[inside] * 8,
        out_specs=(inside,) * 3,
        compiler_params=pltpu.CompilerParams(vmem_limit_bytes=VMEM_BYTES),
        cost_estimate=SMALL,
        name="route",
    )(x, part, other, gain, w_router, expert_col, flat, out_grad)


def rows_back(mine, got, hidden, scales, gain, w_router, flat, out_grad):
    count, d = hidden.shape

    def kernel(mine_ref, got_ref, hidden_ref, scales_ref, gain_ref, w_ref, flat_ref, g_ref,
               mixed_ref, routed_ref, gains_ref):
        sums = (mine_ref[...].astype(F32) + got_ref[...].astype(F32)).astype(BF)
        slots = lax.broadcasted_iota(jnp.int32, (count, EXPERTS * CAP), 1)
        chosen = (slots == flat_ref[...]).astype(F32).astype(BF)
        routed = dot32(chosen, sums[:, :d], NN)
        gate, r2 = scales_ref[:, 0:1], scales_ref[:, 3:4]
        routed_ref[...] = (gate * routed).astype(BF)
        gate_part = jnp.sum(g_ref[...].astype(F32) * routed, axis=-1, keepdims=True)
        grad_logits = [gate_part * scales_ref[:, 1 + e : 2 + e] for e in range(EXPERTS)]
        part = dot32(chosen, sums[:, d:], NN)
        part = part + sum(grad_logits[e] * w_ref[e : e + 1, :] for e in range(EXPERTS))
        mixed_ref[...] = part.astype(BF)
        n = hidden_ref[...] * r2
        gains_ref[0:1, :] = jnp.sum(part * n, axis=0, keepdims=True)
        mixed = n * gain_ref[...]
        for e in range(EXPERTS):
            gains_ref[1 + e : 2 + e, :] = jnp.sum(mixed * grad_logits[e], axis=0, keepdims=True)
        gains_ref[1 + EXPERTS :, :] = jnp.zeros((7 - EXPERTS, d), F32)

    inside = pl.BlockSpec(memory_space=pltpu.VMEM)
    return pl.pallas_call(
        kernel,
        out_shape=(
            jax.ShapeDtypeStruct((count, d), BF),
            jax.ShapeDtypeStruct((count, d), BF),
            jax.ShapeDtypeStruct((8, d), F32),
        ),
        in_specs=[inside] * 8,
        out_specs=(inside,) * 3,
        compiler_params=pltpu.CompilerParams(vmem_limit_bytes=VMEM_BYTES),
        cost_estimate=SMALL,
        name="rows_back",
    )(mine, got, hidden, scales, gain, w_router, flat, out_grad)


def input_back(grad, weights, x, sums, bucket_hits, gains, rank):
    count, d = x.shape
    heads, lanes = sums.shape
    buckets = bucket_hits.shape[1]
    each = d // 128

    def kernel(rank_ref, grad_ref, w_ref, x_ref, sums_ref, hits_ref, gains_ref, low_ref, line_ref):
        part = dot32(grad_ref[...], w_ref[:, pl.ds(0, grad_ref.shape[1])], NT)
        low_ref[...] = part.astype(BF)
        rows = x_ref[...].astype(F32)
        n = rows * lax.rsqrt(jnp.mean(rows * rows, axis=-1, keepdims=True) + EPS)
        vectors = [jnp.sum(part * n, axis=0, keepdims=True)]
        vectors += [gains_ref[k : k + 1, :] for k in range(1 + EXPERTS)]
        for k, vector in enumerate(vectors):
            for j in range(each):
                line_ref[pl.ds(16 + k * each + j, 1), :] = vector[:, j * 128 : (j + 1) * 128]
        rel = jnp.dot(sums_ref[...], hits_ref[...], precision=HIGH, preferred_element_type=F32)
        rel = jnp.concatenate([rel, jnp.zeros((heads, 128 - buckets), F32)], axis=1)
        line_ref[0:16, :] = jnp.zeros((16, 128), F32)
        for k in range(2):
            line_ref[pl.ds(k * heads, heads), :] = jnp.where(rank_ref[0] == k, rel, 0.0)

    inside = pl.BlockSpec(memory_space=pltpu.VMEM)
    return pl.pallas_call(
        kernel,
        out_shape=(
            jax.ShapeDtypeStruct((count, d), BF),
            jax.ShapeDtypeStruct((16 + (2 + EXPERTS) * each, 128), F32),
        ),
        in_specs=[pl.BlockSpec(memory_space=pltpu.SMEM)] + [inside] * 6,
        out_specs=(inside,) * 2,
        compiler_params=pltpu.CompilerParams(vmem_limit_bytes=VMEM_BYTES),
        cost_estimate=SMALL,
        name="input_back",
    )(rank[None], grad, weights, x, sums, bucket_hits, gains)


def body(
    block_in,
    attn_gain,
    w_qkv,
    w_out,
    rel_bias,
    moe_gain,
    w_router,
    w_in,
    w_down,
    seq_lengths,
    expert_ids,
    rel_table,
    out_grad,
):
    rows_local, width = block_in.shape
    rank = lax.axis_index("tensor")
    ring = Ring()
    shard = w_out.shape[0]
    head_cols = w_out.shape[1]
    units = w_in.shape[2]
    heads_local = head_cols // HEAD_DIM
    count = 2 * rows_local

    attn_shard = jnp.concatenate([w_qkv.reshape(shard, 3 * head_cols), w_out], axis=1)
    x_other, g_other = swap_tensor(block_in), swap_tensor(out_grad)
    split = units // 2

    def unit_half(w, core):
        return lax.dynamic_slice_in_dim(w, core * split, split, axis=2)

    if not ring.long:
        ring_a = Gather(ring, attn_shard, False)
        a1 = ring_a.step()
        own_half, other_half = (
            jnp.concatenate(
                [unit_half(w, core).reshape(shard, EXPERTS * split) for w in (w_in, w_down)],
                axis=1,
            )
            for core in (ring.core, 1 - ring.core)
        )
        got_half = ring.other_core(other_half)
        a2 = ring_a.step()
        ring_b = Gather(ring, ring.by_core(own_half, got_half, 0), True)
        a3 = ring_a.step()
        a4 = ring_a.step()
        ring_b.step(*a3, x_other, g_other)
        own_a = assemble(ring_a.pieces, ring_a.owners())
        other_a = ring.other_core(own_a)
        attn_all = interleave(own_a, other_a, ring.core, shard)
    else:
        attn_all = lax.all_gather(attn_shard, "dp", axis=0, tiled=True)
        in_all, down_all = (
            unit_half(lax.all_gather(w, "dp", axis=0, tiled=True), ring.core).reshape(
                -1, EXPERTS * split
            )
            for w in (w_in, w_down)
        )
    x_low = whole_rows(block_in, x_other, rank)
    g_low = whole_rows(out_grad, g_other, rank)

    places = jnp.arange(count, dtype=jnp.int32)
    ends = jnp.cumsum(seq_lengths[0])
    seq_ids = jnp.sum((places[:, None] >= ends[None, :]).astype(jnp.int32), axis=1)
    bias_local = lax.dynamic_slice_in_dim(rel_bias, rank * heads_local, heads_local, 1)
    bucket_hits = (
        rel_table[:, None] == jnp.arange(rel_bias.shape[0], dtype=jnp.int32)[None, :]
    ).astype(F32)
    by_offset = jnp.dot(bucket_hits, bias_local, precision=HIGH)
    lanes = 2 * count
    by_offset = jnp.pad(by_offset.T, ((0, 0), (0, lanes - by_offset.shape[0])))
    normed_one, _, projected, p_full, context, attn_part = attention_forward(
        x_low, attn_gain[None, :], attn_all, by_offset, seq_ids[:, None], seq_ids[None, :]
    )
    if not ring.long:
        ring_b.step(other_a)
        ring_b.step(attn_part)
    attn_other = swap_tensor(attn_part)
    expert_col = expert_ids[:, 0]
    hits = (
        expert_col[:, None] == jnp.arange(EXPERTS, dtype=jnp.int32)[None, :]
    ).astype(jnp.int32)
    flat = expert_col * CAP + jnp.sum(jnp.cumsum(hits, axis=0) * hits, axis=1) - 1
    gain_row, router_rows = moe_gain[None, :], w_router.T
    hidden, own_blocks, scales = route(
        x_low, attn_part, attn_other, gain_row, router_rows, expert_ids, flat[None, :], g_low
    )
    if not ring.long:
        got_blocks = ring.other_core(own_blocks)
        ring_b.step(got_blocks)
        mine, away, terms = expert_layers(
            own_blocks, got_blocks, ring_b.pieces, ring_b.owners(), ring.slot_chips(), 2 * shard
        )
        send = Scatter(ring, terms, 2 * shard)
        c1 = send.step()
    else:
        whole = jnp.concatenate([in_all, down_all], axis=1)
        first = jnp.zeros((1,), jnp.int32)
        mine, away, terms = expert_layers(
            own_blocks, ring.other_core(own_blocks), [whole], first, first, width
        )
    got_sums = ring.other_core(away)
    mixed_low, routed_low, gains = rows_back(
        mine, got_sums, hidden, scales, gain_row, router_rows, flat[:, None], g_low
    )
    if not ring.long:
        c2 = send.step(mixed_low)
    mixed_other = swap_tensor(mixed_low)
    if not ring.long:
        (mixed_other,) = after((mixed_other,), c1)

    def own_rows(x):
        return lax.dynamic_slice_in_dim(x, rank * rows_local, rows_local, 0)

    def other_rows(x):
        return lax.dynamic_slice_in_dim(x, (1 - rank) * rows_local, rows_local, 0)

    routed_other = swap_tensor(other_rows(routed_low))
    result = own_rows(hidden) + (
        own_rows(routed_low).astype(F32) + routed_other.astype(F32)
    )
    grad_hidden, grad_attended, grad_projected, offset_sums = attention_backward(
        mixed_low, mixed_other, hidden, scales, gain_row, g_low, attn_all, projected, p_full, lanes
    )

    attn_pairs = [(normed_one, grad_projected), (grad_attended, context)]
    if not ring.long:
        attn_pairs[0] = (normed_one, after((grad_projected,), c2)[0])
        chips = ring.slot_chips()
        owners = jnp.concatenate([chips * 2 + ring.core, chips * 2 + 1 - ring.core])
        send_a = Scatter(ring, outer(attn_pairs, owners, shard, [ring.chips] * 2), shard)
        c3 = send.step()
        a1 = send_a.step()
    hits_wide = jnp.pad(bucket_hits, ((0, lanes - bucket_hits.shape[0]), (0, 0)))
    normed_low, line = input_back(
        grad_projected, attn_all, x_low, offset_sums, hits_wide, gains, rank
    )
    normed_other = swap_tensor(other_rows(normed_low))
    line = line + swap_tensor(line)
    line = line + ring.other_core(line)
    if not ring.long:
        c4 = send.step(line, *a1)
        a2 = send_a.step(*c3)
        (line,) = after((line,), c4 + a2)
        send_a.step(*c4)
        send_a.step()
    summed = sum_chips(line)
    grad_normed = own_rows(normed_low).astype(F32) + normed_other.astype(F32)
    x_own = block_in.astype(F32)
    scale_own = rms_scale(x_own)
    grad_block = own_rows(grad_hidden) + norm_back(
        grad_normed, x_own * scale_own, scale_own, attn_gain
    )
    if ring.long:
        zeros = jnp.zeros((width, 2 * EXPERTS, units), BF)
        terms = terms[0].reshape(width, 2 * EXPERTS, split)
        terms = lax.dynamic_update_slice_in_dim(zeros, terms, ring.core * split, 2)
        sums = lax.psum_scatter(terms, "dp", scatter_dimension=0, tiled=True).astype(F32)
        grad_w_in_mine, grad_w_down_mine = sums[:, :EXPERTS], sums[:, EXPERTS:]
        terms = jnp.concatenate([dot32(x, y, TN).astype(BF) for x, y in attn_pairs], axis=1)
        attn_mine = lax.psum_scatter(terms, "dp", scatter_dimension=0, tiled=True)
        attn_mine = attn_mine.astype(F32)
    else:
        mine, away = ring_total(send.blocks(0)[0], send.sent, ring.core)
        grad_w_in_mine, grad_w_down_mine = combine(mine, ring.other_core(away), ring.core)
        attn_mine = send_a.total()
    summed_rel = summed[: rel_bias.shape[1], : rel_bias.shape[0]].T
    summed = summed[16:].reshape(2 + EXPERTS, width)
    return (
        result.astype(BF),
        grad_block,
        summed[0],
        attn_mine[:, : 3 * head_cols].reshape(w_qkv.shape),
        attn_mine[:, 3 * head_cols :],
        summed_rel,
        summed[1],
        summed[2:].T,
        grad_w_in_mine,
        grad_w_down_mine,
    )


def solution(mesh):
    placed = (
        P(("dp", "tensor"), None),
        P(),
        P("dp", None, "tensor"),
        P("dp", "tensor"),
        P(),
        P(),
        P(),
        P("dp", None, "tensor"),
        P("dp", None, "tensor"),
        P("dp", None),
        P("dp", None),
        P(),
        P(("dp", "tensor"), None),
    )
    return jax.shard_map(
        body,
        mesh=mesh,
        in_specs=placed,
        out_specs=(
            P(("dp", "tensor"), None),
            P(("dp", "tensor"), None),
            P(),
            P("dp", None, "tensor"),
            P("dp", "tensor"),
            P(),
            P(),
            P(),
            P("dp", None, "tensor"),
            P("dp", None, "tensor"),
        ),
        check_vma=False,
    )
```

time: 228 us -> 215 us (0.943)
  other arithmetic: 32 us -> 9.95 us
  starting transfers between devices: 63.1 us -> 45 us
  Pallas kernels: 19.8 us -> 37.2 us
  waiting for transfers between devices: 70.8 us -> 86.5 us
  matrix products: 11.2 us -> 0.31 us
  local copies, waits for them, and re-layouts: 28.2 us -> 33.7 us
    pallas_call x1 -> x15, Pallas kernels: 3.92 us -> 29.6 us  [the longest x1 9.87 us: expert_layers(): pl.pallas_call(kernel, out_shape=[jax.ShapeDtypeStruct((filled, 2 * d), B...]
    convert_element_type x14 -> x1, other arithmetic: 16.6 us -> 0.01 us  [body(): hits = (expert_col[:, None] == jnp.arange(EXPERTS, dtype=jnp.int32)[None,...]
    ppermute x7, waiting for transfers between devices: 6.57 us -> 21.8 us  [swap_tensor(): return lax.ppermute(x, 'tensor', [(0, 1), (1, 0)])]
    ppermute x18 -> x14, waiting for transfers between devices: 25.8 us -> 39.9 us  [step(): lax.ppermute(r, 'dp', ring.right)]
    dot_general x14 -> x0, matrix products: 10.9 us -> none  [the longest x13 10.6 us: dot32(): return lax.dot_general(a, b, (dims, ((), ())), preferred_element_type=F32)]
    unnamed x163 -> x113, local copies, waits for them, and re-layouts: 14.5 us -> 23 us
    ppermute x18 -> x14, waiting for transfers between devices: 19.3 us -> 11.8 us  [step(): lax.ppermute(l, 'dp', ring.left)]
    ppermute x10 -> x5, waiting for transfers between devices: 17.9 us -> 11.8 us  [the longest x3 5.32 us: sum_chips(): lax.ppermute(x, 'dp', [(i, i ^ step) for i in range(lax.axis_size('dp'))])]
  transfers between devices with their start and end apart: 64 -> 48, of which waited for: 27 -> 31; matrix products, arithmetic and copies ran while one was open for 22% -> 9% of each run, Pallas kernels for 5% -> 10%
where the time goes in v4:
time: 215 us; the launch traced here: 214 us
  waiting for transfers between devices  86.5 us (40%)
  starting transfers between devices  45 us (21%)
  Pallas kernels  37.2 us (17%)
  local copies, waits for them, and re-layouts  33.7 us (16%)
  other arithmetic  9.95 us (5%)
    ppermute x14, waiting for transfers between devices, step(): lax.ppermute(r, 'dp', ring.right)  39.9 us
    unnamed x113, local copies, waits for them, and re-layouts  23 us
    ppermute x7, waiting for transfers between devices, swap_tensor(): return lax.ppermute(x, 'tensor', [(0, 1), (1, 0)])  21.8 us
    ppermute x14, starting transfers between devices, step(): lax.ppermute(r, 'dp', ring.right)  19.1 us
    ppermute x14, waiting for transfers between devices, step(): lax.ppermute(l, 'dp', ring.left)  11.8 us
    ppermute x14, starting transfers between devices, step(): lax.ppermute(l, 'dp', ring.left)  10.8 us
    pallas_call x1, Pallas kernels, expert_layers(): pl.pallas_call(kernel, out_shape=[jax.ShapeDtypeStruct((filled, 2 * d), B...  9.87 us
    ppermute x7, starting transfers between devices, swap_tensor(): return lax.ppermute(x, 'tensor', [(0, 1), (1, 0)])  7.93 us
  transfers between devices with their start and end apart: 48, of which 31 were waited for; matrix products, arithmetic and copies ran while one was open for 9% of the time, Pallas kernels for 10%

profile of v4, /device:TPU:0, one launch (start us, length us, event | category | flops | bytes accessed | tf_op | source)
XLA Modules:
  0.0 213.9 jit_solution(9432016948141478898)
XLA Ops:
  2.4 3.0 %collective-permute-start.1 = (bf16[48,1536]{1,0:T(8,128)(2,1)S(1)}, bf16[48,1536]{1,0:T(8,128)(2,1)S(1)}, u32[]{:S(2)}, u32[]{:S(2)}) collective-permute-start(bf16[48,1536]{1,0:T(8,128)(2,1)S(1)} %constant_dynamic-update-slice_fusion.refs_0_), channel_id=1, source_target_pairs={{0,8},{2,10},{8,16},{10,18},{16,24},{18,26},{24,28},{26,30},{28,20... | collective-permute-start | bytes 442376 | tf_op jit(solution)/shard_map/ppermute | solution.py:85
  5.4 1.6 constant_dynamic-slice_fusion.4
  7.0 2.1 collective-permute-done.1.refs_1_
  9.2 1.8 collective-permute-start.3
  11.1 1.6 collective-permute-start
  14.3 1.8 collective-permute-start.5
  17.2 1.6 collective-permute-done.4.refs_4_
  19.4 1.8 collective-permute-start.7
  21.6 2.4 %collective-permute-done.6.refs_6_ = bf16[48,1536]{1,0:T(8,128)(2,1)S(1)} collective-permute-done((bf16[48,1536]{1,0:T(8,128)(2,1)S(1)}, bf16[48,1536]{1,0:T(8,128)(2,1)S(1)}, u32[]{:S(2)}, u32[]{:S(2)}) %collective-permute-start.6) | collective-permute-done | bytes 147488 | tf_op jit(solution)/shard_map/ppermute | solution.py:85
  24.6 2.3 %assemble.1.own_ref = bf16[384,1536]{1,0:T(8,128)(2,1)S(1)} custom-call(s32[8]{0:T(128)S(1)} %stack.30.owners_ref, bf16[48,1536]{1,0:T(8,128)(2,1)S(1)} %constant_dynamic-update-slice_fusion.refs_0_, bf16[48,1536]{1,0:T(8,128)(2,1)S(1)} %collective-permute-done.1.refs_1_, bf16[48,1536]{1,0:T(8,128)(2,1)S(1)} %collective-permute-done.2.refs_2_, ...), custom_call_target="tpu_custom_call" | custom-call | flops 1 | bytes 1 | tf_op jit(solution)/shard_map/assemble/pallas_call | solution.py:322
  27.4 1.2 maximum_select_fusion.refs_0_
  28.7 1.9 collective-permute-start.13
  32.5 1.3 maximum_select_fusion.1.x_ref
  34.9 1.3 copy-done.7
  36.2 1.3 copy-done.17
  38.3 3.5 %attention_forward.1 = (bf16[256,768]{1,0:T(8,128)(2,1)S(1)}, f32[256,1]{1,0:T(8,128)}, bf16[256,1152]{1,0:T(8,128)(2,1)S(1)}, f32[6,256,256]{2,1,0:T(8,128)S(1)...) custom-call(bf16[256,768]{1,0:T(8,128)(2,1)S(1)} %maximum_select_fusion.1.x_ref, ...), custom_call_target="tpu_custom_call" | custom-call | flops 1 | bytes 1 | tf_op jit(solution)/shard_map/attention_forward/pallas_call | solution.py:501
  44.1 1.8 collective-permute-start.9
  46.6 1.6 collective-permute-start.15
  48.6 1.3 maximum_select_fusion.2.g_ref
  50.0 5.2 %collective-permute-done.9.other_ref = bf16[256,768]{1,0:T(8,128)(2,1)S(1)} collective-permute-done((bf16[256,768]{1,0:T(8,128)(2,1)S(1)}, bf16[256,768]{1,0:T(8,128)(2,1)S(1)}, u32[]{:S(2)}, u32[]{:S(2)}) %collective-permute-start.9) | collective-permute-done | bytes 393248 | tf_op jit(solution)/shard_map/ppermute | solution.py:433
  58.0 3.7 %collective-permute-done.15.refs_3_ = bf16[96,3072]{1,0:T(8,128)(2,1)S(1)} collective-permute-done((bf16[96,3072]{1,0:T(8,128)(2,1)}, bf16[96,3072]{1,0:T(8,128)(2,1)S(1)}, u32[]{:S(2)}, u32[]{:S(2)}) %collective-permute-start.15) | collective-permute-done | bytes 589856 | tf_op jit(solution)/shard_map/ppermute | solution.py:85
  61.7 1.3 collective-permute-done.16.refs_4_
  63.0 1.6 collective-permute-start.17
  66.7 10.0 %collective-permute-done.17.refs_5_ = bf16[96,3072]{1,0:T(8,128)(2,1)S(1)} collective-permute-done((bf16[96,3072]{1,0:T(8,128)(2,1)S(1)}, bf16[96,3072]{1,0:T(8,128)(2,1)S(1)}, u32[]{:S(2)}, u32[]{:S(2)}) %collective-permute-start.17) | collective-permute-done | bytes 589856 | tf_op jit(solution)/shard_map/ppermute | solution.py:85
  76.7 2.1 collective-permute-done.18.refs_6_
  81.4 1.6 collective-permute-start.19
  84.3 4.1 %collective-permute-done.19.refs_7_ = bf16[96,1536]{1,0:T(8,128)(2,1)} collective-permute-done((bf16[96,1536]{1,0:T(8,128)(2,1)}, bf16[96,1536]{1,0:T(8,128)(2,1)}, u32[]{:S(2)}, u32[]{:S(2)}) %collective-permute-start.19) | collective-permute-done | bytes 294944 | tf_op jit(solution)/shard_map/ppermute | solution.py:88
  88.4 2.3 %collective-permute-done.20.refs_8_ = bf16[96,1536]{1,0:T(8,128)(2,1)} collective-permute-done((bf16[96,1536]{1,0:T(8,128)(2,1)}, bf16[96,1536]{1,0:T(8,128)(2,1)}, u32[]{:S(2)}, u32[]{:S(2)}) %collective-permute-start.20) | collective-permute-done | bytes 294944 | tf_op jit(solution)/shard_map/ppermute | solution.py:89
  90.8 1.1 copy-done.9
  94.0 1.2 copy-done.19
  95.2 1.2 copy-done.21
  98.6 9.9 %expert_layers.1 = (bf16[352,1536]{1,0:T(8,128)(2,1)S(1)}, bf16[352,1536]{1,0:T(8,128)(2,1)S(1)}, bf16[96,3072]{1,0:T(8,128)(2,1)S(1)}, bf16[96,3072]{1,0:T(8,12...) custom-call(s32[9]{0:T(128)S(1)} %stack.31.owners_ref, ...), custom_call_target="tpu_custom_call" | custom-call | flops 1 | bytes 1 | tf_op jit(solution)/shard_map/expert_layers/pallas_call | solution.py:391
  108.6 1.5 collective-permute-start.24
  111.3 1.1 rows_back.1
  113.2 4.9 %collective-permute-done.24.refs_1_ = bf16[96,1536]{1,0:T(8,128)(2,1)S(1)} collective-permute-done((bf16[96,1536]{1,0:T(8,128)(2,1)S(1)}, bf16[96,1536]{1,0:T(8,128)(2,1)S(1)}, u32[]{:S(2)}, u32[]{:S(2)}) %collective-permute-start.24) | collective-permute-done | bytes 294944 | tf_op jit(solution)/shard_map/ppermute | solution.py:124
  118.1 1.2 collective-permute-done.25.refs_3_
  120.4 1.4 collective-permute-start.30
  122.9 8.8 %collective-permute-done.23.other_ref = bf16[256,768]{1,0:T(8,128)(2,1)S(1)} collective-permute-done((bf16[256,768]{1,0:T(8,128)(2,1)S(1)}, bf16[256,768]{1,0:T(8,128)(2,1)S(1)}, u32[]{:S(2)}, u32[]{:S(2)}) %collective-permute-start.23) | collective-permute-done | bytes 393248 | tf_op jit(solution)/shard_map/ppermute | solution.py:433
  131.8 4.7 %attention_backward.1 = (f32[256,768]{1,0:T(8,128)S(1)}, bf16[256,768]{1,0:T(8,128)(2,1)S(1)}, bf16[256,1152]{1,0:T(8,128)(2,1)S(1)}, f32[6,512]{1,0:T(8,128)S(1)}) custom-call(bf16[256,768]{1,0:T(8,128)(2,1)S(1)} %get-tuple-element.93.low_ref, bf16[256,768]{1,0:T(8,128)(2,1)S(1)} %collective-permute-done.23.other_ref, f32[256,768]{1,0:T(8,128)S(1)} %copy-done.4, ...), custom_call_target="tpu_custom_call" | custom-call | flops 1 | bytes 1 | tf_op jit(solution)/shard_map/attention_backward/pallas_call | solution.py:554
  136.5 1.6 outer.1
  138.2 1.8 ring_add.7
  140.7 1.4 collective-permute-start.32
  144.2 2.8 %collective-permute-done.27 = f32[40,128]{1,0:T(8,128)S(1)} collective-permute-done((f32[40,128]{1,0:T(8,128)S(1)}, f32[40,128]{1,0:T(8,128)S(1)}, u32[]{:S(2)}, u32[]{:S(2)}) %collective-permute-start.27) | collective-permute-done | bytes 20512 | tf_op jit(solution)/shard_map/ppermute | solution.py:433
  147.7 1.4 collective-permute-start.35
  149.3 7.2 %collective-permute-done.31.refs_1_ = bf16[96,3072]{1,0:T(8,128)(2,1)} collective-permute-done((bf16[96,3072]{1,0:T(8,128)(2,1)}, bf16[96,3072]{1,0:T(8,128)(2,1)}, u32[]{:S(2)}, u32[]{:S(2)}) %collective-permute-start.31) | collective-permute-done | bytes 589856 | tf_op jit(solution)/shard_map/ppermute | solution.py:124
  157.9 1.1 copy-done.29
  160.0 3.6 %ring_add.8 = (bf16[96,3072]{1,0:T(8,128)(2,1)}, bf16[96,3072]{1,0:T(8,128)(2,1)}) custom-call(bf16[96,3072]{1,0:T(8,128)(2,1)S(1)} %copy-done.29, bf16[96,3072]{1,0:T(8,128)(2,1)} %collective-permute-done.31.refs_1_, bf16[96,3072]{1,0:T(8,128)(2,1)S(1)} %copy-done.31, bf16[96,3072]{1,0:T(8,128)(2,1)} %collective-permute-done.32.refs_3_), custom_call_target="tpu_custom_call" | custom-call | flops 1 | bytes 1 | tf_op jit(solution)/shard_map/ring_add/pallas_call | solution.py:187
  164.2 1.4 collective-permute-start.37
  167.3 1.1 collective-permute-start.26
  169.4 5.0 %collective-permute-done.22 = bf16[128,768]{1,0:T(8,128)(2,1)} collective-permute-done((bf16[128,768]{1,0:T(8,128)(2,1)}, bf16[128,768]{1,0:T(8,128)(2,1)}, u32[]{:S(2)}, u32[]{:S(2)}) %collective-permute-start.22) | collective-permute-done | bytes 196640 | tf_op jit(solution)/shard_map/ppermute | solution.py:433
  174.4 1.4 collective-permute-start.39
  175.8 1.7 add_convert_fusion
  177.5 4.1 %collective-permute-done.38.refs_2_ = bf16[48,1536]{1,0:T(8,128)(2,1)S(1)} collective-permute-done((bf16[48,1536]{1,0:T(8,128)(2,1)S(1)}, bf16[48,1536]{1,0:T(8,128)(2,1)S(1)}, u32[]{:S(2)}, u32[]{:S(2)}) %collective-permute-start.38) | collective-permute-done | bytes 147488 | tf_op jit(solution)/shard_map/ppermute | solution.py:124
  181.9 1.4 collective-permute-start.40
  183.6 2.1 %collective-permute-done.40 = f32[40,128]{1,0:T(8,128)S(1)} collective-permute-done((f32[40,128]{1,0:T(8,128)S(1)}, f32[40,128]{1,0:T(8,128)S(1)}, u32[]{:S(2)}, u32[]{:S(2)}) %collective-permute-start.40) | collective-permute-done | bytes 20512 | tf_op jit(solution)/shard_map/ppermute | solution.py:445
  186.5 3.2 %collective-permute-done.41 = f32[40,128]{1,0:T(8,128)S(1)} collective-permute-done((f32[40,128]{1,0:T(8,128)S(1)}, f32[40,128]{1,0:T(8,128)S(1)}, u32[]{:S(2)}, u32[]{:S(2)}) %collective-permute-start.41) | collective-permute-done | bytes 20512 | tf_op jit(solution)/shard_map/ppermute | solution.py:445
  191.5 3.5 %ring_total.1 = (f32[48,3072]{1,0:T(8,128)S(1)}, f32[48,3072]{1,0:T(8,128)}) custom-call(s32[1]{0:T(128)} %bitcast.core_ref, bf16[96,3072]{1,0:T(8,128)(2,1)S(1)} %copy-done.27, bf16[96,3072]{1,0:T(8,128)(2,1)} %collective-permute-done.36.r_ref, bf16[96,3072]{1,0:T(8,128)(2,1)} %collective-permute-done.37.l_ref), custom_call_target="tpu_custom_call" | custom-call | flops 1 | bytes 1 | tf_op jit(solution)/shard_map/ring_total/pallas_call | solution.py:258
  196.2 1.2 collective-permute-start.44
  198.0 3.8 %collective-permute-done.43.refs_2_ = bf16[48,1536]{1,0:T(8,128)(2,1)S(1)} collective-permute-done((bf16[48,1536]{1,0:T(8,128)(2,1)S(1)}, bf16[48,1536]{1,0:T(8,128)(2,1)S(1)}, u32[]{:S(2)}, u32[]{:S(2)}) %collective-permute-start.43) | collective-permute-done | bytes 147488 | tf_op jit(solution)/shard_map/ppermute | solution.py:124
  203.1 1.7 collective-permute-start.45
  206.4 2.4 %collective-permute-done.45 = bf16[48,1536]{1,0:T(8,128)(2,1)} collective-permute-done((bf16[48,1536]{1,0:T(8,128)(2,1)}, bf16[48,1536]{1,0:T(8,128)(2,1)}, u32[]{:S(2)}, u32[]{:S(2)}) %collective-permute-start.45) | collective-permute-done | bytes 147488 | tf_op jit(solution)/shard_map/ppermute | solution.py:124
  208.8 1.6 collective-permute-done.46
  210.3 1.1 convert_add_fusion
  212.8 1.2 combine.1
  (218 shorter events, 49.5 us)
Async XLA Ops:
  0.6 20.6 %copy-start = (f32[32,12]{0,1:T(8,128)S(1)}, f32[32,12]{0,1:T(8,128)}, u32[]{:S(2)}) copy-start(f32[32,12]{0,1:T(8,128)} %param.17) | copy-start | bytes 4612
  2.4 6.8 %collective-permute-start.1 = (bf16[48,1536]{1,0:T(8,128)(2,1)S(1)}, bf16[48,1536]{1,0:T(8,128)(2,1)S(1)}, u32[]{:S(2)}, u32[]{:S(2)}) collective-permute-start(bf16[48,1536]{1,0:T(8,128)(2,1)S(1)} %constant_dynamic-update-slice_fusion.refs_0_), channel_id=1, source_target_pairs={{0,8},{2,10},{8,16},{10,18},{16,24},{18,26},{24,28},{26,30},{28,20... | collective-permute-start | bytes 442376 | tf_op jit(solution)/shard_map/ppermute | solution.py:85
  5.4 7.8 %collective-permute-start.2 = (bf16[48,1536]{1,0:T(8,128)(2,1)S(1)}, bf16[48,1536]{1,0:T(8,128)(2,1)S(1)}, u32[]{:S(2)}, u32[]{:S(2)}) collective-permute-start(bf16[48,1536]{1,0:T(8,128)(2,1)S(1)} %constant_dynamic-update-slice_fusion.refs_0_), channel_id=1, source_target_pairs={{8,0},{10,2},{16,8},{18,10},{24,16},{26,18},{28,24},{30,26},{20,28... | collective-permute-start | bytes 442376 | tf_op jit(solution)/shard_map/ppermute | solution.py:85
  5.4 10.7 %copy-start.49 = (s32[256,1]{0,1:T(1,128)S(1)}, s32[256,1]{0,1:T(1,128)}, u32[]{:S(2)}) copy-start(s32[256,1]{0,1:T(1,128)} %param.23) | copy-start | bytes 3076
  5.4 15.9 %copy-start.51 = (s32[511]{0:T(512)S(1)}, s32[511]{0:T(512)}, u32[]{:S(2)}) copy-start(s32[511]{0:T(512)} %param.24) | copy-start | bytes 6136
  9.2 5.1 %collective-permute-start.3 = (bf16[48,1536]{1,0:T(8,128)(2,1)S(1)}, bf16[48,1536]{1,0:T(8,128)(2,1)S(1)}, u32[]{:S(2)}, u32[]{:S(2)}) collective-permute-start(bf16[48,1536]{1,0:T(8,128)(2,1)S(1)} %collective-permute-done.1.refs_1_), channel_id=1, source_target_pairs={{0,8},{2,10},{8,16},{10,18},{16,24},{18,26},{24,28},{26,30},{28,20... | collective-permute-start | bytes 442376 | tf_op jit(solution)/shard_map/ppermute | solution.py:85
  11.0 16.4 %collective-permute-start.12 = (bf16[48,3072]{1,0:T(8,128)(2,1)S(1)}, bf16[48,3072]{1,0:T(8,128)(2,1)}, u32[]{:S(2)}, u32[]{:S(2)}) collective-permute-start(bf16[48,3072]{1,0:T(8,128)(2,1)S(1)} %pad_maximum_fusion), channel_id=1, source_target_pairs={{0,2},{2,0},{4,6},{6,4},{8,10},{10,8},{12,14},{14,12},{16,18},{18,... | collective-permute-start | bytes 884744 | tf_op jit(solution)/shard_map/ppermute | solution.py:56
  11.1 17.6 %collective-permute-start = (bf16[128,768]{1,0:T(8,128)(2,1)S(1)}, bf16[128,768]{1,0:T(8,128)(2,1)}, u32[]{:S(2)}, u32[]{:S(2)}) collective-permute-start(bf16[128,768]{1,0:T(8,128)(2,1)S(1)} %copy-done.45), channel_id=1, source_target_pairs={{0,1},{1,0},{2,3},{3,2},{4,5},{5,4},{6,7},{7,6},{8,9},{9,8},{10,11... | collective-permute-start | bytes 589832 | tf_op jit(solution)/shard_map/ppermute | solution.py:433
  12.7 16.0 %collective-permute-start.10 = (bf16[128,768]{1,0:T(8,128)(2,1)}, bf16[128,768]{1,0:T(8,128)(2,1)}, u32[]{:S(2)}, u32[]{:S(2)}) collective-permute-start(bf16[128,768]{1,0:T(8,128)(2,1)} %param.25), channel_id=1, source_target_pairs={{0,1},{1,0},{2,3},{3,2},{4,5},{5,4},{6,7},{7,6},{8,9},{9,8},{10,11... | collective-permute-start | bytes 589832 | tf_op jit(solution)/shard_map/ppermute | solution.py:433
  13.2 5.6 %collective-permute-start.4 = (bf16[48,1536]{1,0:T(8,128)(2,1)S(1)}, bf16[48,1536]{1,0:T(8,128)(2,1)S(1)}, u32[]{:S(2)}, u32[]{:S(2)}) collective-permute-start(bf16[48,1536]{1,0:T(8,128)(2,1)S(1)} %collective-permute-done.2.refs_2_), channel_id=1, source_target_pairs={{8,0},{10,2},{16,8},{18,10},{24,16},{26,18},{28,24},{30,26},{20,28... | collective-permute-start | bytes 442376 | tf_op jit(solution)/shard_map/ppermute | solution.py:85
  14.3 5.1 %collective-permute-start.5 = (bf16[48,1536]{1,0:T(8,128)(2,1)S(1)}, bf16[48,1536]{1,0:T(8,128)(2,1)S(1)}, u32[]{:S(2)}, u32[]{:S(2)}) collective-permute-start(bf16[48,1536]{1,0:T(8,128)(2,1)S(1)} %collective-permute-done.3.refs_3_), channel_id=1, source_target_pairs={{0,8},{2,10},{8,16},{10,18},{16,24},{18,26},{24,28},{26,30},{28,20... | collective-permute-start | bytes 442376 | tf_op jit(solution)/shard_map/ppermute | solution.py:85
  18.8 5.1 %collective-permute-start.6 = (bf16[48,1536]{1,0:T(8,128)(2,1)S(1)}, bf16[48,1536]{1,0:T(8,128)(2,1)S(1)}, u32[]{:S(2)}, u32[]{:S(2)}) collective-permute-start(bf16[48,1536]{1,0:T(8,128)(2,1)S(1)} %collective-permute-done.4.refs_4_), channel_id=1, source_target_pairs={{8,0},{10,2},{16,8},{18,10},{24,16},{26,18},{28,24},{30,26},{20,28... | collective-permute-start | bytes 442376 | tf_op jit(solution)/shard_map/ppermute | solution.py:85
  19.4 5.1 %collective-permute-start.7 = (bf16[48,1536]{1,0:T(8,128)(2,1)S(1)}, bf16[48,1536]{1,0:T(8,128)(2,1)S(1)}, u32[]{:S(2)}, u32[]{:S(2)}) collective-permute-start(bf16[48,1536]{1,0:T(8,128)(2,1)S(1)} %collective-permute-done.5.refs_5_), channel_id=1, source_target_pairs={{0,8},{2,10},{8,16},{10,18},{16,24},{18,26},{24,28},{26,30},{28,20... | collective-permute-start | bytes 442376 | tf_op jit(solution)/shard_map/ppermute | solution.py:92
  26.9 6.9 %collective-permute-start.8 = (bf16[384,1536]{1,0:T(8,128)(2,1)S(1)}, bf16[384,1536]{1,0:T(8,128)(2,1)S(1)}, u32[]{:S(2)}, u32[]{:S(2)}) collective-permute-start(bf16[384,1536]{1,0:T(8,128)(2,1)S(1)} %assemble.1.own_ref), channel_id=1, source_target_pairs={{0,2},{2,0},{4,6},{6,4},{8,10},{10,8},{12,14},{14,12},{16,18},{18,... | collective-permute-start | bytes 3538952 | tf_op jit(solution)/shard_map/ppermute | solution.py:56
  28.6 9.0 %copy-start.8 = (bf16[96,3072]{1,0:T(8,128)(2,1)}, bf16[96,3072]{1,0:T(8,128)(2,1)S(1)}, u32[]{:S(2)}) copy-start(bf16[96,3072]{1,0:T(8,128)(2,1)S(1)} %maximum_select_fusion.refs_0_) | copy-start | bytes 1769476
  28.7 17.9 %collective-permute-start.13 = (bf16[96,3072]{1,0:T(8,128)(2,1)S(1)}, bf16[96,3072]{1,0:T(8,128)(2,1)}, u32[]{:S(2)}, u32[]{:S(2)}) collective-permute-start(bf16[96,3072]{1,0:T(8,128)(2,1)S(1)} %maximum_select_fusion.refs_0_), channel_id=1, source_target_pairs={{0,8},{2,10},{8,16},{10,18},{16,24},{18,26},{24,28},{26,30},{28,20... | collective-permute-start | bytes 1769480 | tf_op jit(solution)/shard_map/ppermute | solution.py:85
  30.6 16.0 %collective-permute-start.14 = (bf16[96,3072]{1,0:T(8,128)(2,1)S(1)}, bf16[96,3072]{1,0:T(8,128)(2,1)}, u32[]{:S(2)}, u32[]{:S(2)}) collective-permute-start(bf16[96,3072]{1,0:T(8,128)(2,1)S(1)} %maximum_select_fusion.refs_0_), channel_id=1, source_target_pairs={{8,0},{10,2},{16,8},{18,10},{24,16},{26,18},{28,24},{30,26},{20,28... | collective-permute-start | bytes 1769480 | tf_op jit(solution)/shard_map/ppermute | solution.py:85
  37.6 94.1 %copy-start.1 = (bf16[768,1536]{1,0:T(8,128)(2,1)}, bf16[768,1536]{1,0:T(8,128)(2,1)S(1)}, u32[]{:S(2)}) copy-start(bf16[768,1536]{1,0:T(8,128)(2,1)S(1)} %interleave.1.w_ref) | copy-start | bytes 7077892
  38.3 7.5 %copy-start.47 = (s32[256,1]{1,0:T(8,128)S(1)}, s32[256,1]{1,0:T(8,128)}, u32[]{:S(2)}) copy-start(s32[256,1]{1,0:T(8,128)} %copy.44) | copy-start | bytes 3076
  38.3 8.2 %copy-start.50 = (f32[768]{0:T(1024)S(1)}, f32[768]{0:T(1024)}, u32[]{:S(2)}) copy-start(f32[768]{0:T(1024)} %param.18) | copy-start | bytes 9220
  44.1 12.0 %copy-start.10 = (f32[6,256,256]{2,1,0:T(8,128)}, f32[6,256,256]{2,1,0:T(8,128)S(1)}, u32[]{:S(2)}) copy-start(f32[6,256,256]{2,1,0:T(8,128)S(1)} %get-tuple-element.99.p_ref) | copy-start | bytes 4718596
  44.1 11.1 %copy-start.44 = (f32[768,2]{0,1:T(2,128)S(1)}, f32[768,2]{0,1:T(2,128)}, u32[]{:S(2)}) copy-start(f32[768,2]{0,1:T(2,128)} %param.19) | copy-start | bytes 18436
  44.1 11.1 %collective-permute-start.9 = (bf16[256,768]{1,0:T(8,128)(2,1)S(1)}, bf16[256,768]{1,0:T(8,128)(2,1)S(1)}, u32[]{:S(2)}, u32[]{:S(2)}) collective-permute-start(bf16[256,768]{1,0:T(8,128)(2,1)S(1)} %get-tuple-element.78.part_ref), channel_id=1, source_target_pairs={{0,1},{1,0},{2,3},{3,2},{4,5},{5,4},{6,7},{7,6},{8,9},{9,8},{10,11... | collective-permute-start | bytes 1179656 | tf_op jit(solution)/shard_map/ppermute | solution.py:433
  46.6 15.2 %collective-permute-start.15 = (bf16[96,3072]{1,0:T(8,128)(2,1)}, bf16[96,3072]{1,0:T(8,128)(2,1)S(1)}, u32[]{:S(2)}, u32[]{:S(2)}) collective-permute-start(bf16[96,3072]{1,0:T(8,128)(2,1)} %collective-permute-done.13.refs_1_), channel_id=1, source_target_pairs={{0,8},{2,10},{8,16},{10,18},{16,24},{18,26},{24,28},{26,30},{28,20... | collective-permute-start | bytes 1769480 | tf_op jit(solution)/shard_map/ppermute | solution.py:85
  48.2 14.8 %collective-permute-start.16 = (bf16[96,3072]{1,0:T(8,128)(2,1)}, bf16[96,3072]{1,0:T(8,128)(2,1)S(1)}, u32[]{:S(2)}, u32[]{:S(2)}) collective-permute-start(bf16[96,3072]{1,0:T(8,128)(2,1)} %collective-permute-done.14.refs_2_), channel_id=1, source_target_pairs={{8,0},{10,2},{16,8},{18,10},{24,16},{26,18},{28,24},{30,26},{20,28... | collective-permute-start | bytes 1769480 | tf_op jit(solution)/shard_map/ppermute | solution.py:85
  57.0 21.8 %collective-permute-start.11 = (bf16[352,1536]{1,0:T(8,128)(2,1)S(1)}, bf16[352,1536]{1,0:T(8,128)(2,1)S(1)}, u32[]{:S(2)}, u32[]{:S(2)}) collective-permute-start(bf16[352,1536]{1,0:T(8,128)(2,1)S(1)} %get-tuple-element.80.own_ref), channel_id=1, source_target_pairs={{0,2},{2,0},{4,6},{6,4},{8,10},{10,8},{12,14},{14,12},{16,18},{18,... | collective-permute-start | bytes 3244040 | tf_op jit(solution)/shard_map/ppermute | solution.py:56
  63.0 13.7 %collective-permute-start.17 = (bf16[96,3072]{1,0:T(8,128)(2,1)S(1)}, bf16[96,3072]{1,0:T(8,128)(2,1)S(1)}, u32[]{:S(2)}, u32[]{:S(2)}) collective-permute-start(bf16[96,3072]{1,0:T(8,128)(2,1)S(1)} %collective-permute-done.15.refs_3_), channel_id=1, source_target_pairs={{0,8},{2,10},{8,16},{10,18},{16,24},{18,26},{24,28},{26,30},{28,20... | collective-permute-start | bytes 1769480 | tf_op jit(solution)/shard_map/ppermute | solution.py:85
  65.4 13.4 %collective-permute-start.18 = (bf16[96,3072]{1,0:T(8,128)(2,1)S(1)}, bf16[96,3072]{1,0:T(8,128)(2,1)S(1)}, u32[]{:S(2)}, u32[]{:S(2)}) collective-permute-start(bf16[96,3072]{1,0:T(8,128)(2,1)S(1)} %collective-permute-done.16.refs_4_), channel_id=1, source_target_pairs={{8,0},{10,2},{16,8},{18,10},{24,16},{26,18},{28,24},{30,26},{20,28... | collective-permute-start | bytes 1769480 | tf_op jit(solution)/shard_map/ppermute | solution.py:85
  81.4 7.0 %collective-permute-start.19 = (bf16[96,1536]{1,0:T(8,128)(2,1)}, bf16[96,1536]{1,0:T(8,128)(2,1)}, u32[]{:S(2)}, u32[]{:S(2)}) collective-permute-start(bf16[96,1536]{1,0:T(8,128)(2,1)} %slice.47), channel_id=1, source_target_pairs={{0,8},{2,10},{8,16},{10,18},{16,24},{18,26},{24,28},{26,30},{28,20... | collective-permute-start | bytes 884744 | tf_op jit(solution)/shard_map/ppermute | solution.py:88
  83.7 7.0 %collective-permute-start.20 = (bf16[96,1536]{1,0:T(8,128)(2,1)}, bf16[96,1536]{1,0:T(8,128)(2,1)}, u32[]{:S(2)}, u32[]{:S(2)}) collective-permute-start(bf16[96,1536]{1,0:T(8,128)(2,1)} %slice.48), channel_id=1, source_target_pairs={{8,0},{10,2},{16,8},{18,10},{24,16},{26,18},{28,24},{30,26},{20,28... | collective-permute-start | bytes 884744 | tf_op jit(solution)/shard_map/ppermute | solution.py:89
  84.3 26.9 %copy-start.4 = (f32[256,768]{1,0:T(8,128)S(1)}, f32[256,768]{1,0:T(8,128)}, u32[]{:S(2)}) copy-start(f32[256,768]{1,0:T(8,128)} %copy-done.3) | copy-start | bytes 2359300
  98.6 12.7 %copy-start.34 = (s32[256,1]{1,0:T(8,128)S(1)}, s32[256,1]{1,0:T(8,128)}, u32[]{:S(2)}) copy-start(s32[256,1]{1,0:T(8,128)} %get-tuple-element.190.flat_ref) | copy-start | bytes 3076
  108.5 2.8 %collective-permute-start.21 = (bf16[352,1536]{1,0:T(8,128)(2,1)S(1)}, bf16[352,1536]{1,0:T(8,128)(2,1)S(1)}, u32[]{:S(2)}, u32[]{:S(2)}) collective-permute-start(bf16[352,1536]{1,0:T(8,128)(2,1)S(1)} %get-tuple-element.90), channel_id=1, source_target_pairs={{0,2},{2,0},{4,6},{6,4},{8,10},{10,8},{12,14},{14,12},{16,18},{18,... | collective-permute-start | bytes 3244040 | tf_op jit(solution)/shard_map/ppermute | solution.py:56
  108.6 9.5 %collective-permute-start.24 = (bf16[96,1536]{1,0:T(8,128)(2,1)S(1)}, bf16[96,1536]{1,0:T(8,128)(2,1)S(1)}, u32[]{:S(2)}, u32[]{:S(2)}) collective-permute-start(bf16[96,1536]{1,0:T(8,128)(2,1)S(1)} %get-tuple-element.95), channel_id=1, source_target_pairs={{0,8},{2,10},{8,16},{10,18},{16,24},{18,26},{24,28},{26,30},{28,20... | collective-permute-start | bytes 884744 | tf_op jit(solution)/shard_map/ppermute | solution.py:124
  110.1 9.1 %collective-permute-start.25 = (bf16[96,1536]{1,0:T(8,128)(2,1)S(1)}, bf16[96,1536]{1,0:T(8,128)(2,1)S(1)}, u32[]{:S(2)}, u32[]{:S(2)}) collective-permute-start(bf16[96,1536]{1,0:T(8,128)(2,1)S(1)} %get-tuple-element.96), channel_id=1, source_target_pairs={{8,0},{10,2},{16,8},{18,10},{24,16},{26,18},{28,24},{30,26},{20,28... | collective-permute-start | bytes 884744 | tf_op jit(solution)/shard_map/ppermute | solution.py:124
  111.3 20.5 %copy-start.33 = (bf16[256,1152]{1,0:T(8,128)(2,1)S(1)}, bf16[256,1152]{1,0:T(8,128)(2,1)}, u32[]{:S(2)}) copy-start(bf16[256,1152]{1,0:T(8,128)(2,1)} %copy-done.32) | copy-start | bytes 1769476
  113.2 18.6 %copy-start.11 = (f32[6,256,256]{2,1,0:T(8,128)S(1)}, f32[6,256,256]{2,1,0:T(8,128)}, u32[]{:S(2)}) copy-start(f32[6,256,256]{2,1,0:T(8,128)} %copy-done.10) | copy-start | bytes 4718596
  119.8 16.6 %collective-permute-start.29 = (bf16[96,3072]{1,0:T(8,128)(2,1)S(1)}, bf16[96,3072]{1,0:T(8,128)(2,1)S(1)}, u32[]{:S(2)}, u32[]{:S(2)}) collective-permute-start(bf16[96,3072]{1,0:T(8,128)(2,1)S(1)} %get-tuple-element.112), channel_id=1, source_target_pairs={{0,8},{2,10},{8,16},{10,18},{16,24},{18,26},{24,28},{26,30},{28,20... | collective-permute-start | bytes 1769480 | tf_op jit(solution)/shard_map/ppermute | solution.py:124
  120.4 16.0 %collective-permute-start.30 = (bf16[96,3072]{1,0:T(8,128)(2,1)S(1)}, bf16[96,3072]{1,0:T(8,128)(2,1)S(1)}, u32[]{:S(2)}, u32[]{:S(2)}) collective-permute-start(bf16[96,3072]{1,0:T(8,128)(2,1)S(1)} %get-tuple-element.114), channel_id=1, source_target_pairs={{8,0},{10,2},{16,8},{18,10},{24,16},{26,18},{28,24},{30,26},{20,28... | collective-permute-start | bytes 1769480 | tf_op jit(solution)/shard_map/ppermute | solution.py:124
  121.9 9.9 %collective-permute-start.23 = (bf16[256,768]{1,0:T(8,128)(2,1)S(1)}, bf16[256,768]{1,0:T(8,128)(2,1)S(1)}, u32[]{:S(2)}, u32[]{:S(2)}) collective-permute-start(bf16[256,768]{1,0:T(8,128)(2,1)S(1)} %get-tuple-element.93.low_ref), channel_id=1, source_target_pairs={{0,1},{1,0},{2,3},{3,2},{4,5},{5,4},{6,7},{7,6},{8,9},{9,8},{10,11... | collective-permute-start | bytes 1179656 | tf_op jit(solution)/shard_map/ppermute | solution.py:433
  138.1 8.9 %collective-permute-start.33 = (bf16[384,1536]{1,0:T(8,128)(2,1)S(1)}, bf16[384,1536]{1,0:T(8,128)(2,1)S(1)}, u32[]{:S(2)}, u32[]{:S(2)}) collective-permute-start(bf16[384,1536]{1,0:T(8,128)(2,1)S(1)} %get-tuple-element.122), channel_id=1, source_target_pairs={{0,2},{2,0},{4,6},{6,4},{8,10},{10,8},{12,14},{14,12},{16,18},{18,... | collective-permute-start | bytes 3538952 | tf_op jit(solution)/shard_map/ppermute | solution.py:56
  140.0 16.4 %collective-permute-start.31 = (bf16[96,3072]{1,0:T(8,128)(2,1)}, bf16[96,3072]{1,0:T(8,128)(2,1)}, u32[]{:S(2)}, u32[]{:S(2)}) collective-permute-start(bf16[96,3072]{1,0:T(8,128)(2,1)} %get-tuple-element.115), channel_id=1, source_target_pairs={{0,8},{2,10},{8,16},{10,18},{16,24},{18,26},{24,28},{26,30},{28,20... | collective-permute-start | bytes 1769480 | tf_op jit(solution)/shard_map/ppermute | solution.py:124
  140.7 16.5 %collective-permute-start.32 = (bf16[96,3072]{1,0:T(8,128)(2,1)}, bf16[96,3072]{1,0:T(8,128)(2,1)}, u32[]{:S(2)}, u32[]{:S(2)}) collective-permute-start(bf16[96,3072]{1,0:T(8,128)(2,1)} %get-tuple-element.116), channel_id=1, source_target_pairs={{8,0},{10,2},{16,8},{18,10},{24,16},{26,18},{28,24},{30,26},{20,28... | collective-permute-start | bytes 1769480 | tf_op jit(solution)/shard_map/ppermute | solution.py:124
  143.2 3.8 %collective-permute-start.27 = (f32[40,128]{1,0:T(8,128)S(1)}, f32[40,128]{1,0:T(8,128)S(1)}, u32[]{:S(2)}, u32[]{:S(2)}) collective-permute-start(f32[40,128]{1,0:T(8,128)S(1)} %get-tuple-element.105), channel_id=1, source_target_pairs={{0,1},{1,0},{2,3},{3,2},{4,5},{5,4},{6,7},{7,6},{8,9},{9,8},{10,11... | collective-permute-start | bytes 61448 | tf_op jit(solution)/shard_map/ppermute | solution.py:433
  147.0 2.3 %collective-permute-start.28 = (f32[40,128]{1,0:T(8,128)S(1)}, f32[40,128]{1,0:T(8,128)S(1)}, u32[]{:S(2)}, u32[]{:S(2)}) collective-permute-start(f32[40,128]{1,0:T(8,128)S(1)} %add.335), channel_id=1, source_target_pairs={{0,2},{2,0},{4,6},{6,4},{8,10},{10,8},{12,14},{14,12},{16,18},{18,... | collective-permute-start | bytes 61448 | tf_op jit(solution)/shard_map/ppermute | solution.py:56
  147.1 10.5 %collective-permute-start.34 = (bf16[48,768]{1,0:T(8,128)(2,1)S(1)}, bf16[48,768]{1,0:T(8,128)(2,1)S(1)}, u32[]{:S(2)}, u32[]{:S(2)}) collective-permute-start(bf16[48,768]{1,0:T(8,128)(2,1)S(1)} %get-tuple-element.123), channel_id=1, source_target_pairs={{0,8},{2,10},{8,16},{10,18},{16,24},{18,26},{24,28},{26,30},{28,20... | collective-permute-start | bytes 221192 | tf_op jit(solution)/shard_map/ppermute | solution.py:124
  147.7 10.1 %collective-permute-start.35 = (bf16[48,768]{1,0:T(8,128)(2,1)S(1)}, bf16[48,768]{1,0:T(8,128)(2,1)S(1)}, u32[]{:S(2)}, u32[]{:S(2)}) collective-permute-start(bf16[48,768]{1,0:T(8,128)(2,1)S(1)} %get-tuple-element.124), channel_id=1, source_target_pairs={{8,0},{10,2},{16,8},{18,10},{24,16},{26,18},{28,24},{30,26},{20,28... | collective-permute-start | bytes 221192 | tf_op jit(solution)/shard_map/ppermute | solution.py:124
  163.6 18.3 %collective-permute-start.36 = (bf16[96,3072]{1,0:T(8,128)(2,1)}, bf16[96,3072]{1,0:T(8,128)(2,1)}, u32[]{:S(2)}, u32[]{:S(2)}) collective-permute-start(bf16[96,3072]{1,0:T(8,128)(2,1)} %get-tuple-element.128), channel_id=1, source_target_pairs={{0,8},{2,10},{8,16},{10,18},{16,24},{18,26},{24,28},{26,30},{28,20... | collective-permute-start | bytes 1769480 | tf_op jit(solution)/shard_map/ppermute | solution.py:124
  164.2 17.7 %collective-permute-start.37 = (bf16[96,3072]{1,0:T(8,128)(2,1)}, bf16[96,3072]{1,0:T(8,128)(2,1)}, u32[]{:S(2)}, u32[]{:S(2)}) collective-permute-start(bf16[96,3072]{1,0:T(8,128)(2,1)} %get-tuple-element.129), channel_id=1, source_target_pairs={{8,0},{10,2},{16,8},{18,10},{24,16},{26,18},{28,24},{30,26},{20,28... | collective-permute-start | bytes 1769480 | tf_op jit(solution)/shard_map/ppermute | solution.py:124
  166.3 8.1 %collective-permute-start.22 = (bf16[128,768]{1,0:T(8,128)(2,1)}, bf16[128,768]{1,0:T(8,128)(2,1)}, u32[]{:S(2)}, u32[]{:S(2)}) collective-permute-start(bf16[128,768]{1,0:T(8,128)(2,1)} %constant_dynamic-slice_fusion.1), channel_id=1, source_target_pairs={{0,1},{1,0},{2,3},{3,2},{4,5},{5,4},{6,7},{7,6},{8,9},{9,8},{10,11... | collective-permute-start | bytes 589832 | tf_op jit(solution)/shard_map/ppermute | solution.py:433
  167.3 8.5 %copy-start.5 = (f32[256,768]{1,0:T(8,128)S(1)}, f32[256,768]{1,0:T(8,128)}, u32[]{:S(2)}) copy-start(f32[256,768]{1,0:T(8,128)} %copy-done.3) | copy-start | bytes 2359300
  167.3 16.0 %collective-permute-start.26 = (bf16[128,768]{1,0:T(8,128)(2,1)S(1)}, bf16[128,768]{1,0:T(8,128)(2,1)S(1)}, u32[]{:S(2)}, u32[]{:S(2)}) collective-permute-start(bf16[128,768]{1,0:T(8,128)(2,1)S(1)} %constant_dynamic-slice_fusion), channel_id=1, source_target_pairs={{0,1},{1,0},{2,3},{3,2},{4,5},{5,4},{6,7},{7,6},{8,9},{9,8},{10,11... | collective-permute-start | bytes 589832 | tf_op jit(solution)/shard_map/ppermute | solution.py:433
  168.7 21.8 %copy-start.41 = (f32[256,768]{1,0:T(8,128)S(1)}, f32[256,768]{1,0:T(8,128)}, u32[]{:S(2)}) copy-start(f32[256,768]{1,0:T(8,128)} %copy-done.40) | copy-start | bytes 2359300
  168.7 12.9 %collective-permute-start.38 = (bf16[48,1536]{1,0:T(8,128)(2,1)S(1)}, bf16[48,1536]{1,0:T(8,128)(2,1)S(1)}, u32[]{:S(2)}, u32[]{:S(2)}) collective-permute-start(bf16[48,1536]{1,0:T(8,128)(2,1)S(1)} %get-tuple-element.132), channel_id=1, source_target_pairs={{0,8},{2,10},{8,16},{10,18},{16,24},{18,26},{24,28},{26,30},{28,20... | collective-permute-start | bytes 442376 | tf_op jit(solution)/shard_map/ppermute | solution.py:124
  174.4 7.5 %collective-permute-start.39 = (bf16[48,1536]{1,0:T(8,128)(2,1)S(1)}, bf16[48,1536]{1,0:T(8,128)(2,1)S(1)}, u32[]{:S(2)}, u32[]{:S(2)}) collective-permute-start(bf16[48,1536]{1,0:T(8,128)(2,1)S(1)} %get-tuple-element.133), channel_id=1, source_target_pairs={{8,0},{10,2},{16,8},{18,10},{24,16},{26,18},{28,24},{30,26},{20,28... | collective-permute-start | bytes 442376 | tf_op jit(solution)/shard_map/ppermute | solution.py:124
  177.5 14.0 %copy-start.27 = (bf16[96,3072]{1,0:T(8,128)(2,1)S(1)}, bf16[96,3072]{1,0:T(8,128)(2,1)}, u32[]{:S(2)}) copy-start(bf16[96,3072]{1,0:T(8,128)(2,1)} %copy-done.26) | copy-start | bytes 1769476
  181.9 3.8 %collective-permute-start.40 = (f32[40,128]{1,0:T(8,128)S(1)}, f32[40,128]{1,0:T(8,128)S(1)}, u32[]{:S(2)}, u32[]{:S(2)}) collective-permute-start(f32[40,128]{1,0:T(8,128)S(1)} %add.336), channel_id=1, source_target_pairs={{0,4},{2,6},{4,0},{6,2},{8,12},{10,14},{12,8},{14,10},{16,20},{18,... | collective-permute-start | bytes 61448 | tf_op jit(solution)/shard_map/ppermute | solution.py:445
  185.7 4.0 %collective-permute-start.41 = (f32[40,128]{1,0:T(8,128)S(1)}, f32[40,128]{1,0:T(8,128)S(1)}, u32[]{:S(2)}, u32[]{:S(2)}) collective-permute-start(f32[40,128]{1,0:T(8,128)S(1)} %add.340), channel_id=1, source_target_pairs={{0,8},{2,10},{4,12},{6,14},{8,0},{10,2},{12,4},{14,6},{16,24},{18,... | collective-permute-start | bytes 61448 | tf_op jit(solution)/shard_map/ppermute | solution.py:445
  189.7 7.7 %collective-permute-start.42 = (f32[40,128]{1,0:T(8,128)S(1)}, f32[40,128]{1,0:T(8,128)S(1)}, u32[]{:S(2)}, u32[]{:S(2)}) collective-permute-start(f32[40,128]{1,0:T(8,128)S(1)} %add.341), channel_id=1, source_target_pairs={{0,16},{2,18},{4,20},{6,22},{8,24},{10,26},{12,28},{14,30},{16,0},... | collective-permute-start | bytes 61448 | tf_op jit(solution)/shard_map/ppermute | solution.py:445
  195.0 17.8 %collective-permute-start.47 = (f32[48,3072]{1,0:T(8,128)}, f32[48,3072]{1,0:T(8,128)S(1)}, u32[]{:S(2)}, u32[]{:S(2)}) collective-permute-start(f32[48,3072]{1,0:T(8,128)} %get-tuple-element.143), channel_id=1, source_target_pairs={{0,2},{2,0},{4,6},{6,4},{8,10},{10,8},{12,14},{14,12},{16,18},{18,... | collective-permute-start | bytes 1769480 | tf_op jit(solution)/shard_map/ppermute | solution.py:56
  195.3 6.6 %collective-permute-start.43 = (bf16[48,1536]{1,0:T(8,128)(2,1)S(1)}, bf16[48,1536]{1,0:T(8,128)(2,1)S(1)}, u32[]{:S(2)}, u32[]{:S(2)}) collective-permute-start(bf16[48,1536]{1,0:T(8,128)(2,1)S(1)} %get-tuple-element.137), channel_id=1, source_target_pairs={{0,8},{2,10},{8,16},{10,18},{16,24},{18,26},{24,28},{26,30},{28,20... | collective-permute-start | bytes 442376 | tf_op jit(solution)/shard_map/ppermute | solution.py:124
  196.2 6.0 %collective-permute-start.44 = (bf16[48,1536]{1,0:T(8,128)(2,1)S(1)}, bf16[48,1536]{1,0:T(8,128)(2,1)S(1)}, u32[]{:S(2)}, u32[]{:S(2)}) collective-permute-start(bf16[48,1536]{1,0:T(8,128)(2,1)S(1)} %get-tuple-element.138), channel_id=1, source_target_pairs={{8,0},{10,2},{16,8},{18,10},{24,16},{26,18},{28,24},{30,26},{20,28... | collective-permute-start | bytes 442376 | tf_op jit(solution)/shard_map/ppermute | solution.py:124
  203.1 5.6 %collective-permute-start.45 = (bf16[48,1536]{1,0:T(8,128)(2,1)}, bf16[48,1536]{1,0:T(8,128)(2,1)}, u32[]{:S(2)}, u32[]{:S(2)}) collective-permute-start(bf16[48,1536]{1,0:T(8,128)(2,1)} %get-tuple-element.139), channel_id=1, source_target_pairs={{0,8},{2,10},{8,16},{10,18},{16,24},{18,26},{24,28},{26,30},{28,20... | collective-permute-start | bytes 442376 | tf_op jit(solution)/shard_map/ppermute | solution.py:124
  204.9 5.5 %collective-permute-start.46 = (bf16[48,1536]{1,0:T(8,128)(2,1)}, bf16[48,1536]{1,0:T(8,128)(2,1)}, u32[]{:S(2)}, u32[]{:S(2)}) collective-permute-start(bf16[48,1536]{1,0:T(8,128)(2,1)} %get-tuple-element.140), channel_id=1, source_target_pairs={{8,0},{10,2},{16,8},{18,10},{24,16},{26,18},{28,24},{30,26},{20,28... | collective-permute-start | bytes 442376 | tf_op jit(solution)/shard_map/ppermute | solution.py:124
  (37 other events, 81.3 us)

commit v5 on v4

--- a/solution.py
+++ b/solution.py
@@ -14,6 +14,7 @@
 EPS = 1e-06
 NEG = -1e30
 VMEM_BYTES = 12 << 20
+RING_VMEM_BYTES = 6 << 20
 EXPERT_VMEM_BYTES = 24 << 20
 SMALL = pl.CostEstimate(flops=1, bytes_accessed=1, transcendentals=0)
 HIGH = lax.Precision.HIGHEST
@@ -93,9 +94,8 @@
         self.pieces += self.sent
         return self.sent
 
-    def owners(self):
-        chips = [self.ring.chip_at(d) for d in self.ring.distances]
-        return jnp.stack(chips + chips[-1:] if self.halves else chips)
+    def owners(self, begin=0, end=None):
+        return jnp.stack([self.ring.chip_at(d) for d in self.ring.distances[begin:end]])
 
 
 class Scatter:
@@ -117,10 +117,12 @@
         distance = self.reach - self.steps
         self.steps += 1
         if distance == self.reach:
-            r, l = ring_far(self.blocks(distance), self.rows)
+            r, l = ring_far(self.blocks(distance), self.rows, self.each)
         else:
             sent = after(self.sent, deps)
-            r, l = ring_add(self.blocks(distance), self.blocks(-distance), sent, self.rows)
+            r, l = ring_add(
+                self.blocks(distance), self.blocks(-distance), sent, self.rows, self.each
+            )
         self.sent = (lax.ppermute(r, "dp", ring.right), lax.ppermute(l, "dp", ring.left))
         return self.sent
 
@@ -130,70 +132,6 @@
             x[at * self.rows : (at + 1) * self.rows].astype(F32) for x, at in self.blocks(0)
         ]
         return sum(terms) + r.astype(F32) + l.astype(F32)
-
-
-def row_block(rows, width, at):
-    return pl.BlockSpec((rows, width), lambda i: (at, 0))
-
-
-def ring_far(blocks, rows):
-    width = blocks[0][0].shape[1]
-    half = width // 2
-
-    def kernel(*refs):
-        ins, (r_ref, l_ref) = refs[:-2], refs[-2:]
-        total = sum(ref[...].astype(F32) for ref in ins).astype(BF)
-        r_ref[...] = total[:, :half]
-        l_ref[...] = total[:, half:]
-
-    return pl.pallas_call(
-        kernel,
-        out_shape=[jax.ShapeDtypeStruct((rows, half), BF)] * 2,
-        in_specs=[row_block(rows, width, at) for _, at in blocks],
-        out_specs=[row_block(rows, half, 0)] * 2,
-        compiler_params=pltpu.CompilerParams(vmem_limit_bytes=VMEM_BYTES),
-        cost_estimate=SMALL,
-        grid=(1,),
-        name="ring_far",
-    )(*[x for x, _ in blocks])
-
-
-def ring_add(right, left, sent, rows):
-    width = right[0][0].shape[1]
-    arrived = sent[0].shape[1]
-    number = len(right)
-    tiles = 2 if arrived < width else max(1, width // 768)
-    tile = width // tiles
-
-    def kernel(*refs):
-        ins, outs = refs[:-2], refs[-2:]
-        for k, out_ref in enumerate(outs):
-            own = ins[k * (number + 1) : (k + 1) * (number + 1) - 1]
-            got = ins[(k + 1) * (number + 1) - 1]
-            total = sum(ref[...].astype(F32) for ref in own)
-            more = got[...].astype(F32)
-            if arrived < width:
-                more = jnp.where(pl.program_id(0) == k, more, 0.0)
-            out_ref[...] = (total + more).astype(BF)
-
-    def block(at):
-        return pl.BlockSpec((rows, tile), lambda i: (at, i))
-
-    got_block = block(0) if arrived == width else row_block(rows, tile, 0)
-    specs, args = [], []
-    for blocks, got in ((right, sent[0]), (left, sent[1])):
-        specs += [block(at) for _, at in blocks] + [got_block]
-        args += [x for x, _ in blocks] + [got]
-    return pl.pallas_call(
-        kernel,
-        out_shape=[jax.ShapeDtypeStruct((rows, width), BF)] * 2,
-        in_specs=specs,
-        out_specs=[block(0)] * 2,
-        compiler_params=pltpu.CompilerParams(vmem_limit_bytes=VMEM_BYTES),
-        cost_estimate=SMALL,
-        grid=(tiles,),
-        name="ring_add",
-    )(*args)
 
 
 def outer(pairs, owners, rows, counts):
@@ -239,34 +177,109 @@
     return lax.optimization_barrier((tuple(values), deps))[0]
 
 
+def fetch(refs, places, rows, held_ref, sems):
+    copies = [
+        pltpu.make_async_copy(ref.at[pl.ds(at * rows, rows)], held_ref.at[i], sems.at[i])
+        for i, (ref, at) in enumerate(zip(refs, places))
+    ]
+    for copy in copies:
+        copy.start()
+    for copy in copies:
+        copy.wait()
+
+
+def terms_spec(each):
+    return pl.BlockSpec(memory_space=pltpu.HBM if each else pl.ANY)
+
+
+def ring_far(blocks, rows, each):
+    width = blocks[0][0].shape[1]
+    half = width // 2
+    number = len(blocks)
+
+    def kernel(*refs):
+        ins, (r_ref, l_ref, held_ref, sems) = refs[:number], refs[number:]
+        fetch(ins, [at for _, at in blocks], rows, held_ref, sems)
+        for k, ref in enumerate((r_ref, l_ref)):
+            cols = pl.ds(k * half, half)
+            ref[...] = sum(held_ref[i, :, cols].astype(F32) for i in range(number)).astype(BF)
+
+    inside = pl.BlockSpec(memory_space=pltpu.VMEM)
+    return pl.pallas_call(
+        kernel,
+        out_shape=[jax.ShapeDtypeStruct((rows, half), BF)] * 2,
+        in_specs=[terms_spec(each)] * number,
+        out_specs=[inside] * 2,
+        scratch_shapes=[
+            pltpu.VMEM((number, rows, width), BF), pltpu.SemaphoreType.DMA((number,))
+        ],
+        compiler_params=pltpu.CompilerParams(vmem_limit_bytes=RING_VMEM_BYTES),
+        cost_estimate=SMALL,
+        name="ring_far",
+    )(*[x for x, _ in blocks])
+
+
+def ring_add(right, left, sent, rows, each):
+    width = right[0][0].shape[1]
+    arrived = sent[0].shape[1]
+    number = len(right)
+    blocks = right + left
+
+    def kernel(*refs):
+        ins, got = refs[: 2 * number], refs[2 * number : 2 * number + 2]
+        outs, (held_ref, sems) = refs[2 * number + 2 : 2 * number + 4], refs[2 * number + 4 :]
+        fetch(ins, [at for _, at in blocks], rows, held_ref, sems)
+        for k, out_ref in enumerate(outs):
+            for part in range(width // arrived):
+                cols = pl.ds(part * arrived, arrived)
+                total = sum(
+                    held_ref[k * number + i, :, cols].astype(F32) for i in range(number)
+                )
+                if arrived == width or part == k:
+                    total = total + got[k][...].astype(F32)
+                out_ref[:, cols] = total.astype(BF)
+
+    inside = pl.BlockSpec(memory_space=pltpu.VMEM)
+    return pl.pallas_call(
+        kernel,
+        out_shape=[jax.ShapeDtypeStruct((rows, width), BF)] * 2,
+        in_specs=[terms_spec(each)] * (2 * number) + [inside] * 2,
+        out_specs=[inside] * 2,
+        scratch_shapes=[
+            pltpu.VMEM((2 * number, rows, width), BF), pltpu.SemaphoreType.DMA((2 * number,))
+        ],
+        compiler_params=pltpu.CompilerParams(vmem_limit_bytes=RING_VMEM_BYTES),
+        cost_estimate=SMALL,
+        name="ring_add",
+    )(*[x for x, _ in blocks], *sent)
+
+
 def ring_total(block, sent, core):
-    x, at = block
     rows, width = sent[0].shape
-    tile, half = 768, rows // 2
-
-    def kernel(core_ref, own_ref, r_ref, l_ref, mine_ref, away_ref, total_ref):
-        total_ref[...] = (
-            own_ref[...].astype(F32) + r_ref[...].astype(F32) + l_ref[...].astype(F32)
-        )
-        begin = pl.multiple_of(core_ref[0] * half, 8)
-        mine_ref[...] = total_ref[pl.ds(begin, half), :]
-        away_ref[...] = total_ref[pl.ds(half - begin, half), :]
-
-    def block_of(number, at):
-        return pl.BlockSpec((number, tile), lambda i: (at, i))
-
+    half = rows // 2
+
+    def kernel(core_ref, own_ref, r_ref, l_ref, mine_ref, away_ref, held_ref, sems):
+        fetch([own_ref], [block[1]], rows, held_ref, sems)
+        begin = pl.multiple_of(core_ref[0] * half, 16)
+        for at, out_ref in ((begin, mine_ref), (pl.multiple_of(half - begin, 16), away_ref)):
+            here = pl.ds(at, half)
+            out_ref[...] = (
+                held_ref[0, here, :].astype(F32)
+                + r_ref[here, :].astype(F32)
+                + l_ref[here, :].astype(F32)
+            )
+
+    inside = pl.BlockSpec(memory_space=pltpu.VMEM)
     return pl.pallas_call(
         kernel,
         out_shape=[jax.ShapeDtypeStruct((half, width), F32)] * 2,
-        in_specs=[pl.BlockSpec(memory_space=pltpu.SMEM), block_of(rows, at)]
-        + [block_of(rows, 0)] * 2,
-        out_specs=[block_of(half, 0)] * 2,
-        scratch_shapes=[pltpu.VMEM((rows, tile), F32)],
-        compiler_params=pltpu.CompilerParams(vmem_limit_bytes=VMEM_BYTES),
-        cost_estimate=SMALL,
-        grid=(width // tile,),
+        in_specs=[pl.BlockSpec(memory_space=pltpu.SMEM), terms_spec(True), inside, inside],
+        out_specs=[inside] * 2,
+        scratch_shapes=[pltpu.VMEM((1, rows, width), BF), pltpu.SemaphoreType.DMA((1,))],
+        compiler_params=pltpu.CompilerParams(vmem_limit_bytes=RING_VMEM_BYTES),
+        cost_estimate=SMALL,
         name="ring_total",
-    )(core[None], x, *sent)
+    )(core[None], block[0], *sent)
 
 
 def combine(mine, got, core):
@@ -293,17 +306,37 @@
     )(core[None], mine, got)
 
 
-def place_pieces(ins, owners_ref, outs, sems, rows):
-    copies = []
-    wide = outs[0].shape[1]
-    for i, ref in enumerate(ins):
-        target = pl.ds(pl.multiple_of(owners_ref[i] * rows, 16), rows)
-        shift = wide if i > 0 and ref.shape[1] < ins[0].shape[1] and i == len(ins) - 1 else 0
-        for begin in range(0, ref.shape[1], wide):
-            to = outs[(begin + shift) // wide].at[target]
-            source = ref if ref.shape[1] == wide else ref.at[:, pl.ds(begin, wide)]
-            copies.append(pltpu.make_async_copy(source, to, sems.at[len(copies)]))
-    return copies
+def place(pieces, owners, chips):
+    rows, width = pieces[0].shape
+    half = width // 2
+    number = len(pieces)
+
+    def kernel(owners_ref, *refs):
+        ins, outs, sems = refs[:number], refs[number:-1], refs[-1]
+        copies = []
+        for i, ref in enumerate(ins):
+            target = pl.ds(pl.multiple_of(owners_ref[i] * rows, 16), rows)
+            for k, out_ref in enumerate(outs):
+                source = ref.at[:, pl.ds(k * half, half)]
+                copies.append(
+                    pltpu.make_async_copy(source, out_ref.at[target], sems.at[len(copies)])
+                )
+        for copy in copies:
+            copy.start()
+        for copy in copies:
+            copy.wait()
+
+    return pl.pallas_call(
+        kernel,
+        out_shape=[jax.ShapeDtypeStruct((chips * rows, half), BF)] * 2,
+        in_specs=[pl.BlockSpec(memory_space=pltpu.SMEM)]
+        + [pl.BlockSpec(memory_space=pl.ANY)] * number,
+        out_specs=[pl.BlockSpec(memory_space=pltpu.VMEM)] * 2,
+        scratch_shapes=[pltpu.SemaphoreType.DMA((2 * number,))],
+        compiler_params=pltpu.CompilerParams(vmem_limit_bytes=RING_VMEM_BYTES),
+        cost_estimate=SMALL,
+        name="place",
+    )(owners, *pieces)
 
 
 def assemble(pieces, owners):
@@ -311,9 +344,11 @@
     number = len(pieces)
 
     def kernel(owners_ref, *refs):
-        copies = place_pieces(
-            refs[:number], owners_ref, refs[number : number + 1], refs[number + 1], rows
-        )
+        out_ref, sems = refs[number:]
+        copies = []
+        for i in range(number):
+            target = out_ref.at[pl.ds(pl.multiple_of(owners_ref[i] * rows, 16), rows)]
+            copies.append(pltpu.make_async_copy(refs[i], target, sems.at[i]))
         for copy in copies:
             copy.start()
         for copy in copies:
@@ -344,23 +379,27 @@
     return jnp.concatenate([own_ref[at], got_ref[at]], axis=0)
 
 
-def expert_layers(own, got, pieces, owners, slots, rows_out):
+def expert_layers(own, got, state, last, last_owner, slots, rows_out):
     filled, d = own.shape[0], own.shape[1] // 2
-    rows, width = pieces[0].shape
-    count = len(pieces)
-    number = count - (pieces[-1].shape[1] < width)
+    width = 2 * state[0].shape[1]
     units = width // 2 // EXPERTS
     chips = slots.shape[0]
-
-    def kernel(owners_ref, slots_ref, own_ref, got_ref, *refs):
-        ins, mine_ref, away_ref = refs[:count], refs[count], refs[count + 1]
-        outs = refs[count + 2 : count + 2 + chips]
-        in_ref, down_ref, held_ref, sems, out_sems = refs[count + 2 + chips :]
-        copies = place_pieces(ins, owners_ref, (in_ref, down_ref), sems, rows)
+    number = len(last)
+
+    def kernel(last_ref, slots_ref, own_hbm, got_hbm, *refs):
+        ins, refs = refs[2 : 2 + number], refs[2 + number :]
+        mine_ref, away_ref, outs, refs = refs[0], refs[1], refs[2 : 2 + chips], refs[2 + chips :]
+        in_ref, down_ref, own_ref, got_ref, held_ref, sems, out_sems = refs
+        weights = (in_ref, down_ref)
+        pairs = ((own_hbm, own_ref), (got_hbm, got_ref))
+        copies = [pltpu.make_async_copy(*pair, sems.at[i]) for i, pair in enumerate(pairs)]
         for copy in copies:
             copy.start()
         for copy in copies:
             copy.wait()
+        for ref, weight in zip(ins, weights):
+            rows = ref.shape[0]
+            weight[pl.ds(pl.multiple_of(last_ref[0] * rows, 16), rows), :] = ref[...]
         for e in range(EXPERTS):
             cols = pl.ds(e * units, units)
             w_i, w_d = in_ref[:, cols], down_ref[:, cols]
@@ -386,24 +425,26 @@
             copy.wait()
 
     inside = pl.BlockSpec(memory_space=pltpu.VMEM)
-    anywhere = pl.BlockSpec(memory_space=pl.ANY)
+    outside = pl.BlockSpec(memory_space=pltpu.HBM)
     scalars = pl.BlockSpec(memory_space=pltpu.SMEM)
-    mine, away, *terms = pl.pallas_call(
+    mine, away, *terms, _, _ = pl.pallas_call(
         kernel,
         out_shape=[jax.ShapeDtypeStruct((filled, 2 * d), BF)] * 2
-        + [jax.ShapeDtypeStruct((rows_out, width), BF)] * chips,
-        in_specs=[scalars, scalars, inside, inside] + [anywhere] * count,
-        out_specs=[inside, inside] + [anywhere] * chips,
-        scratch_shapes=[pltpu.VMEM((number * rows, width // 2), BF)] * 2
+        + [jax.ShapeDtypeStruct((rows_out, width), BF)] * chips
+        + [jax.ShapeDtypeStruct((d, width // 2), BF)] * 2,
+        in_specs=[scalars] * 2 + [outside] * 2 + [inside] * (2 + number),
+        out_specs=[inside] * 2 + [outside] * chips + [inside] * 2,
+        input_output_aliases={4: 2 + chips, 5: 3 + chips},
+        scratch_shapes=[pltpu.VMEM((filled, 2 * d), BF)] * 2
         + [
             pltpu.VMEM((d, width), BF),
-            pltpu.SemaphoreType.DMA((2 * number,)),
+            pltpu.SemaphoreType.DMA((2,)),
             pltpu.SemaphoreType.DMA((chips,)),
         ],
         compiler_params=pltpu.CompilerParams(vmem_limit_bytes=EXPERT_VMEM_BYTES),
         cost_estimate=SMALL,
         name="expert_layers",
-    )(owners, slots, own, got, *pieces)
+    )(last_owner[None], slots, own, got, *state, *last)
     return mine, away, terms
 
 
@@ -439,12 +480,9 @@
     )
 
 
-def sum_chips(x):
-    step = 2
-    while step < lax.axis_size("dp"):
-        x = x + lax.ppermute(x, "dp", [(i, i ^ step) for i in range(lax.axis_size("dp"))])
-        step *= 2
-    return x
+def sum_pairs(x, step):
+    pairs = [(i, i ^ step) for i in range(lax.axis_size("dp"))]
+    return x + lax.ppermute(x, "dp", pairs)
 
 
 def rms_scale(rows):
@@ -572,7 +610,7 @@
     count, d = x.shape
 
     def kernel(x_ref, part_ref, other_ref, gain_ref, w_ref, expert_ref, flat_ref, g_ref,
-               hidden_ref, blocks_ref, scales_ref):
+               hidden_ref, out_ref, scales_ref, blocks_ref, sem):
         hidden = x_ref[...].astype(F32) + (part_ref[...].astype(F32) + other_ref[...].astype(F32))
         hidden_ref[...] = hidden
         r2 = lax.rsqrt(jnp.mean(hidden * hidden, axis=-1, keepdims=True) + EPS)
@@ -593,6 +631,9 @@
         blocks_ref[:, pl.ds(0, d)] = dot32(chosen, mixed.astype(BF), NN).astype(BF)
         grad_routed = (gate * g_ref[...].astype(F32)).astype(BF)
         blocks_ref[:, pl.ds(d, d)] = dot32(chosen, grad_routed, NN).astype(BF)
+        copy = pltpu.make_async_copy(blocks_ref, out_ref, sem)
+        copy.start()
+        copy.wait()
 
     inside = pl.BlockSpec(memory_space=pltpu.VMEM)
     return pl.pallas_call(
@@ -603,7 +644,8 @@
             jax.ShapeDtypeStruct((count, 128), F32),
         ),
         in_specs=[inside] * 8,
-        out_specs=(inside,) * 3,
+        out_specs=(inside, pl.BlockSpec(memory_space=pltpu.HBM), inside),
+        scratch_shapes=[pltpu.VMEM((EXPERTS * CAP, 2 * d), BF), pltpu.SemaphoreType.DMA],
         compiler_params=pltpu.CompilerParams(vmem_limit_bytes=VMEM_BYTES),
         cost_estimate=SMALL,
         name="route",
@@ -761,7 +803,7 @@
         x_low, attn_gain[None, :], attn_all, by_offset, seq_ids[:, None], seq_ids[None, :]
     )
     if not ring.long:
-        ring_b.step(other_a)
+        ring_b.step()
         ring_b.step(attn_part)
     attn_other = swap_tensor(attn_part)
     expert_col = expert_ids[:, 0]
@@ -775,17 +817,29 @@
     )
     if not ring.long:
         got_blocks = ring.other_core(own_blocks)
-        ring_b.step(got_blocks)
+        state = place(ring_b.pieces, ring_b.owners(0, ring.chips - 1), ring.chips)
+        last = ring_b.step(got_blocks)
         mine, away, terms = expert_layers(
-            own_blocks, got_blocks, ring_b.pieces, ring_b.owners(), ring.slot_chips(), 2 * shard
+            own_blocks,
+            got_blocks,
+            state,
+            last,
+            ring.chip_at(ring.chips // 2),
+            ring.slot_chips(),
+            2 * shard,
         )
         send = Scatter(ring, terms, 2 * shard)
         c1 = send.step()
     else:
-        whole = jnp.concatenate([in_all, down_all], axis=1)
         first = jnp.zeros((1,), jnp.int32)
         mine, away, terms = expert_layers(
-            own_blocks, ring.other_core(own_blocks), [whole], first, first, width
+            own_blocks,
+            ring.other_core(own_blocks),
+            (in_all, down_all),
+            (),
+            first[0],
+            first,
+            width,
         )
     got_sums = ring.other_core(away)
     mixed_low, routed_low, gains = rows_back(
@@ -827,12 +881,21 @@
     line = line + swap_tensor(line)
     line = line + ring.other_core(line)
     if not ring.long:
-        c4 = send.step(line, *a1)
+        c4 = send.step(*a1)
         a2 = send_a.step(*c3)
-        (line,) = after((line,), c4 + a2)
-        send_a.step(*c4)
-        send_a.step()
-    summed = sum_chips(line)
+        a3 = send_a.step(*c4)
+        (line,) = after((line,), c4)
+        line = sum_pairs(line, 2)
+        mine, away = ring_total(send.blocks(0)[0], send.sent, ring.core)
+        line = sum_pairs(line, 4)
+        (line,) = after((line,), a3)
+    else:
+        line = sum_pairs(sum_pairs(line, 2), 4)
+    step = 8
+    while step < ring.n:
+        line = sum_pairs(line, step)
+        step *= 2
+    summed = line
     grad_normed = own_rows(normed_low).astype(F32) + normed_other.astype(F32)
     x_own = block_in.astype(F32)
     scale_own = rms_scale(x_own)
@@ -849,7 +912,7 @@
         attn_mine = lax.psum_scatter(terms, "dp", scatter_dimension=0, tiled=True)
         attn_mine = attn_mine.astype(F32)
     else:
-        mine, away = ring_total(send.blocks(0)[0], send.sent, ring.core)
+        send_a.step(mine, grad_block)
         grad_w_in_mine, grad_w_down_mine = combine(mine, ring.other_core(away), ring.core)
         attn_mine = send_a.total()
     summed_rel = summed[: rel_bias.shape[1], : rel_bias.shape[0]].T

time: 215 us -> 197 us (0.916)
  waiting for transfers between devices: 86.5 us -> 68.7 us
  local copies, waits for them, and re-layouts: 33.7 us -> 29.1 us
    ppermute x14, waiting for transfers between devices: 39.9 us -> 35 us  [step(): lax.ppermute(r, 'dp', ring.right)]
    unnamed x113 -> x117, local copies, waits for them, and re-layouts: 23 us -> 18.4 us
    ppermute x7, waiting for transfers between devices: 21.8 us -> 17.3 us  [swap_tensor(): return lax.ppermute(x, 'tensor', [(0, 1), (1, 0)])]
    ppermute x1, waiting for transfers between devices: 4.09 us -> 0.01 us  [step(): lax.ppermute(r[:, :half], 'dp', ring.right)]
    ppermute x1, waiting for transfers between devices: 2.34 us -> 0.01 us  [step(): lax.ppermute(l[:, half:], 'dp', ring.left)]
  transfers between devices with their start and end apart: 48 -> 48, of which waited for: 31 -> 26; matrix products, arithmetic and copies ran while one was open for 9% -> 10% of each run, Pallas kernels for 10% -> 12%
where the time goes in v5:
time: 197 us
  waiting for transfers between devices  68.7 us (35%)
  starting transfers between devices  46.9 us (24%)
  Pallas kernels  39.3 us (20%)
  local copies, waits for them, and re-layouts  29.1 us (15%)
  other arithmetic  10.9 us (6%)
    ppermute x14, waiting for transfers between devices, step(): lax.ppermute(r, 'dp', ring.right)  35 us
    ppermute x14, starting transfers between devices, step(): lax.ppermute(r, 'dp', ring.right)  20.6 us
    unnamed x117, local copies, waits for them, and re-layouts  18.4 us
    ppermute x7, waiting for transfers between devices, swap_tensor(): return lax.ppermute(x, 'tensor', [(0, 1), (1, 0)])  17.3 us
    ppermute x14, waiting for transfers between devices, step(): lax.ppermute(l, 'dp', ring.left)  11.8 us
    ppermute x14, starting transfers between devices, step(): lax.ppermute(l, 'dp', ring.left)  9.8 us
    ppermute x7, starting transfers between devices, swap_tensor(): return lax.ppermute(x, 'tensor', [(0, 1), (1, 0)])  9.42 us
    pallas_call x1, Pallas kernels, expert_layers(): pl.pallas_call(kernel, out_shape=[jax.ShapeDtypeStruct((filled, 2 * d), B...  8.91 us
  transfers between devices with their start and end apart: 48, of which 26 were waited for; matrix products, arithmetic and copies ran while one was open for 10% of the time, Pallas kernels for 12%

profile of v5, /device:TPU:0, one launch (start us, length us, event | category | flops | bytes accessed | tf_op | source)
XLA Modules:
  0.0 196.6 jit_solution(6843275397908649934)
XLA Ops:
  2.4 3.0 %collective-permute-start.1 = (bf16[48,1536]{1,0:T(8,128)(2,1)S(1)}, bf16[48,1536]{1,0:T(8,128)(2,1)S(1)}, u32[]{:S(2)}, u32[]{:S(2)}) collective-permute-start(bf16[48,1536]{1,0:T(8,128)(2,1)S(1)} %constant_dynamic-update-slice_fusion.refs_0_), channel_id=1, source_target_pairs={{0,8},{2,10},{8,16},{10,18},{16,24},{18,26},{24,28},{26,30},{28,20... | collective-permute-start | bytes 442376 | tf_op jit(solution)/shard_map/ppermute | solution.py:86
  5.4 2.0 %collective-permute-start = (bf16[128,768]{1,0:T(8,128)(2,1)}, bf16[128,768]{1,0:T(8,128)(2,1)}, u32[]{:S(2)}, u32[]{:S(2)}) collective-permute-start(bf16[128,768]{1,0:T(8,128)(2,1)} %param.13), channel_id=1, source_target_pairs={{0,1},{1,0},{2,3},{3,2},{4,5},{5,4},{6,7},{7,6},{8,9},{9,8},{10,11... | collective-permute-start | bytes 589832 | tf_op jit(solution)/shard_map/ppermute | solution.py:474
  7.4 1.5 constant_dynamic-slice_fusion.4
  9.2 1.8 collective-permute-start.3
  11.1 1.6 collective-permute-start.10
  13.1 1.2 collective-permute-done.3.refs_3_
  14.3 1.8 collective-permute-start.5
  17.2 1.4 collective-permute-done.4.refs_4_
  19.4 1.8 collective-permute-start.7
  21.6 2.2 %collective-permute-done.6.refs_6_ = bf16[48,1536]{1,0:T(8,128)(2,1)S(1)} collective-permute-done((bf16[48,1536]{1,0:T(8,128)(2,1)S(1)}, bf16[48,1536]{1,0:T(8,128)(2,1)S(1)}, u32[]{:S(2)}, u32[]{:S(2)}) %collective-permute-start.6) | collective-permute-done | bytes 147488 | tf_op jit(solution)/shard_map/ppermute | solution.py:86
  24.6 2.3 %assemble.1.own_ref = bf16[384,1536]{1,0:T(8,128)(2,1)S(1)} custom-call(s32[8]{0:T(128)S(1)} %stack.30.owners_ref, bf16[48,1536]{1,0:T(8,128)(2,1)S(1)} %constant_dynamic-update-slice_fusion.refs_0_, bf16[48,1536]{1,0:T(8,128)(2,1)S(1)} %collective-permute-done.1.refs_1_, bf16[48,1536]{1,0:T(8,128)(2,1)S(1)} %collective-permute-done.2.refs_2_, ...), custom_call_target="tpu_custom_call" | custom-call | flops 1 | bytes 1 | tf_op jit(solution)/shard_map/assemble/pallas_call | solution.py:357
  27.4 1.2 maximum_select_fusion.refs_0_
  28.7 1.9 collective-permute-start.13
  32.5 1.3 maximum_select_fusion.1.x_ref
  34.9 1.3 copy-done.7
  36.1 1.3 copy-done.19
  38.3 3.5 %attention_forward.1 = (bf16[256,768]{1,0:T(8,128)(2,1)S(1)}, f32[256,1]{1,0:T(8,128)}, bf16[256,1152]{1,0:T(8,128)(2,1)S(1)}, f32[6,256,256]{2,1,0:T(8,128)S(1)...) custom-call(bf16[256,768]{1,0:T(8,128)(2,1)S(1)} %maximum_select_fusion.1.x_ref, ...), custom_call_target="tpu_custom_call" | custom-call | flops 1 | bytes 1 | tf_op jit(solution)/shard_map/attention_forward/pallas_call | solution.py:539
  44.1 1.8 collective-permute-start.9
  46.6 1.6 collective-permute-start.15
  48.7 1.3 maximum_select_fusion.2.g_ref
  50.0 5.2 %collective-permute-done.9.other_ref = bf16[256,768]{1,0:T(8,128)(2,1)S(1)} collective-permute-done((bf16[256,768]{1,0:T(8,128)(2,1)S(1)}, bf16[256,768]{1,0:T(8,128)(2,1)S(1)}, u32[]{:S(2)}, u32[]{:S(2)}) %collective-permute-start.9) | collective-permute-done | bytes 393248 | tf_op jit(solution)/shard_map/ppermute | solution.py:474
  55.2 1.1 route.1
  58.2 3.6 %collective-permute-done.15.refs_3_ = bf16[96,3072]{1,0:T(8,128)(2,1)S(1)} collective-permute-done((bf16[96,3072]{1,0:T(8,128)(2,1)}, bf16[96,3072]{1,0:T(8,128)(2,1)S(1)}, u32[]{:S(2)}, u32[]{:S(2)}) %collective-permute-start.15) | collective-permute-done | bytes 589856 | tf_op jit(solution)/shard_map/ppermute | solution.py:86
  61.7 1.3 collective-permute-done.16.refs_4_
  63.0 1.6 collective-permute-start.17
  66.7 10.0 %collective-permute-done.17.refs_5_ = bf16[96,3072]{1,0:T(8,128)(2,1)S(1)} collective-permute-done((bf16[96,3072]{1,0:T(8,128)(2,1)S(1)}, bf16[96,3072]{1,0:T(8,128)(2,1)S(1)}, u32[]{:S(2)}, u32[]{:S(2)}) %collective-permute-start.17) | collective-permute-done | bytes 589856 | tf_op jit(solution)/shard_map/ppermute | solution.py:86
  76.7 2.1 %collective-permute-done.18.refs_6_ = bf16[96,3072]{1,0:T(8,128)(2,1)S(1)} collective-permute-done((bf16[96,3072]{1,0:T(8,128)(2,1)S(1)}, bf16[96,3072]{1,0:T(8,128)(2,1)S(1)}, u32[]{:S(2)}, u32[]{:S(2)}) %collective-permute-start.18) | collective-permute-done | bytes 589856 | tf_op jit(solution)/shard_map/ppermute | solution.py:86
  81.4 1.6 collective-permute-start.19
  84.4 1.1 copy-done.9
  85.4 1.1 copy-done.15
  86.5 1.1 copy-done.17
  87.6 1.1 copy-done.25
  88.6 1.1 copy-done.27
  89.7 2.0 %place.1 = (bf16[768,1536]{1,0:T(8,128)(2,1)S(1)}, bf16[768,1536]{1,0:T(8,128)(2,1)S(1)}) custom-call(s32[7]{0:T(128)S(1)} %stack.32.owners_ref, bf16[96,3072]{1,0:T(8,128)(2,1)S(1)} %copy-done.9, bf16[96,3072]{1,0:T(8,128)(2,1)} %collective-permute-done.13.refs_1_, bf16[96,3072]{1,0:T(8,128)(2,1)} %collective-permute-done.14.refs_2_, ...), custom_call_target="tpu_custom_call" | custom-call | flops 1 | bytes 1 | tf_op jit(solution)/shard_map/place/pallas_call | solution.py:329
  91.8 8.9 %expert_layers.1 = (bf16[352,1536]{1,0:T(8,128)(2,1)S(1)}, bf16[352,1536]{1,0:T(8,128)(2,1)S(1)}, bf16[96,3072]{1,0:T(8,128)(2,1)S(1)}, bf16[96,3072]{1,0:T(8,12...) custom-call(s32[1]{0:T(128)} %bitcast.8.last_ref, ...), custom_call_target="tpu_custom_call", output_to_operand_aliasing={{10}: (4, {}), {11}: (5, {})} | custom-call | flops 1 | bytes 1 | tf_op jit(solution)/shard_map/expert_layers/pallas_call | solution.py:430
  101.0 1.6 collective-permute-start.24
  103.5 1.1 rows_back.1
  105.4 5.0 %collective-permute-done.24.refs_2_ = bf16[96,1536]{1,0:T(8,128)(2,1)S(1)} collective-permute-done((bf16[96,1536]{1,0:T(8,128)(2,1)S(1)}, bf16[96,1536]{1,0:T(8,128)(2,1)S(1)}, u32[]{:S(2)}, u32[]{:S(2)}) %collective-permute-start.24) | collective-permute-done | bytes 294944 | tf_op jit(solution)/shard_map/ppermute | solution.py:126
  110.5 1.3 collective-permute-done.25.refs_3_
  112.2 1.5 collective-permute-start.29
  115.3 8.8 %collective-permute-done.23.other_ref = bf16[256,768]{1,0:T(8,128)(2,1)S(1)} collective-permute-done((bf16[256,768]{1,0:T(8,128)(2,1)S(1)}, bf16[256,768]{1,0:T(8,128)(2,1)S(1)}, u32[]{:S(2)}, u32[]{:S(2)}) %collective-permute-start.23) | collective-permute-done | bytes 393248 | tf_op jit(solution)/shard_map/ppermute | solution.py:474
  124.2 4.7 %attention_backward.1 = (f32[256,768]{1,0:T(8,128)S(1)}, bf16[256,768]{1,0:T(8,128)(2,1)S(1)}, bf16[256,1152]{1,0:T(8,128)(2,1)S(1)}, f32[6,512]{1,0:T(8,128)S(1)}) custom-call(bf16[256,768]{1,0:T(8,128)(2,1)S(1)} %get-tuple-element.96.low_ref, bf16[256,768]{1,0:T(8,128)(2,1)S(1)} %collective-permute-done.23.other_ref, f32[256,768]{1,0:T(8,128)S(1)} %copy-done.4, ...), custom_call_target="tpu_custom_call" | custom-call | flops 1 | bytes 1 | tf_op jit(solution)/shard_map/attention_backward/pallas_call | solution.py:592
  128.9 2.6 %outer.1 = (bf16[384,1536]{1,0:T(8,128)(2,1)S(1)}, bf16[384,1536]{1,0:T(8,128)(2,1)}) custom-call(s32[16]{0:T(128)S(1)} %pad_add_fusion.owners_ref, bf16[256,768]{1,0:T(8,128)(2,1)S(1)} %copy-done.42, bf16[256,1152]{1,0:T(8,128)(2,1)S(1)} %get-tuple-element.122.grad_ref.refs_1_, bf16[256,768]{1,0:T(8,128)(2,1)S(1)} %get-tuple-element.123.refs_2_, ...), custom_call_target="tpu_custom_call" | custom-call | flops 1 | bytes 1 | tf_op jit(solution)/shard_map/outer/pallas_call | solution.py:162
  131.6 1.5 ring_add.7
  133.1 1.5 collective-permute-start.31
  136.9 1.5 collective-permute-start.34
  139.0 10.5 %collective-permute-done.31.refs_2_ = bf16[96,3072]{1,0:T(8,128)(2,1)S(1)} collective-permute-done((bf16[96,3072]{1,0:T(8,128)(2,1)}, bf16[96,3072]{1,0:T(8,128)(2,1)S(1)}, u32[]{:S(2)}, u32[]{:S(2)}) %collective-permute-start.31) | collective-permute-done | bytes 589856 | tf_op jit(solution)/shard_map/ppermute | solution.py:126
  149.5 1.6 collective-permute-done.32.refs_3_
  151.9 2.6 %ring_add.8 = (bf16[96,3072]{1,0:T(8,128)(2,1)}, bf16[96,3072]{1,0:T(8,128)(2,1)}) custom-call(bf16[96,3072]{1,0:T(8,128)(2,1)S(1)} %copy-done.33, bf16[96,3072]{1,0:T(8,128)(2,1)S(1)} %copy-done.35, bf16[96,3072]{1,0:T(8,128)(2,1)S(1)} %collective-permute-done.31.refs_2_, bf16[96,3072]{1,0:T(8,128)(2,1)} %collective-permute-done.32.refs_3_), custom_call_target="tpu_custom_call" | custom-call | flops 1 | bytes 1 | tf_op jit(solution)/shard_map/ring_add/pallas_call | solution.py:243
  155.2 1.4 collective-permute-start.37
  159.2 1.1 collective-permute-start.27
  160.3 3.3 %collective-permute-done.27 = f32[40,128]{1,0:T(8,128)S(1)} collective-permute-done((f32[40,128]{1,0:T(8,128)S(1)}, f32[40,128]{1,0:T(8,128)S(1)}, u32[]{:S(2)}, u32[]{:S(2)}) %collective-permute-start.27) | collective-permute-done | bytes 20512 | tf_op jit(solution)/shard_map/ppermute | solution.py:474
  166.3 1.4 collective-permute-start.41
  167.7 1.7 add_convert_fusion
  169.4 1.1 collective-permute-done.36.r_ref
  170.8 1.4 collective-permute-start.38
  174.5 1.4 collective-permute-start.43
  176.6 3.3 %collective-permute-done.39 = f32[40,128]{1,0:T(8,128)S(1)} collective-permute-done((f32[40,128]{1,0:T(8,128)S(1)}, f32[40,128]{1,0:T(8,128)S(1)}, u32[]{:S(2)}, u32[]{:S(2)}) %collective-permute-start.39) | collective-permute-done | bytes 20512 | tf_op jit(solution)/shard_map/ppermute | solution.py:485
  181.7 2.3 %ring_total.1 = (f32[48,3072]{1,0:T(8,128)S(1)}, f32[48,3072]{1,0:T(8,128)}) custom-call(s32[1]{0:T(128)} %bitcast.core_ref, bf16[96,3072]{1,0:T(8,128)(2,1)S(1)} %copy-done.29, bf16[96,3072]{1,0:T(8,128)(2,1)} %collective-permute-done.36.r_ref, bf16[96,3072]{1,0:T(8,128)(2,1)} %collective-permute-done.37.l_ref), custom_call_target="tpu_custom_call" | custom-call | flops 1 | bytes 1 | tf_op jit(solution)/shard_map/ring_total/pallas_call | solution.py:273
  184.1 1.6 ring_add.11
  186.3 1.4 collective-permute-start.46
  189.6 2.7 %collective-permute-done.45 = bf16[48,1536]{1,0:T(8,128)(2,1)} collective-permute-done((bf16[48,1536]{1,0:T(8,128)(2,1)}, bf16[48,1536]{1,0:T(8,128)(2,1)}, u32[]{:S(2)}, u32[]{:S(2)}) %collective-permute-start.45) | collective-permute-done | bytes 147488 | tf_op jit(solution)/shard_map/ppermute | solution.py:126
  192.9 1.1 convert_add_fusion
  195.4 1.2 combine.1
  (223 shorter events, 44.3 us)
Async XLA Ops:
  0.6 20.6 %copy-start = (f32[32,12]{0,1:T(8,128)S(1)}, f32[32,12]{0,1:T(8,128)}, u32[]{:S(2)}) copy-start(f32[32,12]{0,1:T(8,128)} %param.17) | copy-start | bytes 4612
  2.4 6.8 %collective-permute-start.1 = (bf16[48,1536]{1,0:T(8,128)(2,1)S(1)}, bf16[48,1536]{1,0:T(8,128)(2,1)S(1)}, u32[]{:S(2)}, u32[]{:S(2)}) collective-permute-start(bf16[48,1536]{1,0:T(8,128)(2,1)S(1)} %constant_dynamic-update-slice_fusion.refs_0_), channel_id=1, source_target_pairs={{0,8},{2,10},{8,16},{10,18},{16,24},{18,26},{24,28},{26,30},{28,20... | collective-permute-start | bytes 442376 | tf_op jit(solution)/shard_map/ppermute | solution.py:86
  5.4 7.3 %collective-permute-start.2 = (bf16[48,1536]{1,0:T(8,128)(2,1)S(1)}, bf16[48,1536]{1,0:T(8,128)(2,1)S(1)}, u32[]{:S(2)}, u32[]{:S(2)}) collective-permute-start(bf16[48,1536]{1,0:T(8,128)(2,1)S(1)} %constant_dynamic-update-slice_fusion.refs_0_), channel_id=1, source_target_pairs={{8,0},{10,2},{16,8},{18,10},{24,16},{26,18},{28,24},{30,26},{20,28... | collective-permute-start | bytes 442376 | tf_op jit(solution)/shard_map/ppermute | solution.py:86
  5.4 23.3 %collective-permute-start = (bf16[128,768]{1,0:T(8,128)(2,1)}, bf16[128,768]{1,0:T(8,128)(2,1)}, u32[]{:S(2)}, u32[]{:S(2)}) collective-permute-start(bf16[128,768]{1,0:T(8,128)(2,1)} %param.13), channel_id=1, source_target_pairs={{0,1},{1,0},{2,3},{3,2},{4,5},{5,4},{6,7},{7,6},{8,9},{9,8},{10,11... | collective-permute-start | bytes 589832 | tf_op jit(solution)/shard_map/ppermute | solution.py:474
  7.4 8.8 %copy-start.51 = (s32[256,1]{0,1:T(1,128)S(1)}, s32[256,1]{0,1:T(1,128)}, u32[]{:S(2)}) copy-start(s32[256,1]{0,1:T(1,128)} %param.23) | copy-start | bytes 3076
  7.4 13.9 %copy-start.53 = (s32[511]{0:T(512)S(1)}, s32[511]{0:T(512)}, u32[]{:S(2)}) copy-start(s32[511]{0:T(512)} %param.24) | copy-start | bytes 6136
  9.2 5.1 %collective-permute-start.3 = (bf16[48,1536]{1,0:T(8,128)(2,1)S(1)}, bf16[48,1536]{1,0:T(8,128)(2,1)S(1)}, u32[]{:S(2)}, u32[]{:S(2)}) collective-permute-start(bf16[48,1536]{1,0:T(8,128)(2,1)S(1)} %collective-permute-done.1.refs_1_), channel_id=1, source_target_pairs={{0,8},{2,10},{8,16},{10,18},{16,24},{18,26},{24,28},{26,30},{28,20... | collective-permute-start | bytes 442376 | tf_op jit(solution)/shard_map/ppermute | solution.py:86
  11.0 16.4 %collective-permute-start.12 = (bf16[48,3072]{1,0:T(8,128)(2,1)S(1)}, bf16[48,3072]{1,0:T(8,128)(2,1)}, u32[]{:S(2)}, u32[]{:S(2)}) collective-permute-start(bf16[48,3072]{1,0:T(8,128)(2,1)S(1)} %pad_maximum_fusion), channel_id=1, source_target_pairs={{0,2},{2,0},{4,6},{6,4},{8,10},{10,8},{12,14},{14,12},{16,18},{18,... | collective-permute-start | bytes 884744 | tf_op jit(solution)/shard_map/ppermute | solution.py:57
  11.1 17.6 %collective-permute-start.10 = (bf16[128,768]{1,0:T(8,128)(2,1)}, bf16[128,768]{1,0:T(8,128)(2,1)}, u32[]{:S(2)}, u32[]{:S(2)}) collective-permute-start(bf16[128,768]{1,0:T(8,128)(2,1)} %param.25), channel_id=1, source_target_pairs={{0,1},{1,0},{2,3},{3,2},{4,5},{5,4},{6,7},{7,6},{8,9},{9,8},{10,11... | collective-permute-start | bytes 589832 | tf_op jit(solution)/shard_map/ppermute | solution.py:474
  12.7 5.9 %collective-permute-start.4 = (bf16[48,1536]{1,0:T(8,128)(2,1)S(1)}, bf16[48,1536]{1,0:T(8,128)(2,1)S(1)}, u32[]{:S(2)}, u32[]{:S(2)}) collective-permute-start(bf16[48,1536]{1,0:T(8,128)(2,1)S(1)} %collective-permute-done.2.refs_2_), channel_id=1, source_target_pairs={{8,0},{10,2},{16,8},{18,10},{24,16},{26,18},{28,24},{30,26},{20,28... | collective-permute-start | bytes 442376 | tf_op jit(solution)/shard_map/ppermute | solution.py:86
  14.3 5.1 %collective-permute-start.5 = (bf16[48,1536]{1,0:T(8,128)(2,1)S(1)}, bf16[48,1536]{1,0:T(8,128)(2,1)S(1)}, u32[]{:S(2)}, u32[]{:S(2)}) collective-permute-start(bf16[48,1536]{1,0:T(8,128)(2,1)S(1)} %collective-permute-done.3.refs_3_), channel_id=1, source_target_pairs={{0,8},{2,10},{8,16},{10,18},{16,24},{18,26},{24,28},{26,30},{28,20... | collective-permute-start | bytes 442376 | tf_op jit(solution)/shard_map/ppermute | solution.py:86
  18.6 5.2 %collective-permute-start.6 = (bf16[48,1536]{1,0:T(8,128)(2,1)S(1)}, bf16[48,1536]{1,0:T(8,128)(2,1)S(1)}, u32[]{:S(2)}, u32[]{:S(2)}) collective-permute-start(bf16[48,1536]{1,0:T(8,128)(2,1)S(1)} %collective-permute-done.4.refs_4_), channel_id=1, source_target_pairs={{8,0},{10,2},{16,8},{18,10},{24,16},{26,18},{28,24},{30,26},{20,28... | collective-permute-start | bytes 442376 | tf_op jit(solution)/shard_map/ppermute | solution.py:86
  19.4 5.1 %collective-permute-start.7 = (bf16[48,1536]{1,0:T(8,128)(2,1)S(1)}, bf16[48,1536]{1,0:T(8,128)(2,1)S(1)}, u32[]{:S(2)}, u32[]{:S(2)}) collective-permute-start(bf16[48,1536]{1,0:T(8,128)(2,1)S(1)} %collective-permute-done.5.refs_5_), channel_id=1, source_target_pairs={{0,8},{2,10},{8,16},{10,18},{16,24},{18,26},{24,28},{26,30},{28,20... | collective-permute-start | bytes 442376 | tf_op jit(solution)/shard_map/ppermute | solution.py:93
  26.9 6.9 %collective-permute-start.8 = (bf16[384,1536]{1,0:T(8,128)(2,1)S(1)}, bf16[384,1536]{1,0:T(8,128)(2,1)S(1)}, u32[]{:S(2)}, u32[]{:S(2)}) collective-permute-start(bf16[384,1536]{1,0:T(8,128)(2,1)S(1)} %assemble.1.own_ref), channel_id=1, source_target_pairs={{0,2},{2,0},{4,6},{6,4},{8,10},{10,8},{12,14},{14,12},{16,18},{18,... | collective-permute-start | bytes 3538952 | tf_op jit(solution)/shard_map/ppermute | solution.py:57
  28.6 9.0 %copy-start.8 = (bf16[96,3072]{1,0:T(8,128)(2,1)}, bf16[96,3072]{1,0:T(8,128)(2,1)S(1)}, u32[]{:S(2)}) copy-start(bf16[96,3072]{1,0:T(8,128)(2,1)S(1)} %maximum_select_fusion.refs_0_) | copy-start | bytes 1769476
  28.7 17.9 %collective-permute-start.13 = (bf16[96,3072]{1,0:T(8,128)(2,1)S(1)}, bf16[96,3072]{1,0:T(8,128)(2,1)}, u32[]{:S(2)}, u32[]{:S(2)}) collective-permute-start(bf16[96,3072]{1,0:T(8,128)(2,1)S(1)} %maximum_select_fusion.refs_0_), channel_id=1, source_target_pairs={{0,8},{2,10},{8,16},{10,18},{16,24},{18,26},{24,28},{26,30},{28,20... | collective-permute-start | bytes 1769480 | tf_op jit(solution)/shard_map/ppermute | solution.py:86
  30.6 17.7 %collective-permute-start.14 = (bf16[96,3072]{1,0:T(8,128)(2,1)S(1)}, bf16[96,3072]{1,0:T(8,128)(2,1)}, u32[]{:S(2)}, u32[]{:S(2)}) collective-permute-start(bf16[96,3072]{1,0:T(8,128)(2,1)S(1)} %maximum_select_fusion.refs_0_), channel_id=1, source_target_pairs={{8,0},{10,2},{16,8},{18,10},{24,16},{26,18},{28,24},{30,26},{20,28... | collective-permute-start | bytes 1769480 | tf_op jit(solution)/shard_map/ppermute | solution.py:86
  37.6 86.5 %copy-start.1 = (bf16[768,1536]{1,0:T(8,128)(2,1)}, bf16[768,1536]{1,0:T(8,128)(2,1)S(1)}, u32[]{:S(2)}) copy-start(bf16[768,1536]{1,0:T(8,128)(2,1)S(1)} %interleave.1.w_ref) | copy-start | bytes 7077892
  44.1 12.1 %copy-start.12 = (f32[6,256,256]{2,1,0:T(8,128)}, f32[6,256,256]{2,1,0:T(8,128)S(1)}, u32[]{:S(2)}) copy-start(f32[6,256,256]{2,1,0:T(8,128)S(1)} %get-tuple-element.102.p_ref) | copy-start | bytes 4718596
  44.1 11.0 %copy-start.47 = (f32[768,2]{0,1:T(2,128)S(1)}, f32[768,2]{0,1:T(2,128)}, u32[]{:S(2)}) copy-start(f32[768,2]{0,1:T(2,128)} %param.19) | copy-start | bytes 18436
  44.1 11.0 %collective-permute-start.9 = (bf16[256,768]{1,0:T(8,128)(2,1)S(1)}, bf16[256,768]{1,0:T(8,128)(2,1)S(1)}, u32[]{:S(2)}, u32[]{:S(2)}) collective-permute-start(bf16[256,768]{1,0:T(8,128)(2,1)S(1)} %get-tuple-element.81.part_ref), channel_id=1, source_target_pairs={{0,1},{1,0},{2,3},{3,2},{4,5},{5,4},{6,7},{7,6},{8,9},{9,8},{10,11... | collective-permute-start | bytes 1179656 | tf_op jit(solution)/shard_map/ppermute | solution.py:474
  46.6 15.1 %collective-permute-start.15 = (bf16[96,3072]{1,0:T(8,128)(2,1)}, bf16[96,3072]{1,0:T(8,128)(2,1)S(1)}, u32[]{:S(2)}, u32[]{:S(2)}) collective-permute-start(bf16[96,3072]{1,0:T(8,128)(2,1)} %collective-permute-done.13.refs_1_), channel_id=1, source_target_pairs={{0,8},{2,10},{8,16},{10,18},{16,24},{18,26},{24,28},{26,30},{28,20... | collective-permute-start | bytes 1769480 | tf_op jit(solution)/shard_map/ppermute | solution.py:86
  48.2 14.8 %collective-permute-start.16 = (bf16[96,3072]{1,0:T(8,128)(2,1)}, bf16[96,3072]{1,0:T(8,128)(2,1)S(1)}, u32[]{:S(2)}, u32[]{:S(2)}) collective-permute-start(bf16[96,3072]{1,0:T(8,128)(2,1)} %collective-permute-done.14.refs_2_), channel_id=1, source_target_pairs={{8,0},{10,2},{16,8},{18,10},{24,16},{26,18},{28,24},{30,26},{20,28... | collective-permute-start | bytes 1769480 | tf_op jit(solution)/shard_map/ppermute | solution.py:86
  57.2 21.7 %collective-permute-start.11 = (bf16[352,1536]{1,0:T(8,128)(2,1)S(1)}, bf16[352,1536]{1,0:T(8,128)(2,1)S(1)}, u32[]{:S(2)}, u32[]{:S(2)}) collective-permute-start(bf16[352,1536]{1,0:T(8,128)(2,1)S(1)} %get-tuple-element.83.own_hbm), channel_id=1, source_target_pairs={{0,2},{2,0},{4,6},{6,4},{8,10},{10,8},{12,14},{14,12},{16,18},{18,... | collective-permute-start | bytes 3244040 | tf_op jit(solution)/shard_map/ppermute | solution.py:57
  63.0 13.7 %collective-permute-start.17 = (bf16[96,3072]{1,0:T(8,128)(2,1)S(1)}, bf16[96,3072]{1,0:T(8,128)(2,1)S(1)}, u32[]{:S(2)}, u32[]{:S(2)}) collective-permute-start(bf16[96,3072]{1,0:T(8,128)(2,1)S(1)} %collective-permute-done.15.refs_3_), channel_id=1, source_target_pairs={{0,8},{2,10},{8,16},{10,18},{16,24},{18,26},{24,28},{26,30},{28,20... | collective-permute-start | bytes 1769480 | tf_op jit(solution)/shard_map/ppermute | solution.py:86
  65.4 13.4 %collective-permute-start.18 = (bf16[96,3072]{1,0:T(8,128)(2,1)S(1)}, bf16[96,3072]{1,0:T(8,128)(2,1)S(1)}, u32[]{:S(2)}, u32[]{:S(2)}) collective-permute-start(bf16[96,3072]{1,0:T(8,128)(2,1)S(1)} %collective-permute-done.16.refs_4_), channel_id=1, source_target_pairs={{8,0},{10,2},{16,8},{18,10},{24,16},{26,18},{28,24},{30,26},{20,28... | collective-permute-start | bytes 1769480 | tf_op jit(solution)/shard_map/ppermute | solution.py:86
  81.4 10.3 %collective-permute-start.19 = (bf16[96,1536]{1,0:T(8,128)(2,1)}, bf16[96,1536]{1,0:T(8,128)(2,1)}, u32[]{:S(2)}, u32[]{:S(2)}) collective-permute-start(bf16[96,1536]{1,0:T(8,128)(2,1)} %slice.47), channel_id=1, source_target_pairs={{0,8},{2,10},{8,16},{10,18},{16,24},{18,26},{24,28},{26,30},{28,20... | collective-permute-start | bytes 884744 | tf_op jit(solution)/shard_map/ppermute | solution.py:89
  83.7 8.0 %collective-permute-start.20 = (bf16[96,1536]{1,0:T(8,128)(2,1)}, bf16[96,1536]{1,0:T(8,128)(2,1)}, u32[]{:S(2)}, u32[]{:S(2)}) collective-permute-start(bf16[96,1536]{1,0:T(8,128)(2,1)} %slice.48), channel_id=1, source_target_pairs={{8,0},{10,2},{16,8},{18,10},{24,16},{26,18},{28,24},{30,26},{20,28... | collective-permute-start | bytes 884744 | tf_op jit(solution)/shard_map/ppermute | solution.py:90
  91.8 11.7 %copy-start.4 = (f32[256,768]{1,0:T(8,128)S(1)}, f32[256,768]{1,0:T(8,128)}, u32[]{:S(2)}) copy-start(f32[256,768]{1,0:T(8,128)} %copy-done.3) | copy-start | bytes 2359300
  91.8 11.7 %copy-start.36 = (s32[256,1]{1,0:T(8,128)S(1)}, s32[256,1]{1,0:T(8,128)}, u32[]{:S(2)}) copy-start(s32[256,1]{1,0:T(8,128)} %get-tuple-element.196.flat_ref) | copy-start | bytes 3076
  100.8 2.8 %collective-permute-start.21 = (bf16[352,1536]{1,0:T(8,128)(2,1)S(1)}, bf16[352,1536]{1,0:T(8,128)(2,1)S(1)}, u32[]{:S(2)}, u32[]{:S(2)}) collective-permute-start(bf16[352,1536]{1,0:T(8,128)(2,1)S(1)} %get-tuple-element.93), channel_id=1, source_target_pairs={{0,2},{2,0},{4,6},{6,4},{8,10},{10,8},{12,14},{14,12},{16,18},{18,... | collective-permute-start | bytes 3244040 | tf_op jit(solution)/shard_map/ppermute | solution.py:57
  101.0 9.5 %collective-permute-start.24 = (bf16[96,1536]{1,0:T(8,128)(2,1)S(1)}, bf16[96,1536]{1,0:T(8,128)(2,1)S(1)}, u32[]{:S(2)}, u32[]{:S(2)}) collective-permute-start(bf16[96,1536]{1,0:T(8,128)(2,1)S(1)} %get-tuple-element.98), channel_id=1, source_target_pairs={{0,8},{2,10},{8,16},{10,18},{16,24},{18,26},{24,28},{26,30},{28,20... | collective-permute-start | bytes 884744 | tf_op jit(solution)/shard_map/ppermute | solution.py:126
  102.6 9.1 %collective-permute-start.25 = (bf16[96,1536]{1,0:T(8,128)(2,1)S(1)}, bf16[96,1536]{1,0:T(8,128)(2,1)S(1)}, u32[]{:S(2)}, u32[]{:S(2)}) collective-permute-start(bf16[96,1536]{1,0:T(8,128)(2,1)S(1)} %get-tuple-element.99), channel_id=1, source_target_pairs={{8,0},{10,2},{16,8},{18,10},{24,16},{26,18},{28,24},{30,26},{20,28... | collective-permute-start | bytes 884744 | tf_op jit(solution)/shard_map/ppermute | solution.py:126
  103.5 20.6 %copy-start.31 = (bf16[256,1152]{1,0:T(8,128)(2,1)S(1)}, bf16[256,1152]{1,0:T(8,128)(2,1)}, u32[]{:S(2)}) copy-start(bf16[256,1152]{1,0:T(8,128)(2,1)} %copy-done.30) | copy-start | bytes 1769476
  105.4 18.7 %copy-start.13 = (f32[6,256,256]{2,1,0:T(8,128)S(1)}, f32[6,256,256]{2,1,0:T(8,128)}, u32[]{:S(2)}) copy-start(f32[6,256,256]{2,1,0:T(8,128)} %copy-done.12) | copy-start | bytes 4718596
  112.2 16.7 %collective-permute-start.29 = (bf16[96,3072]{1,0:T(8,128)(2,1)S(1)}, bf16[96,3072]{1,0:T(8,128)(2,1)S(1)}, u32[]{:S(2)}, u32[]{:S(2)}) collective-permute-start(bf16[96,3072]{1,0:T(8,128)(2,1)S(1)} %get-tuple-element.117), channel_id=1, source_target_pairs={{0,8},{2,10},{8,16},{10,18},{16,24},{18,26},{24,28},{26,30},{28,20... | collective-permute-start | bytes 1769480 | tf_op jit(solution)/shard_map/ppermute | solution.py:126
  113.7 15.1 %collective-permute-start.30 = (bf16[96,3072]{1,0:T(8,128)(2,1)S(1)}, bf16[96,3072]{1,0:T(8,128)(2,1)S(1)}, u32[]{:S(2)}, u32[]{:S(2)}) collective-permute-start(bf16[96,3072]{1,0:T(8,128)(2,1)S(1)} %get-tuple-element.118), channel_id=1, source_target_pairs={{8,0},{10,2},{16,8},{18,10},{24,16},{26,18},{28,24},{30,26},{20,28... | collective-permute-start | bytes 1769480 | tf_op jit(solution)/shard_map/ppermute | solution.py:126
  114.3 9.9 %collective-permute-start.23 = (bf16[256,768]{1,0:T(8,128)(2,1)S(1)}, bf16[256,768]{1,0:T(8,128)(2,1)S(1)}, u32[]{:S(2)}, u32[]{:S(2)}) collective-permute-start(bf16[256,768]{1,0:T(8,128)(2,1)S(1)} %get-tuple-element.96.low_ref), channel_id=1, source_target_pairs={{0,1},{1,0},{2,3},{3,2},{4,5},{5,4},{6,7},{7,6},{8,9},{9,8},{10,11... | collective-permute-start | bytes 1179656 | tf_op jit(solution)/shard_map/ppermute | solution.py:474
  131.5 4.8 %collective-permute-start.33 = (bf16[384,1536]{1,0:T(8,128)(2,1)}, bf16[384,1536]{1,0:T(8,128)(2,1)S(1)}, u32[]{:S(2)}, u32[]{:S(2)}) collective-permute-start(bf16[384,1536]{1,0:T(8,128)(2,1)} %get-tuple-element.126), channel_id=1, source_target_pairs={{0,2},{2,0},{4,6},{6,4},{8,10},{10,8},{12,14},{14,12},{16,18},{18,... | collective-permute-start | bytes 3538952 | tf_op jit(solution)/shard_map/ppermute | solution.py:57
  133.1 16.4 %collective-permute-start.31 = (bf16[96,3072]{1,0:T(8,128)(2,1)}, bf16[96,3072]{1,0:T(8,128)(2,1)S(1)}, u32[]{:S(2)}, u32[]{:S(2)}) collective-permute-start(bf16[96,3072]{1,0:T(8,128)(2,1)} %get-tuple-element.119), channel_id=1, source_target_pairs={{0,8},{2,10},{8,16},{10,18},{16,24},{18,26},{24,28},{26,30},{28,20... | collective-permute-start | bytes 1769480 | tf_op jit(solution)/shard_map/ppermute | solution.py:126
  134.6 16.5 %collective-permute-start.32 = (bf16[96,3072]{1,0:T(8,128)(2,1)}, bf16[96,3072]{1,0:T(8,128)(2,1)}, u32[]{:S(2)}, u32[]{:S(2)}) collective-permute-start(bf16[96,3072]{1,0:T(8,128)(2,1)} %get-tuple-element.120), channel_id=1, source_target_pairs={{8,0},{10,2},{16,8},{18,10},{24,16},{26,18},{28,24},{30,26},{20,28... | collective-permute-start | bytes 1769480 | tf_op jit(solution)/shard_map/ppermute | solution.py:126
  136.4 15.5 %copy-start.33 = (bf16[96,3072]{1,0:T(8,128)(2,1)S(1)}, bf16[96,3072]{1,0:T(8,128)(2,1)}, u32[]{:S(2)}) copy-start(bf16[96,3072]{1,0:T(8,128)(2,1)} %copy-done.32) | copy-start | bytes 1769476
  136.4 15.5 %copy-start.35 = (bf16[96,3072]{1,0:T(8,128)(2,1)S(1)}, bf16[96,3072]{1,0:T(8,128)(2,1)}, u32[]{:S(2)}) copy-start(bf16[96,3072]{1,0:T(8,128)(2,1)} %copy-done.34) | copy-start | bytes 1769476
  136.4 20.2 %copy-start.39 = (bf16[256,768]{1,0:T(8,128)(2,1)S(1)}, bf16[256,768]{1,0:T(8,128)(2,1)}, u32[]{:S(2)}) copy-start(bf16[256,768]{1,0:T(8,128)(2,1)} %copy-done.38) | copy-start | bytes 1179652
  136.9 14.3 %collective-permute-start.34 = (bf16[48,768]{1,0:T(8,128)(2,1)S(1)}, bf16[48,768]{1,0:T(8,128)(2,1)S(1)}, u32[]{:S(2)}, u32[]{:S(2)}) collective-permute-start(bf16[48,768]{1,0:T(8,128)(2,1)S(1)} %get-tuple-element.127), channel_id=1, source_target_pairs={{0,8},{2,10},{8,16},{10,18},{16,24},{18,26},{24,28},{26,30},{28,20... | collective-permute-start | bytes 221192 | tf_op jit(solution)/shard_map/ppermute | solution.py:126
  138.4 13.5 %collective-permute-start.35 = (bf16[48,768]{1,0:T(8,128)(2,1)S(1)}, bf16[48,768]{1,0:T(8,128)(2,1)S(1)}, u32[]{:S(2)}, u32[]{:S(2)}) collective-permute-start(bf16[48,768]{1,0:T(8,128)(2,1)S(1)} %get-tuple-element.128), channel_id=1, source_target_pairs={{8,0},{10,2},{16,8},{18,10},{24,16},{26,18},{28,24},{30,26},{20,28... | collective-permute-start | bytes 221192 | tf_op jit(solution)/shard_map/ppermute | solution.py:126
  138.9 19.4 %copy-start.11 = (bf16[256,1152]{1,0:T(8,128)(2,1)S(1)}, bf16[256,1152]{1,0:T(8,128)(2,1)}, u32[]{:S(2)}) copy-start(bf16[256,1152]{1,0:T(8,128)(2,1)} %copy-done.10) | copy-start | bytes 1769476
  154.5 15.9 %collective-permute-start.36 = (bf16[96,3072]{1,0:T(8,128)(2,1)}, bf16[96,3072]{1,0:T(8,128)(2,1)}, u32[]{:S(2)}, u32[]{:S(2)}) collective-permute-start(bf16[96,3072]{1,0:T(8,128)(2,1)} %get-tuple-element.131), channel_id=1, source_target_pairs={{0,8},{2,10},{8,16},{10,18},{16,24},{18,26},{24,28},{26,30},{28,20... | collective-permute-start | bytes 1769480 | tf_op jit(solution)/shard_map/ppermute | solution.py:126
  155.2 15.6 %collective-permute-start.37 = (bf16[96,3072]{1,0:T(8,128)(2,1)}, bf16[96,3072]{1,0:T(8,128)(2,1)}, u32[]{:S(2)}, u32[]{:S(2)}) collective-permute-start(bf16[96,3072]{1,0:T(8,128)(2,1)} %get-tuple-element.132), channel_id=1, source_target_pairs={{8,0},{10,2},{16,8},{18,10},{24,16},{26,18},{28,24},{30,26},{20,28... | collective-permute-start | bytes 1769480 | tf_op jit(solution)/shard_map/ppermute | solution.py:126
  157.3 8.3 %collective-permute-start.22 = (bf16[128,768]{1,0:T(8,128)(2,1)}, bf16[128,768]{1,0:T(8,128)(2,1)}, u32[]{:S(2)}, u32[]{:S(2)}) collective-permute-start(bf16[128,768]{1,0:T(8,128)(2,1)} %constant_dynamic-slice_fusion.1), channel_id=1, source_target_pairs={{0,1},{1,0},{2,3},{3,2},{4,5},{5,4},{6,7},{7,6},{8,9},{9,8},{10,11... | collective-permute-start | bytes 589832 | tf_op jit(solution)/shard_map/ppermute | solution.py:474
  159.2 4.4 %collective-permute-start.27 = (f32[40,128]{1,0:T(8,128)S(1)}, f32[40,128]{1,0:T(8,128)S(1)}, u32[]{:S(2)}, u32[]{:S(2)}) collective-permute-start(f32[40,128]{1,0:T(8,128)S(1)} %get-tuple-element.108), channel_id=1, source_target_pairs={{0,1},{1,0},{2,3},{3,2},{4,5},{5,4},{6,7},{7,6},{8,9},{9,8},{10,11... | collective-permute-start | bytes 61448 | tf_op jit(solution)/shard_map/ppermute | solution.py:474
  163.6 2.7 %collective-permute-start.28 = (f32[40,128]{1,0:T(8,128)S(1)}, f32[40,128]{1,0:T(8,128)S(1)}, u32[]{:S(2)}, u32[]{:S(2)}) collective-permute-start(f32[40,128]{1,0:T(8,128)S(1)} %add.335), channel_id=1, source_target_pairs={{0,2},{2,0},{4,6},{6,4},{8,10},{10,8},{12,14},{14,12},{16,18},{18,... | collective-permute-start | bytes 61448 | tf_op jit(solution)/shard_map/ppermute | solution.py:57
  163.7 8.5 %collective-permute-start.26 = (bf16[128,768]{1,0:T(8,128)(2,1)S(1)}, bf16[128,768]{1,0:T(8,128)(2,1)S(1)}, u32[]{:S(2)}, u32[]{:S(2)}) collective-permute-start(bf16[128,768]{1,0:T(8,128)(2,1)S(1)} %constant_dynamic-slice_fusion), channel_id=1, source_target_pairs={{0,1},{1,0},{2,3},{3,2},{4,5},{5,4},{6,7},{7,6},{8,9},{9,8},{10,11... | collective-permute-start | bytes 589832 | tf_op jit(solution)/shard_map/ppermute | solution.py:474
  165.6 7.2 %collective-permute-start.40 = (bf16[48,1536]{1,0:T(8,128)(2,1)S(1)}, bf16[48,1536]{1,0:T(8,128)(2,1)S(1)}, u32[]{:S(2)}, u32[]{:S(2)}) collective-permute-start(bf16[48,1536]{1,0:T(8,128)(2,1)S(1)} %get-tuple-element.136), channel_id=1, source_target_pairs={{0,8},{2,10},{8,16},{10,18},{16,24},{18,26},{24,28},{26,30},{28,20... | collective-permute-start | bytes 442376 | tf_op jit(solution)/shard_map/ppermute | solution.py:126
  166.3 6.6 %collective-permute-start.41 = (bf16[48,1536]{1,0:T(8,128)(2,1)S(1)}, bf16[48,1536]{1,0:T(8,128)(2,1)S(1)}, u32[]{:S(2)}, u32[]{:S(2)}) collective-permute-start(bf16[48,1536]{1,0:T(8,128)(2,1)S(1)} %get-tuple-element.137), channel_id=1, source_target_pairs={{8,0},{10,2},{16,8},{18,10},{24,16},{26,18},{28,24},{30,26},{20,28... | collective-permute-start | bytes 442376 | tf_op jit(solution)/shard_map/ppermute | solution.py:126
  170.8 5.2 %collective-permute-start.38 = (f32[40,128]{1,0:T(8,128)S(1)}, f32[40,128]{1,0:T(8,128)S(1)}, u32[]{:S(2)}, u32[]{:S(2)}) collective-permute-start(f32[40,128]{1,0:T(8,128)S(1)} %add.336), channel_id=1, source_target_pairs={{0,4},{2,6},{4,0},{6,2},{8,12},{10,14},{12,8},{14,10},{16,20},{18,... | collective-permute-start | bytes 61448 | tf_op jit(solution)/shard_map/ppermute | solution.py:485
  172.4 8.4 %copy-start.44 = (f32[256,768]{1,0:T(8,128)S(1)}, f32[256,768]{1,0:T(8,128)}, u32[]{:S(2)}) copy-start(f32[256,768]{1,0:T(8,128)} %copy-done.43) | copy-start | bytes 2359300
  173.8 6.0 %collective-permute-start.42 = (bf16[48,1536]{1,0:T(8,128)(2,1)S(1)}, bf16[48,1536]{1,0:T(8,128)(2,1)S(1)}, u32[]{:S(2)}, u32[]{:S(2)}) collective-permute-start(bf16[48,1536]{1,0:T(8,128)(2,1)S(1)} %get-tuple-element.140), channel_id=1, source_target_pairs={{0,8},{2,10},{8,16},{10,18},{16,24},{18,26},{24,28},{26,30},{28,20... | collective-permute-start | bytes 442376 | tf_op jit(solution)/shard_map/ppermute | solution.py:126
  174.5 5.4 %collective-permute-start.43 = (bf16[48,1536]{1,0:T(8,128)(2,1)S(1)}, bf16[48,1536]{1,0:T(8,128)(2,1)S(1)}, u32[]{:S(2)}, u32[]{:S(2)}) collective-permute-start(bf16[48,1536]{1,0:T(8,128)(2,1)S(1)} %get-tuple-element.141), channel_id=1, source_target_pairs={{8,0},{10,2},{16,8},{18,10},{24,16},{26,18},{28,24},{30,26},{20,28... | collective-permute-start | bytes 442376 | tf_op jit(solution)/shard_map/ppermute | solution.py:126
  175.9 3.9 %collective-permute-start.39 = (f32[40,128]{1,0:T(8,128)S(1)}, f32[40,128]{1,0:T(8,128)S(1)}, u32[]{:S(2)}, u32[]{:S(2)}) collective-permute-start(f32[40,128]{1,0:T(8,128)S(1)} %add.340), channel_id=1, source_target_pairs={{0,8},{2,10},{4,12},{6,14},{8,0},{10,2},{12,4},{14,6},{16,24},{18,... | collective-permute-start | bytes 61448 | tf_op jit(solution)/shard_map/ppermute | solution.py:485
  179.9 7.9 %collective-permute-start.44 = (f32[40,128]{1,0:T(8,128)S(1)}, f32[40,128]{1,0:T(8,128)S(1)}, u32[]{:S(2)}, u32[]{:S(2)}) collective-permute-start(f32[40,128]{1,0:T(8,128)S(1)} %add.341), channel_id=1, source_target_pairs={{0,16},{2,18},{4,20},{6,22},{8,24},{10,26},{12,28},{14,30},{16,0},... | collective-permute-start | bytes 61448 | tf_op jit(solution)/shard_map/ppermute | solution.py:485
  184.0 11.3 %collective-permute-start.47 = (f32[48,3072]{1,0:T(8,128)}, f32[48,3072]{1,0:T(8,128)S(1)}, u32[]{:S(2)}, u32[]{:S(2)}) collective-permute-start(f32[48,3072]{1,0:T(8,128)} %get-tuple-element.149), channel_id=1, source_target_pairs={{0,2},{2,0},{4,6},{6,4},{8,10},{10,8},{12,14},{14,12},{16,18},{18,... | collective-permute-start | bytes 1769480 | tf_op jit(solution)/shard_map/ppermute | solution.py:57
  185.7 6.6 %collective-permute-start.45 = (bf16[48,1536]{1,0:T(8,128)(2,1)}, bf16[48,1536]{1,0:T(8,128)(2,1)}, u32[]{:S(2)}, u32[]{:S(2)}) collective-permute-start(bf16[48,1536]{1,0:T(8,128)(2,1)} %get-tuple-element.147), channel_id=1, source_target_pairs={{0,8},{2,10},{8,16},{10,18},{16,24},{18,26},{24,28},{26,30},{28,20... | collective-permute-start | bytes 442376 | tf_op jit(solution)/shard_map/ppermute | solution.py:126
  186.3 6.6 %collective-permute-start.46 = (bf16[48,1536]{1,0:T(8,128)(2,1)}, bf16[48,1536]{1,0:T(8,128)(2,1)}, u32[]{:S(2)}, u32[]{:S(2)}) collective-permute-start(bf16[48,1536]{1,0:T(8,128)(2,1)} %get-tuple-element.148), channel_id=1, source_target_pairs={{8,0},{10,2},{16,8},{18,10},{24,16},{26,18},{28,24},{30,26},{20,28... | collective-permute-start | bytes 442376 | tf_op jit(solution)/shard_map/ppermute | solution.py:126
  (39 other events, 112.8 us)

commit v6 on v5

--- a/solution.py
+++ b/solution.py
@@ -123,6 +123,7 @@
             r, l = ring_add(
                 self.blocks(distance), self.blocks(-distance), sent, self.rows, self.each
             )
+        self.going = (r, l)
         self.sent = (lax.ppermute(r, "dp", ring.right), lax.ppermute(l, "dp", ring.left))
         return self.sent
 
@@ -886,7 +887,6 @@
         a3 = send_a.step(*c4)
         (line,) = after((line,), c4)
         line = sum_pairs(line, 2)
-        mine, away = ring_total(send.blocks(0)[0], send.sent, ring.core)
         line = sum_pairs(line, 4)
         (line,) = after((line,), a3)
     else:
@@ -912,7 +912,9 @@
         attn_mine = lax.psum_scatter(terms, "dp", scatter_dimension=0, tiled=True)
         attn_mine = attn_mine.astype(F32)
     else:
-        send_a.step(mine, grad_block)
+        send_a.step()
+        sent = after(send.sent, send_a.going)
+        mine, away = ring_total(send.blocks(0)[0], sent, ring.core)
         grad_w_in_mine, grad_w_down_mine = combine(mine, ring.other_core(away), ring.core)
         attn_mine = send_a.total()
     summed_rel = summed[: rel_bias.shape[1], : rel_bias.shape[0]].T

time: 197 us -> 194 us (0.985)
  waiting for transfers between devices: 68.7 us -> 65.3 us
    ppermute x14, waiting for transfers between devices: 35 us -> 32.3 us  [step(): lax.ppermute(r, 'dp', ring.right)]
  transfers between devices with their start and end apart: 48 -> 48, of which waited for: 26 -> 24; matrix products, arithmetic and copies ran while one was open for 10% -> 10% of each run, Pallas kernels for 12% -> 12%
where the time goes in v6:
time: 194 us; the launch traced here: 193 us
  waiting for transfers between devices  65.3 us (34%)
  starting transfers between devices  46.9 us (24%)
  Pallas kernels  39.2 us (20%)
  local copies, waits for them, and re-layouts  29.1 us (15%)
  other arithmetic  10.9 us (6%)
    ppermute x14, waiting for transfers between devices, step(): lax.ppermute(r, 'dp', ring.right)  32.3 us
    ppermute x14, starting transfers between devices, step(): lax.ppermute(r, 'dp', ring.right)  20.6 us
    unnamed x117, local copies, waits for them, and re-layouts  18.4 us
    ppermute x7, waiting for transfers between devices, swap_tensor(): return lax.ppermute(x, 'tensor', [(0, 1), (1, 0)])  17.3 us
    ppermute x14, waiting for transfers between devices, step(): lax.ppermute(l, 'dp', ring.left)  11.1 us
    ppermute x14, starting transfers between devices, step(): lax.ppermute(l, 'dp', ring.left)  9.8 us
    ppermute x7, starting transfers between devices, swap_tensor(): return lax.ppermute(x, 'tensor', [(0, 1), (1, 0)])  9.43 us
    pallas_call x1, Pallas kernels, expert_layers(): pl.pallas_call(kernel, out_shape=[jax.ShapeDtypeStruct((filled, 2 * d), B...  8.91 us
  transfers between devices with their start and end apart: 48, of which 24 were waited for; matrix products, arithmetic and copies ran while one was open for 10% of the time, Pallas kernels for 12%

profile of v6, /device:TPU:0, one launch (start us, length us, event | category | flops | bytes accessed | tf_op | source)
XLA Modules:
  0.0 193.2 jit_solution(159949003508878541)
XLA Ops:
  2.4 3.0 %collective-permute-start.1 = (bf16[48,1536]{1,0:T(8,128)(2,1)S(1)}, bf16[48,1536]{1,0:T(8,128)(2,1)S(1)}, u32[]{:S(2)}, u32[]{:S(2)}) collective-permute-start(bf16[48,1536]{1,0:T(8,128)(2,1)S(1)} %constant_dynamic-update-slice_fusion.refs_0_), channel_id=1, source_target_pairs={{0,8},{2,10},{8,16},{10,18},{16,24},{18,26},{24,28},{26,30},{28,20... | collective-permute-start | bytes 442376 | tf_op jit(solution)/shard_map/ppermute | solution.py:86
  5.4 2.0 %collective-permute-start = (bf16[128,768]{1,0:T(8,128)(2,1)}, bf16[128,768]{1,0:T(8,128)(2,1)}, u32[]{:S(2)}, u32[]{:S(2)}) collective-permute-start(bf16[128,768]{1,0:T(8,128)(2,1)} %param.13), channel_id=1, source_target_pairs={{0,1},{1,0},{2,3},{3,2},{4,5},{5,4},{6,7},{7,6},{8,9},{9,8},{10,11... | collective-permute-start | bytes 589832 | tf_op jit(solution)/shard_map/ppermute | solution.py:475
  7.4 1.5 constant_dynamic-slice_fusion.4
  9.2 1.8 collective-permute-start.3
  11.1 1.6 collective-permute-start.10
  13.1 1.2 collective-permute-done.3.refs_3_
  14.3 1.8 collective-permute-start.5
  17.2 1.4 collective-permute-done.4.refs_4_
  19.4 1.8 collective-permute-start.7
  21.6 2.2 %collective-permute-done.6.refs_6_ = bf16[48,1536]{1,0:T(8,128)(2,1)S(1)} collective-permute-done((bf16[48,1536]{1,0:T(8,128)(2,1)S(1)}, bf16[48,1536]{1,0:T(8,128)(2,1)S(1)}, u32[]{:S(2)}, u32[]{:S(2)}) %collective-permute-start.6) | collective-permute-done | bytes 147488 | tf_op jit(solution)/shard_map/ppermute | solution.py:86
  24.6 2.3 %assemble.1.own_ref = bf16[384,1536]{1,0:T(8,128)(2,1)S(1)} custom-call(s32[8]{0:T(128)S(1)} %stack.30.owners_ref, bf16[48,1536]{1,0:T(8,128)(2,1)S(1)} %constant_dynamic-update-slice_fusion.refs_0_, bf16[48,1536]{1,0:T(8,128)(2,1)S(1)} %collective-permute-done.1.refs_1_, bf16[48,1536]{1,0:T(8,128)(2,1)S(1)} %collective-permute-done.2.refs_2_, ...), custom_call_target="tpu_custom_call" | custom-call | flops 1 | bytes 1 | tf_op jit(solution)/shard_map/assemble/pallas_call | solution.py:358
  27.4 1.2 maximum_select_fusion.refs_0_
  28.7 1.9 collective-permute-start.13
  32.5 1.3 maximum_select_fusion.1.x_ref
  34.9 1.3 copy-done.7
  36.1 1.3 copy-done.19
  38.3 3.5 %attention_forward.1 = (bf16[256,768]{1,0:T(8,128)(2,1)S(1)}, f32[256,1]{1,0:T(8,128)}, bf16[256,1152]{1,0:T(8,128)(2,1)S(1)}, f32[6,256,256]{2,1,0:T(8,128)S(1)...) custom-call(bf16[256,768]{1,0:T(8,128)(2,1)S(1)} %maximum_select_fusion.1.x_ref, ...), custom_call_target="tpu_custom_call" | custom-call | flops 1 | bytes 1 | tf_op jit(solution)/shard_map/attention_forward/pallas_call | solution.py:540
  44.1 1.8 collective-permute-start.9
  46.6 1.6 collective-permute-start.15
  48.7 1.3 maximum_select_fusion.2.g_ref
  50.0 5.2 %collective-permute-done.9.other_ref = bf16[256,768]{1,0:T(8,128)(2,1)S(1)} collective-permute-done((bf16[256,768]{1,0:T(8,128)(2,1)S(1)}, bf16[256,768]{1,0:T(8,128)(2,1)S(1)}, u32[]{:S(2)}, u32[]{:S(2)}) %collective-permute-start.9) | collective-permute-done | bytes 393248 | tf_op jit(solution)/shard_map/ppermute | solution.py:475
  55.2 1.1 route.1
  58.2 3.6 %collective-permute-done.15.refs_3_ = bf16[96,3072]{1,0:T(8,128)(2,1)S(1)} collective-permute-done((bf16[96,3072]{1,0:T(8,128)(2,1)}, bf16[96,3072]{1,0:T(8,128)(2,1)S(1)}, u32[]{:S(2)}, u32[]{:S(2)}) %collective-permute-start.15) | collective-permute-done | bytes 589856 | tf_op jit(solution)/shard_map/ppermute | solution.py:86
  61.7 1.3 collective-permute-done.16.refs_4_
  63.0 1.6 collective-permute-start.17
  66.7 10.0 %collective-permute-done.17.refs_5_ = bf16[96,3072]{1,0:T(8,128)(2,1)S(1)} collective-permute-done((bf16[96,3072]{1,0:T(8,128)(2,1)S(1)}, bf16[96,3072]{1,0:T(8,128)(2,1)S(1)}, u32[]{:S(2)}, u32[]{:S(2)}) %collective-permute-start.17) | collective-permute-done | bytes 589856 | tf_op jit(solution)/shard_map/ppermute | solution.py:86
  76.7 2.1 %collective-permute-done.18.refs_6_ = bf16[96,3072]{1,0:T(8,128)(2,1)S(1)} collective-permute-done((bf16[96,3072]{1,0:T(8,128)(2,1)S(1)}, bf16[96,3072]{1,0:T(8,128)(2,1)S(1)}, u32[]{:S(2)}, u32[]{:S(2)}) %collective-permute-start.18) | collective-permute-done | bytes 589856 | tf_op jit(solution)/shard_map/ppermute | solution.py:86
  81.4 1.6 collective-permute-start.19
  84.4 1.1 copy-done.9
  85.4 1.1 copy-done.15
  86.5 1.1 copy-done.17
  87.6 1.1 copy-done.25
  88.6 1.1 copy-done.27
  89.7 2.0 %place.1 = (bf16[768,1536]{1,0:T(8,128)(2,1)S(1)}, bf16[768,1536]{1,0:T(8,128)(2,1)S(1)}) custom-call(s32[7]{0:T(128)S(1)} %stack.32.owners_ref, bf16[96,3072]{1,0:T(8,128)(2,1)S(1)} %copy-done.9, bf16[96,3072]{1,0:T(8,128)(2,1)} %collective-permute-done.13.refs_1_, bf16[96,3072]{1,0:T(8,128)(2,1)} %collective-permute-done.14.refs_2_, ...), custom_call_target="tpu_custom_call" | custom-call | flops 1 | bytes 1 | tf_op jit(solution)/shard_map/place/pallas_call | solution.py:330
  91.8 8.9 %expert_layers.1 = (bf16[352,1536]{1,0:T(8,128)(2,1)S(1)}, bf16[352,1536]{1,0:T(8,128)(2,1)S(1)}, bf16[96,3072]{1,0:T(8,128)(2,1)S(1)}, bf16[96,3072]{1,0:T(8,12...) custom-call(s32[1]{0:T(128)} %bitcast.8.last_ref, ...), custom_call_target="tpu_custom_call", output_to_operand_aliasing={{10}: (4, {}), {11}: (5, {})} | custom-call | flops 1 | bytes 1 | tf_op jit(solution)/shard_map/expert_layers/pallas_call | solution.py:431
  101.0 1.6 collective-permute-start.24
  103.5 1.1 rows_back.1
  105.4 5.0 %collective-permute-done.24.refs_2_ = bf16[96,1536]{1,0:T(8,128)(2,1)S(1)} collective-permute-done((bf16[96,1536]{1,0:T(8,128)(2,1)S(1)}, bf16[96,1536]{1,0:T(8,128)(2,1)S(1)}, u32[]{:S(2)}, u32[]{:S(2)}) %collective-permute-start.24) | collective-permute-done | bytes 294944 | tf_op jit(solution)/shard_map/ppermute | solution.py:127
  110.5 1.3 collective-permute-done.25.refs_3_
  112.2 1.5 collective-permute-start.29
  115.3 8.8 %collective-permute-done.23.other_ref = bf16[256,768]{1,0:T(8,128)(2,1)S(1)} collective-permute-done((bf16[256,768]{1,0:T(8,128)(2,1)S(1)}, bf16[256,768]{1,0:T(8,128)(2,1)S(1)}, u32[]{:S(2)}, u32[]{:S(2)}) %collective-permute-start.23) | collective-permute-done | bytes 393248 | tf_op jit(solution)/shard_map/ppermute | solution.py:475
  124.2 4.7 %attention_backward.1 = (f32[256,768]{1,0:T(8,128)S(1)}, bf16[256,768]{1,0:T(8,128)(2,1)S(1)}, bf16[256,1152]{1,0:T(8,128)(2,1)S(1)}, f32[6,512]{1,0:T(8,128)S(1)}) custom-call(bf16[256,768]{1,0:T(8,128)(2,1)S(1)} %get-tuple-element.96.low_ref, bf16[256,768]{1,0:T(8,128)(2,1)S(1)} %collective-permute-done.23.other_ref, f32[256,768]{1,0:T(8,128)S(1)} %copy-done.4, ...), custom_call_target="tpu_custom_call" | custom-call | flops 1 | bytes 1 | tf_op jit(solution)/shard_map/attention_backward/pallas_call | solution.py:593
  128.9 2.6 %outer.1 = (bf16[384,1536]{1,0:T(8,128)(2,1)S(1)}, bf16[384,1536]{1,0:T(8,128)(2,1)}) custom-call(s32[16]{0:T(128)S(1)} %pad_add_fusion.owners_ref, bf16[256,768]{1,0:T(8,128)(2,1)S(1)} %copy-done.42, bf16[256,1152]{1,0:T(8,128)(2,1)S(1)} %get-tuple-element.122.grad_ref.refs_1_, bf16[256,768]{1,0:T(8,128)(2,1)S(1)} %get-tuple-element.123.refs_2_, ...), custom_call_target="tpu_custom_call" | custom-call | flops 1 | bytes 1 | tf_op jit(solution)/shard_map/outer/pallas_call | solution.py:163
  131.6 1.5 ring_add.7
  133.1 1.5 collective-permute-start.31
  136.9 1.5 collective-permute-start.34
  139.0 10.5 %collective-permute-done.31.refs_2_ = bf16[96,3072]{1,0:T(8,128)(2,1)S(1)} collective-permute-done((bf16[96,3072]{1,0:T(8,128)(2,1)}, bf16[96,3072]{1,0:T(8,128)(2,1)S(1)}, u32[]{:S(2)}, u32[]{:S(2)}) %collective-permute-start.31) | collective-permute-done | bytes 589856 | tf_op jit(solution)/shard_map/ppermute | solution.py:127
  149.5 1.6 collective-permute-done.32.refs_3_
  151.9 2.6 %ring_add.8 = (bf16[96,3072]{1,0:T(8,128)(2,1)}, bf16[96,3072]{1,0:T(8,128)(2,1)}) custom-call(bf16[96,3072]{1,0:T(8,128)(2,1)S(1)} %copy-done.33, bf16[96,3072]{1,0:T(8,128)(2,1)S(1)} %copy-done.35, bf16[96,3072]{1,0:T(8,128)(2,1)S(1)} %collective-permute-done.31.refs_2_, bf16[96,3072]{1,0:T(8,128)(2,1)} %collective-permute-done.32.refs_3_), custom_call_target="tpu_custom_call" | custom-call | flops 1 | bytes 1 | tf_op jit(solution)/shard_map/ring_add/pallas_call | solution.py:244
  155.2 1.4 collective-permute-start.37
  159.2 1.1 collective-permute-start.27
  160.3 3.3 %collective-permute-done.27 = f32[40,128]{1,0:T(8,128)S(1)} collective-permute-done((f32[40,128]{1,0:T(8,128)S(1)}, f32[40,128]{1,0:T(8,128)S(1)}, u32[]{:S(2)}, u32[]{:S(2)}) %collective-permute-start.27) | collective-permute-done | bytes 20512 | tf_op jit(solution)/shard_map/ppermute | solution.py:475
  163.7 1.1 collective-permute-start.26
  166.3 1.4 collective-permute-start.41
  167.7 1.7 add_convert_fusion
  169.4 1.1 collective-permute-done.36.r_ref
  170.8 1.4 collective-permute-start.38
  174.5 1.4 collective-permute-start.43
  176.6 3.3 %collective-permute-done.39 = f32[40,128]{1,0:T(8,128)S(1)} collective-permute-done((f32[40,128]{1,0:T(8,128)S(1)}, f32[40,128]{1,0:T(8,128)S(1)}, u32[]{:S(2)}, u32[]{:S(2)}) %collective-permute-start.39) | collective-permute-done | bytes 20512 | tf_op jit(solution)/shard_map/ppermute | solution.py:486
  181.7 1.5 ring_add.11
  183.9 1.4 collective-permute-start.46
  185.3 2.3 %ring_total.1 = (f32[48,3072]{1,0:T(8,128)S(1)}, f32[48,3072]{1,0:T(8,128)}) custom-call(s32[1]{0:T(128)} %bitcast.core_ref, bf16[96,3072]{1,0:T(8,128)(2,1)S(1)} %copy-done.29, bf16[96,3072]{1,0:T(8,128)(2,1)} %collective-permute-done.36.r_ref, bf16[96,3072]{1,0:T(8,128)(2,1)} %collective-permute-done.37.l_ref), custom_call_target="tpu_custom_call" | custom-call | flops 1 | bytes 1 | tf_op jit(solution)/shard_map/ring_total/pallas_call | solution.py:274
  189.6 1.1 convert_add_fusion
  192.0 1.2 combine.1
  (223 shorter events, 42.6 us)
Async XLA Ops:
  0.6 20.6 %copy-start = (f32[32,12]{0,1:T(8,128)S(1)}, f32[32,12]{0,1:T(8,128)}, u32[]{:S(2)}) copy-start(f32[32,12]{0,1:T(8,128)} %param.17) | copy-start | bytes 4612
  2.4 6.8 %collective-permute-start.1 = (bf16[48,1536]{1,0:T(8,128)(2,1)S(1)}, bf16[48,1536]{1,0:T(8,128)(2,1)S(1)}, u32[]{:S(2)}, u32[]{:S(2)}) collective-permute-start(bf16[48,1536]{1,0:T(8,128)(2,1)S(1)} %constant_dynamic-update-slice_fusion.refs_0_), channel_id=1, source_target_pairs={{0,8},{2,10},{8,16},{10,18},{16,24},{18,26},{24,28},{26,30},{28,20... | collective-permute-start | bytes 442376 | tf_op jit(solution)/shard_map/ppermute | solution.py:86
  5.4 7.3 %collective-permute-start.2 = (bf16[48,1536]{1,0:T(8,128)(2,1)S(1)}, bf16[48,1536]{1,0:T(8,128)(2,1)S(1)}, u32[]{:S(2)}, u32[]{:S(2)}) collective-permute-start(bf16[48,1536]{1,0:T(8,128)(2,1)S(1)} %constant_dynamic-update-slice_fusion.refs_0_), channel_id=1, source_target_pairs={{8,0},{10,2},{16,8},{18,10},{24,16},{26,18},{28,24},{30,26},{20,28... | collective-permute-start | bytes 442376 | tf_op jit(solution)/shard_map/ppermute | solution.py:86
  5.4 23.3 %collective-permute-start = (bf16[128,768]{1,0:T(8,128)(2,1)}, bf16[128,768]{1,0:T(8,128)(2,1)}, u32[]{:S(2)}, u32[]{:S(2)}) collective-permute-start(bf16[128,768]{1,0:T(8,128)(2,1)} %param.13), channel_id=1, source_target_pairs={{0,1},{1,0},{2,3},{3,2},{4,5},{5,4},{6,7},{7,6},{8,9},{9,8},{10,11... | collective-permute-start | bytes 589832 | tf_op jit(solution)/shard_map/ppermute | solution.py:475
  7.4 8.8 %copy-start.51 = (s32[256,1]{0,1:T(1,128)S(1)}, s32[256,1]{0,1:T(1,128)}, u32[]{:S(2)}) copy-start(s32[256,1]{0,1:T(1,128)} %param.23) | copy-start | bytes 3076
  7.4 13.9 %copy-start.53 = (s32[511]{0:T(512)S(1)}, s32[511]{0:T(512)}, u32[]{:S(2)}) copy-start(s32[511]{0:T(512)} %param.24) | copy-start | bytes 6136
  9.2 5.1 %collective-permute-start.3 = (bf16[48,1536]{1,0:T(8,128)(2,1)S(1)}, bf16[48,1536]{1,0:T(8,128)(2,1)S(1)}, u32[]{:S(2)}, u32[]{:S(2)}) collective-permute-start(bf16[48,1536]{1,0:T(8,128)(2,1)S(1)} %collective-permute-done.1.refs_1_), channel_id=1, source_target_pairs={{0,8},{2,10},{8,16},{10,18},{16,24},{18,26},{24,28},{26,30},{28,20... | collective-permute-start | bytes 442376 | tf_op jit(solution)/shard_map/ppermute | solution.py:86
  11.0 16.4 %collective-permute-start.12 = (bf16[48,3072]{1,0:T(8,128)(2,1)S(1)}, bf16[48,3072]{1,0:T(8,128)(2,1)}, u32[]{:S(2)}, u32[]{:S(2)}) collective-permute-start(bf16[48,3072]{1,0:T(8,128)(2,1)S(1)} %pad_maximum_fusion), channel_id=1, source_target_pairs={{0,2},{2,0},{4,6},{6,4},{8,10},{10,8},{12,14},{14,12},{16,18},{18,... | collective-permute-start | bytes 884744 | tf_op jit(solution)/shard_map/ppermute | solution.py:57
  11.1 17.6 %collective-permute-start.10 = (bf16[128,768]{1,0:T(8,128)(2,1)}, bf16[128,768]{1,0:T(8,128)(2,1)}, u32[]{:S(2)}, u32[]{:S(2)}) collective-permute-start(bf16[128,768]{1,0:T(8,128)(2,1)} %param.25), channel_id=1, source_target_pairs={{0,1},{1,0},{2,3},{3,2},{4,5},{5,4},{6,7},{7,6},{8,9},{9,8},{10,11... | collective-permute-start | bytes 589832 | tf_op jit(solution)/shard_map/ppermute | solution.py:475
  12.7 5.9 %collective-permute-start.4 = (bf16[48,1536]{1,0:T(8,128)(2,1)S(1)}, bf16[48,1536]{1,0:T(8,128)(2,1)S(1)}, u32[]{:S(2)}, u32[]{:S(2)}) collective-permute-start(bf16[48,1536]{1,0:T(8,128)(2,1)S(1)} %collective-permute-done.2.refs_2_), channel_id=1, source_target_pairs={{8,0},{10,2},{16,8},{18,10},{24,16},{26,18},{28,24},{30,26},{20,28... | collective-permute-start | bytes 442376 | tf_op jit(solution)/shard_map/ppermute | solution.py:86
  14.3 5.1 %collective-permute-start.5 = (bf16[48,1536]{1,0:T(8,128)(2,1)S(1)}, bf16[48,1536]{1,0:T(8,128)(2,1)S(1)}, u32[]{:S(2)}, u32[]{:S(2)}) collective-permute-start(bf16[48,1536]{1,0:T(8,128)(2,1)S(1)} %collective-permute-done.3.refs_3_), channel_id=1, source_target_pairs={{0,8},{2,10},{8,16},{10,18},{16,24},{18,26},{24,28},{26,30},{28,20... | collective-permute-start | bytes 442376 | tf_op jit(solution)/shard_map/ppermute | solution.py:86
  18.6 5.2 %collective-permute-start.6 = (bf16[48,1536]{1,0:T(8,128)(2,1)S(1)}, bf16[48,1536]{1,0:T(8,128)(2,1)S(1)}, u32[]{:S(2)}, u32[]{:S(2)}) collective-permute-start(bf16[48,1536]{1,0:T(8,128)(2,1)S(1)} %collective-permute-done.4.refs_4_), channel_id=1, source_target_pairs={{8,0},{10,2},{16,8},{18,10},{24,16},{26,18},{28,24},{30,26},{20,28... | collective-permute-start | bytes 442376 | tf_op jit(solution)/shard_map/ppermute | solution.py:86
  19.4 5.1 %collective-permute-start.7 = (bf16[48,1536]{1,0:T(8,128)(2,1)S(1)}, bf16[48,1536]{1,0:T(8,128)(2,1)S(1)}, u32[]{:S(2)}, u32[]{:S(2)}) collective-permute-start(bf16[48,1536]{1,0:T(8,128)(2,1)S(1)} %collective-permute-done.5.refs_5_), channel_id=1, source_target_pairs={{0,8},{2,10},{8,16},{10,18},{16,24},{18,26},{24,28},{26,30},{28,20... | collective-permute-start | bytes 442376 | tf_op jit(solution)/shard_map/ppermute | solution.py:93
  26.9 6.9 %collective-permute-start.8 = (bf16[384,1536]{1,0:T(8,128)(2,1)S(1)}, bf16[384,1536]{1,0:T(8,128)(2,1)S(1)}, u32[]{:S(2)}, u32[]{:S(2)}) collective-permute-start(bf16[384,1536]{1,0:T(8,128)(2,1)S(1)} %assemble.1.own_ref), channel_id=1, source_target_pairs={{0,2},{2,0},{4,6},{6,4},{8,10},{10,8},{12,14},{14,12},{16,18},{18,... | collective-permute-start | bytes 3538952 | tf_op jit(solution)/shard_map/ppermute | solution.py:57
  28.6 9.0 %copy-start.8 = (bf16[96,3072]{1,0:T(8,128)(2,1)}, bf16[96,3072]{1,0:T(8,128)(2,1)S(1)}, u32[]{:S(2)}) copy-start(bf16[96,3072]{1,0:T(8,128)(2,1)S(1)} %maximum_select_fusion.refs_0_) | copy-start | bytes 1769476
  28.7 17.9 %collective-permute-start.13 = (bf16[96,3072]{1,0:T(8,128)(2,1)S(1)}, bf16[96,3072]{1,0:T(8,128)(2,1)}, u32[]{:S(2)}, u32[]{:S(2)}) collective-permute-start(bf16[96,3072]{1,0:T(8,128)(2,1)S(1)} %maximum_select_fusion.refs_0_), channel_id=1, source_target_pairs={{0,8},{2,10},{8,16},{10,18},{16,24},{18,26},{24,28},{26,30},{28,20... | collective-permute-start | bytes 1769480 | tf_op jit(solution)/shard_map/ppermute | solution.py:86
  30.6 17.7 %collective-permute-start.14 = (bf16[96,3072]{1,0:T(8,128)(2,1)S(1)}, bf16[96,3072]{1,0:T(8,128)(2,1)}, u32[]{:S(2)}, u32[]{:S(2)}) collective-permute-start(bf16[96,3072]{1,0:T(8,128)(2,1)S(1)} %maximum_select_fusion.refs_0_), channel_id=1, source_target_pairs={{8,0},{10,2},{16,8},{18,10},{24,16},{26,18},{28,24},{30,26},{20,28... | collective-permute-start | bytes 1769480 | tf_op jit(solution)/shard_map/ppermute | solution.py:86
  37.6 86.5 %copy-start.1 = (bf16[768,1536]{1,0:T(8,128)(2,1)}, bf16[768,1536]{1,0:T(8,128)(2,1)S(1)}, u32[]{:S(2)}) copy-start(bf16[768,1536]{1,0:T(8,128)(2,1)S(1)} %interleave.1.w_ref) | copy-start | bytes 7077892
  44.1 12.1 %copy-start.12 = (f32[6,256,256]{2,1,0:T(8,128)}, f32[6,256,256]{2,1,0:T(8,128)S(1)}, u32[]{:S(2)}) copy-start(f32[6,256,256]{2,1,0:T(8,128)S(1)} %get-tuple-element.102.p_ref) | copy-start | bytes 4718596
  44.1 11.0 %copy-start.47 = (f32[768,2]{0,1:T(2,128)S(1)}, f32[768,2]{0,1:T(2,128)}, u32[]{:S(2)}) copy-start(f32[768,2]{0,1:T(2,128)} %param.19) | copy-start | bytes 18436
  44.1 11.0 %collective-permute-start.9 = (bf16[256,768]{1,0:T(8,128)(2,1)S(1)}, bf16[256,768]{1,0:T(8,128)(2,1)S(1)}, u32[]{:S(2)}, u32[]{:S(2)}) collective-permute-start(bf16[256,768]{1,0:T(8,128)(2,1)S(1)} %get-tuple-element.81.part_ref), channel_id=1, source_target_pairs={{0,1},{1,0},{2,3},{3,2},{4,5},{5,4},{6,7},{7,6},{8,9},{9,8},{10,11... | collective-permute-start | bytes 1179656 | tf_op jit(solution)/shard_map/ppermute | solution.py:475
  46.6 15.1 %collective-permute-start.15 = (bf16[96,3072]{1,0:T(8,128)(2,1)}, bf16[96,3072]{1,0:T(8,128)(2,1)S(1)}, u32[]{:S(2)}, u32[]{:S(2)}) collective-permute-start(bf16[96,3072]{1,0:T(8,128)(2,1)} %collective-permute-done.13.refs_1_), channel_id=1, source_target_pairs={{0,8},{2,10},{8,16},{10,18},{16,24},{18,26},{24,28},{26,30},{28,20... | collective-permute-start | bytes 1769480 | tf_op jit(solution)/shard_map/ppermute | solution.py:86
  48.2 14.8 %collective-permute-start.16 = (bf16[96,3072]{1,0:T(8,128)(2,1)}, bf16[96,3072]{1,0:T(8,128)(2,1)S(1)}, u32[]{:S(2)}, u32[]{:S(2)}) collective-permute-start(bf16[96,3072]{1,0:T(8,128)(2,1)} %collective-permute-done.14.refs_2_), channel_id=1, source_target_pairs={{8,0},{10,2},{16,8},{18,10},{24,16},{26,18},{28,24},{30,26},{20,28... | collective-permute-start | bytes 1769480 | tf_op jit(solution)/shard_map/ppermute | solution.py:86
  57.2 21.7 %collective-permute-start.11 = (bf16[352,1536]{1,0:T(8,128)(2,1)S(1)}, bf16[352,1536]{1,0:T(8,128)(2,1)S(1)}, u32[]{:S(2)}, u32[]{:S(2)}) collective-permute-start(bf16[352,1536]{1,0:T(8,128)(2,1)S(1)} %get-tuple-element.83.own_hbm), channel_id=1, source_target_pairs={{0,2},{2,0},{4,6},{6,4},{8,10},{10,8},{12,14},{14,12},{16,18},{18,... | collective-permute-start | bytes 3244040 | tf_op jit(solution)/shard_map/ppermute | solution.py:57
  63.0 13.7 %collective-permute-start.17 = (bf16[96,3072]{1,0:T(8,128)(2,1)S(1)}, bf16[96,3072]{1,0:T(8,128)(2,1)S(1)}, u32[]{:S(2)}, u32[]{:S(2)}) collective-permute-start(bf16[96,3072]{1,0:T(8,128)(2,1)S(1)} %collective-permute-done.15.refs_3_), channel_id=1, source_target_pairs={{0,8},{2,10},{8,16},{10,18},{16,24},{18,26},{24,28},{26,30},{28,20... | collective-permute-start | bytes 1769480 | tf_op jit(solution)/shard_map/ppermute | solution.py:86
  65.4 13.4 %collective-permute-start.18 = (bf16[96,3072]{1,0:T(8,128)(2,1)S(1)}, bf16[96,3072]{1,0:T(8,128)(2,1)S(1)}, u32[]{:S(2)}, u32[]{:S(2)}) collective-permute-start(bf16[96,3072]{1,0:T(8,128)(2,1)S(1)} %collective-permute-done.16.refs_4_), channel_id=1, source_target_pairs={{8,0},{10,2},{16,8},{18,10},{24,16},{26,18},{28,24},{30,26},{20,28... | collective-permute-start | bytes 1769480 | tf_op jit(solution)/shard_map/ppermute | solution.py:86
  81.4 10.3 %collective-permute-start.19 = (bf16[96,1536]{1,0:T(8,128)(2,1)}, bf16[96,1536]{1,0:T(8,128)(2,1)}, u32[]{:S(2)}, u32[]{:S(2)}) collective-permute-start(bf16[96,1536]{1,0:T(8,128)(2,1)} %slice.47), channel_id=1, source_target_pairs={{0,8},{2,10},{8,16},{10,18},{16,24},{18,26},{24,28},{26,30},{28,20... | collective-permute-start | bytes 884744 | tf_op jit(solution)/shard_map/ppermute | solution.py:89
  83.7 8.0 %collective-permute-start.20 = (bf16[96,1536]{1,0:T(8,128)(2,1)}, bf16[96,1536]{1,0:T(8,128)(2,1)}, u32[]{:S(2)}, u32[]{:S(2)}) collective-permute-start(bf16[96,1536]{1,0:T(8,128)(2,1)} %slice.48), channel_id=1, source_target_pairs={{8,0},{10,2},{16,8},{18,10},{24,16},{26,18},{28,24},{30,26},{20,28... | collective-permute-start | bytes 884744 | tf_op jit(solution)/shard_map/ppermute | solution.py:90
  91.8 11.7 %copy-start.4 = (f32[256,768]{1,0:T(8,128)S(1)}, f32[256,768]{1,0:T(8,128)}, u32[]{:S(2)}) copy-start(f32[256,768]{1,0:T(8,128)} %copy-done.3) | copy-start | bytes 2359300
  91.8 11.7 %copy-start.36 = (s32[256,1]{1,0:T(8,128)S(1)}, s32[256,1]{1,0:T(8,128)}, u32[]{:S(2)}) copy-start(s32[256,1]{1,0:T(8,128)} %get-tuple-element.196.flat_ref) | copy-start | bytes 3076
  100.8 2.8 %collective-permute-start.21 = (bf16[352,1536]{1,0:T(8,128)(2,1)S(1)}, bf16[352,1536]{1,0:T(8,128)(2,1)S(1)}, u32[]{:S(2)}, u32[]{:S(2)}) collective-permute-start(bf16[352,1536]{1,0:T(8,128)(2,1)S(1)} %get-tuple-element.93), channel_id=1, source_target_pairs={{0,2},{2,0},{4,6},{6,4},{8,10},{10,8},{12,14},{14,12},{16,18},{18,... | collective-permute-start | bytes 3244040 | tf_op jit(solution)/shard_map/ppermute | solution.py:57
  101.0 9.5 %collective-permute-start.24 = (bf16[96,1536]{1,0:T(8,128)(2,1)S(1)}, bf16[96,1536]{1,0:T(8,128)(2,1)S(1)}, u32[]{:S(2)}, u32[]{:S(2)}) collective-permute-start(bf16[96,1536]{1,0:T(8,128)(2,1)S(1)} %get-tuple-element.98), channel_id=1, source_target_pairs={{0,8},{2,10},{8,16},{10,18},{16,24},{18,26},{24,28},{26,30},{28,20... | collective-permute-start | bytes 884744 | tf_op jit(solution)/shard_map/ppermute | solution.py:127
  102.6 9.1 %collective-permute-start.25 = (bf16[96,1536]{1,0:T(8,128)(2,1)S(1)}, bf16[96,1536]{1,0:T(8,128)(2,1)S(1)}, u32[]{:S(2)}, u32[]{:S(2)}) collective-permute-start(bf16[96,1536]{1,0:T(8,128)(2,1)S(1)} %get-tuple-element.99), channel_id=1, source_target_pairs={{8,0},{10,2},{16,8},{18,10},{24,16},{26,18},{28,24},{30,26},{20,28... | collective-permute-start | bytes 884744 | tf_op jit(solution)/shard_map/ppermute | solution.py:127
  103.5 20.6 %copy-start.31 = (bf16[256,1152]{1,0:T(8,128)(2,1)S(1)}, bf16[256,1152]{1,0:T(8,128)(2,1)}, u32[]{:S(2)}) copy-start(bf16[256,1152]{1,0:T(8,128)(2,1)} %copy-done.30) | copy-start | bytes 1769476
  105.4 18.7 %copy-start.13 = (f32[6,256,256]{2,1,0:T(8,128)S(1)}, f32[6,256,256]{2,1,0:T(8,128)}, u32[]{:S(2)}) copy-start(f32[6,256,256]{2,1,0:T(8,128)} %copy-done.12) | copy-start | bytes 4718596
  112.2 16.7 %collective-permute-start.29 = (bf16[96,3072]{1,0:T(8,128)(2,1)S(1)}, bf16[96,3072]{1,0:T(8,128)(2,1)S(1)}, u32[]{:S(2)}, u32[]{:S(2)}) collective-permute-start(bf16[96,3072]{1,0:T(8,128)(2,1)S(1)} %get-tuple-element.117), channel_id=1, source_target_pairs={{0,8},{2,10},{8,16},{10,18},{16,24},{18,26},{24,28},{26,30},{28,20... | collective-permute-start | bytes 1769480 | tf_op jit(solution)/shard_map/ppermute | solution.py:127
  113.7 15.1 %collective-permute-start.30 = (bf16[96,3072]{1,0:T(8,128)(2,1)S(1)}, bf16[96,3072]{1,0:T(8,128)(2,1)S(1)}, u32[]{:S(2)}, u32[]{:S(2)}) collective-permute-start(bf16[96,3072]{1,0:T(8,128)(2,1)S(1)} %get-tuple-element.118), channel_id=1, source_target_pairs={{8,0},{10,2},{16,8},{18,10},{24,16},{26,18},{28,24},{30,26},{20,28... | collective-permute-start | bytes 1769480 | tf_op jit(solution)/shard_map/ppermute | solution.py:127
  114.3 9.9 %collective-permute-start.23 = (bf16[256,768]{1,0:T(8,128)(2,1)S(1)}, bf16[256,768]{1,0:T(8,128)(2,1)S(1)}, u32[]{:S(2)}, u32[]{:S(2)}) collective-permute-start(bf16[256,768]{1,0:T(8,128)(2,1)S(1)} %get-tuple-element.96.low_ref), channel_id=1, source_target_pairs={{0,1},{1,0},{2,3},{3,2},{4,5},{5,4},{6,7},{7,6},{8,9},{9,8},{10,11... | collective-permute-start | bytes 1179656 | tf_op jit(solution)/shard_map/ppermute | solution.py:475
  131.5 4.8 %collective-permute-start.33 = (bf16[384,1536]{1,0:T(8,128)(2,1)}, bf16[384,1536]{1,0:T(8,128)(2,1)S(1)}, u32[]{:S(2)}, u32[]{:S(2)}) collective-permute-start(bf16[384,1536]{1,0:T(8,128)(2,1)} %get-tuple-element.126), channel_id=1, source_target_pairs={{0,2},{2,0},{4,6},{6,4},{8,10},{10,8},{12,14},{14,12},{16,18},{18,... | collective-permute-start | bytes 3538952 | tf_op jit(solution)/shard_map/ppermute | solution.py:57
  133.1 16.4 %collective-permute-start.31 = (bf16[96,3072]{1,0:T(8,128)(2,1)}, bf16[96,3072]{1,0:T(8,128)(2,1)S(1)}, u32[]{:S(2)}, u32[]{:S(2)}) collective-permute-start(bf16[96,3072]{1,0:T(8,128)(2,1)} %get-tuple-element.119), channel_id=1, source_target_pairs={{0,8},{2,10},{8,16},{10,18},{16,24},{18,26},{24,28},{26,30},{28,20... | collective-permute-start | bytes 1769480 | tf_op jit(solution)/shard_map/ppermute | solution.py:127
  134.6 16.5 %collective-permute-start.32 = (bf16[96,3072]{1,0:T(8,128)(2,1)}, bf16[96,3072]{1,0:T(8,128)(2,1)}, u32[]{:S(2)}, u32[]{:S(2)}) collective-permute-start(bf16[96,3072]{1,0:T(8,128)(2,1)} %get-tuple-element.120), channel_id=1, source_target_pairs={{8,0},{10,2},{16,8},{18,10},{24,16},{26,18},{28,24},{30,26},{20,28... | collective-permute-start | bytes 1769480 | tf_op jit(solution)/shard_map/ppermute | solution.py:127
  136.4 15.5 %copy-start.33 = (bf16[96,3072]{1,0:T(8,128)(2,1)S(1)}, bf16[96,3072]{1,0:T(8,128)(2,1)}, u32[]{:S(2)}) copy-start(bf16[96,3072]{1,0:T(8,128)(2,1)} %copy-done.32) | copy-start | bytes 1769476
  136.4 15.5 %copy-start.35 = (bf16[96,3072]{1,0:T(8,128)(2,1)S(1)}, bf16[96,3072]{1,0:T(8,128)(2,1)}, u32[]{:S(2)}) copy-start(bf16[96,3072]{1,0:T(8,128)(2,1)} %copy-done.34) | copy-start | bytes 1769476
  136.4 20.2 %copy-start.39 = (bf16[256,768]{1,0:T(8,128)(2,1)S(1)}, bf16[256,768]{1,0:T(8,128)(2,1)}, u32[]{:S(2)}) copy-start(bf16[256,768]{1,0:T(8,128)(2,1)} %copy-done.38) | copy-start | bytes 1179652
  136.9 14.3 %collective-permute-start.34 = (bf16[48,768]{1,0:T(8,128)(2,1)S(1)}, bf16[48,768]{1,0:T(8,128)(2,1)S(1)}, u32[]{:S(2)}, u32[]{:S(2)}) collective-permute-start(bf16[48,768]{1,0:T(8,128)(2,1)S(1)} %get-tuple-element.127), channel_id=1, source_target_pairs={{0,8},{2,10},{8,16},{10,18},{16,24},{18,26},{24,28},{26,30},{28,20... | collective-permute-start | bytes 221192 | tf_op jit(solution)/shard_map/ppermute | solution.py:127
  138.4 13.5 %collective-permute-start.35 = (bf16[48,768]{1,0:T(8,128)(2,1)S(1)}, bf16[48,768]{1,0:T(8,128)(2,1)S(1)}, u32[]{:S(2)}, u32[]{:S(2)}) collective-permute-start(bf16[48,768]{1,0:T(8,128)(2,1)S(1)} %get-tuple-element.128), channel_id=1, source_target_pairs={{8,0},{10,2},{16,8},{18,10},{24,16},{26,18},{28,24},{30,26},{20,28... | collective-permute-start | bytes 221192 | tf_op jit(solution)/shard_map/ppermute | solution.py:127
  138.9 19.4 %copy-start.11 = (bf16[256,1152]{1,0:T(8,128)(2,1)S(1)}, bf16[256,1152]{1,0:T(8,128)(2,1)}, u32[]{:S(2)}) copy-start(bf16[256,1152]{1,0:T(8,128)(2,1)} %copy-done.10) | copy-start | bytes 1769476
  154.5 15.9 %collective-permute-start.36 = (bf16[96,3072]{1,0:T(8,128)(2,1)}, bf16[96,3072]{1,0:T(8,128)(2,1)}, u32[]{:S(2)}, u32[]{:S(2)}) collective-permute-start(bf16[96,3072]{1,0:T(8,128)(2,1)} %get-tuple-element.131), channel_id=1, source_target_pairs={{0,8},{2,10},{8,16},{10,18},{16,24},{18,26},{24,28},{26,30},{28,20... | collective-permute-start | bytes 1769480 | tf_op jit(solution)/shard_map/ppermute | solution.py:127
  155.2 15.6 %collective-permute-start.37 = (bf16[96,3072]{1,0:T(8,128)(2,1)}, bf16[96,3072]{1,0:T(8,128)(2,1)}, u32[]{:S(2)}, u32[]{:S(2)}) collective-permute-start(bf16[96,3072]{1,0:T(8,128)(2,1)} %get-tuple-element.132), channel_id=1, source_target_pairs={{8,0},{10,2},{16,8},{18,10},{24,16},{26,18},{28,24},{30,26},{20,28... | collective-permute-start | bytes 1769480 | tf_op jit(solution)/shard_map/ppermute | solution.py:127
  157.3 8.3 %collective-permute-start.22 = (bf16[128,768]{1,0:T(8,128)(2,1)}, bf16[128,768]{1,0:T(8,128)(2,1)}, u32[]{:S(2)}, u32[]{:S(2)}) collective-permute-start(bf16[128,768]{1,0:T(8,128)(2,1)} %constant_dynamic-slice_fusion.1), channel_id=1, source_target_pairs={{0,1},{1,0},{2,3},{3,2},{4,5},{5,4},{6,7},{7,6},{8,9},{9,8},{10,11... | collective-permute-start | bytes 589832 | tf_op jit(solution)/shard_map/ppermute | solution.py:475
  159.2 4.4 %collective-permute-start.27 = (f32[40,128]{1,0:T(8,128)S(1)}, f32[40,128]{1,0:T(8,128)S(1)}, u32[]{:S(2)}, u32[]{:S(2)}) collective-permute-start(f32[40,128]{1,0:T(8,128)S(1)} %get-tuple-element.108), channel_id=1, source_target_pairs={{0,1},{1,0},{2,3},{3,2},{4,5},{5,4},{6,7},{7,6},{8,9},{9,8},{10,11... | collective-permute-start | bytes 61448 | tf_op jit(solution)/shard_map/ppermute | solution.py:475
  163.6 2.7 %collective-permute-start.28 = (f32[40,128]{1,0:T(8,128)S(1)}, f32[40,128]{1,0:T(8,128)S(1)}, u32[]{:S(2)}, u32[]{:S(2)}) collective-permute-start(f32[40,128]{1,0:T(8,128)S(1)} %add.335), channel_id=1, source_target_pairs={{0,2},{2,0},{4,6},{6,4},{8,10},{10,8},{12,14},{14,12},{16,18},{18,... | collective-permute-start | bytes 61448 | tf_op jit(solution)/shard_map/ppermute | solution.py:57
  163.7 8.5 %collective-permute-start.26 = (bf16[128,768]{1,0:T(8,128)(2,1)S(1)}, bf16[128,768]{1,0:T(8,128)(2,1)S(1)}, u32[]{:S(2)}, u32[]{:S(2)}) collective-permute-start(bf16[128,768]{1,0:T(8,128)(2,1)S(1)} %constant_dynamic-slice_fusion), channel_id=1, source_target_pairs={{0,1},{1,0},{2,3},{3,2},{4,5},{5,4},{6,7},{7,6},{8,9},{9,8},{10,11... | collective-permute-start | bytes 589832 | tf_op jit(solution)/shard_map/ppermute | solution.py:475
  165.6 7.2 %collective-permute-start.40 = (bf16[48,1536]{1,0:T(8,128)(2,1)S(1)}, bf16[48,1536]{1,0:T(8,128)(2,1)S(1)}, u32[]{:S(2)}, u32[]{:S(2)}) collective-permute-start(bf16[48,1536]{1,0:T(8,128)(2,1)S(1)} %get-tuple-element.136), channel_id=1, source_target_pairs={{0,8},{2,10},{8,16},{10,18},{16,24},{18,26},{24,28},{26,30},{28,20... | collective-permute-start | bytes 442376 | tf_op jit(solution)/shard_map/ppermute | solution.py:127
  166.3 6.6 %collective-permute-start.41 = (bf16[48,1536]{1,0:T(8,128)(2,1)S(1)}, bf16[48,1536]{1,0:T(8,128)(2,1)S(1)}, u32[]{:S(2)}, u32[]{:S(2)}) collective-permute-start(bf16[48,1536]{1,0:T(8,128)(2,1)S(1)} %get-tuple-element.137), channel_id=1, source_target_pairs={{8,0},{10,2},{16,8},{18,10},{24,16},{26,18},{28,24},{30,26},{20,28... | collective-permute-start | bytes 442376 | tf_op jit(solution)/shard_map/ppermute | solution.py:127
  170.8 5.1 %collective-permute-start.38 = (f32[40,128]{1,0:T(8,128)S(1)}, f32[40,128]{1,0:T(8,128)S(1)}, u32[]{:S(2)}, u32[]{:S(2)}) collective-permute-start(f32[40,128]{1,0:T(8,128)S(1)} %add.336), channel_id=1, source_target_pairs={{0,4},{2,6},{4,0},{6,2},{8,12},{10,14},{12,8},{14,10},{16,20},{18,... | collective-permute-start | bytes 61448 | tf_op jit(solution)/shard_map/ppermute | solution.py:486
  172.4 8.4 %copy-start.44 = (f32[256,768]{1,0:T(8,128)S(1)}, f32[256,768]{1,0:T(8,128)}, u32[]{:S(2)}) copy-start(f32[256,768]{1,0:T(8,128)} %copy-done.43) | copy-start | bytes 2359300
  173.8 6.0 %collective-permute-start.42 = (bf16[48,1536]{1,0:T(8,128)(2,1)S(1)}, bf16[48,1536]{1,0:T(8,128)(2,1)S(1)}, u32[]{:S(2)}, u32[]{:S(2)}) collective-permute-start(bf16[48,1536]{1,0:T(8,128)(2,1)S(1)} %get-tuple-element.140), channel_id=1, source_target_pairs={{0,8},{2,10},{8,16},{10,18},{16,24},{18,26},{24,28},{26,30},{28,20... | collective-permute-start | bytes 442376 | tf_op jit(solution)/shard_map/ppermute | solution.py:127
  174.5 5.4 %collective-permute-start.43 = (bf16[48,1536]{1,0:T(8,128)(2,1)S(1)}, bf16[48,1536]{1,0:T(8,128)(2,1)S(1)}, u32[]{:S(2)}, u32[]{:S(2)}) collective-permute-start(bf16[48,1536]{1,0:T(8,128)(2,1)S(1)} %get-tuple-element.141), channel_id=1, source_target_pairs={{8,0},{10,2},{16,8},{18,10},{24,16},{26,18},{28,24},{30,26},{20,28... | collective-permute-start | bytes 442376 | tf_op jit(solution)/shard_map/ppermute | solution.py:127
  175.9 3.9 %collective-permute-start.39 = (f32[40,128]{1,0:T(8,128)S(1)}, f32[40,128]{1,0:T(8,128)S(1)}, u32[]{:S(2)}, u32[]{:S(2)}) collective-permute-start(f32[40,128]{1,0:T(8,128)S(1)} %add.340), channel_id=1, source_target_pairs={{0,8},{2,10},{4,12},{6,14},{8,0},{10,2},{12,4},{14,6},{16,24},{18,... | collective-permute-start | bytes 61448 | tf_op jit(solution)/shard_map/ppermute | solution.py:486
  179.9 7.9 %collective-permute-start.44 = (f32[40,128]{1,0:T(8,128)S(1)}, f32[40,128]{1,0:T(8,128)S(1)}, u32[]{:S(2)}, u32[]{:S(2)}) collective-permute-start(f32[40,128]{1,0:T(8,128)S(1)} %add.341), channel_id=1, source_target_pairs={{0,16},{2,18},{4,20},{6,22},{8,24},{10,26},{12,28},{14,30},{16,0},... | collective-permute-start | bytes 61448 | tf_op jit(solution)/shard_map/ppermute | solution.py:486
  183.3 6.3 %collective-permute-start.45 = (bf16[48,1536]{1,0:T(8,128)(2,1)}, bf16[48,1536]{1,0:T(8,128)(2,1)}, u32[]{:S(2)}, u32[]{:S(2)}) collective-permute-start(bf16[48,1536]{1,0:T(8,128)(2,1)} %get-tuple-element.143), channel_id=1, source_target_pairs={{0,8},{2,10},{8,16},{10,18},{16,24},{18,26},{24,28},{26,30},{28,20... | collective-permute-start | bytes 442376 | tf_op jit(solution)/shard_map/ppermute | solution.py:127
  183.9 5.7 %collective-permute-start.46 = (bf16[48,1536]{1,0:T(8,128)(2,1)}, bf16[48,1536]{1,0:T(8,128)(2,1)}, u32[]{:S(2)}, u32[]{:S(2)}) collective-permute-start(bf16[48,1536]{1,0:T(8,128)(2,1)} %get-tuple-element.144), channel_id=1, source_target_pairs={{8,0},{10,2},{16,8},{18,10},{24,16},{26,18},{28,24},{30,26},{20,28... | collective-permute-start | bytes 442376 | tf_op jit(solution)/shard_map/ppermute | solution.py:127
  187.7 4.4 %collective-permute-start.47 = (f32[48,3072]{1,0:T(8,128)}, f32[48,3072]{1,0:T(8,128)S(1)}, u32[]{:S(2)}, u32[]{:S(2)}) collective-permute-start(f32[48,3072]{1,0:T(8,128)} %get-tuple-element.149), channel_id=1, source_target_pairs={{0,2},{2,0},{4,6},{6,4},{8,10},{10,8},{12,14},{14,12},{16,18},{18,... | collective-permute-start | bytes 1769480 | tf_op jit(solution)/shard_map/ppermute | solution.py:57
  (39 other events, 108.5 us)

commit v7 on v6

--- a/solution.py
+++ b/solution.py
@@ -85,9 +85,10 @@
         if self.steps < self.reach:
             self.sent = (lax.ppermute(r, "dp", ring.right), lax.ppermute(l, "dp", ring.left))
         elif self.halves:
+            r, l = left_and_right(r, l)
             self.sent = (
-                lax.ppermute(r[:, :half], "dp", ring.right),
-                lax.ppermute(l[:, half:], "dp", ring.left),
+                lax.ppermute(r, "dp", ring.right),
+                lax.ppermute(l, "dp", ring.left),
             )
         else:
             self.sent = (lax.ppermute(r, "dp", ring.right),)
@@ -170,6 +171,26 @@
         cost_estimate=SMALL,
         name="outer",
     )(owners, *[x for pair in pairs for x in pair])
+
+
+def left_and_right(r, l):
+    rows, width = r.shape
+    half = width // 2
+
+    def kernel(r_ref, l_ref, r_out, l_out):
+        r_out[...] = r_ref[:, pl.ds(0, half)]
+        l_out[...] = l_ref[:, pl.ds(half, half)]
+
+    inside = pl.BlockSpec(memory_space=pltpu.VMEM)
+    return pl.pallas_call(
+        kernel,
+        out_shape=[jax.ShapeDtypeStruct((rows, half), BF)] * 2,
+        in_specs=[inside] * 2,
+        out_specs=[inside] * 2,
+        compiler_params=pltpu.CompilerParams(vmem_limit_bytes=RING_VMEM_BYTES),
+        cost_estimate=SMALL,
+        name="left_and_right",
+    )(r, l)
 
 
 def after(values, deps):

time: 194 us -> 193 us (level)
    ppermute x2 -> x0, starting transfers between devices: 2.03 us -> none  [the longest x1 1.56 us: step(): lax.ppermute(r[:, :half], 'dp', ring.right)]
    ppermute x14 -> x15, starting transfers between devices: 20.6 us -> 22.3 us  [step(): lax.ppermute(r, 'dp', ring.right)]
    ppermute x14 -> x15, starting transfers between devices: 9.8 us -> 10.1 us  [step(): lax.ppermute(l, 'dp', ring.left)]
    ppermute x14 -> x15, waiting for transfers between devices: 32.3 us -> 32.4 us  [step(): lax.ppermute(r, 'dp', ring.right)]
    ppermute x14 -> x15, waiting for transfers between devices: 11.1 us -> 11.2 us  [step(): lax.ppermute(l, 'dp', ring.left)]
where the time goes in v7:
time: 193 us
  waiting for transfers between devices  65.4 us (34%)
  starting transfers between devices  46.9 us (24%)
  Pallas kernels  40.1 us (21%)
  local copies, waits for them, and re-layouts  27.6 us (14%)
  other arithmetic  10.9 us (6%)
    ppermute x15, waiting for transfers between devices, step(): lax.ppermute(r, 'dp', ring.right)  32.4 us
    ppermute x15, starting transfers between devices, step(): lax.ppermute(r, 'dp', ring.right)  22.3 us
    unnamed x117, local copies, waits for them, and re-layouts  18.4 us
    ppermute x7, waiting for transfers between devices, swap_tensor(): return lax.ppermute(x, 'tensor', [(0, 1), (1, 0)])  17.3 us
    ppermute x15, waiting for transfers between devices, step(): lax.ppermute(l, 'dp', ring.left)  11.2 us
    ppermute x15, starting transfers between devices, step(): lax.ppermute(l, 'dp', ring.left)  10.1 us
    ppermute x7, starting transfers between devices, swap_tensor(): return lax.ppermute(x, 'tensor', [(0, 1), (1, 0)])  9.42 us
    pallas_call x1, Pallas kernels, expert_layers(): pl.pallas_call(kernel, out_shape=[jax.ShapeDtypeStruct((filled, 2 * d), B...  8.91 us
  transfers between devices with their start and end apart: 48, of which 24 were waited for; matrix products, arithmetic and copies ran while one was open for 10% of the time, Pallas kernels for 12%

profile of v7, /device:TPU:0, one launch (start us, length us, event | category | flops | bytes accessed | tf_op | source)
XLA Modules:
  0.0 192.6 jit_solution(12687364201943234192)
XLA Ops:
  2.4 3.0 %collective-permute-start.1 = (bf16[48,1536]{1,0:T(8,128)(2,1)S(1)}, bf16[48,1536]{1,0:T(8,128)(2,1)S(1)}, u32[]{:S(2)}, u32[]{:S(2)}) collective-permute-start(bf16[48,1536]{1,0:T(8,128)(2,1)S(1)} %constant_dynamic-update-slice_fusion.refs_0_), channel_id=1, source_target_pairs={{0,8},{2,10},{8,16},{10,18},{16,24},{18,26},{24,28},{26,30},{28,20... | collective-permute-start | bytes 442376 | tf_op jit(solution)/shard_map/ppermute | solution.py:86
  5.4 2.0 %collective-permute-start = (bf16[128,768]{1,0:T(8,128)(2,1)}, bf16[128,768]{1,0:T(8,128)(2,1)}, u32[]{:S(2)}, u32[]{:S(2)}) collective-permute-start(bf16[128,768]{1,0:T(8,128)(2,1)} %param.13), channel_id=1, source_target_pairs={{0,1},{1,0},{2,3},{3,2},{4,5},{5,4},{6,7},{7,6},{8,9},{9,8},{10,11... | collective-permute-start | bytes 589832 | tf_op jit(solution)/shard_map/ppermute | solution.py:496
  7.4 1.5 constant_dynamic-slice_fusion.4
  9.2 1.8 collective-permute-start.3
  11.1 1.6 collective-permute-start.10
  13.1 1.2 collective-permute-done.3.refs_3_
  14.3 1.8 collective-permute-start.5
  17.2 1.4 collective-permute-done.4.refs_4_
  19.4 1.8 collective-permute-start.7
  21.6 2.2 %collective-permute-done.6.refs_6_ = bf16[48,1536]{1,0:T(8,128)(2,1)S(1)} collective-permute-done((bf16[48,1536]{1,0:T(8,128)(2,1)S(1)}, bf16[48,1536]{1,0:T(8,128)(2,1)S(1)}, u32[]{:S(2)}, u32[]{:S(2)}) %collective-permute-start.6) | collective-permute-done | bytes 147488 | tf_op jit(solution)/shard_map/ppermute | solution.py:86
  24.6 2.3 %assemble.1.own_ref = bf16[384,1536]{1,0:T(8,128)(2,1)S(1)} custom-call(s32[8]{0:T(128)S(1)} %stack.30.owners_ref, bf16[48,1536]{1,0:T(8,128)(2,1)S(1)} %constant_dynamic-update-slice_fusion.refs_0_, bf16[48,1536]{1,0:T(8,128)(2,1)S(1)} %collective-permute-done.1.refs_1_, bf16[48,1536]{1,0:T(8,128)(2,1)S(1)} %collective-permute-done.2.refs_2_, ...), custom_call_target="tpu_custom_call" | custom-call | flops 1 | bytes 1 | tf_op jit(solution)/shard_map/assemble/pallas_call | solution.py:379
  27.4 1.2 maximum_select_fusion.refs_0_
  28.7 1.9 collective-permute-start.13
  32.6 1.3 maximum_select_fusion.1.x_ref
  34.9 1.3 copy-done.7
  36.2 1.3 copy-done.19
  38.4 3.5 %attention_forward.1 = (bf16[256,768]{1,0:T(8,128)(2,1)S(1)}, f32[256,1]{1,0:T(8,128)}, bf16[256,1152]{1,0:T(8,128)(2,1)S(1)}, f32[6,256,256]{2,1,0:T(8,128)S(1)...) custom-call(bf16[256,768]{1,0:T(8,128)(2,1)S(1)} %maximum_select_fusion.1.x_ref, ...), custom_call_target="tpu_custom_call" | custom-call | flops 1 | bytes 1 | tf_op jit(solution)/shard_map/attention_forward/pallas_call | solution.py:561
  44.1 1.8 collective-permute-start.9
  46.6 1.6 collective-permute-start.15
  48.7 1.3 maximum_select_fusion.2.g_ref
  50.0 5.2 %collective-permute-done.9.other_ref = bf16[256,768]{1,0:T(8,128)(2,1)S(1)} collective-permute-done((bf16[256,768]{1,0:T(8,128)(2,1)S(1)}, bf16[256,768]{1,0:T(8,128)(2,1)S(1)}, u32[]{:S(2)}, u32[]{:S(2)}) %collective-permute-start.9) | collective-permute-done | bytes 393248 | tf_op jit(solution)/shard_map/ppermute | solution.py:496
  55.2 1.1 route.1
  58.2 3.6 %collective-permute-done.15.refs_3_ = bf16[96,3072]{1,0:T(8,128)(2,1)S(1)} collective-permute-done((bf16[96,3072]{1,0:T(8,128)(2,1)}, bf16[96,3072]{1,0:T(8,128)(2,1)S(1)}, u32[]{:S(2)}, u32[]{:S(2)}) %collective-permute-start.15) | collective-permute-done | bytes 589856 | tf_op jit(solution)/shard_map/ppermute | solution.py:86
  61.7 1.3 collective-permute-done.16.refs_4_
  63.0 1.6 collective-permute-start.17
  66.7 10.0 %collective-permute-done.17.refs_5_.r_ref = bf16[96,3072]{1,0:T(8,128)(2,1)S(1)} collective-permute-done((bf16[96,3072]{1,0:T(8,128)(2,1)S(1)}, bf16[96,3072]{1,0:T(8,128)(2,1)S(1)}, u32[]{:S(2)}, u32[]{:S(2)}) %collective-permute-start.17) | collective-permute-done | bytes 589856 | tf_op jit(solution)/shard_map/ppermute | solution.py:86
  76.7 2.1 %collective-permute-done.18.refs_6_.l_ref = bf16[96,3072]{1,0:T(8,128)(2,1)S(1)} collective-permute-done((bf16[96,3072]{1,0:T(8,128)(2,1)S(1)}, bf16[96,3072]{1,0:T(8,128)(2,1)S(1)}, u32[]{:S(2)}, u32[]{:S(2)}) %collective-permute-start.18) | collective-permute-done | bytes 589856 | tf_op jit(solution)/shard_map/ppermute | solution.py:86
  81.6 1.6 collective-permute-start.19
  83.8 1.1 copy-done.9
  84.8 1.1 copy-done.11
  85.9 1.1 copy-done.13
  87.0 1.1 copy-done.25
  88.0 1.1 copy-done.27
  89.1 2.0 %place.1 = (bf16[768,1536]{1,0:T(8,128)(2,1)S(1)}, bf16[768,1536]{1,0:T(8,128)(2,1)S(1)}) custom-call(s32[7]{0:T(128)S(1)} %stack.32.owners_ref, bf16[96,3072]{1,0:T(8,128)(2,1)S(1)} %copy-done.9, bf16[96,3072]{1,0:T(8,128)(2,1)} %collective-permute-done.13.refs_1_, bf16[96,3072]{1,0:T(8,128)(2,1)} %collective-permute-done.14.refs_2_, ...), custom_call_target="tpu_custom_call" | custom-call | flops 1 | bytes 1 | tf_op jit(solution)/shard_map/place/pallas_call | solution.py:351
  91.2 8.9 %expert_layers.1 = (bf16[352,1536]{1,0:T(8,128)(2,1)S(1)}, bf16[352,1536]{1,0:T(8,128)(2,1)S(1)}, bf16[96,3072]{1,0:T(8,128)(2,1)S(1)}, bf16[96,3072]{1,0:T(8,12...) custom-call(s32[1]{0:T(128)} %bitcast.8.last_ref, ...), custom_call_target="tpu_custom_call", output_to_operand_aliasing={{10}: (4, {}), {11}: (5, {})} | custom-call | flops 1 | bytes 1 | tf_op jit(solution)/shard_map/expert_layers/pallas_call | solution.py:452
  100.4 1.6 collective-permute-start.24
  102.9 1.1 rows_back.1
  104.8 5.0 %collective-permute-done.24.refs_2_ = bf16[96,1536]{1,0:T(8,128)(2,1)S(1)} collective-permute-done((bf16[96,1536]{1,0:T(8,128)(2,1)S(1)}, bf16[96,1536]{1,0:T(8,128)(2,1)S(1)}, u32[]{:S(2)}, u32[]{:S(2)}) %collective-permute-start.24) | collective-permute-done | bytes 294944 | tf_op jit(solution)/shard_map/ppermute | solution.py:128
  109.8 1.3 collective-permute-done.25.refs_3_
  111.6 1.6 collective-permute-start.29
  114.7 8.8 %collective-permute-done.23.other_ref = bf16[256,768]{1,0:T(8,128)(2,1)S(1)} collective-permute-done((bf16[256,768]{1,0:T(8,128)(2,1)S(1)}, bf16[256,768]{1,0:T(8,128)(2,1)S(1)}, u32[]{:S(2)}, u32[]{:S(2)}) %collective-permute-start.23) | collective-permute-done | bytes 393248 | tf_op jit(solution)/shard_map/ppermute | solution.py:496
  123.6 4.7 %attention_backward.1 = (f32[256,768]{1,0:T(8,128)S(1)}, bf16[256,768]{1,0:T(8,128)(2,1)S(1)}, bf16[256,1152]{1,0:T(8,128)(2,1)S(1)}, f32[6,512]{1,0:T(8,128)S(1)}) custom-call(bf16[256,768]{1,0:T(8,128)(2,1)S(1)} %get-tuple-element.100.low_ref, bf16[256,768]{1,0:T(8,128)(2,1)S(1)} %collective-permute-done.23.other_ref, f32[256,768]{1,0:T(8,128)S(1)} %copy-done.4, ...), custom_call_target="tpu_custom_call" | custom-call | flops 1 | bytes 1 | tf_op jit(solution)/shard_map/attention_backward/pallas_call | solution.py:614
  128.3 2.6 %outer.1 = (bf16[384,1536]{1,0:T(8,128)(2,1)S(1)}, bf16[384,1536]{1,0:T(8,128)(2,1)}) custom-call(s32[16]{0:T(128)S(1)} %pad_add_fusion.owners_ref, bf16[256,768]{1,0:T(8,128)(2,1)S(1)} %copy-done.42, bf16[256,1152]{1,0:T(8,128)(2,1)S(1)} %get-tuple-element.126.grad_ref.refs_1_, bf16[256,768]{1,0:T(8,128)(2,1)S(1)} %get-tuple-element.127.refs_2_, ...), custom_call_target="tpu_custom_call" | custom-call | flops 1 | bytes 1 | tf_op jit(solution)/shard_map/outer/pallas_call | solution.py:164
  130.9 1.5 ring_add.7
  132.5 1.6 collective-permute-start.31
  134.6 1.0 fusion.6
  136.2 1.6 collective-permute-start.34
  138.4 10.5 %collective-permute-done.31.refs_2_ = bf16[96,3072]{1,0:T(8,128)(2,1)S(1)} collective-permute-done((bf16[96,3072]{1,0:T(8,128)(2,1)}, bf16[96,3072]{1,0:T(8,128)(2,1)S(1)}, u32[]{:S(2)}, u32[]{:S(2)}) %collective-permute-start.31) | collective-permute-done | bytes 589856 | tf_op jit(solution)/shard_map/ppermute | solution.py:128
  148.9 1.7 collective-permute-done.32.refs_3_
  151.3 2.6 %ring_add.8 = (bf16[96,3072]{1,0:T(8,128)(2,1)}, bf16[96,3072]{1,0:T(8,128)(2,1)}) custom-call(bf16[96,3072]{1,0:T(8,128)(2,1)S(1)} %copy-done.33, bf16[96,3072]{1,0:T(8,128)(2,1)S(1)} %copy-done.35, bf16[96,3072]{1,0:T(8,128)(2,1)S(1)} %collective-permute-done.31.refs_2_, bf16[96,3072]{1,0:T(8,128)(2,1)} %collective-permute-done.32.refs_3_), custom_call_target="tpu_custom_call" | custom-call | flops 1 | bytes 1 | tf_op jit(solution)/shard_map/ring_add/pallas_call | solution.py:265
  154.6 1.4 collective-permute-start.37
  158.6 1.1 collective-permute-start.27
  159.7 3.3 %collective-permute-done.27 = f32[40,128]{1,0:T(8,128)S(1)} collective-permute-done((f32[40,128]{1,0:T(8,128)S(1)}, f32[40,128]{1,0:T(8,128)S(1)}, u32[]{:S(2)}, u32[]{:S(2)}) %collective-permute-start.27) | collective-permute-done | bytes 20512 | tf_op jit(solution)/shard_map/ppermute | solution.py:496
  165.7 1.4 collective-permute-start.41
  167.1 1.7 add_convert_fusion
  168.8 1.1 collective-permute-done.36.r_ref
  170.2 1.4 collective-permute-start.38
  173.9 1.4 collective-permute-start.43
  176.0 3.3 %collective-permute-done.39 = f32[40,128]{1,0:T(8,128)S(1)} collective-permute-done((f32[40,128]{1,0:T(8,128)S(1)}, f32[40,128]{1,0:T(8,128)S(1)}, u32[]{:S(2)}, u32[]{:S(2)}) %collective-permute-start.39) | collective-permute-done | bytes 20512 | tf_op jit(solution)/shard_map/ppermute | solution.py:507
  181.1 1.6 ring_add.11
  183.3 1.4 collective-permute-start.46
  184.7 2.3 %ring_total.1 = (f32[48,3072]{1,0:T(8,128)S(1)}, f32[48,3072]{1,0:T(8,128)}) custom-call(s32[1]{0:T(128)} %bitcast.core_ref, bf16[96,3072]{1,0:T(8,128)(2,1)S(1)} %copy-done.29, bf16[96,3072]{1,0:T(8,128)(2,1)} %collective-permute-done.36.r_ref, bf16[96,3072]{1,0:T(8,128)(2,1)} %collective-permute-done.37.l_ref), custom_call_target="tpu_custom_call" | custom-call | flops 1 | bytes 1 | tf_op jit(solution)/shard_map/ring_total/pallas_call | solution.py:295
  189.0 1.1 convert_add_fusion
  191.4 1.2 combine.1
  (222 shorter events, 41.8 us)
Async XLA Ops:
  0.6 20.6 %copy-start = (f32[32,12]{0,1:T(8,128)S(1)}, f32[32,12]{0,1:T(8,128)}, u32[]{:S(2)}) copy-start(f32[32,12]{0,1:T(8,128)} %param.17) | copy-start | bytes 4612
  2.4 6.8 %collective-permute-start.1 = (bf16[48,1536]{1,0:T(8,128)(2,1)S(1)}, bf16[48,1536]{1,0:T(8,128)(2,1)S(1)}, u32[]{:S(2)}, u32[]{:S(2)}) collective-permute-start(bf16[48,1536]{1,0:T(8,128)(2,1)S(1)} %constant_dynamic-update-slice_fusion.refs_0_), channel_id=1, source_target_pairs={{0,8},{2,10},{8,16},{10,18},{16,24},{18,26},{24,28},{26,30},{28,20... | collective-permute-start | bytes 442376 | tf_op jit(solution)/shard_map/ppermute | solution.py:86
  5.4 7.3 %collective-permute-start.2 = (bf16[48,1536]{1,0:T(8,128)(2,1)S(1)}, bf16[48,1536]{1,0:T(8,128)(2,1)S(1)}, u32[]{:S(2)}, u32[]{:S(2)}) collective-permute-start(bf16[48,1536]{1,0:T(8,128)(2,1)S(1)} %constant_dynamic-update-slice_fusion.refs_0_), channel_id=1, source_target_pairs={{8,0},{10,2},{16,8},{18,10},{24,16},{26,18},{28,24},{30,26},{20,28... | collective-permute-start | bytes 442376 | tf_op jit(solution)/shard_map/ppermute | solution.py:86
  5.4 23.3 %collective-permute-start = (bf16[128,768]{1,0:T(8,128)(2,1)}, bf16[128,768]{1,0:T(8,128)(2,1)}, u32[]{:S(2)}, u32[]{:S(2)}) collective-permute-start(bf16[128,768]{1,0:T(8,128)(2,1)} %param.13), channel_id=1, source_target_pairs={{0,1},{1,0},{2,3},{3,2},{4,5},{5,4},{6,7},{7,6},{8,9},{9,8},{10,11... | collective-permute-start | bytes 589832 | tf_op jit(solution)/shard_map/ppermute | solution.py:496
  7.4 8.8 %copy-start.51 = (s32[256,1]{0,1:T(1,128)S(1)}, s32[256,1]{0,1:T(1,128)}, u32[]{:S(2)}) copy-start(s32[256,1]{0,1:T(1,128)} %param.23) | copy-start | bytes 3076
  7.4 13.9 %copy-start.53 = (s32[511]{0:T(512)S(1)}, s32[511]{0:T(512)}, u32[]{:S(2)}) copy-start(s32[511]{0:T(512)} %param.24) | copy-start | bytes 6136
  9.2 5.1 %collective-permute-start.3 = (bf16[48,1536]{1,0:T(8,128)(2,1)S(1)}, bf16[48,1536]{1,0:T(8,128)(2,1)S(1)}, u32[]{:S(2)}, u32[]{:S(2)}) collective-permute-start(bf16[48,1536]{1,0:T(8,128)(2,1)S(1)} %collective-permute-done.1.refs_1_), channel_id=1, source_target_pairs={{0,8},{2,10},{8,16},{10,18},{16,24},{18,26},{24,28},{26,30},{28,20... | collective-permute-start | bytes 442376 | tf_op jit(solution)/shard_map/ppermute | solution.py:86
  11.0 16.4 %collective-permute-start.12 = (bf16[48,3072]{1,0:T(8,128)(2,1)S(1)}, bf16[48,3072]{1,0:T(8,128)(2,1)}, u32[]{:S(2)}, u32[]{:S(2)}) collective-permute-start(bf16[48,3072]{1,0:T(8,128)(2,1)S(1)} %pad_maximum_fusion), channel_id=1, source_target_pairs={{0,2},{2,0},{4,6},{6,4},{8,10},{10,8},{12,14},{14,12},{16,18},{18,... | collective-permute-start | bytes 884744 | tf_op jit(solution)/shard_map/ppermute | solution.py:57
  11.1 17.6 %collective-permute-start.10 = (bf16[128,768]{1,0:T(8,128)(2,1)}, bf16[128,768]{1,0:T(8,128)(2,1)}, u32[]{:S(2)}, u32[]{:S(2)}) collective-permute-start(bf16[128,768]{1,0:T(8,128)(2,1)} %param.25), channel_id=1, source_target_pairs={{0,1},{1,0},{2,3},{3,2},{4,5},{5,4},{6,7},{7,6},{8,9},{9,8},{10,11... | collective-permute-start | bytes 589832 | tf_op jit(solution)/shard_map/ppermute | solution.py:496
  12.7 5.9 %collective-permute-start.4 = (bf16[48,1536]{1,0:T(8,128)(2,1)S(1)}, bf16[48,1536]{1,0:T(8,128)(2,1)S(1)}, u32[]{:S(2)}, u32[]{:S(2)}) collective-permute-start(bf16[48,1536]{1,0:T(8,128)(2,1)S(1)} %collective-permute-done.2.refs_2_), channel_id=1, source_target_pairs={{8,0},{10,2},{16,8},{18,10},{24,16},{26,18},{28,24},{30,26},{20,28... | collective-permute-start | bytes 442376 | tf_op jit(solution)/shard_map/ppermute | solution.py:86
  14.3 5.1 %collective-permute-start.5 = (bf16[48,1536]{1,0:T(8,128)(2,1)S(1)}, bf16[48,1536]{1,0:T(8,128)(2,1)S(1)}, u32[]{:S(2)}, u32[]{:S(2)}) collective-permute-start(bf16[48,1536]{1,0:T(8,128)(2,1)S(1)} %collective-permute-done.3.refs_3_), channel_id=1, source_target_pairs={{0,8},{2,10},{8,16},{10,18},{16,24},{18,26},{24,28},{26,30},{28,20... | collective-permute-start | bytes 442376 | tf_op jit(solution)/shard_map/ppermute | solution.py:86
  18.6 5.2 %collective-permute-start.6 = (bf16[48,1536]{1,0:T(8,128)(2,1)S(1)}, bf16[48,1536]{1,0:T(8,128)(2,1)S(1)}, u32[]{:S(2)}, u32[]{:S(2)}) collective-permute-start(bf16[48,1536]{1,0:T(8,128)(2,1)S(1)} %collective-permute-done.4.refs_4_), channel_id=1, source_target_pairs={{8,0},{10,2},{16,8},{18,10},{24,16},{26,18},{28,24},{30,26},{20,28... | collective-permute-start | bytes 442376 | tf_op jit(solution)/shard_map/ppermute | solution.py:86
  19.4 5.1 %collective-permute-start.7 = (bf16[48,1536]{1,0:T(8,128)(2,1)S(1)}, bf16[48,1536]{1,0:T(8,128)(2,1)S(1)}, u32[]{:S(2)}, u32[]{:S(2)}) collective-permute-start(bf16[48,1536]{1,0:T(8,128)(2,1)S(1)} %collective-permute-done.5.refs_5_), channel_id=1, source_target_pairs={{0,8},{2,10},{8,16},{10,18},{16,24},{18,26},{24,28},{26,30},{28,20... | collective-permute-start | bytes 442376 | tf_op jit(solution)/shard_map/ppermute | solution.py:94
  26.9 7.0 %collective-permute-start.8 = (bf16[384,1536]{1,0:T(8,128)(2,1)S(1)}, bf16[384,1536]{1,0:T(8,128)(2,1)S(1)}, u32[]{:S(2)}, u32[]{:S(2)}) collective-permute-start(bf16[384,1536]{1,0:T(8,128)(2,1)S(1)} %assemble.1.own_ref), channel_id=1, source_target_pairs={{0,2},{2,0},{4,6},{6,4},{8,10},{10,8},{12,14},{14,12},{16,18},{18,... | collective-permute-start | bytes 3538952 | tf_op jit(solution)/shard_map/ppermute | solution.py:57
  28.7 9.0 %copy-start.8 = (bf16[96,3072]{1,0:T(8,128)(2,1)}, bf16[96,3072]{1,0:T(8,128)(2,1)S(1)}, u32[]{:S(2)}) copy-start(bf16[96,3072]{1,0:T(8,128)(2,1)S(1)} %maximum_select_fusion.refs_0_) | copy-start | bytes 1769476
  28.7 17.9 %collective-permute-start.13 = (bf16[96,3072]{1,0:T(8,128)(2,1)S(1)}, bf16[96,3072]{1,0:T(8,128)(2,1)}, u32[]{:S(2)}, u32[]{:S(2)}) collective-permute-start(bf16[96,3072]{1,0:T(8,128)(2,1)S(1)} %maximum_select_fusion.refs_0_), channel_id=1, source_target_pairs={{0,8},{2,10},{8,16},{10,18},{16,24},{18,26},{24,28},{26,30},{28,20... | collective-permute-start | bytes 1769480 | tf_op jit(solution)/shard_map/ppermute | solution.py:86
  30.6 17.6 %collective-permute-start.14 = (bf16[96,3072]{1,0:T(8,128)(2,1)S(1)}, bf16[96,3072]{1,0:T(8,128)(2,1)}, u32[]{:S(2)}, u32[]{:S(2)}) collective-permute-start(bf16[96,3072]{1,0:T(8,128)(2,1)S(1)} %maximum_select_fusion.refs_0_), channel_id=1, source_target_pairs={{8,0},{10,2},{16,8},{18,10},{24,16},{26,18},{28,24},{30,26},{20,28... | collective-permute-start | bytes 1769480 | tf_op jit(solution)/shard_map/ppermute | solution.py:86
  37.6 85.9 %copy-start.1 = (bf16[768,1536]{1,0:T(8,128)(2,1)}, bf16[768,1536]{1,0:T(8,128)(2,1)S(1)}, u32[]{:S(2)}) copy-start(bf16[768,1536]{1,0:T(8,128)(2,1)S(1)} %interleave.1.w_ref) | copy-start | bytes 7077892
  44.1 12.1 %copy-start.16 = (f32[6,256,256]{2,1,0:T(8,128)}, f32[6,256,256]{2,1,0:T(8,128)S(1)}, u32[]{:S(2)}) copy-start(f32[6,256,256]{2,1,0:T(8,128)S(1)} %get-tuple-element.106.p_ref) | copy-start | bytes 4718596
  44.1 11.0 %copy-start.47 = (f32[768,2]{0,1:T(2,128)S(1)}, f32[768,2]{0,1:T(2,128)}, u32[]{:S(2)}) copy-start(f32[768,2]{0,1:T(2,128)} %param.19) | copy-start | bytes 18436
  44.1 11.0 %collective-permute-start.9 = (bf16[256,768]{1,0:T(8,128)(2,1)S(1)}, bf16[256,768]{1,0:T(8,128)(2,1)S(1)}, u32[]{:S(2)}, u32[]{:S(2)}) collective-permute-start(bf16[256,768]{1,0:T(8,128)(2,1)S(1)} %get-tuple-element.83.part_ref), channel_id=1, source_target_pairs={{0,1},{1,0},{2,3},{3,2},{4,5},{5,4},{6,7},{7,6},{8,9},{9,8},{10,11... | collective-permute-start | bytes 1179656 | tf_op jit(solution)/shard_map/ppermute | solution.py:496
  46.6 15.2 %collective-permute-start.15 = (bf16[96,3072]{1,0:T(8,128)(2,1)}, bf16[96,3072]{1,0:T(8,128)(2,1)S(1)}, u32[]{:S(2)}, u32[]{:S(2)}) collective-permute-start(bf16[96,3072]{1,0:T(8,128)(2,1)} %collective-permute-done.13.refs_1_), channel_id=1, source_target_pairs={{0,8},{2,10},{8,16},{10,18},{16,24},{18,26},{24,28},{26,30},{28,20... | collective-permute-start | bytes 1769480 | tf_op jit(solution)/shard_map/ppermute | solution.py:86
  48.2 14.8 %collective-permute-start.16 = (bf16[96,3072]{1,0:T(8,128)(2,1)}, bf16[96,3072]{1,0:T(8,128)(2,1)S(1)}, u32[]{:S(2)}, u32[]{:S(2)}) collective-permute-start(bf16[96,3072]{1,0:T(8,128)(2,1)} %collective-permute-done.14.refs_2_), channel_id=1, source_target_pairs={{8,0},{10,2},{16,8},{18,10},{24,16},{26,18},{28,24},{30,26},{20,28... | collective-permute-start | bytes 1769480 | tf_op jit(solution)/shard_map/ppermute | solution.py:86
  57.2 21.7 %collective-permute-start.11 = (bf16[352,1536]{1,0:T(8,128)(2,1)S(1)}, bf16[352,1536]{1,0:T(8,128)(2,1)S(1)}, u32[]{:S(2)}, u32[]{:S(2)}) collective-permute-start(bf16[352,1536]{1,0:T(8,128)(2,1)S(1)} %get-tuple-element.85.own_hbm), channel_id=1, source_target_pairs={{0,2},{2,0},{4,6},{6,4},{8,10},{10,8},{12,14},{14,12},{16,18},{18,... | collective-permute-start | bytes 3244040 | tf_op jit(solution)/shard_map/ppermute | solution.py:57
  63.0 13.7 %collective-permute-start.17 = (bf16[96,3072]{1,0:T(8,128)(2,1)S(1)}, bf16[96,3072]{1,0:T(8,128)(2,1)S(1)}, u32[]{:S(2)}, u32[]{:S(2)}) collective-permute-start(bf16[96,3072]{1,0:T(8,128)(2,1)S(1)} %collective-permute-done.15.refs_3_), channel_id=1, source_target_pairs={{0,8},{2,10},{8,16},{10,18},{16,24},{18,26},{24,28},{26,30},{28,20... | collective-permute-start | bytes 1769480 | tf_op jit(solution)/shard_map/ppermute | solution.py:86
  65.4 13.4 %collective-permute-start.18 = (bf16[96,3072]{1,0:T(8,128)(2,1)S(1)}, bf16[96,3072]{1,0:T(8,128)(2,1)S(1)}, u32[]{:S(2)}, u32[]{:S(2)}) collective-permute-start(bf16[96,3072]{1,0:T(8,128)(2,1)S(1)} %collective-permute-done.16.refs_4_), channel_id=1, source_target_pairs={{8,0},{10,2},{16,8},{18,10},{24,16},{26,18},{28,24},{30,26},{20,28... | collective-permute-start | bytes 1769480 | tf_op jit(solution)/shard_map/ppermute | solution.py:86
  81.6 9.6 %collective-permute-start.19 = (bf16[96,1536]{1,0:T(8,128)(2,1)}, bf16[96,1536]{1,0:T(8,128)(2,1)}, u32[]{:S(2)}, u32[]{:S(2)}) collective-permute-start(bf16[96,1536]{1,0:T(8,128)(2,1)} %get-tuple-element.94), channel_id=1, source_target_pairs={{0,8},{2,10},{8,16},{10,18},{16,24},{18,26},{24,28},{26,30},{28,20... | collective-permute-start | bytes 884744 | tf_op jit(solution)/shard_map/ppermute | solution.py:90
  83.1 8.0 %collective-permute-start.20 = (bf16[96,1536]{1,0:T(8,128)(2,1)}, bf16[96,1536]{1,0:T(8,128)(2,1)}, u32[]{:S(2)}, u32[]{:S(2)}) collective-permute-start(bf16[96,1536]{1,0:T(8,128)(2,1)} %get-tuple-element.95), channel_id=1, source_target_pairs={{8,0},{10,2},{16,8},{18,10},{24,16},{26,18},{28,24},{30,26},{20,28... | collective-permute-start | bytes 884744 | tf_op jit(solution)/shard_map/ppermute | solution.py:91
  91.2 11.7 %copy-start.4 = (f32[256,768]{1,0:T(8,128)S(1)}, f32[256,768]{1,0:T(8,128)}, u32[]{:S(2)}) copy-start(f32[256,768]{1,0:T(8,128)} %copy-done.3) | copy-start | bytes 2359300
  91.2 11.7 %copy-start.36 = (s32[256,1]{1,0:T(8,128)S(1)}, s32[256,1]{1,0:T(8,128)}, u32[]{:S(2)}) copy-start(s32[256,1]{1,0:T(8,128)} %get-tuple-element.200.flat_ref) | copy-start | bytes 3076
  100.1 2.8 %collective-permute-start.21 = (bf16[352,1536]{1,0:T(8,128)(2,1)S(1)}, bf16[352,1536]{1,0:T(8,128)(2,1)S(1)}, u32[]{:S(2)}, u32[]{:S(2)}) collective-permute-start(bf16[352,1536]{1,0:T(8,128)(2,1)S(1)} %get-tuple-element.97), channel_id=1, source_target_pairs={{0,2},{2,0},{4,6},{6,4},{8,10},{10,8},{12,14},{14,12},{16,18},{18,... | collective-permute-start | bytes 3244040 | tf_op jit(solution)/shard_map/ppermute | solution.py:57
  100.4 9.5 %collective-permute-start.24 = (bf16[96,1536]{1,0:T(8,128)(2,1)S(1)}, bf16[96,1536]{1,0:T(8,128)(2,1)S(1)}, u32[]{:S(2)}, u32[]{:S(2)}) collective-permute-start(bf16[96,1536]{1,0:T(8,128)(2,1)S(1)} %get-tuple-element.102), channel_id=1, source_target_pairs={{0,8},{2,10},{8,16},{10,18},{16,24},{18,26},{24,28},{26,30},{28,20... | collective-permute-start | bytes 884744 | tf_op jit(solution)/shard_map/ppermute | solution.py:128
  102.0 9.1 %collective-permute-start.25 = (bf16[96,1536]{1,0:T(8,128)(2,1)S(1)}, bf16[96,1536]{1,0:T(8,128)(2,1)S(1)}, u32[]{:S(2)}, u32[]{:S(2)}) collective-permute-start(bf16[96,1536]{1,0:T(8,128)(2,1)S(1)} %get-tuple-element.103), channel_id=1, source_target_pairs={{8,0},{10,2},{16,8},{18,10},{24,16},{26,18},{28,24},{30,26},{20,28... | collective-permute-start | bytes 884744 | tf_op jit(solution)/shard_map/ppermute | solution.py:128
  102.9 20.6 %copy-start.31 = (bf16[256,1152]{1,0:T(8,128)(2,1)S(1)}, bf16[256,1152]{1,0:T(8,128)(2,1)}, u32[]{:S(2)}) copy-start(bf16[256,1152]{1,0:T(8,128)(2,1)} %copy-done.30) | copy-start | bytes 1769476
  104.8 18.7 %copy-start.17 = (f32[6,256,256]{2,1,0:T(8,128)S(1)}, f32[6,256,256]{2,1,0:T(8,128)}, u32[]{:S(2)}) copy-start(f32[6,256,256]{2,1,0:T(8,128)} %copy-done.16) | copy-start | bytes 4718596
  111.6 16.7 %collective-permute-start.29 = (bf16[96,3072]{1,0:T(8,128)(2,1)S(1)}, bf16[96,3072]{1,0:T(8,128)(2,1)S(1)}, u32[]{:S(2)}, u32[]{:S(2)}) collective-permute-start(bf16[96,3072]{1,0:T(8,128)(2,1)S(1)} %get-tuple-element.121), channel_id=1, source_target_pairs={{0,8},{2,10},{8,16},{10,18},{16,24},{18,26},{24,28},{26,30},{28,20... | collective-permute-start | bytes 1769480 | tf_op jit(solution)/shard_map/ppermute | solution.py:128
  113.2 15.1 %collective-permute-start.30 = (bf16[96,3072]{1,0:T(8,128)(2,1)S(1)}, bf16[96,3072]{1,0:T(8,128)(2,1)S(1)}, u32[]{:S(2)}, u32[]{:S(2)}) collective-permute-start(bf16[96,3072]{1,0:T(8,128)(2,1)S(1)} %get-tuple-element.122), channel_id=1, source_target_pairs={{8,0},{10,2},{16,8},{18,10},{24,16},{26,18},{28,24},{30,26},{20,28... | collective-permute-start | bytes 1769480 | tf_op jit(solution)/shard_map/ppermute | solution.py:128
  113.7 9.9 %collective-permute-start.23 = (bf16[256,768]{1,0:T(8,128)(2,1)S(1)}, bf16[256,768]{1,0:T(8,128)(2,1)S(1)}, u32[]{:S(2)}, u32[]{:S(2)}) collective-permute-start(bf16[256,768]{1,0:T(8,128)(2,1)S(1)} %get-tuple-element.100.low_ref), channel_id=1, source_target_pairs={{0,1},{1,0},{2,3},{3,2},{4,5},{5,4},{6,7},{7,6},{8,9},{9,8},{10,11... | collective-permute-start | bytes 1179656 | tf_op jit(solution)/shard_map/ppermute | solution.py:496
  130.9 4.8 %collective-permute-start.33 = (bf16[384,1536]{1,0:T(8,128)(2,1)}, bf16[384,1536]{1,0:T(8,128)(2,1)S(1)}, u32[]{:S(2)}, u32[]{:S(2)}) collective-permute-start(bf16[384,1536]{1,0:T(8,128)(2,1)} %get-tuple-element.130), channel_id=1, source_target_pairs={{0,2},{2,0},{4,6},{6,4},{8,10},{10,8},{12,14},{14,12},{16,18},{18,... | collective-permute-start | bytes 3538952 | tf_op jit(solution)/shard_map/ppermute | solution.py:57
  132.5 16.4 %collective-permute-start.31 = (bf16[96,3072]{1,0:T(8,128)(2,1)}, bf16[96,3072]{1,0:T(8,128)(2,1)S(1)}, u32[]{:S(2)}, u32[]{:S(2)}) collective-permute-start(bf16[96,3072]{1,0:T(8,128)(2,1)} %get-tuple-element.123), channel_id=1, source_target_pairs={{0,8},{2,10},{8,16},{10,18},{16,24},{18,26},{24,28},{26,30},{28,20... | collective-permute-start | bytes 1769480 | tf_op jit(solution)/shard_map/ppermute | solution.py:128
  134.0 16.5 %collective-permute-start.32 = (bf16[96,3072]{1,0:T(8,128)(2,1)}, bf16[96,3072]{1,0:T(8,128)(2,1)}, u32[]{:S(2)}, u32[]{:S(2)}) collective-permute-start(bf16[96,3072]{1,0:T(8,128)(2,1)} %get-tuple-element.124), channel_id=1, source_target_pairs={{8,0},{10,2},{16,8},{18,10},{24,16},{26,18},{28,24},{30,26},{20,28... | collective-permute-start | bytes 1769480 | tf_op jit(solution)/shard_map/ppermute | solution.py:128
  135.8 15.5 %copy-start.33 = (bf16[96,3072]{1,0:T(8,128)(2,1)S(1)}, bf16[96,3072]{1,0:T(8,128)(2,1)}, u32[]{:S(2)}) copy-start(bf16[96,3072]{1,0:T(8,128)(2,1)} %copy-done.32) | copy-start | bytes 1769476
  135.8 15.5 %copy-start.35 = (bf16[96,3072]{1,0:T(8,128)(2,1)S(1)}, bf16[96,3072]{1,0:T(8,128)(2,1)}, u32[]{:S(2)}) copy-start(bf16[96,3072]{1,0:T(8,128)(2,1)} %copy-done.34) | copy-start | bytes 1769476
  135.8 20.2 %copy-start.39 = (bf16[256,768]{1,0:T(8,128)(2,1)S(1)}, bf16[256,768]{1,0:T(8,128)(2,1)}, u32[]{:S(2)}) copy-start(bf16[256,768]{1,0:T(8,128)(2,1)} %copy-done.38) | copy-start | bytes 1179652
  136.2 14.3 %collective-permute-start.34 = (bf16[48,768]{1,0:T(8,128)(2,1)S(1)}, bf16[48,768]{1,0:T(8,128)(2,1)S(1)}, u32[]{:S(2)}, u32[]{:S(2)}) collective-permute-start(bf16[48,768]{1,0:T(8,128)(2,1)S(1)} %get-tuple-element.131), channel_id=1, source_target_pairs={{0,8},{2,10},{8,16},{10,18},{16,24},{18,26},{24,28},{26,30},{28,20... | collective-permute-start | bytes 221192 | tf_op jit(solution)/shard_map/ppermute | solution.py:128
  137.8 13.5 %collective-permute-start.35 = (bf16[48,768]{1,0:T(8,128)(2,1)S(1)}, bf16[48,768]{1,0:T(8,128)(2,1)S(1)}, u32[]{:S(2)}, u32[]{:S(2)}) collective-permute-start(bf16[48,768]{1,0:T(8,128)(2,1)S(1)} %get-tuple-element.132), channel_id=1, source_target_pairs={{8,0},{10,2},{16,8},{18,10},{24,16},{26,18},{28,24},{30,26},{20,28... | collective-permute-start | bytes 221192 | tf_op jit(solution)/shard_map/ppermute | solution.py:128
  138.3 19.4 %copy-start.15 = (bf16[256,1152]{1,0:T(8,128)(2,1)S(1)}, bf16[256,1152]{1,0:T(8,128)(2,1)}, u32[]{:S(2)}) copy-start(bf16[256,1152]{1,0:T(8,128)(2,1)} %copy-done.14) | copy-start | bytes 1769476
  154.0 15.9 %collective-permute-start.36 = (bf16[96,3072]{1,0:T(8,128)(2,1)}, bf16[96,3072]{1,0:T(8,128)(2,1)}, u32[]{:S(2)}, u32[]{:S(2)}) collective-permute-start(bf16[96,3072]{1,0:T(8,128)(2,1)} %get-tuple-element.135), channel_id=1, source_target_pairs={{0,8},{2,10},{8,16},{10,18},{16,24},{18,26},{24,28},{26,30},{28,20... | collective-permute-start | bytes 1769480 | tf_op jit(solution)/shard_map/ppermute | solution.py:128
  154.6 15.6 %collective-permute-start.37 = (bf16[96,3072]{1,0:T(8,128)(2,1)}, bf16[96,3072]{1,0:T(8,128)(2,1)}, u32[]{:S(2)}, u32[]{:S(2)}) collective-permute-start(bf16[96,3072]{1,0:T(8,128)(2,1)} %get-tuple-element.136), channel_id=1, source_target_pairs={{8,0},{10,2},{16,8},{18,10},{24,16},{26,18},{28,24},{30,26},{20,28... | collective-permute-start | bytes 1769480 | tf_op jit(solution)/shard_map/ppermute | solution.py:128
  156.7 8.3 %collective-permute-start.22 = (bf16[128,768]{1,0:T(8,128)(2,1)}, bf16[128,768]{1,0:T(8,128)(2,1)}, u32[]{:S(2)}, u32[]{:S(2)}) collective-permute-start(bf16[128,768]{1,0:T(8,128)(2,1)} %constant_dynamic-slice_fusion.1), channel_id=1, source_target_pairs={{0,1},{1,0},{2,3},{3,2},{4,5},{5,4},{6,7},{7,6},{8,9},{9,8},{10,11... | collective-permute-start | bytes 589832 | tf_op jit(solution)/shard_map/ppermute | solution.py:496
  158.6 4.5 %collective-permute-start.27 = (f32[40,128]{1,0:T(8,128)S(1)}, f32[40,128]{1,0:T(8,128)S(1)}, u32[]{:S(2)}, u32[]{:S(2)}) collective-permute-start(f32[40,128]{1,0:T(8,128)S(1)} %get-tuple-element.112), channel_id=1, source_target_pairs={{0,1},{1,0},{2,3},{3,2},{4,5},{5,4},{6,7},{7,6},{8,9},{9,8},{10,11... | collective-permute-start | bytes 61448 | tf_op jit(solution)/shard_map/ppermute | solution.py:496
  163.0 2.6 %collective-permute-start.28 = (f32[40,128]{1,0:T(8,128)S(1)}, f32[40,128]{1,0:T(8,128)S(1)}, u32[]{:S(2)}, u32[]{:S(2)}) collective-permute-start(f32[40,128]{1,0:T(8,128)S(1)} %add.335), channel_id=1, source_target_pairs={{0,2},{2,0},{4,6},{6,4},{8,10},{10,8},{12,14},{14,12},{16,18},{18,... | collective-permute-start | bytes 61448 | tf_op jit(solution)/shard_map/ppermute | solution.py:57
  163.1 8.5 %collective-permute-start.26 = (bf16[128,768]{1,0:T(8,128)(2,1)S(1)}, bf16[128,768]{1,0:T(8,128)(2,1)S(1)}, u32[]{:S(2)}, u32[]{:S(2)}) collective-permute-start(bf16[128,768]{1,0:T(8,128)(2,1)S(1)} %constant_dynamic-slice_fusion), channel_id=1, source_target_pairs={{0,1},{1,0},{2,3},{3,2},{4,5},{5,4},{6,7},{7,6},{8,9},{9,8},{10,11... | collective-permute-start | bytes 589832 | tf_op jit(solution)/shard_map/ppermute | solution.py:496
  165.0 7.2 %collective-permute-start.40 = (bf16[48,1536]{1,0:T(8,128)(2,1)S(1)}, bf16[48,1536]{1,0:T(8,128)(2,1)S(1)}, u32[]{:S(2)}, u32[]{:S(2)}) collective-permute-start(bf16[48,1536]{1,0:T(8,128)(2,1)S(1)} %get-tuple-element.140), channel_id=1, source_target_pairs={{0,8},{2,10},{8,16},{10,18},{16,24},{18,26},{24,28},{26,30},{28,20... | collective-permute-start | bytes 442376 | tf_op jit(solution)/shard_map/ppermute | solution.py:128
  165.7 6.7 %collective-permute-start.41 = (bf16[48,1536]{1,0:T(8,128)(2,1)S(1)}, bf16[48,1536]{1,0:T(8,128)(2,1)S(1)}, u32[]{:S(2)}, u32[]{:S(2)}) collective-permute-start(bf16[48,1536]{1,0:T(8,128)(2,1)S(1)} %get-tuple-element.141), channel_id=1, source_target_pairs={{8,0},{10,2},{16,8},{18,10},{24,16},{26,18},{28,24},{30,26},{20,28... | collective-permute-start | bytes 442376 | tf_op jit(solution)/shard_map/ppermute | solution.py:128
  170.2 5.1 %collective-permute-start.38 = (f32[40,128]{1,0:T(8,128)S(1)}, f32[40,128]{1,0:T(8,128)S(1)}, u32[]{:S(2)}, u32[]{:S(2)}) collective-permute-start(f32[40,128]{1,0:T(8,128)S(1)} %add.336), channel_id=1, source_target_pairs={{0,4},{2,6},{4,0},{6,2},{8,12},{10,14},{12,8},{14,10},{16,20},{18,... | collective-permute-start | bytes 61448 | tf_op jit(solution)/shard_map/ppermute | solution.py:507
  171.8 8.3 %copy-start.44 = (f32[256,768]{1,0:T(8,128)S(1)}, f32[256,768]{1,0:T(8,128)}, u32[]{:S(2)}) copy-start(f32[256,768]{1,0:T(8,128)} %copy-done.43) | copy-start | bytes 2359300
  173.2 6.0 %collective-permute-start.42 = (bf16[48,1536]{1,0:T(8,128)(2,1)S(1)}, bf16[48,1536]{1,0:T(8,128)(2,1)S(1)}, u32[]{:S(2)}, u32[]{:S(2)}) collective-permute-start(bf16[48,1536]{1,0:T(8,128)(2,1)S(1)} %get-tuple-element.144), channel_id=1, source_target_pairs={{0,8},{2,10},{8,16},{10,18},{16,24},{18,26},{24,28},{26,30},{28,20... | collective-permute-start | bytes 442376 | tf_op jit(solution)/shard_map/ppermute | solution.py:128
  173.9 5.4 %collective-permute-start.43 = (bf16[48,1536]{1,0:T(8,128)(2,1)S(1)}, bf16[48,1536]{1,0:T(8,128)(2,1)S(1)}, u32[]{:S(2)}, u32[]{:S(2)}) collective-permute-start(bf16[48,1536]{1,0:T(8,128)(2,1)S(1)} %get-tuple-element.145), channel_id=1, source_target_pairs={{8,0},{10,2},{16,8},{18,10},{24,16},{26,18},{28,24},{30,26},{20,28... | collective-permute-start | bytes 442376 | tf_op jit(solution)/shard_map/ppermute | solution.py:128
  175.3 3.9 %collective-permute-start.39 = (f32[40,128]{1,0:T(8,128)S(1)}, f32[40,128]{1,0:T(8,128)S(1)}, u32[]{:S(2)}, u32[]{:S(2)}) collective-permute-start(f32[40,128]{1,0:T(8,128)S(1)} %add.340), channel_id=1, source_target_pairs={{0,8},{2,10},{4,12},{6,14},{8,0},{10,2},{12,4},{14,6},{16,24},{18,... | collective-permute-start | bytes 61448 | tf_op jit(solution)/shard_map/ppermute | solution.py:507
  179.3 7.9 %collective-permute-start.44 = (f32[40,128]{1,0:T(8,128)S(1)}, f32[40,128]{1,0:T(8,128)S(1)}, u32[]{:S(2)}, u32[]{:S(2)}) collective-permute-start(f32[40,128]{1,0:T(8,128)S(1)} %add.341), channel_id=1, source_target_pairs={{0,16},{2,18},{4,20},{6,22},{8,24},{10,26},{12,28},{14,30},{16,0},... | collective-permute-start | bytes 61448 | tf_op jit(solution)/shard_map/ppermute | solution.py:507
  182.7 6.3 %collective-permute-start.45 = (bf16[48,1536]{1,0:T(8,128)(2,1)}, bf16[48,1536]{1,0:T(8,128)(2,1)}, u32[]{:S(2)}, u32[]{:S(2)}) collective-permute-start(bf16[48,1536]{1,0:T(8,128)(2,1)} %get-tuple-element.147), channel_id=1, source_target_pairs={{0,8},{2,10},{8,16},{10,18},{16,24},{18,26},{24,28},{26,30},{28,20... | collective-permute-start | bytes 442376 | tf_op jit(solution)/shard_map/ppermute | solution.py:128
  183.3 5.7 %collective-permute-start.46 = (bf16[48,1536]{1,0:T(8,128)(2,1)}, bf16[48,1536]{1,0:T(8,128)(2,1)}, u32[]{:S(2)}, u32[]{:S(2)}) collective-permute-start(bf16[48,1536]{1,0:T(8,128)(2,1)} %get-tuple-element.148), channel_id=1, source_target_pairs={{8,0},{10,2},{16,8},{18,10},{24,16},{26,18},{28,24},{30,26},{20,28... | collective-permute-start | bytes 442376 | tf_op jit(solution)/shard_map/ppermute | solution.py:128
  187.1 4.4 %collective-permute-start.47 = (f32[48,3072]{1,0:T(8,128)}, f32[48,3072]{1,0:T(8,128)S(1)}, u32[]{:S(2)}, u32[]{:S(2)}) collective-permute-start(f32[48,3072]{1,0:T(8,128)} %get-tuple-element.153), channel_id=1, source_target_pairs={{0,2},{2,0},{4,6},{6,4},{8,10},{10,8},{12,14},{14,12},{16,18},{18,... | collective-permute-start | bytes 1769480 | tf_op jit(solution)/shard_map/ppermute | solution.py:57
  (39 other events, 106.2 us)
